TPU v7x, 32 devices: a whole 2x2x4 slice. The times are simulated.
32 devices in a mesh: groups: 2 (over y), tiles: 16 (over z, x, core).
Axes of the slice: x: 2, y: 2, z: 4, core: 2. Of those that a mesh axis runs over, the one named last changes fastest.
Arguments:
- node_latent: bfloat16 [8192, 512], P(('groups', 'tiles')), parts along dimension 0, may hold values from -6 to 6
- edge_latent: bfloat16 [49152, 512], P(('groups', 'tiles')), parts along dimension 0, may hold values from -6 to 6
- node_cot: bfloat16 [8192, 512], P(('groups', 'tiles')), parts along dimension 0, may hold values from -6 to 6
- edge_cot: bfloat16 [49152, 512], P(('groups', 'tiles')), parts along dimension 0, may hold values from -6 to 6
- edge_w1: bfloat16 [1536, 512], replicated, may hold values from -0.15625 to 0.15625
- edge_b1: float32 [512], replicated, may hold values from -3 to 3
- edge_w2: bfloat16 [512, 512], replicated, may hold values from -0.25 to 0.25
- edge_b2: float32 [512], replicated, may hold values from -3 to 3
- edge_gain: float32 [512], replicated, may hold values from 0.1 to 1.9
- node_w1: bfloat16 [1024, 512], replicated, may hold values from -0.1875 to 0.1875
- node_b1: float32 [512], replicated, may hold values from -3 to 3
- node_w2: bfloat16 [512, 512], replicated, may hold values from -0.25 to 0.25
- node_b2: float32 [512], replicated, may hold values from -3 to 3
- node_gain: float32 [512], replicated, may hold values from 0.1 to 1.9
- send_index: int32 [32, 16, 2], P(('groups', 'tiles')), parts along dimension 0, may hold values from 0 to 255
- edge_sender: int32 [49152], P(('groups', 'tiles')), parts along dimension 0, may hold values from 0 to 415, as said below
- edge_receiver: int32 [49152], P(('groups', 'tiles')), parts along dimension 0, may hold values from 0 to 255
- edge_count: int32 [32], P('groups'), parts along dimension 0, may hold values from 32 to 1536, as said below
Outputs:
- grad_node: bfloat16 [8192, 512], P(('groups', 'tiles')), parts along dimension 0
- grad_edge: bfloat16 [49152, 512], P(('groups', 'tiles')), parts along dimension 0
- grad_edge_w1: float32 [3072, 512], P(('groups', 'tiles')), parts along dimension 0
- grad_edge_w2: float32 [1024, 512], P(('groups', 'tiles')), parts along dimension 0
- grad_node_w1: float32 [2048, 512], P(('groups', 'tiles')), parts along dimension 0
- grad_node_w2: float32 [1024, 512], P(('groups', 'tiles')), parts along dimension 0
There are 2 independent parts, one for each index of `groups`. A program takes and returns all parts, laid end to end along the dimension named above; an argument that names none is the same for every part. Nothing has to cross between parts.
Inputs may be any that keep to these rules, and one draw needn't show every extreme that they name: `edge_count`: the count of some device is exactly 1536, and that of the device 16 / 2 indices away from it exactly 32. `edge_sender`: an index into the device's sender table: below 64 the previous device's last 64 nodes, then its own 256 nodes, then the next device's first 64 nodes, then the 32 coarse-level rows listed for it; the first device never names the first part and the last never the third; in each device's block of 1536 slots the first 32 name every coarse-level row once.
All inputs are finite; a program needn't handle non-finite values.
Results may differ from a plain program's by a relative error of at most 0.0085.
Values may be sent and summed in bfloat16 or wider, within the bound.
No kernel may reach another device: no remote copies, remote signals or barrier semaphores. Data moves between devices by JAX's collectives and lax.ppermute only.
A program may use at most 128 MiB of HBM per device.

v0:
```python
import jax
import jax.numpy as jnp
from jax import lax
from jax.sharding import PartitionSpec as P

NEAR = 64


EPSILON = 1e-05


def extended(cells, sides, width):
    for axis, dim in sides:
        count = lax.axis_size(axis)
        ends = count - 1
        head = lax.slice_in_dim(cells, 0, width, axis=dim)
        tail = lax.slice_in_dim(cells, cells.shape[dim] - width, cells.shape[dim], axis=dim)
        cells = jnp.concatenate(
            [
                lax.ppermute(tail, axis, [(i, (i + 1) % count) for i in range(ends)]),
                cells,
                lax.ppermute(head, axis, [((i + 1) % count, i) for i in range(ends)]),
            ],
            axis=dim,
        )
    return cells


def silu_slope(preact):
    sigmoid_value = jax.nn.sigmoid(preact)
    return sigmoid_value * (1.0 + preact * (1.0 - sigmoid_value))


def mlp_forward(inputs, w_first, b_first, w_second, b_second):
    preact = jnp.dot(inputs, w_first, preferred_element_type=jnp.float32) + b_first
    hidden = jax.nn.silu(preact).astype(jnp.bfloat16)
    output_pre = jnp.dot(hidden, w_second, preferred_element_type=jnp.float32) + b_second
    centred = output_pre - jnp.mean(output_pre, axis=-1, keepdims=True)
    inverse = lax.rsqrt(jnp.mean(centred * centred, axis=-1, keepdims=True) + EPSILON)
    return (preact, hidden, centred * inverse, inverse)


def mlp_backward(inputs, preact, hidden, normed, inverse, grad_out, gain, w_first, w_second):
    scaled = grad_out * gain
    grad_outer = inverse * (
        scaled
        - jnp.mean(scaled, axis=-1, keepdims=True)
        - normed * jnp.mean(scaled * normed, axis=-1, keepdims=True)
    )
    grad_outer = grad_outer.astype(jnp.bfloat16)
    grad_second = jnp.dot(hidden.T, grad_outer, preferred_element_type=jnp.float32)
    grad_hidden = jnp.dot(grad_outer, w_second.T, preferred_element_type=jnp.float32)
    grad_preact = (grad_hidden * silu_slope(preact)).astype(jnp.bfloat16)
    grad_first = jnp.dot(inputs.T, grad_preact, preferred_element_type=jnp.float32)
    grad_inputs = jnp.dot(grad_preact, w_first.T, preferred_element_type=jnp.float32)
    return (grad_inputs, grad_first, grad_second)


def shards(
    node_latent,
    edge_latent,
    node_cot,
    edge_cot,
    edge_w1,
    edge_b1,
    edge_w2,
    edge_b2,
    edge_gain,
    node_w1,
    node_b1,
    node_w2,
    node_b2,
    node_gain,
    send_index,
    edge_sender,
    edge_receiver,
    edge_count,
):
    tile_count = lax.axis_size("tiles")
    here = lax.axis_index("tiles")
    node_count, latent = node_latent.shape
    edge_total = edge_latent.shape[0]
    places = send_index.shape[2]
    rim_width = NEAR
    pick_rows = send_index[0].reshape(-1)
    outgoing = jnp.take(node_latent, pick_rows, axis=0).reshape(tile_count, places, latent)
    incoming = lax.all_to_all(outgoing, "tiles", split_axis=0, concat_axis=0, tiled=True).reshape(
        tile_count * places, latent
    )
    padded = extended(node_latent, (("tiles", 0),), rim_width)
    table = jnp.concatenate([padded, incoming], axis=0)
    table_len = table.shape[0]
    senders = jnp.take(table, edge_sender, axis=0)
    receivers = jnp.take(node_latent, edge_receiver, axis=0)
    live_count = edge_count[here]
    live_mask = (jnp.arange(edge_total, dtype=jnp.int32) < live_count).astype(jnp.float32)[:, None]
    inputs = jnp.concatenate([edge_latent, senders, receivers], axis=1)
    preact, hidden, normed, inverse = mlp_forward(inputs, edge_w1, edge_b1, edge_w2, edge_b2)
    update = (normed * edge_gain * live_mask).astype(jnp.bfloat16)
    summed = jax.ops.segment_sum(
        update.astype(jnp.float32), edge_receiver, num_segments=node_count
    ).astype(jnp.bfloat16)
    node_inputs = jnp.concatenate([node_latent, summed], axis=1)
    preact_n, hidden_n, normed_n, inverse_n = mlp_forward(
        node_inputs, node_w1, node_b1, node_w2, node_b2
    )
    grad_node_inputs, node_first, node_second = mlp_backward(
        node_inputs,
        preact_n,
        hidden_n,
        normed_n,
        inverse_n,
        node_cot.astype(jnp.float32),
        node_gain,
        node_w1,
        node_w2,
    )
    direct = grad_node_inputs[:, :latent]
    grad_summed = grad_node_inputs[:, latent:]
    grad_update = edge_cot.astype(jnp.float32) + jnp.take(grad_summed, edge_receiver, axis=0)
    edge_gains = edge_gain[None, :] * live_mask
    grad_inputs, first_sum, second_sum = mlp_backward(
        inputs, preact, hidden, normed, inverse, grad_update, edge_gains, edge_w1, edge_w2
    )
    grad_edge = (edge_cot.astype(jnp.float32) + grad_inputs[:, :latent]).astype(jnp.bfloat16)
    table_sums = jax.ops.segment_sum(
        grad_inputs[:, latent : 2 * latent], edge_sender, num_segments=table_len
    )
    lower_sums = table_sums[:rim_width]
    own_sums = table_sums[rim_width : rim_width + node_count]
    upper_sums = table_sums[rim_width + node_count : 2 * rim_width + node_count]
    far_sums = table_sums[2 * rim_width + node_count :].reshape(tile_count, places, latent)
    back = extended(
        jnp.concatenate([lower_sums, upper_sums], axis=0).astype(jnp.bfloat16),
        (("tiles", 0),),
        rim_width,
    ).astype(jnp.float32)
    rim_terms = jnp.concatenate(
        [
            back[:rim_width],
            jnp.zeros((node_count - 2 * rim_width, latent), jnp.float32),
            back[3 * rim_width :],
        ],
        axis=0,
    )
    returned = (
        lax.all_to_all(
            far_sums.astype(jnp.bfloat16), "tiles", split_axis=0, concat_axis=0, tiled=True
        )
        .astype(far_sums.dtype)
        .reshape(tile_count * places, latent)
    )
    owned = jax.ops.segment_sum(returned, pick_rows, num_segments=node_count)
    receiver_part = jax.ops.segment_sum(
        grad_inputs[:, 2 * latent :], edge_receiver, num_segments=node_count
    )
    grad_node = (
        node_cot.astype(jnp.float32) + direct + receiver_part + own_sums + rim_terms + owned
    ).astype(jnp.bfloat16)
    grad_edge_w1, grad_edge_w2, grad_node_w1, grad_node_w2 = (
        lax.psum_scatter(first_sum, "tiles", scatter_dimension=0, tiled=True),
        lax.psum_scatter(second_sum, "tiles", scatter_dimension=0, tiled=True),
        lax.psum_scatter(node_first, "tiles", scatter_dimension=0, tiled=True),
        lax.psum_scatter(node_second, "tiles", scatter_dimension=0, tiled=True),
    )
    return (grad_node, grad_edge, grad_edge_w1, grad_edge_w2, grad_node_w1, grad_node_w2)


def solution(mesh):
    placed = (
        P(("groups", "tiles"), None),
        P(("groups", "tiles"), None),
        P(("groups", "tiles"), None),
        P(("groups", "tiles"), None),
        P(),
        P(),
        P(),
        P(),
        P(),
        P(),
        P(),
        P(),
        P(),
        P(),
        P(("groups", "tiles"), None, None),
        P(("groups", "tiles")),
        P(("groups", "tiles")),
        P("groups"),
    )
    return jax.shard_map(
        shards,
        mesh=mesh,
        in_specs=placed,
        out_specs=(
            P(("groups", "tiles"), None),
            P(("groups", "tiles"), None),
            P(("groups", "tiles"), None),
            P(("groups", "tiles"), None),
            P(("groups", "tiles"), None),
            P(("groups", "tiles"), None),
        ),
        check_vma=False,
    )
```

profile of v0, /device:TPU:0, one launch (start us, length us, event | category | flops | bytes accessed | tf_op | source)
XLA Modules:
  0.0 341.8 jit_solution(9066728410505680133)
XLA Ops:
  11.4 7.4 %all-to-all-start = ((bf16[16,2,512]{2,1,0:T(2,128)(2,1)}), bf16[16,2,512]{2,1,0:T(2,128)(2,1)S(1)}, u32[]{:S(2)}, u32[]{:S(2)}) async-start(bf16[16,2,512]{2,1,0:T(2,128)(2,1)} %broadcast_select_fusion.2), calls=%async_computation | async-start | bytes 65536 | tf_op jit(solution)/shard_map/all_to_all | solution.py:87
  20.3 2.9 collective-permute-start
  33.5 4.8 %gather_fusion.2 = bf16[1536,512]{1,0:T(8,128)(2,1)S(1)} fusion(bf16[256,512]{1,0:T(8,128)(2,1)S(1)} %copy-done.1, s32[2048]{0:T(1024)S(1)} %pad_clamp_fusion), kind=kCustom, calls=%fused_computation.2 | custom fusion | bytes 3151872 | tf_op jit(solution)/shard_map/jit(_take)/gather | solution.py:94
  40.8 5.4 %gather_fusion.1 = bf16[1536,512]{1,0:T(8,128)(2,1)} fusion(bf16[416,512]{1,0:T(8,128)(2,1)S(1)} %pad_maximum_fusion.4, s32[2048]{0:T(1024)S(1)} %pad_clamp_fusion.1), kind=kCustom, calls=%fused_computation.1 | custom fusion | bytes 3151872 | tf_op jit(solution)/shard_map/jit(_take)/gather | solution.py:93
  50.9 4.4 %multiply_convert_fusion.2 = (bf16[1536,512]{1,0:T(8,128)(2,1)S(1)}, f32[1536,512]{1,0:T(8,128)}) fusion(f32[512]{0:T(512)S(1)} %copy-done.29, bf16[1536,512]{1,0:T(8,128)(2,1)S(1)} %copy-done, bf16[1536,512]{0,1:T(8,128)(2,1)S(1)} %get-tuple-element.34, bf16[1536,512]{0,1:T(8,128)(2,1)S(1)} %get-tuple-element.35, bf16[1536,512]{0,1:T(8,128)(2,1)S(1)} %copy-done.14), kind=kOutput, calls=%fused_computation.24 | convolution fusion | flops 2434793472 | bytes 11012096 | tf_op jit(solution)/shard_map/dot_general | solution.py:35
  60.3 3.6 %copy.39 = f32[1536,512]{1,0:T(8,128)} copy(f32[1536,512]{0,1:T(8,128)} %fusion.8) | data formatting | bytes 6291456 | tf_op jit(solution)/shard_map/convert_element_type | solution.py:101
  63.9 10.5 %scatter_custom_fusion = f32[256,512]{1,0:T(8,128)S(1)} fusion(s32[1536]{0:T(1024)} %param.34, f32[1536,512]{1,0:T(8,128)} %copy.39, f32[]{:T(128)} %constant.55.clone.1), kind=kCustom, calls=%fused_computation.57 | custom fusion | flops 786432 | bytes 524800 | tf_op jit(solution)/shard_map/scatter-add | solution.py:100
  80.7 4.9 %gather_fusion.3 = f32[1536,512]{1,0:T(8,128)} fusion(f32[256,512]{1,0:T(8,128)S(1)} %slice.66, s32[2048]{0:T(1024)S(1)} %pad_clamp_fusion), kind=kCustom, calls=%fused_computation.3 | custom fusion | bytes 6297600 | tf_op jit(solution)/shard_map/jit(_take)/gather | solution.py:120
  85.6 3.7 %copy.41 = f32[1536,512]{0,1:T(8,128)} copy(f32[1536,512]{1,0:T(8,128)} %gather_fusion.3) | data formatting | bytes 6291456 | tf_op jit(solution)/shard_map/jit(_take)/gather | solution.py:120
  89.4 4.2 %fusion.35 = (f32[1536]{0:T(1024)S(1)}, f32[1536]{0:T(1024)S(1)}) fusion(f32[1536]{0:T(1024)S(1)} %fusion.26, f32[512]{0:T(512)S(1)} %copy-done.25, f32[1536,512]{0,1:T(8,128)} %copy.41, pred[1536]{0:T(1024)(128)(4,1)S(1)} %compare_and_fusion, bf16[1536,512]{0,1:T(8,128)(2,1)S(1)} %copy-done.5, f32[1536]{0:T(1024)S(1)} %add_rsqrt_fusion, ...), kind=kLoop, calls=%fused_computation.91 | loop fusion | flops 7861248 | bytes 7898624 | tf_op jit(solution)/shard_map/reduce_sum | solution.py:47
  98.9 2.8 fusion.20
  102.0 4.5 %fusion.6 = bf16[1536,512]{1,0:T(8,128)(2,1)S(1)} fusion(f32[1536,512]{1,0:T(8,128)} %get-tuple-element.29, bf16[1536,512]{0,1:T(8,128)(2,1)} %copy-done.12, bf16[512,512]{1,0:T(8,128)(2,1)} %param.24), kind=kOutput, calls=%fused_computation.26 | convolution fusion | flops 812384256 | bytes 6815744 | tf_op jit(solution)/shard_map/dot_general | solution.py:52
  107.6 6.4 %fusion.7 = f32[1536,512]{1,0:T(8,128)} fusion(bf16[1536,512]{1,0:T(8,128)(2,1)S(1)} %fusion.6, bf16[1536,512]{0,1:T(8,128)(2,1)S(1)} %copy-done.17, bf16[1536,512]{0,1:T(8,128)(2,1)S(1)} %copy-done.19, bf16[1536,512]{0,1:T(8,128)(2,1)S(1)} %copy-done.15), kind=kOutput, calls=%fused_computation.28 | convolution fusion | flops 2430074880 | bytes 9437184 | tf_op jit(solution)/shard_map/dot_general | solution.py:54
  114.2 6.6 %fusion.41 = f32[1536,1536]{1,0:T(8,128)} fusion(bf16[1536,512]{1,0:T(8,128)(2,1)} %copy-done.35, bf16[1536,512]{1,0:T(8,128)(2,1)S(1)} %copy-done), kind=kOutput, calls=%fused_computation.97 | convolution fusion | flops 2415919104 | bytes 12582912 | tf_op jit(solution)/shard_map/dot_general | solution.py:55
  120.8 11.4 %scatter_custom_fusion.1 = f32[416,512]{1,0:T(8,128)} fusion(s32[1536]{0:T(1024)} %param.33, f32[1536,1536]{1,0:T(8,128)} %fusion.41, f32[]{:T(128)} %constant.55.clone.1), kind=kCustom, calls=%fused_computation.18 | custom fusion | flops 786432 | bytes 3998208 | tf_op jit(solution)/shard_map/scatter-add | solution.py:126
  132.2 3.9 %slice.73 = f32[1536,512]{1,0:T(8,128)} slice(f32[1536,1536]{1,0:T(8,128)} %fusion.41), slice={[0:1536], [0:512]} | slice | bytes 6291456 | tf_op jit(solution)/shard_map/slice | solution.py:125
  137.6 7.4 %all-to-all-start.1 = ((bf16[16,2,512]{2,1,0:T(2,128)(2,1)}), bf16[16,2,512]{2,1,0:T(2,128)(2,1)}, u32[]{:S(2)}, u32[]{:S(2)}) async-start(bf16[16,2,512]{2,1,0:T(2,128)(2,1)} %convert_element_type.70), calls=%async_computation.1 | async-start | bytes 65536 | tf_op jit(solution)/shard_map/all_to_all | solution.py:147
  146.5 2.9 collective-permute-start.2
  150.7 3.6 %copy.45 = f32[1536,512]{0,1:T(8,128)} copy(f32[1536,512]{1,0:T(8,128)} %slice.73) | data formatting | bytes 6291456
  154.3 3.6 %fusion.1 = bf16[1536,512]{0,1:T(8,128)(2,1)} fusion(f32[1536,512]{0,1:T(8,128)} %copy.45, bf16[1536,512]{0,1:T(8,128)(2,1)S(1)} %copy-done.5), kind=kLoop, calls=%fused_computation.15 | loop fusion | flops 2359296 | bytes 6291456 | tf_op jit(solution)/shard_map/convert_element_type | solution.py:125
  166.7 12.3 %scatter_custom_fusion.2 = f32[256,512]{1,0:T(8,128)} fusion(f32[256,512]{1,0:T(8,128)} %fusion.18, s32[1536]{0:T(1024)} %param.34, f32[1536,1536]{1,0:T(8,128)} %fusion.41), kind=kCustom, calls=%fused_computation.16 | custom fusion | flops 786432 | bytes 3670016 | tf_op jit(solution)/shard_map/scatter-add | solution.py:154
  180.9 19.6 %reduce-scatter.7.cloned.1.call-done = f32[32,512]{1,0:T(8,128)} async-done(((f32[512,512]{1,0:T(8,128)}), f32[32,512]{1,0:T(8,128)}) %reduce-scatter.7.cloned.1.call-update) | async-done | bytes 65552 | tf_op jit(solution)/shard_map/reduce_scatter | solution.py:162
  200.5 64.9 %reduce-scatter.9.cloned.1.call-done = f32[64,512]{1,0:T(8,128)} async-done(((f32[1024,512]{1,0:T(8,128)}), f32[64,512]{1,0:T(8,128)}) %reduce-scatter.9.cloned.1.call-update) | async-done | bytes 131088 | tf_op jit(solution)/shard_map/reduce_scatter | solution.py:163
  265.3 70.0 %reduce-scatter.5.cloned.1.call-done = f32[96,512]{1,0:T(8,128)} async-done(((f32[1536,512]{1,0:T(8,128)}), f32[96,512]{1,0:T(8,128)}) %reduce-scatter.5.cloned.1.call-update) | async-done | bytes 196624 | tf_op jit(solution)/shard_map/reduce_scatter | solution.py:161
  (149 shorter events, 55.7 us)
Async XLA Ops:
  7.2 43.7 %copy-start = (bf16[1536,512]{1,0:T(8,128)(2,1)S(1)}, bf16[1536,512]{1,0:T(8,128)(2,1)}, u32[]{:S(2)}) copy-start(bf16[1536,512]{1,0:T(8,128)(2,1)} %param.22) | copy-start | bytes 4718596
  7.2 24.7 %copy-start.13 = (bf16[1536,512]{1,0:T(8,128)(2,1)S(1)}, bf16[1536,512]{1,0:T(8,128)(2,1)}, u32[]{:S(2)}) copy-start(bf16[1536,512]{1,0:T(8,128)(2,1)} %param.19) | copy-start | bytes 4718596
  11.4 28.5 %all-to-all-start = ((bf16[16,2,512]{2,1,0:T(2,128)(2,1)}), bf16[16,2,512]{2,1,0:T(2,128)(2,1)S(1)}, u32[]{:S(2)}, u32[]{:S(2)}) async-start(bf16[16,2,512]{2,1,0:T(2,128)(2,1)} %broadcast_select_fusion.2), calls=%async_computation | async-start | bytes 65536 | tf_op jit(solution)/shard_map/all_to_all | solution.py:87
  18.8 162.1 %reduce-scatter.11.cloned.1.call-start = ((), (), s32[]{:S(2)}) async-start(), calls=%async_computation.9 | async-start | bytes 1114112 | tf_op jit(solution)/shard_map/reduce_scatter | solution.py:164
  20.3 19.6 %collective-permute-start = (bf16[64,512]{1,0:T(8,128)(2,1)}, bf16[64,512]{1,0:T(8,128)(2,1)}, u32[]{:S(2)}, u32[]{:S(2)}) collective-permute-start(bf16[64,512]{1,0:T(8,128)(2,1)} %get-tuple-element.26), channel_id=1, source_target_pairs={{0,1},{1,2},{2,3},{3,4},{4,5},{5,6},{6,7},{7,8},{8,9},{9,10},{10,1... | collective-permute-start | bytes 196616 | tf_op jit(solution)/shard_map/ppermute | solution.py:20
  23.2 16.7 %collective-permute-start.1 = (bf16[64,512]{1,0:T(8,128)(2,1)S(1)}, bf16[64,512]{1,0:T(8,128)(2,1)}, u32[]{:S(2)}, u32[]{:S(2)}) collective-permute-start(bf16[64,512]{1,0:T(8,128)(2,1)S(1)} %get-tuple-element.27), channel_id=1, source_target_pairs={{1,0},{2,1},{3,2},{4,3},{5,4},{6,5},{7,6},{8,7},{9,8},{10,9},{11,1... | collective-permute-start | bytes 196616 | tf_op jit(solution)/shard_map/ppermute | solution.py:22
  50.8 4.5 %copy-start.16 = (bf16[1536,512]{0,1:T(8,128)(2,1)}, bf16[1536,512]{0,1:T(8,128)(2,1)S(1)}, u32[]{:S(2)}) copy-start(bf16[1536,512]{0,1:T(8,128)(2,1)S(1)} %get-tuple-element.34) | copy-start | bytes 4718596
  50.8 4.5 %copy-start.18 = (bf16[1536,512]{0,1:T(8,128)(2,1)}, bf16[1536,512]{0,1:T(8,128)(2,1)S(1)}, u32[]{:S(2)}) copy-start(bf16[1536,512]{0,1:T(8,128)(2,1)S(1)} %get-tuple-element.35) | copy-start | bytes 4718596
  60.3 14.2 %copy-start.20 = (bf16[1024,512]{1,0:T(8,128)(2,1)S(1)}, bf16[1024,512]{1,0:T(8,128)(2,1)}, u32[]{:S(2)}) copy-start(bf16[1024,512]{1,0:T(8,128)(2,1)} %param.27) | copy-start | bytes 3145732
  60.3 14.2 %copy-start.31 = (f32[512]{0:T(512)S(1)}, f32[512]{0:T(512)}, u32[]{:S(2)}) copy-start(f32[512]{0:T(512)} %param.28) | copy-start | bytes 6148
  63.9 11.1 %copy-start.32 = (f32[512]{0:T(512)S(1)}, f32[512]{0:T(512)}, u32[]{:S(2)}) copy-start(f32[512]{0:T(512)} %param.30) | copy-start | bytes 6148
  79.1 121.4 %reduce-scatter.7.cloned.1.call-start = ((), (), s32[]{:S(2)}) async-start(), calls=%async_computation.7 | async-start | bytes 1114112 | tf_op jit(solution)/shard_map/reduce_scatter | solution.py:162
  89.4 4.9 %copy-start.4 = (f32[1536,512]{0,1:T(8,128)S(1)}, f32[1536,512]{0,1:T(8,128)}, u32[]{:S(2)}) copy-start(f32[1536,512]{0,1:T(8,128)} %copy.41) | copy-start | bytes 9437188
  98.8 166.5 %reduce-scatter.9.cloned.1.call-start = ((), (), s32[]{:S(2)}) async-start(), calls=%async_computation.8 | async-start | bytes 2228224 | tf_op jit(solution)/shard_map/reduce_scatter | solution.py:163
  101.7 233.6 %reduce-scatter.5.cloned.1.call-start = ((), (), s32[]{:S(2)}) async-start(), calls=%async_computation.6 | async-start | bytes 3342336 | tf_op jit(solution)/shard_map/reduce_scatter | solution.py:161
  102.0 5.7 %copy-start.15 = (bf16[1536,512]{0,1:T(8,128)(2,1)S(1)}, bf16[1536,512]{0,1:T(8,128)(2,1)}, u32[]{:S(2)}) copy-start(bf16[1536,512]{0,1:T(8,128)(2,1)} %copy.38) | copy-start | bytes 4718596
  102.0 5.6 %copy-start.17 = (bf16[1536,512]{0,1:T(8,128)(2,1)S(1)}, bf16[1536,512]{0,1:T(8,128)(2,1)}, u32[]{:S(2)}) copy-start(bf16[1536,512]{0,1:T(8,128)(2,1)} %copy-done.16) | copy-start | bytes 4718596
  102.0 5.6 %copy-start.19 = (bf16[1536,512]{0,1:T(8,128)(2,1)S(1)}, bf16[1536,512]{0,1:T(8,128)(2,1)}, u32[]{:S(2)}) copy-start(bf16[1536,512]{0,1:T(8,128)(2,1)} %copy-done.18) | copy-start | bytes 4718596
  137.6 23.0 %all-to-all-start.1 = ((bf16[16,2,512]{2,1,0:T(2,128)(2,1)}), bf16[16,2,512]{2,1,0:T(2,128)(2,1)}, u32[]{:S(2)}, u32[]{:S(2)}) async-start(bf16[16,2,512]{2,1,0:T(2,128)(2,1)} %convert_element_type.70), calls=%async_computation.1 | async-start | bytes 65536 | tf_op jit(solution)/shard_map/all_to_all | solution.py:147
  146.5 17.4 %collective-permute-start.2 = (bf16[64,512]{1,0:T(8,128)(2,1)S(1)}, bf16[64,512]{1,0:T(8,128)(2,1)}, u32[]{:S(2)}, u32[]{:S(2)}) collective-permute-start(bf16[64,512]{1,0:T(8,128)(2,1)S(1)} %get-tuple-element.22), channel_id=1, source_target_pairs={{0,1},{1,2},{2,3},{3,4},{4,5},{5,6},{6,7},{7,8},{8,9},{9,10},{10,1... | collective-permute-start | bytes 196616 | tf_op jit(solution)/shard_map/ppermute | solution.py:20
  149.4 14.5 %collective-permute-start.3 = (bf16[64,512]{1,0:T(8,128)(2,1)}, bf16[64,512]{1,0:T(8,128)(2,1)}, u32[]{:S(2)}, u32[]{:S(2)}) collective-permute-start(bf16[64,512]{1,0:T(8,128)(2,1)} %get-tuple-element.23), channel_id=1, source_target_pairs={{1,0},{2,1},{3,2},{4,3},{5,4},{6,5},{7,6},{8,7},{9,8},{10,9},{11,1... | collective-permute-start | bytes 196616 | tf_op jit(solution)/shard_map/ppermute | solution.py:22
  157.9 6.9 %copy-start.8 = (f32[416,512]{1,0:T(8,128)S(1)}, f32[416,512]{1,0:T(8,128)}, u32[]{:S(2)}) copy-start(f32[416,512]{1,0:T(8,128)} %scatter_custom_fusion.1) | copy-start | bytes 2555908
  157.9 6.9 %copy-start.10 = (f32[256,1024]{1,0:T(8,128)S(1)}, f32[256,1024]{1,0:T(8,128)}, u32[]{:S(2)}) copy-start(f32[256,1024]{1,0:T(8,128)} %copy-done.9) | copy-start | bytes 3145732
  166.7 12.3 %copy-start.11 = (f32[256,512]{1,0:T(8,128)S(1)}, f32[256,512]{1,0:T(8,128)}, u32[]{:S(2)}) copy-start(f32[256,512]{1,0:T(8,128)} %scatter_custom_fusion.3) | copy-start | bytes 1572868
  (22 other events, 55.0 us)
Sparse Core Ops, SparseCore 0:
  79.2 60.1 reduce-scatter.10
  144.0 56.4 reduce-scatter.6
  204.8 60.5 reduce-scatter.8
  270.1 65.2 reduce-scatter.4
where the time goes:
time: 343 us; the launch traced here: 342 us
  waiting for transfers between devices  155 us (45%)
  other arithmetic  60.8 us (18%)
  local copies, waits for them, and re-layouts  56.5 us (16%)
  matrix products  32.1 us (9%)
  starting transfers between devices  23.5 us (7%)
  between operations  14.3 us (4%)
    reduce_scatter x1, waiting for transfers between devices, shards(): lax.psum_scatter(first_sum, 'tiles', scatter_dimension=0, tiled=True)  70 us
    reduce_scatter x1, waiting for transfers between devices, shards(): lax.psum_scatter(node_first, 'tiles', scatter_dimension=0, tiled=True)  64.9 us
    reduce_scatter x1, waiting for transfers between devices, shards(): lax.psum_scatter(second_sum, 'tiles', scatter_dimension=0, tiled=True)  19.6 us
    unnamed x77, local copies, waits for them, and re-layouts  17.5 us
    scatter-add x1, other arithmetic, shards(): jax.ops.segment_sum(grad_inputs[:, 2 * latent:], edge_receiver, num_segme...  12.3 us
    scatter-add x1, other arithmetic, shards(): jax.ops.segment_sum(grad_inputs[:, latent:2 * latent], edge_sender, num_s...  11.4 us
    scatter-add x1, other arithmetic, shards(): jax.ops.segment_sum(update.astype(jnp.float32), edge_receiver, num_segmen...  10.5 us
    dot_general x2, matrix products, mlp_backward(): jnp.dot(inputs.T, grad_preact, preferred_element_type=jnp.float32)  9.2 us
  transfers between devices with their start and end apart: 10, of which 3 were waited for; matrix products, arithmetic and copies ran while one was open for 30% of the time, Pallas kernels for 0%

commit v1 on v0

v1 whole, which is shorter than its diff:
```python
import functools

import jax
import jax.numpy as jnp
from jax import lax
from jax.experimental import pallas as pl
from jax.experimental.pallas import tpu as pltpu
from jax.sharding import PartitionSpec as P

NEAR = 64
EPSILON = 1e-05
TILE = 256
LANES = 128
F32 = jnp.float32
BF16 = jnp.bfloat16
MIB = 1024 * 1024

NN = (((1,), (0,)), ((), ()))
NT = (((1,), (1,)), ((), ()))
TN = (((0,), (0,)), ((), ()))


def dot(a, b, dims=NN):
    return lax.dot_general(a, b, dims, preferred_element_type=F32)


def sigmoid(x):
    return 0.5 * jnp.tanh(0.5 * x) + 0.5


def row_mean(x):
    return jnp.sum(x, axis=-1, keepdims=True) * (1.0 / x.shape[-1])


def ones_where(mask):
    return jnp.where(mask, 1.0, 0.0).astype(BF16)


def index_columns(idx_ref, step, tile):
    per = tile // LANES
    parts = []
    for j in range(per):
        row = idx_ref[pl.ds(step * per + j, 1), :]
        parts.append(jnp.transpose(jnp.broadcast_to(row, (LANES, LANES))))
    return jnp.concatenate(parts, axis=0)


def pick_columns(columns, width):
    lane = lax.broadcasted_iota(jnp.int32, columns.shape, 1)
    return [ones_where(columns == lane + c * LANES) for c in range(width // LANES)]


def pick_rows(idx_ref, step, tile, width):
    per = tile // LANES
    row = jnp.concatenate([idx_ref[pl.ds(step * per + j, 1), :] for j in range(per)], axis=1)
    return ones_where(lax.broadcasted_iota(jnp.int32, (width, tile), 0) == row)


def norm_forward(out):
    centred = out - row_mean(out)
    inverse = lax.rsqrt(row_mean(centred * centred) + EPSILON)
    return centred, inverse


def norm_backward(scaled, normed, inverse):
    return (
        inverse * (scaled - row_mean(scaled) - normed * row_mean(scaled * normed))
    ).astype(BF16)


def split_halves(bit, total_ref, at, rows, send_ref, keep_ref, offset):
    half = send_ref.shape[0]
    for q in range(half):
        there = pl.multiple_of((2 * q + 1 - bit) * rows, rows)
        here = pl.multiple_of((2 * q + bit) * rows, rows)
        send_ref[q, offset : offset + rows, :] = total_ref[pl.ds(at + there, rows), :].astype(BF16)
        keep_ref[q, offset : offset + rows, :] = total_ref[pl.ds(at + here, rows), :]


def outgoing_kernel(index_ref, node_ref, far_ref, head_ref, tail_ref):
    tiles, places = index_ref.shape[1], index_ref.shape[2]
    nodes = node_ref.shape[0]
    lane = lax.broadcasted_iota(jnp.int32, (tiles, nodes), 1)
    index = index_ref[0]
    for j in range(places):
        far_ref[j] = dot(ones_where(index[:, j : j + 1] == lane), node_ref[...]).astype(BF16)
    head_ref[...] = node_ref[:NEAR, :]
    tail_ref[...] = node_ref[nodes - NEAR :, :]


def sender_table_index(sender_ref, places, tiles, base):
    raw = sender_ref[...]
    far = raw - base
    moved = base + lax.rem(far, places) * tiles + lax.div(far, places)
    return jnp.where(raw >= base, moved, raw)


def forward_kernel(
    tiles, places, fast,
    count_ref, edge_ref, sender_ref, receiver_ref, node_ref, lower_ref, upper_ref, far_ref,
    w1_ref, b1_ref, w2_ref, b2_ref, gain_ref,
    nw1_ref, nb1_ref, nw2_ref, nb2_ref, ngain_ref, ncot_ref,
    hidden_ref, slope_ref, normed_ref, inverse_ref, table_ref, moved_ref, dsum_ref, base_ref,
    gsend_ref, gkeep_ref,
    weights, summed, grads,
):
    step = pl.program_id(0)
    last = pl.num_programs(0) - 1
    here = lax.axis_index("tiles")
    tile, latent = edge_ref.shape
    nodes = node_ref.shape[0]
    rows = table_ref.shape[0]
    far_base = nodes + 2 * NEAR

    @pl.when(step == 0)
    def _():
        moved_ref[...] = sender_table_index(sender_ref, places, tiles, far_base)
        table_ref[:NEAR, :] = lower_ref[...]
        table_ref[NEAR : NEAR + nodes, :] = node_ref[...]
        table_ref[NEAR + nodes : far_base, :] = upper_ref[...]
        for j in range(places):
            table_ref[far_base + j * tiles : far_base + (j + 1) * tiles, :] = far_ref[j]
        used = far_base + places * tiles
        if used < rows:
            table_ref[used:, :] = jnp.zeros((rows - used, latent), BF16)
        weights[:latent, :] = w1_ref[:latent, :]
        weights[latent : latent + rows, :] = dot(
            table_ref[...], w1_ref[latent : 2 * latent, :]
        ).astype(BF16)
        weights[latent + rows :, :] = dot(node_ref[...], w1_ref[2 * latent :, :]).astype(BF16)
        summed[...] = jnp.zeros_like(summed)

    senders = pick_columns(index_columns(moved_ref, step, tile), rows)
    receivers = pick_columns(index_columns(receiver_ref, step, tile), nodes)
    inputs = jnp.concatenate([edge_ref[...]] + senders + receivers, axis=1)
    preact = dot(inputs, weights[...]) + b1_ref[...]
    sig = sigmoid(preact)
    hidden = (preact * sig).astype(BF16)
    hidden_ref[...] = hidden
    slope_ref[...] = (sig * (1.0 + preact * (1.0 - sig))).astype(BF16)
    centred, inverse = norm_forward(dot(hidden, w2_ref[...]) + b2_ref[...])
    position = step * tile + lax.broadcasted_iota(jnp.int32, inverse.shape, 0)
    inverse = jnp.where(position < count_ref[here], inverse, 0.0)
    normed = centred * inverse
    normed_ref[...] = normed
    inverse_ref[...] = jnp.broadcast_to(inverse, inverse_ref.shape)
    update = (normed * gain_ref[...]).astype(BF16)
    summed[...] += dot(pick_rows(receiver_ref, step, tile, nodes), update)

    @pl.when(step == last)
    def _():
        node_in = jnp.concatenate([node_ref[...], summed[...].astype(BF16)], axis=1)
        preact_n = dot(node_in, nw1_ref[...]) + nb1_ref[...]
        sig_n = sigmoid(preact_n)
        hidden_n = (preact_n * sig_n).astype(BF16)
        centred_n, inverse_n = norm_forward(dot(hidden_n, nw2_ref[...]) + nb2_ref[...])
        cot = ncot_ref[...].astype(F32)
        dout = norm_backward(cot * ngain_ref[...], centred_n * inverse_n, inverse_n)
        slope_n = sig_n * (1.0 + preact_n * (1.0 - sig_n))
        dpre = (dot(dout, nw2_ref[...], NT) * slope_n).astype(BF16)
        grads[: 2 * latent, :] = dot(node_in, dpre, TN)
        grads[2 * latent :, :] = dot(hidden_n, dout, TN)
        base_ref[...] = cot + dot(dpre, nw1_ref[:latent, :], NT)
        dsum_ref[...] = dot(dpre, nw1_ref[latent:, :], NT).astype(BF16)
        if fast:
            bit = lax.rem(here, 2)
            first = 2 * latent // tiles
            split_halves(bit, grads, 0, first, gsend_ref, gkeep_ref, 0)
            split_halves(bit, grads, 2 * latent, latent // tiles, gsend_ref, gkeep_ref, first)
        else:
            gkeep_ref[...] = grads[: 2 * latent, :]
            gsend_ref[...] = grads[2 * latent :, :]


def slope_kernel(
    tiles, fast,
    cot_ref, receiver_ref, dsum_ref, hidden_ref, slope_ref, normed_ref, inverse_ref, w2_ref, gain_ref,
    dpre_ref, gsend_ref, gkeep_ref,
    grads,
):
    step = pl.program_id(0)
    last = pl.num_programs(0) - 1
    here = lax.axis_index("tiles")
    tile, latent = cot_ref.shape
    nodes = dsum_ref.shape[0]

    @pl.when(step == 0)
    def _():
        grads[...] = jnp.zeros_like(grads)

    receivers = jnp.concatenate(
        pick_columns(index_columns(receiver_ref, step, tile), nodes), axis=1
    )
    grad_update = cot_ref[...].astype(F32) + dot(receivers, dsum_ref[...])
    inverse = inverse_ref[:, :1]
    dout = norm_backward(grad_update * gain_ref[...], normed_ref[...], inverse)
    grads[...] += dot(hidden_ref[...], dout, TN)
    dpre_ref[...] = (dot(dout, w2_ref[...], NT) * slope_ref[...].astype(F32)).astype(BF16)

    @pl.when(step == last)
    def _():
        if fast:
            split_halves(lax.rem(here, 2), grads, 0, latent // tiles, gsend_ref, gkeep_ref, 0)
        else:
            gkeep_ref[...] = grads[...]
            gsend_ref[...] = jnp.zeros_like(gsend_ref)


def first_kernel(
    tiles, places, fast,
    dpre_ref, edge_ref, sender_ref, receiver_ref, table_ref, node_ref, w1_ref, base_ref,
    gsend_ref, gkeep_ref, lower_ref, upper_ref, far_ref, partial_ref,
    grads, sums,
):
    step = pl.program_id(0)
    last = pl.num_programs(0) - 1
    here = lax.axis_index("tiles")
    tile, latent = edge_ref.shape
    nodes = node_ref.shape[0]
    rows = table_ref.shape[0]

    @pl.when(step == 0)
    def _():
        grads[:latent, :] = jnp.zeros((latent, latent), F32)
        sums[...] = jnp.zeros_like(sums)

    dpre = dpre_ref[...]
    grads[:latent, :] += dot(edge_ref[...], dpre, TN)
    picks = jnp.concatenate(
        [
            pick_rows(sender_ref, step, tile, rows),
            pick_rows(receiver_ref, step, tile, nodes),
        ],
        axis=0,
    )
    sums[...] += dot(picks, dpre)

    @pl.when(step == last)
    def _():
        by_sender = sums[:rows, :].astype(BF16)
        by_receiver = sums[rows:, :].astype(BF16)
        grads[latent : 2 * latent, :] = dot(table_ref[...], by_sender, TN)
        grads[2 * latent :, :] = dot(node_ref[...], by_receiver, TN)
        if fast:
            split_halves(
                lax.rem(here, 2), grads, 0, 3 * latent // tiles, gsend_ref, gkeep_ref, 0
            )
        else:
            gkeep_ref[...] = grads[...]
            gsend_ref[...] = jnp.zeros_like(gsend_ref)
        back = dot(by_sender, w1_ref[latent : 2 * latent, :], NT)
        lower_ref[...] = back[:NEAR, :].astype(BF16)
        upper_ref[...] = back[NEAR + nodes : 2 * NEAR + nodes, :].astype(BF16)
        for j in range(places):
            at = 2 * NEAR + nodes + j * tiles
            far_ref[j] = back[at : at + tiles, :].astype(BF16)
        partial_ref[...] = (
            base_ref[...]
            + back[NEAR : NEAR + nodes, :]
            + dot(by_receiver, w1_ref[2 * latent :, :], NT)
        )


def edge_kernel(dpre_ref, cot_ref, w1_ref, out_ref):
    latent = cot_ref.shape[1]
    out_ref[...] = (
        cot_ref[...].astype(F32) + dot(dpre_ref[...], w1_ref[...], NT)
    ).astype(BF16)


def node_kernel(index_ref, partial_ref, below_ref, above_ref, far_ref, out_ref):
    tiles, places = index_ref.shape[1], index_ref.shape[2]
    nodes = partial_ref.shape[0]
    lane = lax.broadcasted_iota(jnp.int32, (tiles, nodes), 1)
    index = index_ref[0]
    total = partial_ref[...]
    for j in range(places):
        total = total + dot(ones_where(index[:, j : j + 1] == lane), far_ref[j], TN)
    out_ref[:NEAR, :] = (total[:NEAR, :] + below_ref[...].astype(F32)).astype(BF16)
    out_ref[NEAR : nodes - NEAR, :] = total[NEAR : nodes - NEAR, :].astype(BF16)
    out_ref[nodes - NEAR :, :] = (
        total[nodes - NEAR :, :] + above_ref[...].astype(F32)
    ).astype(BF16)


def halve_kernel(shift, keep_ref, got_ref, send_ref, kept_ref):
    bit = lax.rem(lax.div(lax.axis_index("tiles"), 2**shift), 2)
    send_ref[0] = (keep_ref[1 - bit] + got_ref[1 - bit].astype(F32)).astype(BF16)
    kept_ref[0] = keep_ref[bit] + got_ref[bit].astype(F32)


def spread_kernel(keep_ref, got_ref, own_ref, *send_refs):
    count = keep_ref.shape[0]
    place = lax.div(lax.axis_index("tiles"), 4)
    own_ref[...] = keep_ref[place] + got_ref[place].astype(F32)
    for k, send_ref in enumerate(send_refs):
        there = lax.rem(place + k + 1, count)
        send_ref[...] = (keep_ref[there] + got_ref[there].astype(F32)).astype(BF16)


def whole(shape=None):
    return pl.BlockSpec(memory_space=pltpu.VMEM)


def tiled(shape):
    zeros = (0,) * (len(shape) - 1)
    return pl.BlockSpec(shape, lambda i: (i,) + zeros)


def fixed(shape):
    zeros = (0,) * len(shape)
    return pl.BlockSpec(shape, lambda i: zeros, pipeline_mode=pl.Buffered(1))


def shaped(shape, dtype):
    return jax.ShapeDtypeStruct(shape, dtype)


def flip(tiles, bit):
    return [(i, i ^ bit) for i in range(tiles)]


def fold(send, keep, tiles):
    half, rows, width = keep.shape
    got = lax.ppermute(send, "tiles", flip(tiles, 1))
    quarter = half // 2
    send, keep = pl.pallas_call(
        functools.partial(halve_kernel, 1),
        grid=(quarter,),
        in_specs=[tiled((2, rows, width)), tiled((2, rows, width))],
        out_specs=[tiled((1, rows, width)), tiled((1, rows, width))],
        out_shape=[shaped((quarter, rows, width), BF16), shaped((quarter, rows, width), F32)],
        name="halve",
    )(keep, got)
    got = lax.ppermute(send, "tiles", flip(tiles, 2))
    own, *sends = pl.pallas_call(
        spread_kernel,
        out_shape=[shaped((rows, width), F32)] + [shaped((rows, width), BF16)] * (quarter - 1),
        name="spread",
    )(keep, got)
    total = own
    for k, send in enumerate(sends):
        pairs = [(i, (i // 4 + k + 1) % quarter * 4 + i % 4) for i in range(tiles)]
        total = total + lax.ppermute(send, "tiles", pairs).astype(F32)
    return total


def shards(
    node_latent, edge_latent, node_cot, edge_cot,
    edge_w1, edge_b1, edge_w2, edge_b2, edge_gain,
    node_w1, node_b1, node_w2, node_b2, node_gain,
    send_index, edge_sender, edge_receiver, edge_count,
):
    tiles = lax.axis_size("tiles")
    nodes, latent = node_latent.shape
    edges = edge_latent.shape[0]
    places = send_index.shape[2]
    steps = edges // TILE
    used = nodes + 2 * NEAR + places * tiles
    rows = -(-used // LANES) * LANES
    fast = tiles == 16
    half = tiles // 2
    upward = [(i, i + 1) for i in range(tiles - 1)]
    downward = [(i + 1, i) for i in range(tiles - 1)]
    sender = edge_sender.reshape(edges // LANES, LANES)
    receiver = edge_receiver.reshape(edges // LANES, LANES)
    row = lambda vector: vector.reshape(1, -1)
    params = pltpu.CompilerParams(vmem_limit_bytes=40 * MIB)
    edge_block = tiled((TILE, latent))
    vector = fixed((1, latent))
    square = fixed((latent, latent))

    outgoing, head, tail = pl.pallas_call(
        outgoing_kernel,
        out_shape=[
            shaped((places, tiles, latent), BF16),
            shaped((NEAR, latent), BF16),
            shaped((NEAR, latent), BF16),
        ],
        name="outgoing",
    )(send_index, node_latent)
    lower = lax.ppermute(tail, "tiles", upward)
    upper = lax.ppermute(head, "tiles", downward)
    incoming = lax.all_to_all(outgoing, "tiles", split_axis=1, concat_axis=1, tiled=True)

    if fast:
        grad_shapes = lambda count: [
            shaped((half, count // tiles, latent), BF16),
            shaped((half, count // tiles, latent), F32),
        ]
    else:
        grad_shapes = lambda count: [shaped((latent, latent), F32), shaped((count, latent), F32)]
    node_grads = grad_shapes(3 * latent) if fast else grad_shapes(2 * latent)
    hidden, slope, normed, inverse, table, moved, dsum, base, node_send, node_keep = pl.pallas_call(
        functools.partial(forward_kernel, tiles, places, fast),
        grid=(steps,),
        in_specs=[
            pl.BlockSpec(memory_space=pltpu.SMEM),
            edge_block,
            fixed(sender.shape), fixed(receiver.shape),
            fixed((nodes, latent)), fixed((NEAR, latent)), fixed((NEAR, latent)),
            fixed((places, tiles, latent)),
            fixed(edge_w1.shape), vector, square, vector, vector,
            fixed(node_w1.shape), vector, square, vector, vector,
            fixed((nodes, latent)),
        ],
        out_specs=[
            edge_block, edge_block, edge_block, tiled((TILE, LANES)),
            fixed((rows, latent)), fixed(sender.shape),
            fixed((nodes, latent)), fixed((nodes, latent)),
            fixed(node_grads[0].shape), fixed(node_grads[1].shape),
        ],
        out_shape=[
            shaped((edges, latent), BF16),
            shaped((edges, latent), BF16),
            shaped((edges, latent), F32),
            shaped((edges, LANES), F32),
            shaped((rows, latent), BF16),
            shaped(sender.shape, jnp.int32),
            shaped((nodes, latent), BF16),
            shaped((nodes, latent), F32),
        ] + node_grads,
        scratch_shapes=[
            pltpu.VMEM((latent + rows + nodes, latent), BF16),
            pltpu.VMEM((nodes, latent), F32),
            pltpu.VMEM((3 * latent, latent), F32),
        ],
        compiler_params=params,
        name="forward",
    )(
        edge_count, edge_latent, sender, receiver, node_latent, lower, upper, incoming,
        edge_w1, row(edge_b1), edge_w2, row(edge_b2), row(edge_gain),
        node_w1, row(node_b1), node_w2, row(node_b2), row(node_gain), node_cot,
    )

    second_grads = grad_shapes(latent)
    dpre, second_send, second_keep = pl.pallas_call(
        functools.partial(slope_kernel, tiles, fast),
        grid=(steps,),
        in_specs=[
            edge_block, fixed(receiver.shape), fixed((nodes, latent)),
            edge_block, edge_block, edge_block, tiled((TILE, LANES)), square, vector,
        ],
        out_specs=[edge_block, fixed(second_grads[0].shape), fixed(second_grads[1].shape)],
        out_shape=[shaped((edges, latent), BF16)] + second_grads,
        scratch_shapes=[pltpu.VMEM((latent, latent), F32)],
        compiler_params=params,
        name="slope",
    )(edge_cot, receiver, dsum, hidden, slope, normed, inverse, edge_w2, row(edge_gain))

    first_grads = grad_shapes(3 * latent)
    first_send, first_keep, to_lower, to_upper, to_far, partial = pl.pallas_call(
        functools.partial(first_kernel, tiles, places, fast),
        grid=(steps,),
        in_specs=[
            edge_block, edge_block, fixed(sender.shape), fixed(receiver.shape),
            fixed((rows, latent)), fixed((nodes, latent)), fixed(edge_w1.shape),
            fixed((nodes, latent)),
        ],
        out_specs=[
            fixed(first_grads[0].shape), fixed(first_grads[1].shape),
            fixed((NEAR, latent)), fixed((NEAR, latent)), fixed((places, tiles, latent)),
            fixed((nodes, latent)),
        ],
        out_shape=first_grads + [
            shaped((NEAR, latent), BF16),
            shaped((NEAR, latent), BF16),
            shaped((places, tiles, latent), BF16),
            shaped((nodes, latent), F32),
        ],
        scratch_shapes=[
            pltpu.VMEM((3 * latent, latent), F32),
            pltpu.VMEM((rows + nodes, latent), F32),
        ],
        compiler_params=params,
        name="first",
    )(dpre, edge_latent, moved, receiver, table, node_latent, edge_w1, base)

    grad_edge = pl.pallas_call(
        edge_kernel,
        grid=(steps,),
        in_specs=[edge_block, edge_block, square],
        out_specs=edge_block,
        out_shape=shaped((edges, latent), BF16),
        compiler_params=params,
        name="edge",
    )(dpre, edge_cot, edge_w1)

    above = lax.ppermute(to_lower, "tiles", downward)
    below = lax.ppermute(to_upper, "tiles", upward)
    returned = lax.all_to_all(to_far, "tiles", split_axis=1, concat_axis=1, tiled=True)
    grad_node = pl.pallas_call(
        node_kernel,
        out_shape=shaped((nodes, latent), BF16),
        name="node",
    )(send_index, partial, below, above, returned)

    if fast:
        node_total = fold(node_send, node_keep, tiles)
        cut = 2 * latent // tiles
        grad_node_w1, grad_node_w2 = node_total[:cut], node_total[cut:]
        grad_edge_w2 = fold(second_send, second_keep, tiles)
        grad_edge_w1 = fold(first_send, first_keep, tiles)
    else:
        scatter = functools.partial(
            lax.psum_scatter, axis_name="tiles", scatter_dimension=0, tiled=True
        )
        grad_node_w1, grad_node_w2 = scatter(node_keep), scatter(node_send)
        grad_edge_w1, grad_edge_w2 = scatter(first_keep), scatter(second_keep)
    return (grad_node, grad_edge, grad_edge_w1, grad_edge_w2, grad_node_w1, grad_node_w2)


def solution(mesh):
    split = P(("groups", "tiles"), None)
    return jax.shard_map(
        shards,
        mesh=mesh,
        in_specs=(split,) * 4
        + (P(),) * 10
        + (
            P(("groups", "tiles"), None, None),
            P(("groups", "tiles")),
            P(("groups", "tiles")),
            P("groups"),
        ),
        out_specs=(split,) * 6,
        check_vma=False,
    )
```

time: 343 us -> 130 us (0.38)
  waiting for transfers between devices: 155 us -> 5.14 us
  other arithmetic: 60.8 us -> 3.27 us
  Pallas kernels: 0 us -> 47 us
  matrix products: 32.1 us -> 0 us
  local copies, waits for them, and re-layouts: 56.5 us -> 27.5 us
  blocking collectives: 0 us -> 15.7 us
  between operations: 14.3 us -> 0.84 us
  starting transfers between devices: 23.5 us -> 29.7 us
    reduce_scatter x4 -> x0, waiting for transfers between devices: 154 us -> none  [the longest x1 70 us: shards(): lax.psum_scatter(first_sum, 'tiles', scatter_dimension=0, tiled=True)]
    pallas_call x0 -> x12, Pallas kernels: none -> 47 us  [the longest x1 12.2 us: shards(): pl.pallas_call(functools.partial(forward_kernel, tiles, places, fast), gr...]
    scatter-add x4 -> x0, other arithmetic: 36.2 us -> none  [the longest x1 12.3 us: shards(): jax.ops.segment_sum(grad_inputs[:, 2 * latent:], edge_receiver, num_segme...]
    dot_general x12 -> x0, matrix products: 32.1 us -> none  [the longest x2 9.2 us: mlp_backward(): jnp.dot(inputs.T, grad_preact, preferred_element_type=jnp.float32)]
    gather x8 -> x0, local copies, waits for them, and re-layouts: 24.8 us -> none  [the longest x2 8.69 us: shards(): jnp.take(grad_summed, edge_receiver, axis=0)]
    all_to_all x0 -> x1, blocking collectives: none -> 15.7 us  [shards(): lax.all_to_all(outgoing, 'tiles', split_axis=1, concat_axis=1, tiled=True)]
    ppermute x4 -> x19, starting transfers between devices: 8.34 us -> 23.9 us  [the longest x9 14.5 us: fold(): total = total + lax.ppermute(send, 'tiles', pairs).astype(F32)]
    convert_element_type x6 -> x0, other arithmetic: 9.61 us -> none  [the longest x1 3.58 us: shards(): (edge_cot.astype(jnp.float32) + grad_inputs[:, :latent]).astype(jnp.bfloa...]
  transfers between devices with their start and end apart: 10 -> 20, of which waited for: 3 -> 2; matrix products, arithmetic and copies ran while one was open for 30% -> 4% of each run, Pallas kernels for 0% -> 26%
where the time goes in v1:
time: 130 us; the launch traced here: 129 us
  Pallas kernels  47 us (36%)
  starting transfers between devices  29.7 us (23%)
  local copies, waits for them, and re-layouts  27.5 us (21%)
  blocking collectives  15.7 us (12%)
  waiting for transfers between devices  5.14 us (4%)
  other arithmetic  3.27 us (3%)
    unnamed x71, local copies, waits for them, and re-layouts  24.1 us
    all_to_all x1, blocking collectives, shards(): lax.all_to_all(outgoing, 'tiles', split_axis=1, concat_axis=1, tiled=True)  15.7 us
    ppermute x9, starting transfers between devices, fold(): total = total + lax.ppermute(send, 'tiles', pairs).astype(F32)  14.5 us
    pallas_call x1, Pallas kernels, shards(): pl.pallas_call(functools.partial(forward_kernel, tiles, places, fast), gr...  12.2 us
    pallas_call x3, Pallas kernels, fold(): pl.pallas_call(functools.partial(halve_kernel, 1), grid=(quarter,), in_sp...  10.4 us
    all_to_all x1, starting transfers between devices, shards(): lax.all_to_all(to_far, 'tiles', split_axis=1, concat_axis=1, tiled=True)  5.79 us
    pallas_call x3, Pallas kernels, fold(): pl.pallas_call(spread_kernel, out_shape=[shaped((rows, width), F32)] + [s...  5.74 us
    pallas_call x1, Pallas kernels, shards(): pl.pallas_call(functools.partial(first_kernel, tiles, places, fast), grid...  5.67 us
  transfers between devices with their start and end apart: 20, of which 2 were waited for; matrix products, arithmetic and copies ran while one was open for 4% of the time, Pallas kernels for 26%

profile of v1, /device:TPU:0, one launch (start us, length us, event | category | flops | bytes accessed | tf_op | source)
XLA Modules:
  0.0 129.1 jit_solution(17057137375350529672)
XLA Ops:
  2.0 1.8 %outgoing.1 = (bf16[2,16,512]{2,1,0:T(8,128)(2,1)}, bf16[64,512]{1,0:T(8,128)(2,1)}, bf16[64,512]{1,0:T(8,128)(2,1)}) custom-call(s32[1,16,2]{2,1,0:T(8,128)} %copy.30.index_ref, bf16[256,512]{1,0:T(8,128)(2,1)} %node_ref.5), custom_call_target="tpu_custom_call" | custom-call | tf_op jit(solution)/shard_map/outgoing/pallas_call | solution.py:373
  3.8 2.3 %collective-permute-start = (bf16[64,512]{1,0:T(8,128)(2,1)}, bf16[64,512]{1,0:T(8,128)(2,1)S(1)}, u32[]{:S(2)}, u32[]{:S(2)}) collective-permute-start(bf16[64,512]{1,0:T(8,128)(2,1)} %get-tuple-element.46), channel_id=1, source_target_pairs={{0,1},{1,2},{2,3},{3,4},{4,5},{5,6},{6,7},{7,8},{8,9},{9,10},{10,1... | collective-permute-start | bytes 196616 | tf_op jit(solution)/shard_map/ppermute | solution.py:382
  8.2 15.7 %all_to_all.10 = bf16[2,16,512]{2,0,1:T(2,128)(2,1)S(1)} all-to-all(bf16[2,16,512]{2,0,1:T(2,128)(2,1)S(1)} %copy.27), channel_id=1, replica_groups=mesh['groups'=2,'tiles'=16] {'tiles'}, dimensions={1} | all-to-all | bytes 65536 | tf_op jit(solution)/shard_map/all_to_all | solution.py:384
  38.1 12.2 %forward.1 = (bf16[1536,512]{1,0:T(8,128)(2,1)S(1)}, bf16[1536,512]{1,0:T(8,128)(2,1)S(1)}, f32[1536,512]{1,0:T(8,128)}, f32[1536,128]{1,0:T(8,128)S(1)}, bf16[5...) custom-call(s32[16]{0:T(128)S(1)} %copy-done.28, ...), custom_call_target="tpu_custom_call" | custom-call | tf_op jit(solution)/shard_map/forward/pallas_call | solution.py:394
  51.6 1.9 %copy-done.6 = f32[1536,512]{1,0:T(8,128)S(1)} copy-done((f32[1536,512]{1,0:T(8,128)S(1)}, f32[1536,512]{1,0:T(8,128)}, u32[]{:S(2)}) %copy-start.6) | copy-done | bytes 3145752
  53.5 5.5 %slope.1 = (bf16[1536,512]{1,0:T(8,128)(2,1)S(1)}, bf16[8,32,512]{2,1,0:T(8,128)(2,1)S(1)}, f32[8,32,512]{2,1,0:T(8,128)S(1)}) custom-call(bf16[1536,512]{1,0:T(8,128)(2,1)S(1)} %copy-done.4, s32[12,128]{1,0:T(8,128)S(1)} %bitcast.9, bf16[256,512]{1,0:T(8,128)(2,1)S(1)} %get-tuple-element.49.dsum_ref, bf16[1536,512]{1,0:T(8,128)(2,1)S(1)} %get-tuple-element.50.hidden_ref, ...), custom_call_target="tpu_custom_call" | custom-call | tf_op jit(solution)/shard_map/slope/pallas_call | solution.py:437
  59.0 5.7 %first.1 = (bf16[8,96,512]{2,1,0:T(8,128)(2,1)}, f32[8,96,512]{2,1,0:T(8,128)S(1)}, bf16[64,512]{1,0:T(8,128)(2,1)S(1)}, bf16[64,512]{1,0:T(8,128)(2,1)S(1)}, bf...) custom-call(bf16[1536,512]{1,0:T(8,128)(2,1)S(1)} %get-tuple-element.54.dpre_ref, bf16[1536,512]{1,0:T(8,128)(2,1)S(1)} %copy-done.3, ...), custom_call_target="tpu_custom_call" | custom-call | tf_op jit(solution)/shard_map/first/pallas_call | solution.py:452
  68.7 3.6 %halve.5 = (bf16[4,96,512]{2,1,0:T(8,128)(2,1)}, f32[4,96,512]{2,1,0:T(8,128)}) custom-call(f32[8,96,512]{2,1,0:T(8,128)} %copy-done.12, bf16[8,96,512]{2,1,0:T(8,128)(2,1)} %copy-done.31), custom_call_target="tpu_custom_call" | custom-call | tf_op jit(solution)/shard_map/halve/pallas_call | solution.py:327
  72.8 3.2 %halve.4 = (bf16[4,32,512]{2,1,0:T(8,128)(2,1)}, f32[4,32,512]{2,1,0:T(8,128)}) custom-call(f32[8,32,512]{2,1,0:T(8,128)} %copy-done.14, bf16[8,32,512]{2,1,0:T(8,128)(2,1)} %collective-permute-done.9.got_ref), custom_call_target="tpu_custom_call" | custom-call | tf_op jit(solution)/shard_map/halve/pallas_call | solution.py:327
  76.0 1.5 %collective-permute-start.10 = (bf16[4,32,512]{2,1,0:T(8,128)(2,1)}, bf16[4,32,512]{2,1,0:T(8,128)(2,1)S(1)}, u32[]{:S(2)}, u32[]{:S(2)}) collective-permute-start(bf16[4,32,512]{2,1,0:T(8,128)(2,1)} %get-tuple-element.73), channel_id=1, source_target_pairs={{0,2},{1,3},{2,0},{3,1},{4,6},{5,7},{6,4},{7,5},{8,10},{9,11},{10,... | collective-permute-start | bytes 393224 | tf_op jit(solution)/shard_map/ppermute | solution.py:335
  77.5 3.6 %halve.3 = (bf16[4,96,512]{2,1,0:T(8,128)(2,1)}, f32[4,96,512]{2,1,0:T(8,128)}) custom-call(f32[8,96,512]{2,1,0:T(8,128)} %copy-done.11, bf16[8,96,512]{2,1,0:T(8,128)(2,1)} %collective-permute-done.4.got_ref), custom_call_target="tpu_custom_call" | custom-call | tf_op jit(solution)/shard_map/halve/pallas_call | solution.py:327
  85.0 5.8 %all-to-all-start.1 = ((bf16[2,16,512]{2,0,1:T(2,128)(2,1)}), bf16[2,16,512]{2,0,1:T(2,128)(2,1)S(1)}, u32[]{:S(2)}, u32[]{:S(2)}) async-start(bf16[2,16,512]{2,0,1:T(2,128)(2,1)} %copy.29), calls=%async_computation.1 | async-start | bytes 65536 | tf_op jit(solution)/shard_map/all_to_all | solution.py:491
  91.5 1.7 %spread.4 = (f32[32,512]{1,0:T(8,128)}, bf16[32,512]{1,0:T(8,128)(2,1)}, bf16[32,512]{1,0:T(8,128)(2,1)}, bf16[32,512]{1,0:T(8,128)(2,1)}) custom-call(f32[4,32,512]{2,1,0:T(8,128)} %get-tuple-element.72.keep_ref, bf16[4,32,512]{2,1,0:T(8,128)(2,1)} %copy-done.32), custom_call_target="tpu_custom_call" | custom-call | tf_op jit(solution)/shard_map/spread/pallas_call | solution.py:336
  93.1 2.0 %collective-permute-start.11 = (bf16[32,512]{1,0:T(8,128)(2,1)}, bf16[32,512]{1,0:T(8,128)(2,1)S(1)}, u32[]{:S(2)}, u32[]{:S(2)}) collective-permute-start(bf16[32,512]{1,0:T(8,128)(2,1)} %get-tuple-element.75), channel_id=1, source_target_pairs={{0,4},{1,5},{2,6},{3,7},{4,8},{5,9},{6,10},{7,11},{8,12},{9,13},{1... | collective-permute-start | bytes 98312 | tf_op jit(solution)/shard_map/ppermute | solution.py:344
  95.1 2.3 %collective-permute-start.12 = (bf16[32,512]{1,0:T(8,128)(2,1)}, bf16[32,512]{1,0:T(8,128)(2,1)S(1)}, u32[]{:S(2)}, u32[]{:S(2)}) collective-permute-start(bf16[32,512]{1,0:T(8,128)(2,1)} %get-tuple-element.76), channel_id=1, source_target_pairs={{0,8},{1,9},{2,10},{3,11},{4,12},{5,13},{6,14},{7,15},{8,0},{9,1},... | collective-permute-start | bytes 98312 | tf_op jit(solution)/shard_map/ppermute | solution.py:344
  97.4 1.5 %collective-permute-start.13 = (bf16[32,512]{1,0:T(8,128)(2,1)}, bf16[32,512]{1,0:T(8,128)(2,1)S(1)}, u32[]{:S(2)}, u32[]{:S(2)}) collective-permute-start(bf16[32,512]{1,0:T(8,128)(2,1)} %get-tuple-element.77), channel_id=1, source_target_pairs={{0,12},{1,13},{2,14},{3,15},{4,0},{5,1},{6,2},{7,3},{8,4},{9,5},{1... | collective-permute-start | bytes 98312 | tf_op jit(solution)/shard_map/ppermute | solution.py:344
  100.3 3.5 %edge.1 = bf16[1536,512]{1,0:T(8,128)(2,1)} custom-call(bf16[1536,512]{1,0:T(8,128)(2,1)S(1)} %get-tuple-element.54.dpre_ref, bf16[1536,512]{1,0:T(8,128)(2,1)S(1)} %copy-done.5, bf16[1536,512]{1,0:T(8,128)(2,1)S(1)} %copy-done.1), custom_call_target="tpu_custom_call" | custom-call | tf_op jit(solution)/shard_map/edge/pallas_call | solution.py:479
  104.4 2.2 %node.1 = bf16[256,512]{1,0:T(8,128)(2,1)} custom-call(s32[1,16,2]{2,1,0:T(8,128)} %copy.30.index_ref, f32[256,512]{1,0:T(8,128)} %copy-done.15, bf16[64,512]{1,0:T(8,128)(2,1)} %copy-done.34, bf16[64,512]{1,0:T(8,128)(2,1)} %collective-permute-done.3.above_ref, bf16[2,16,512]{2,1,0:T(8,128)(2,1)} %copy.31.far_ref), custom_call_target="tpu_custom_call" | custom-call | tf_op jit(solution)/shard_map/node/pallas_call | solution.py:492
  106.5 2.0 %spread.5 = (f32[96,512]{1,0:T(8,128)}, bf16[96,512]{1,0:T(8,128)(2,1)}, bf16[96,512]{1,0:T(8,128)(2,1)}, bf16[96,512]{1,0:T(8,128)(2,1)}) custom-call(f32[4,96,512]{2,1,0:T(8,128)} %get-tuple-element.80.keep_ref, bf16[4,96,512]{2,1,0:T(8,128)(2,1)} %collective-permute-done.15.got_ref), custom_call_target="tpu_custom_call" | custom-call | tf_op jit(solution)/shard_map/spread/pallas_call | solution.py:336
  109.8 2.7 %collective-permute-start.18 = (bf16[96,512]{1,0:T(8,128)(2,1)}, bf16[96,512]{1,0:T(8,128)(2,1)S(1)}, u32[]{:S(2)}, u32[]{:S(2)}) collective-permute-start(bf16[96,512]{1,0:T(8,128)(2,1)} %get-tuple-element.85), channel_id=1, source_target_pairs={{0,12},{1,13},{2,14},{3,15},{4,0},{5,1},{6,2},{7,3},{8,4},{9,5},{1... | collective-permute-start | bytes 294920 | tf_op jit(solution)/shard_map/ppermute | solution.py:344
  113.1 2.0 %spread.3 = (f32[96,512]{1,0:T(8,128)}, bf16[96,512]{1,0:T(8,128)(2,1)}, bf16[96,512]{1,0:T(8,128)(2,1)}, bf16[96,512]{1,0:T(8,128)(2,1)}) custom-call(f32[4,96,512]{2,1,0:T(8,128)} %get-tuple-element.64.keep_ref, bf16[4,96,512]{2,1,0:T(8,128)(2,1)} %collective-permute-done.5.got_ref), custom_call_target="tpu_custom_call" | custom-call | tf_op jit(solution)/shard_map/spread/pallas_call | solution.py:336
  117.2 2.9 %collective-permute-start.8 = (bf16[96,512]{1,0:T(8,128)(2,1)}, bf16[96,512]{1,0:T(8,128)(2,1)S(1)}, u32[]{:S(2)}, u32[]{:S(2)}) collective-permute-start(bf16[96,512]{1,0:T(8,128)(2,1)} %get-tuple-element.69), channel_id=1, source_target_pairs={{0,12},{1,13},{2,14},{3,15},{4,0},{5,1},{6,2},{7,3},{8,4},{9,5},{1... | collective-permute-start | bytes 294920 | tf_op jit(solution)/shard_map/ppermute | solution.py:344
  123.7 3.7 %collective-permute-done.7 = bf16[96,512]{1,0:T(8,128)(2,1)S(1)} collective-permute-done((bf16[96,512]{1,0:T(8,128)(2,1)}, bf16[96,512]{1,0:T(8,128)(2,1)S(1)}, u32[]{:S(2)}, u32[]{:S(2)}) %collective-permute-start.7) | collective-permute-done | bytes 98336 | tf_op jit(solution)/shard_map/ppermute | solution.py:344
  127.5 1.7 %convert_add_fusion.1 = f32[96,512]{1,0:T(8,128)} fusion(bf16[96,512]{1,0:T(8,128)(2,1)S(1)} %collective-permute-done.8, bf16[96,512]{1,0:T(8,128)(2,1)S(1)} %collective-permute-done.7, f32[96,512]{1,0:T(8,128)} %get-tuple-element.66, bf16[96,512]{1,0:T(8,128)(2,1)S(1)} %collective-permute-done.6), kind=kLoop, calls=%fused_computation.1 | loop fusion | flops 294912 | bytes 688128 | tf_op jit(solution)/shard_map/add | solution.py:344
  (109 shorter events, 37.3 us)
Async XLA Ops:
  3.8 20.2 %collective-permute-start = (bf16[64,512]{1,0:T(8,128)(2,1)}, bf16[64,512]{1,0:T(8,128)(2,1)S(1)}, u32[]{:S(2)}, u32[]{:S(2)}) collective-permute-start(bf16[64,512]{1,0:T(8,128)(2,1)} %get-tuple-element.46), channel_id=1, source_target_pairs={{0,1},{1,2},{2,3},{3,4},{4,5},{5,6},{6,7},{7,8},{8,9},{9,10},{10,1... | collective-permute-start | bytes 196616 | tf_op jit(solution)/shard_map/ppermute | solution.py:382
  6.1 17.8 %collective-permute-start.1 = (bf16[64,512]{1,0:T(8,128)(2,1)}, bf16[64,512]{1,0:T(8,128)(2,1)S(1)}, u32[]{:S(2)}, u32[]{:S(2)}) collective-permute-start(bf16[64,512]{1,0:T(8,128)(2,1)} %get-tuple-element.47), channel_id=1, source_target_pairs={{1,0},{2,1},{3,2},{4,3},{5,4},{6,5},{7,6},{8,7},{9,8},{10,9},{11,1... | collective-permute-start | bytes 196616 | tf_op jit(solution)/shard_map/ppermute | solution.py:383
  38.1 13.4 %copy-start.4 = (bf16[1536,512]{1,0:T(8,128)(2,1)S(1)}, bf16[1536,512]{1,0:T(8,128)(2,1)}, u32[]{:S(2)}) copy-start(bf16[1536,512]{1,0:T(8,128)(2,1)} %cot_ref.3) | copy-start | bytes 4718596
  38.1 13.4 %copy-start.10 = (bf16[512,512]{1,0:T(8,128)(2,1)S(1)}, bf16[512,512]{1,0:T(8,128)(2,1)}, u32[]{:S(2)}) copy-start(bf16[512,512]{1,0:T(8,128)(2,1)} %w2_ref.3) | copy-start | bytes 1572868
  38.1 13.4 %copy-start.22 = (f32[512]{0:T(512)S(1)}, f32[512]{0:T(512)}, u32[]{:S(2)}) copy-start(f32[512]{0:T(512)} %param.26) | copy-start | bytes 6148
  51.5 16.3 %collective-permute-start.14 = (bf16[8,96,512]{2,1,0:T(8,128)(2,1)S(1)}, bf16[8,96,512]{2,1,0:T(8,128)(2,1)S(1)}, u32[]{:S(2)}, u32[]{:S(2)}) collective-permute-start(bf16[8,96,512]{2,1,0:T(8,128)(2,1)S(1)} %get-tuple-element.79), channel_id=1, source_target_pairs={{0,1},{1,0},{2,3},{3,2},{4,5},{5,4},{6,7},{7,6},{8,9},{9,8},{10,11... | collective-permute-start | bytes 2359304 | tf_op jit(solution)/shard_map/ppermute | solution.py:325
  67.3 10.3 %collective-permute-start.4 = (bf16[8,96,512]{2,1,0:T(8,128)(2,1)}, bf16[8,96,512]{2,1,0:T(8,128)(2,1)}, u32[]{:S(2)}, u32[]{:S(2)}) collective-permute-start(bf16[8,96,512]{2,1,0:T(8,128)(2,1)} %get-tuple-element.63), channel_id=1, source_target_pairs={{0,1},{1,0},{2,3},{3,2},{4,5},{5,4},{6,7},{7,6},{8,9},{9,8},{10,11... | collective-permute-start | bytes 2359304 | tf_op jit(solution)/shard_map/ppermute | solution.py:325
  67.8 5.0 %collective-permute-start.9 = (bf16[8,32,512]{2,1,0:T(8,128)(2,1)S(1)}, bf16[8,32,512]{2,1,0:T(8,128)(2,1)}, u32[]{:S(2)}, u32[]{:S(2)}) collective-permute-start(bf16[8,32,512]{2,1,0:T(8,128)(2,1)S(1)} %get-tuple-element.71), channel_id=1, source_target_pairs={{0,1},{1,0},{2,3},{3,2},{4,5},{5,4},{6,7},{7,6},{8,9},{9,8},{10,11... | collective-permute-start | bytes 786440 | tf_op jit(solution)/shard_map/ppermute | solution.py:325
  72.3 34.2 %collective-permute-start.15 = (bf16[4,96,512]{2,1,0:T(8,128)(2,1)}, bf16[4,96,512]{2,1,0:T(8,128)(2,1)}, u32[]{:S(2)}, u32[]{:S(2)}) collective-permute-start(bf16[4,96,512]{2,1,0:T(8,128)(2,1)} %get-tuple-element.81), channel_id=1, source_target_pairs={{0,2},{1,3},{2,0},{3,1},{4,6},{5,7},{6,4},{7,5},{8,10},{9,11},{10,... | collective-permute-start | bytes 1179656 | tf_op jit(solution)/shard_map/ppermute | solution.py:335
  72.8 8.8 %copy-start.30 = (bf16[64,512]{1,0:T(8,128)(2,1)S(1)}, bf16[64,512]{1,0:T(8,128)(2,1)}, u32[]{:S(2)}) copy-start(bf16[64,512]{1,0:T(8,128)(2,1)} %copy-done.29) | copy-start | bytes 196612
  76.0 14.8 %collective-permute-start.10 = (bf16[4,32,512]{2,1,0:T(8,128)(2,1)}, bf16[4,32,512]{2,1,0:T(8,128)(2,1)S(1)}, u32[]{:S(2)}, u32[]{:S(2)}) collective-permute-start(bf16[4,32,512]{2,1,0:T(8,128)(2,1)} %get-tuple-element.73), channel_id=1, source_target_pairs={{0,2},{1,3},{2,0},{3,1},{4,6},{5,7},{6,4},{7,5},{8,10},{9,11},{10,... | collective-permute-start | bytes 393224 | tf_op jit(solution)/shard_map/ppermute | solution.py:335
  81.2 32.0 %collective-permute-start.5 = (bf16[4,96,512]{2,1,0:T(8,128)(2,1)}, bf16[4,96,512]{2,1,0:T(8,128)(2,1)}, u32[]{:S(2)}, u32[]{:S(2)}) collective-permute-start(bf16[4,96,512]{2,1,0:T(8,128)(2,1)} %get-tuple-element.65), channel_id=1, source_target_pairs={{0,2},{1,3},{2,0},{3,1},{4,6},{5,7},{6,4},{7,5},{8,10},{9,11},{10,... | collective-permute-start | bytes 1179656 | tf_op jit(solution)/shard_map/ppermute | solution.py:335
  81.6 13.5 %collective-permute-start.2 = (bf16[64,512]{1,0:T(8,128)(2,1)S(1)}, bf16[64,512]{1,0:T(8,128)(2,1)S(1)}, u32[]{:S(2)}, u32[]{:S(2)}) collective-permute-start(bf16[64,512]{1,0:T(8,128)(2,1)S(1)} %copy-done.30), channel_id=1, source_target_pairs={{0,1},{1,2},{2,3},{3,4},{4,5},{5,6},{6,7},{7,8},{8,9},{9,10},{10,1... | collective-permute-start | bytes 196616 | tf_op jit(solution)/shard_map/ppermute | solution.py:490
  83.1 14.4 %collective-permute-start.3 = (bf16[64,512]{1,0:T(8,128)(2,1)S(1)}, bf16[64,512]{1,0:T(8,128)(2,1)}, u32[]{:S(2)}, u32[]{:S(2)}) collective-permute-start(bf16[64,512]{1,0:T(8,128)(2,1)S(1)} %get-tuple-element.60), channel_id=1, source_target_pairs={{1,0},{2,1},{3,2},{4,3},{5,4},{6,5},{7,6},{8,7},{9,8},{10,9},{11,1... | collective-permute-start | bytes 196616 | tf_op jit(solution)/shard_map/ppermute | solution.py:489
  85.0 18.7 %all-to-all-start.1 = ((bf16[2,16,512]{2,0,1:T(2,128)(2,1)}), bf16[2,16,512]{2,0,1:T(2,128)(2,1)S(1)}, u32[]{:S(2)}, u32[]{:S(2)}) async-start(bf16[2,16,512]{2,0,1:T(2,128)(2,1)} %copy.29), calls=%async_computation.1 | async-start | bytes 65536 | tf_op jit(solution)/shard_map/all_to_all | solution.py:491
  93.1 16.0 %collective-permute-start.11 = (bf16[32,512]{1,0:T(8,128)(2,1)}, bf16[32,512]{1,0:T(8,128)(2,1)S(1)}, u32[]{:S(2)}, u32[]{:S(2)}) collective-permute-start(bf16[32,512]{1,0:T(8,128)(2,1)} %get-tuple-element.75), channel_id=1, source_target_pairs={{0,4},{1,5},{2,6},{3,7},{4,8},{5,9},{6,10},{7,11},{8,12},{9,13},{1... | collective-permute-start | bytes 98312 | tf_op jit(solution)/shard_map/ppermute | solution.py:344
  95.1 14.7 %collective-permute-start.12 = (bf16[32,512]{1,0:T(8,128)(2,1)}, bf16[32,512]{1,0:T(8,128)(2,1)S(1)}, u32[]{:S(2)}, u32[]{:S(2)}) collective-permute-start(bf16[32,512]{1,0:T(8,128)(2,1)} %get-tuple-element.76), channel_id=1, source_target_pairs={{0,8},{1,9},{2,10},{3,11},{4,12},{5,13},{6,14},{7,15},{8,0},{9,1},... | collective-permute-start | bytes 98312 | tf_op jit(solution)/shard_map/ppermute | solution.py:344
  97.4 15.1 %collective-permute-start.13 = (bf16[32,512]{1,0:T(8,128)(2,1)}, bf16[32,512]{1,0:T(8,128)(2,1)S(1)}, u32[]{:S(2)}, u32[]{:S(2)}) collective-permute-start(bf16[32,512]{1,0:T(8,128)(2,1)} %get-tuple-element.77), channel_id=1, source_target_pairs={{0,12},{1,13},{2,14},{3,15},{4,0},{5,1},{6,2},{7,3},{8,4},{9,5},{1... | collective-permute-start | bytes 98312 | tf_op jit(solution)/shard_map/ppermute | solution.py:344
  108.6 8.6 %collective-permute-start.16 = (bf16[96,512]{1,0:T(8,128)(2,1)}, bf16[96,512]{1,0:T(8,128)(2,1)S(1)}, u32[]{:S(2)}, u32[]{:S(2)}) collective-permute-start(bf16[96,512]{1,0:T(8,128)(2,1)} %get-tuple-element.83), channel_id=1, source_target_pairs={{0,4},{1,5},{2,6},{3,7},{4,8},{5,9},{6,10},{7,11},{8,12},{9,13},{1... | collective-permute-start | bytes 294920 | tf_op jit(solution)/shard_map/ppermute | solution.py:344
  109.2 12.3 %collective-permute-start.17 = (bf16[96,512]{1,0:T(8,128)(2,1)}, bf16[96,512]{1,0:T(8,128)(2,1)S(1)}, u32[]{:S(2)}, u32[]{:S(2)}) collective-permute-start(bf16[96,512]{1,0:T(8,128)(2,1)} %get-tuple-element.84), channel_id=1, source_target_pairs={{0,8},{1,9},{2,10},{3,11},{4,12},{5,13},{6,14},{7,15},{8,0},{9,1},... | collective-permute-start | bytes 294920 | tf_op jit(solution)/shard_map/ppermute | solution.py:344
  109.8 11.7 %collective-permute-start.18 = (bf16[96,512]{1,0:T(8,128)(2,1)}, bf16[96,512]{1,0:T(8,128)(2,1)S(1)}, u32[]{:S(2)}, u32[]{:S(2)}) collective-permute-start(bf16[96,512]{1,0:T(8,128)(2,1)} %get-tuple-element.85), channel_id=1, source_target_pairs={{0,12},{1,13},{2,14},{3,15},{4,0},{5,1},{6,2},{7,3},{8,4},{9,5},{1... | collective-permute-start | bytes 294920 | tf_op jit(solution)/shard_map/ppermute | solution.py:344
  115.2 8.5 %collective-permute-start.6 = (bf16[96,512]{1,0:T(8,128)(2,1)}, bf16[96,512]{1,0:T(8,128)(2,1)S(1)}, u32[]{:S(2)}, u32[]{:S(2)}) collective-permute-start(bf16[96,512]{1,0:T(8,128)(2,1)} %get-tuple-element.67), channel_id=1, source_target_pairs={{0,4},{1,5},{2,6},{3,7},{4,8},{5,9},{6,10},{7,11},{8,12},{9,13},{1... | collective-permute-start | bytes 294920 | tf_op jit(solution)/shard_map/ppermute | solution.py:344
  115.7 11.8 %collective-permute-start.7 = (bf16[96,512]{1,0:T(8,128)(2,1)}, bf16[96,512]{1,0:T(8,128)(2,1)S(1)}, u32[]{:S(2)}, u32[]{:S(2)}) collective-permute-start(bf16[96,512]{1,0:T(8,128)(2,1)} %get-tuple-element.68), channel_id=1, source_target_pairs={{0,8},{1,9},{2,10},{3,11},{4,12},{5,13},{6,14},{7,15},{8,0},{9,1},... | collective-permute-start | bytes 294920 | tf_op jit(solution)/shard_map/ppermute | solution.py:344
  117.2 10.3 %collective-permute-start.8 = (bf16[96,512]{1,0:T(8,128)(2,1)}, bf16[96,512]{1,0:T(8,128)(2,1)S(1)}, u32[]{:S(2)}, u32[]{:S(2)}) collective-permute-start(bf16[96,512]{1,0:T(8,128)(2,1)} %get-tuple-element.69), channel_id=1, source_target_pairs={{0,12},{1,13},{2,14},{3,15},{4,0},{5,1},{6,2},{7,3},{8,4},{9,5},{1... | collective-permute-start | bytes 294920 | tf_op jit(solution)/shard_map/ppermute | solution.py:344
  (31 other events, 68.1 us)

commit v2 on v1

--- a/solution.py
+++ b/solution.py
@@ -9,7 +9,7 @@
 
 NEAR = 64
 EPSILON = 1e-05
-TILE = 256
+TILE = 512
 LANES = 128
 F32 = jnp.float32
 BF16 = jnp.bfloat16
@@ -78,12 +78,12 @@
 
 
 def outgoing_kernel(index_ref, node_ref, far_ref, head_ref, tail_ref):
-    tiles, places = index_ref.shape[1], index_ref.shape[2]
+    places, tiles = index_ref.shape[1], index_ref.shape[2]
     nodes = node_ref.shape[0]
-    lane = lax.broadcasted_iota(jnp.int32, (tiles, nodes), 1)
-    index = index_ref[0]
+    place = lax.broadcasted_iota(jnp.int32, (nodes, tiles), 0)
     for j in range(places):
-        far_ref[j] = dot(ones_where(index[:, j : j + 1] == lane), node_ref[...]).astype(BF16)
+        picks = ones_where(place == index_ref[0, j : j + 1, :])
+        far_ref[:, j, :] = dot(picks, node_ref[...], TN).astype(BF16)
     head_ref[...] = node_ref[:NEAR, :]
     tail_ref[...] = node_ref[nodes - NEAR :, :]
 
@@ -119,7 +119,7 @@
         table_ref[NEAR : NEAR + nodes, :] = node_ref[...]
         table_ref[NEAR + nodes : far_base, :] = upper_ref[...]
         for j in range(places):
-            table_ref[far_base + j * tiles : far_base + (j + 1) * tiles, :] = far_ref[j]
+            table_ref[far_base + j * tiles : far_base + (j + 1) * tiles, :] = far_ref[:, j, :]
         used = far_base + places * tiles
         if used < rows:
             table_ref[used:, :] = jnp.zeros((rows - used, latent), BF16)
@@ -253,7 +253,7 @@
         upper_ref[...] = back[NEAR + nodes : 2 * NEAR + nodes, :].astype(BF16)
         for j in range(places):
             at = 2 * NEAR + nodes + j * tiles
-            far_ref[j] = back[at : at + tiles, :].astype(BF16)
+            far_ref[:, j, :] = back[at : at + tiles, :].astype(BF16)
         partial_ref[...] = (
             base_ref[...]
             + back[NEAR : NEAR + nodes, :]
@@ -269,13 +269,13 @@
 
 
 def node_kernel(index_ref, partial_ref, below_ref, above_ref, far_ref, out_ref):
-    tiles, places = index_ref.shape[1], index_ref.shape[2]
+    places, tiles = index_ref.shape[1], index_ref.shape[2]
     nodes = partial_ref.shape[0]
-    lane = lax.broadcasted_iota(jnp.int32, (tiles, nodes), 1)
-    index = index_ref[0]
+    place = lax.broadcasted_iota(jnp.int32, (nodes, tiles), 0)
     total = partial_ref[...]
     for j in range(places):
-        total = total + dot(ones_where(index[:, j : j + 1] == lane), far_ref[j], TN)
+        picks = ones_where(place == index_ref[0, j : j + 1, :])
+        total = total + dot(picks, far_ref[:, j, :])
     out_ref[:NEAR, :] = (total[:NEAR, :] + below_ref[...].astype(F32)).astype(BF16)
     out_ref[NEAR : nodes - NEAR, :] = total[NEAR : nodes - NEAR, :].astype(BF16)
     out_ref[nodes - NEAR :, :] = (
@@ -283,10 +283,20 @@
     ).astype(BF16)
 
 
-def halve_kernel(shift, keep_ref, got_ref, send_ref, kept_ref):
+def halve_kernel(shift, count, *refs):
+    keeps, gots = refs[:count], refs[count : 2 * count]
+    send_ref, kept_ref = refs[2 * count :]
     bit = lax.rem(lax.div(lax.axis_index("tiles"), 2**shift), 2)
-    send_ref[0] = (keep_ref[1 - bit] + got_ref[1 - bit].astype(F32)).astype(BF16)
-    kept_ref[0] = keep_ref[bit] + got_ref[bit].astype(F32)
+    at = 0
+    for keep_ref, got_ref in zip(keeps, gots):
+        rows = keep_ref.shape[1]
+        for q in range(keep_ref.shape[0] // 2):
+            there, here = 2 * q + 1 - bit, 2 * q + bit
+            send_ref[q, at : at + rows, :] = (
+                keep_ref[there] + got_ref[there].astype(F32)
+            ).astype(BF16)
+            kept_ref[q, at : at + rows, :] = keep_ref[here] + got_ref[here].astype(F32)
+        at += rows
 
 
 def spread_kernel(keep_ref, got_ref, own_ref, *send_refs):
@@ -298,8 +308,14 @@
         send_ref[...] = (keep_ref[there] + got_ref[there].astype(F32)).astype(BF16)
 
 
-def whole(shape=None):
-    return pl.BlockSpec(memory_space=pltpu.VMEM)
+def finish_kernel(count, own_ref, *refs):
+    total = own_ref[...]
+    for got_ref in refs[:count]:
+        total = total + got_ref[...].astype(F32)
+    at = 0
+    for out_ref in refs[count:]:
+        out_ref[...] = total[at : at + out_ref.shape[0], :]
+        at += out_ref.shape[0]
 
 
 def tiled(shape):
@@ -316,33 +332,47 @@
     return jax.ShapeDtypeStruct(shape, dtype)
 
 
-def flip(tiles, bit):
-    return [(i, i ^ bit) for i in range(tiles)]
-
-
-def fold(send, keep, tiles):
-    half, rows, width = keep.shape
-    got = lax.ppermute(send, "tiles", flip(tiles, 1))
-    quarter = half // 2
-    send, keep = pl.pallas_call(
-        functools.partial(halve_kernel, 1),
-        grid=(quarter,),
-        in_specs=[tiled((2, rows, width)), tiled((2, rows, width))],
-        out_specs=[tiled((1, rows, width)), tiled((1, rows, width))],
-        out_shape=[shaped((quarter, rows, width), BF16), shaped((quarter, rows, width), F32)],
+def swap(tiles, bit, send):
+    return lax.ppermute(send, "tiles", [(i, i ^ bit) for i in range(tiles)])
+
+
+def halve(keeps, gots):
+    half, _, width = keeps[0].shape
+    rows = sum(keep.shape[1] for keep in keeps)
+    return pl.pallas_call(
+        functools.partial(halve_kernel, 1, len(keeps)),
+        out_shape=[shaped((half // 2, rows, width), BF16), shaped((half // 2, rows, width), F32)],
+        compiler_params=pltpu.CompilerParams(vmem_limit_bytes=16 * MIB),
         name="halve",
-    )(keep, got)
-    got = lax.ppermute(send, "tiles", flip(tiles, 2))
-    own, *sends = pl.pallas_call(
+    )(*keeps, *gots)
+
+
+def spread(keep, got):
+    quarter, rows, width = keep.shape
+    return pl.pallas_call(
         spread_kernel,
         out_shape=[shaped((rows, width), F32)] + [shaped((rows, width), BF16)] * (quarter - 1),
+        compiler_params=pltpu.CompilerParams(vmem_limit_bytes=16 * MIB),
         name="spread",
     )(keep, got)
-    total = own
+
+
+def exchange(tiles, sends):
+    quarter = len(sends) + 1
+    gots = []
     for k, send in enumerate(sends):
         pairs = [(i, (i // 4 + k + 1) % quarter * 4 + i % 4) for i in range(tiles)]
-        total = total + lax.ppermute(send, "tiles", pairs).astype(F32)
-    return total
+        gots.append(lax.ppermute(send, "tiles", pairs))
+    return gots
+
+
+def finish(own, gots, sizes):
+    return pl.pallas_call(
+        functools.partial(finish_kernel, len(gots)),
+        out_shape=[shaped((size, own.shape[1]), F32) for size in sizes],
+        compiler_params=pltpu.CompilerParams(vmem_limit_bytes=16 * MIB),
+        name="finish",
+    )(own, *gots)
 
 
 def shards(
@@ -364,8 +394,9 @@
     downward = [(i + 1, i) for i in range(tiles - 1)]
     sender = edge_sender.reshape(edges // LANES, LANES)
     receiver = edge_receiver.reshape(edges // LANES, LANES)
+    listed = jnp.swapaxes(send_index, 1, 2)
     row = lambda vector: vector.reshape(1, -1)
-    params = pltpu.CompilerParams(vmem_limit_bytes=40 * MIB)
+    params = pltpu.CompilerParams(vmem_limit_bytes=60 * MIB)
     edge_block = tiled((TILE, latent))
     vector = fixed((1, latent))
     square = fixed((latent, latent))
@@ -373,15 +404,16 @@
     outgoing, head, tail = pl.pallas_call(
         outgoing_kernel,
         out_shape=[
-            shaped((places, tiles, latent), BF16),
+            shaped((tiles, places, latent), BF16),
             shaped((NEAR, latent), BF16),
             shaped((NEAR, latent), BF16),
         ],
+        compiler_params=pltpu.CompilerParams(vmem_limit_bytes=16 * MIB),
         name="outgoing",
-    )(send_index, node_latent)
+    )(listed, node_latent)
     lower = lax.ppermute(tail, "tiles", upward)
     upper = lax.ppermute(head, "tiles", downward)
-    incoming = lax.all_to_all(outgoing, "tiles", split_axis=1, concat_axis=1, tiled=True)
+    incoming = lax.all_to_all(outgoing, "tiles", split_axis=0, concat_axis=0, tiled=True)
 
     if fast:
         grad_shapes = lambda count: [
@@ -399,7 +431,7 @@
             edge_block,
             fixed(sender.shape), fixed(receiver.shape),
             fixed((nodes, latent)), fixed((NEAR, latent)), fixed((NEAR, latent)),
-            fixed((places, tiles, latent)),
+            fixed((tiles, places, latent)),
             fixed(edge_w1.shape), vector, square, vector, vector,
             fixed(node_w1.shape), vector, square, vector, vector,
             fixed((nodes, latent)),
@@ -448,6 +480,14 @@
         name="slope",
     )(edge_cot, receiver, dsum, hidden, slope, normed, inverse, edge_w2, row(edge_gain))
 
+    if fast:
+        send, chain = halve(
+            [node_keep, second_keep],
+            [swap(tiles, 1, node_send), swap(tiles, 1, second_send)],
+        )
+        dpre, send = lax.optimization_barrier((dpre, send))
+        got = swap(tiles, 2, send)
+
     first_grads = grad_shapes(3 * latent)
     first_send, first_keep, to_lower, to_upper, to_far, partial = pl.pallas_call(
         functools.partial(first_kernel, tiles, places, fast),
@@ -459,13 +499,13 @@
         ],
         out_specs=[
             fixed(first_grads[0].shape), fixed(first_grads[1].shape),
-            fixed((NEAR, latent)), fixed((NEAR, latent)), fixed((places, tiles, latent)),
+            fixed((NEAR, latent)), fixed((NEAR, latent)), fixed((tiles, places, latent)),
             fixed((nodes, latent)),
         ],
         out_shape=first_grads + [
             shaped((NEAR, latent), BF16),
             shaped((NEAR, latent), BF16),
-            shaped((places, tiles, latent), BF16),
+            shaped((tiles, places, latent), BF16),
             shaped((nodes, latent), F32),
         ],
         scratch_shapes=[
@@ -488,19 +528,24 @@
 
     above = lax.ppermute(to_lower, "tiles", downward)
     below = lax.ppermute(to_upper, "tiles", upward)
-    returned = lax.all_to_all(to_far, "tiles", split_axis=1, concat_axis=1, tiled=True)
+    returned = lax.all_to_all(to_far, "tiles", split_axis=0, concat_axis=0, tiled=True)
     grad_node = pl.pallas_call(
         node_kernel,
         out_shape=shaped((nodes, latent), BF16),
+        compiler_params=pltpu.CompilerParams(vmem_limit_bytes=16 * MIB),
         name="node",
-    )(send_index, partial, below, above, returned)
+    )(listed, partial, below, above, returned)
 
     if fast:
-        node_total = fold(node_send, node_keep, tiles)
-        cut = 2 * latent // tiles
-        grad_node_w1, grad_node_w2 = node_total[:cut], node_total[cut:]
-        grad_edge_w2 = fold(second_send, second_keep, tiles)
-        grad_edge_w1 = fold(first_send, first_keep, tiles)
+        send, late_chain = halve([first_keep], [swap(tiles, 1, first_send)])
+        late_got = swap(tiles, 2, send)
+        own, *sends = spread(chain, got)
+        per = latent // tiles
+        grad_node_w1, grad_node_w2, grad_edge_w2 = finish(
+            own, exchange(tiles, sends), [2 * per, per, per]
+        )
+        own, *sends = spread(late_chain, late_got)
+        (grad_edge_w1,) = finish(own, exchange(tiles, sends), [3 * per])
     else:
         scatter = functools.partial(
             lax.psum_scatter, axis_name="tiles", scatter_dimension=0, tiled=True

time: 130 us -> 102 us (0.78)
  local copies, waits for them, and re-layouts: 27.5 us -> 4.73 us
  waiting for transfers between devices: 5.14 us -> 17.2 us
  Pallas kernels: 47 us -> 38.7 us
  starting transfers between devices: 29.7 us -> 24.3 us
  other arithmetic: 3.27 us -> 0 us
    unnamed x71 -> x22, local copies, waits for them, and re-layouts: 24.1 us -> 4.73 us
    pallas_call x8, Pallas kernels: 20.1 us -> 3.12 us  [the longest x2 1.45 us: finish(): pl.pallas_call(functools.partial(finish_kernel, len(gots)), out_shape=[sh...]
    ppermute x15 -> x11, waiting for transfers between devices: 5.13 us -> 13.9 us  [the longest x5 13.9 us: swap(): return lax.ppermute(send, 'tiles', [(i, i ^ bit) for i in range(tiles)])]
    all_to_all x1, waiting for transfers between devices: 0.01 us -> 3.32 us  [shards(): lax.all_to_all(to_far, 'tiles', split_axis=0, concat_axis=0, tiled=True)]
    add x3 -> x0, other arithmetic: 3.27 us -> none  [fold(): total = total + lax.ppermute(send, 'tiles', pairs).astype(F32)]
    pallas_call x1, Pallas kernels: 5.52 us -> 8.51 us  [shards(): pl.pallas_call(functools.partial(slope_kernel, tiles, fast), grid=(steps,...]
    ppermute x15 -> x11, starting transfers between devices: 17.6 us -> 14.6 us  [the longest x6 12.8 us: exchange(): gots.append(lax.ppermute(send, 'tiles', pairs))]
    pallas_call x1, Pallas kernels: 5.67 us -> 8.23 us  [shards(): pl.pallas_call(functools.partial(first_kernel, tiles, places, fast), grid...]
  transfers between devices with their start and end apart: 20 -> 16, of which waited for: 2 -> 4; matrix products, arithmetic and copies ran while one was open for 4% -> 0% of each run, Pallas kernels for 26% -> 15%
where the time goes in v2:
time: 102 us
  Pallas kernels  38.7 us (38%)
  starting transfers between devices  24.3 us (24%)
  waiting for transfers between devices  17.2 us (17%)
  blocking collectives  15.8 us (15%)
  local copies, waits for them, and re-layouts  4.73 us (5%)
    all_to_all x1, blocking collectives, shards(): lax.all_to_all(outgoing, 'tiles', split_axis=0, concat_axis=0, tiled=True)  15.8 us
    pallas_call x1, Pallas kernels, shards(): pl.pallas_call(functools.partial(forward_kernel, tiles, places, fast), gr...  14.3 us
    ppermute x5, waiting for transfers between devices, swap(): return lax.ppermute(send, 'tiles', [(i, i ^ bit) for i in range(tiles)])  13.9 us
    ppermute x6, starting transfers between devices, exchange(): gots.append(lax.ppermute(send, 'tiles', pairs))  12.8 us
    pallas_call x1, Pallas kernels, shards(): pl.pallas_call(functools.partial(slope_kernel, tiles, fast), grid=(steps,...  8.51 us
    pallas_call x1, Pallas kernels, shards(): pl.pallas_call(functools.partial(first_kernel, tiles, places, fast), grid...  8.23 us
    unnamed x22, local copies, waits for them, and re-layouts  4.73 us
    pallas_call x1, Pallas kernels, shards(): pl.pallas_call(edge_kernel, grid=(steps,), in_specs=[edge_block, edge_blo...  4.59 us
  transfers between devices with their start and end apart: 16, of which 4 were waited for; matrix products, arithmetic and copies ran while one was open for 0% of the time, Pallas kernels for 15%

profile of v2, /device:TPU:0, one launch (start us, length us, event | category | flops | bytes accessed | tf_op | source)
XLA Modules:
  0.0 101.6 jit_solution(2579325788839360436)
XLA Ops:
  0.6 0.9 copy-done
  2.5 2.4 %collective-permute-start = (bf16[64,512]{1,0:T(8,128)(2,1)S(1)}, bf16[64,512]{1,0:T(8,128)(2,1)S(1)}, u32[]{:S(2)}, u32[]{:S(2)}) collective-permute-start(bf16[64,512]{1,0:T(8,128)(2,1)S(1)} %get-tuple-element.45), channel_id=1, source_target_pairs={{0,1},{1,2},{2,3},{3,4},{4,5},{5,6},{6,7},{7,8},{8,9},{9,10},{10,1... | collective-permute-start | bytes 196616 | tf_op jit(solution)/shard_map/ppermute | solution.py:414
  4.9 1.3 %collective-permute-start.1 = (bf16[64,512]{1,0:T(8,128)(2,1)S(1)}, bf16[64,512]{1,0:T(8,128)(2,1)S(1)}, u32[]{:S(2)}, u32[]{:S(2)}) collective-permute-start(bf16[64,512]{1,0:T(8,128)(2,1)S(1)} %get-tuple-element.46), channel_id=1, source_target_pairs={{1,0},{2,1},{3,2},{4,3},{5,4},{6,5},{7,6},{8,7},{9,8},{10,9},{11,1... | collective-permute-start | bytes 196616 | tf_op jit(solution)/shard_map/ppermute | solution.py:415
  6.2 15.8 %all_to_all.10.far_ref = bf16[16,2,512]{2,1,0:T(2,128)(2,1)} all-to-all(bf16[16,2,512]{2,1,0:T(2,128)(2,1)S(1)} %get-tuple-element.47), channel_id=1, replica_groups=mesh['groups'=2,'tiles'=16] {'tiles'}, dimensions={0} | all-to-all | bytes 65536 | tf_op jit(solution)/shard_map/all_to_all | solution.py:416
  22.6 14.3 %forward.1 = (bf16[1536,512]{1,0:T(8,128)(2,1)}, bf16[1536,512]{1,0:T(8,128)(2,1)}, f32[1536,512]{1,0:T(8,128)}, f32[1536,128]{1,0:T(8,128)}, bf16[512,512]{1,0:...) custom-call(s32[16]{0:T(128)} %count_ref.1, ...), custom_call_target="tpu_custom_call" | custom-call | tf_op jit(solution)/shard_map/forward/pallas_call | solution.py:426
  37.0 8.5 %slope.1 = (bf16[1536,512]{1,0:T(8,128)(2,1)}, bf16[8,32,512]{2,1,0:T(8,128)(2,1)}, f32[8,32,512]{2,1,0:T(8,128)}) custom-call(bf16[1536,512]{1,0:T(8,128)(2,1)} %cot_ref.3, s32[12,128]{1,0:T(8,128)} %bitcast.12, bf16[256,512]{1,0:T(8,128)(2,1)} %get-tuple-element.48.dsum_ref, bf16[1536,512]{1,0:T(8,128)(2,1)} %get-tuple-element.49.hidden_ref, ...), custom_call_target="tpu_custom_call" | custom-call | tf_op jit(solution)/shard_map/slope/pallas_call | solution.py:469
  46.0 1.4 %collective-permute-done.3.refs_3_ = bf16[8,32,512]{2,1,0:T(8,128)(2,1)S(1)} collective-permute-done((bf16[8,32,512]{2,1,0:T(8,128)(2,1)}, bf16[8,32,512]{2,1,0:T(8,128)(2,1)S(1)}, u32[]{:S(2)}, u32[]{:S(2)}) %collective-permute-start.3) | collective-permute-done | bytes 262176 | tf_op jit(solution)/shard_map/ppermute | solution.py:336
  47.4 1.0 %copy-done.4 = f32[8,32,512]{2,1,0:T(8,128)S(1)} copy-done((f32[8,32,512]{2,1,0:T(8,128)S(1)}, f32[8,32,512]{2,1,0:T(8,128)}, u32[]{:S(2)}) %copy-start.4) | copy-done | bytes 524312
  48.6 8.2 %first.1 = (bf16[8,96,512]{2,1,0:T(8,128)(2,1)}, f32[8,96,512]{2,1,0:T(8,128)}, bf16[64,512]{1,0:T(8,128)(2,1)}, bf16[64,512]{1,0:T(8,128)(2,1)}, bf16[16,2,512]{2,1,0:T(2,128)(2,1)}, /*index=5*/f32[256,512]{1,0:T(8,128)}) custom-call(bf16[1536,512]{1,0:T(8,128)(2,1)} %get-tuple-element.59.dpre_ref, bf16[1536,512]{1,0:T(8,128)(2,1)} %edge_ref.3, ...), custom_call_target="tpu_custom_call" | custom-call | tf_op jit(solution)/shard_map/first/pallas_call | solution.py:492
  57.6 1.8 %collective-permute-done.6.refs_1_ = bf16[8,96,512]{2,1,0:T(8,128)(2,1)S(1)} collective-permute-done((bf16[8,96,512]{2,1,0:T(8,128)(2,1)}, bf16[8,96,512]{2,1,0:T(8,128)(2,1)S(1)}, u32[]{:S(2)}, u32[]{:S(2)}) %collective-permute-start.6) | collective-permute-done | bytes 786464 | tf_op jit(solution)/shard_map/ppermute | solution.py:336
  59.4 1.4 %copy-done.2 = f32[8,96,512]{2,1,0:T(8,128)S(1)} copy-done((f32[8,96,512]{2,1,0:T(8,128)S(1)}, f32[8,96,512]{2,1,0:T(8,128)}, u32[]{:S(2)}) %copy-start.2) | copy-done | bytes 1572888
  61.3 10.7 %collective-permute-done.11.got_ref = bf16[4,128,512]{2,1,0:T(8,128)(2,1)S(1)} collective-permute-done((bf16[4,128,512]{2,1,0:T(8,128)(2,1)S(1)}, bf16[4,128,512]{2,1,0:T(8,128)(2,1)S(1)}, u32[]{:S(2)}, u32[]{:S(2)}) %collective-permute-start.11) | collective-permute-done | bytes 524320 | tf_op jit(solution)/shard_map/ppermute | solution.py:336
  72.5 1.3 %collective-permute-start.4 = (bf16[64,512]{1,0:T(8,128)(2,1)S(1)}, bf16[64,512]{1,0:T(8,128)(2,1)S(1)}, u32[]{:S(2)}, u32[]{:S(2)}) collective-permute-start(bf16[64,512]{1,0:T(8,128)(2,1)S(1)} %copy-done.10), channel_id=1, source_target_pairs={{0,1},{1,2},{2,3},{3,4},{4,5},{5,6},{6,7},{7,8},{8,9},{9,10},{10,1... | collective-permute-start | bytes 196616 | tf_op jit(solution)/shard_map/ppermute | solution.py:530
  73.8 1.3 %collective-permute-start.5 = (bf16[64,512]{1,0:T(8,128)(2,1)S(1)}, bf16[64,512]{1,0:T(8,128)(2,1)S(1)}, u32[]{:S(2)}, u32[]{:S(2)}) collective-permute-start(bf16[64,512]{1,0:T(8,128)(2,1)S(1)} %copy-done.9), channel_id=1, source_target_pairs={{1,0},{2,1},{3,2},{4,3},{5,4},{6,5},{7,6},{8,7},{9,8},{10,9},{11,1... | collective-permute-start | bytes 196616 | tf_op jit(solution)/shard_map/ppermute | solution.py:529
  75.1 4.6 %collective-permute-start.13 = (bf16[128,512]{1,0:T(8,128)(2,1)S(1)}, bf16[128,512]{1,0:T(8,128)(2,1)S(1)}, u32[]{:S(2)}, u32[]{:S(2)}) collective-permute-start(bf16[128,512]{1,0:T(8,128)(2,1)S(1)} %get-tuple-element.79), channel_id=1, source_target_pairs={{0,8},{1,9},{2,10},{3,11},{4,12},{5,13},{6,14},{7,15},{8,0},{9,1},... | collective-permute-start | bytes 393224 | tf_op jit(solution)/shard_map/ppermute | solution.py:365
  79.7 2.9 %collective-permute-start.14 = (bf16[128,512]{1,0:T(8,128)(2,1)S(1)}, bf16[128,512]{1,0:T(8,128)(2,1)S(1)}, u32[]{:S(2)}, u32[]{:S(2)}) collective-permute-start(bf16[128,512]{1,0:T(8,128)(2,1)S(1)} %get-tuple-element.80), channel_id=1, source_target_pairs={{0,12},{1,13},{2,14},{3,15},{4,0},{5,1},{6,2},{7,3},{8,4},{9,5},{1... | collective-permute-start | bytes 393224 | tf_op jit(solution)/shard_map/ppermute | solution.py:365
  83.2 1.5 %collective-permute-start.9 = (bf16[96,512]{1,0:T(8,128)(2,1)S(1)}, bf16[96,512]{1,0:T(8,128)(2,1)S(1)}, u32[]{:S(2)}, u32[]{:S(2)}) collective-permute-start(bf16[96,512]{1,0:T(8,128)(2,1)S(1)} %get-tuple-element.73), channel_id=1, source_target_pairs={{0,8},{1,9},{2,10},{3,11},{4,12},{5,13},{6,14},{7,15},{8,0},{9,1},... | collective-permute-start | bytes 294920 | tf_op jit(solution)/shard_map/ppermute | solution.py:365
  84.8 2.8 %collective-permute-start.10 = (bf16[96,512]{1,0:T(8,128)(2,1)S(1)}, bf16[96,512]{1,0:T(8,128)(2,1)S(1)}, u32[]{:S(2)}, u32[]{:S(2)}) collective-permute-start(bf16[96,512]{1,0:T(8,128)(2,1)S(1)} %get-tuple-element.74), channel_id=1, source_target_pairs={{0,12},{1,13},{2,14},{3,15},{4,0},{5,1},{6,2},{7,3},{8,4},{9,5},{1... | collective-permute-start | bytes 294920 | tf_op jit(solution)/shard_map/ppermute | solution.py:365
  87.6 3.5 %all-to-all-start.1 = ((bf16[16,2,512]{2,1,0:T(2,128)(2,1)}), bf16[16,2,512]{2,1,0:T(2,128)(2,1)S(1)}, u32[]{:S(2)}, u32[]{:S(2)}) async-start(bf16[16,2,512]{2,1,0:T(2,128)(2,1)} %get-tuple-element.66), calls=%async_computation.1 | async-start | bytes 65536 | tf_op jit(solution)/shard_map/all_to_all | solution.py:531
  91.1 4.6 %edge.1 = bf16[1536,512]{1,0:T(8,128)(2,1)} custom-call(bf16[1536,512]{1,0:T(8,128)(2,1)} %get-tuple-element.59.dpre_ref, bf16[1536,512]{1,0:T(8,128)(2,1)} %cot_ref.3, bf16[1536,512]{1,0:T(8,128)(2,1)} %w1_ref.5), custom_call_target="tpu_custom_call" | custom-call | tf_op jit(solution)/shard_map/edge/pallas_call | solution.py:519
  95.7 3.3 %all-to-all-done.1.far_ref = bf16[16,2,512]{2,1,0:T(2,128)(2,1)S(1)} async-done(((bf16[16,2,512]{2,1,0:T(2,128)(2,1)}), bf16[16,2,512]{2,1,0:T(2,128)(2,1)S(1)}, u32[]{:S(2)}, u32[]{:S(2)}) %all-to-all-start.1) | async-done | bytes 32800 | tf_op jit(solution)/shard_map/all_to_all | solution.py:531
  99.1 1.0 %node.1 = bf16[256,512]{1,0:T(8,128)(2,1)} custom-call(s32[1,2,16]{2,1,0:T(2,128)S(1)} %bitcast.10, f32[256,512]{1,0:T(8,128)S(1)} %copy-done.3, bf16[64,512]{1,0:T(8,128)(2,1)S(1)} %collective-permute-done.4.below_ref, bf16[64,512]{1,0:T(8,128)(2,1)S(1)} %collective-permute-done.5.above_ref, bf16[16,2,512]{2,1,0:T(2,128)(2,1)S(1)} %all-to-all-done.1.far_ref), custom_call_target="tpu_custom_call" | custom-call | tf_op jit(solution)/shard_map/node/pallas_call | solution.py:532
  100.1 0.7 finish.3
  100.8 0.7 finish.2
  (43 shorter events, 4.7 us)
Async XLA Ops:
  0.6 1.0 copy-start
  2.5 19.5 %collective-permute-start = (bf16[64,512]{1,0:T(8,128)(2,1)S(1)}, bf16[64,512]{1,0:T(8,128)(2,1)S(1)}, u32[]{:S(2)}, u32[]{:S(2)}) collective-permute-start(bf16[64,512]{1,0:T(8,128)(2,1)S(1)} %get-tuple-element.45), channel_id=1, source_target_pairs={{0,1},{1,2},{2,3},{3,4},{4,5},{5,6},{6,7},{7,8},{8,9},{9,10},{10,1... | collective-permute-start | bytes 196616 | tf_op jit(solution)/shard_map/ppermute | solution.py:414
  4.9 17.1 %collective-permute-start.1 = (bf16[64,512]{1,0:T(8,128)(2,1)S(1)}, bf16[64,512]{1,0:T(8,128)(2,1)S(1)}, u32[]{:S(2)}, u32[]{:S(2)}) collective-permute-start(bf16[64,512]{1,0:T(8,128)(2,1)S(1)} %get-tuple-element.46), channel_id=1, source_target_pairs={{1,0},{2,1},{3,2},{4,3},{5,4},{6,5},{7,6},{8,7},{9,8},{10,9},{11,1... | collective-permute-start | bytes 196616 | tf_op jit(solution)/shard_map/ppermute | solution.py:415
  36.9 10.5 %collective-permute-start.2 = (bf16[8,96,512]{2,1,0:T(8,128)(2,1)}, bf16[8,96,512]{2,1,0:T(8,128)(2,1)S(1)}, u32[]{:S(2)}, u32[]{:S(2)}) collective-permute-start(bf16[8,96,512]{2,1,0:T(8,128)(2,1)} %get-tuple-element.56), channel_id=1, source_target_pairs={{0,1},{1,0},{2,3},{3,2},{4,5},{5,4},{6,7},{7,6},{8,9},{9,8},{10,11... | collective-permute-start | bytes 2359304 | tf_op jit(solution)/shard_map/ppermute | solution.py:336
  37.0 10.5 %copy-start.1 = (f32[8,96,512]{2,1,0:T(8,128)S(1)}, f32[8,96,512]{2,1,0:T(8,128)}, u32[]{:S(2)}) copy-start(f32[8,96,512]{2,1,0:T(8,128)} %get-tuple-element.54.refs_0_) | copy-start | bytes 4718596
  45.5 1.9 %collective-permute-start.3 = (bf16[8,32,512]{2,1,0:T(8,128)(2,1)}, bf16[8,32,512]{2,1,0:T(8,128)(2,1)S(1)}, u32[]{:S(2)}, u32[]{:S(2)}) collective-permute-start(bf16[8,32,512]{2,1,0:T(8,128)(2,1)} %get-tuple-element.57), channel_id=1, source_target_pairs={{0,1},{1,0},{2,3},{3,2},{4,5},{5,4},{6,7},{7,6},{8,9},{9,8},{10,11... | collective-permute-start | bytes 786440 | tf_op jit(solution)/shard_map/ppermute | solution.py:336
  47.4 1.0 %copy-start.4 = (f32[8,32,512]{2,1,0:T(8,128)S(1)}, f32[8,32,512]{2,1,0:T(8,128)}, u32[]{:S(2)}) copy-start(f32[8,32,512]{2,1,0:T(8,128)} %get-tuple-element.55.refs_1_) | copy-start | bytes 1572868
  56.8 2.5 %collective-permute-start.6 = (bf16[8,96,512]{2,1,0:T(8,128)(2,1)}, bf16[8,96,512]{2,1,0:T(8,128)(2,1)S(1)}, u32[]{:S(2)}, u32[]{:S(2)}) collective-permute-start(bf16[8,96,512]{2,1,0:T(8,128)(2,1)} %get-tuple-element.68), channel_id=1, source_target_pairs={{0,1},{1,0},{2,3},{3,2},{4,5},{5,4},{6,7},{7,6},{8,9},{9,8},{10,11... | collective-permute-start | bytes 2359304 | tf_op jit(solution)/shard_map/ppermute | solution.py:336
  57.2 14.8 %collective-permute-start.11 = (bf16[4,128,512]{2,1,0:T(8,128)(2,1)S(1)}, bf16[4,128,512]{2,1,0:T(8,128)(2,1)S(1)}, u32[]{:S(2)}, u32[]{:S(2)}) collective-permute-start(bf16[4,128,512]{2,1,0:T(8,128)(2,1)S(1)} %get-tuple-element.76), channel_id=1, source_target_pairs={{0,2},{1,3},{2,0},{3,1},{4,6},{5,7},{6,4},{7,5},{8,10},{9,11},{10,... | collective-permute-start | bytes 1572872 | tf_op jit(solution)/shard_map/ppermute | solution.py:336
  59.4 1.4 %copy-start.2 = (f32[8,96,512]{2,1,0:T(8,128)S(1)}, f32[8,96,512]{2,1,0:T(8,128)}, u32[]{:S(2)}) copy-start(f32[8,96,512]{2,1,0:T(8,128)} %get-tuple-element.67.refs_0_) | copy-start | bytes 4718596
  60.8 11.7 %copy-start.10 = (bf16[64,512]{1,0:T(8,128)(2,1)S(1)}, bf16[64,512]{1,0:T(8,128)(2,1)}, u32[]{:S(2)}) copy-start(bf16[64,512]{1,0:T(8,128)(2,1)} %get-tuple-element.64) | copy-start | bytes 196612
  60.8 13.0 %copy-start.9 = (bf16[64,512]{1,0:T(8,128)(2,1)S(1)}, bf16[64,512]{1,0:T(8,128)(2,1)}, u32[]{:S(2)}) copy-start(bf16[64,512]{1,0:T(8,128)(2,1)} %get-tuple-element.65) | copy-start | bytes 196612
  60.9 18.8 %collective-permute-start.7 = (bf16[4,96,512]{2,1,0:T(8,128)(2,1)S(1)}, bf16[4,96,512]{2,1,0:T(8,128)(2,1)S(1)}, u32[]{:S(2)}, u32[]{:S(2)}) collective-permute-start(bf16[4,96,512]{2,1,0:T(8,128)(2,1)S(1)} %get-tuple-element.70), channel_id=1, source_target_pairs={{0,2},{1,3},{2,0},{3,1},{4,6},{5,7},{6,4},{7,5},{8,10},{9,11},{10,... | collective-permute-start | bytes 1179656 | tf_op jit(solution)/shard_map/ppermute | solution.py:336
  72.1 12.7 %collective-permute-start.12 = (bf16[128,512]{1,0:T(8,128)(2,1)S(1)}, bf16[128,512]{1,0:T(8,128)(2,1)S(1)}, u32[]{:S(2)}, u32[]{:S(2)}) collective-permute-start(bf16[128,512]{1,0:T(8,128)(2,1)S(1)} %get-tuple-element.78), channel_id=1, source_target_pairs={{0,4},{1,5},{2,6},{3,7},{4,8},{5,9},{6,10},{7,11},{8,12},{9,13},{1... | collective-permute-start | bytes 393224 | tf_op jit(solution)/shard_map/ppermute | solution.py:365
  72.5 10.2 %collective-permute-start.4 = (bf16[64,512]{1,0:T(8,128)(2,1)S(1)}, bf16[64,512]{1,0:T(8,128)(2,1)S(1)}, u32[]{:S(2)}, u32[]{:S(2)}) collective-permute-start(bf16[64,512]{1,0:T(8,128)(2,1)S(1)} %copy-done.10), channel_id=1, source_target_pairs={{0,1},{1,2},{2,3},{3,4},{4,5},{5,6},{6,7},{7,8},{8,9},{9,10},{10,1... | collective-permute-start | bytes 196616 | tf_op jit(solution)/shard_map/ppermute | solution.py:530
  73.8 9.4 %collective-permute-start.5 = (bf16[64,512]{1,0:T(8,128)(2,1)S(1)}, bf16[64,512]{1,0:T(8,128)(2,1)S(1)}, u32[]{:S(2)}, u32[]{:S(2)}) collective-permute-start(bf16[64,512]{1,0:T(8,128)(2,1)S(1)} %copy-done.9), channel_id=1, source_target_pairs={{1,0},{2,1},{3,2},{4,3},{5,4},{6,5},{7,6},{8,7},{9,8},{10,9},{11,1... | collective-permute-start | bytes 196616 | tf_op jit(solution)/shard_map/ppermute | solution.py:529
  75.1 25.0 %collective-permute-start.13 = (bf16[128,512]{1,0:T(8,128)(2,1)S(1)}, bf16[128,512]{1,0:T(8,128)(2,1)S(1)}, u32[]{:S(2)}, u32[]{:S(2)}) collective-permute-start(bf16[128,512]{1,0:T(8,128)(2,1)S(1)} %get-tuple-element.79), channel_id=1, source_target_pairs={{0,8},{1,9},{2,10},{3,11},{4,12},{5,13},{6,14},{7,15},{8,0},{9,1},... | collective-permute-start | bytes 393224 | tf_op jit(solution)/shard_map/ppermute | solution.py:365
  79.7 20.4 %collective-permute-start.14 = (bf16[128,512]{1,0:T(8,128)(2,1)S(1)}, bf16[128,512]{1,0:T(8,128)(2,1)S(1)}, u32[]{:S(2)}, u32[]{:S(2)}) collective-permute-start(bf16[128,512]{1,0:T(8,128)(2,1)S(1)} %get-tuple-element.80), channel_id=1, source_target_pairs={{0,12},{1,13},{2,14},{3,15},{4,0},{5,1},{6,2},{7,3},{8,4},{9,5},{1... | collective-permute-start | bytes 393224 | tf_op jit(solution)/shard_map/ppermute | solution.py:365
  82.7 18.1 %collective-permute-start.8 = (bf16[96,512]{1,0:T(8,128)(2,1)S(1)}, bf16[96,512]{1,0:T(8,128)(2,1)S(1)}, u32[]{:S(2)}, u32[]{:S(2)}) collective-permute-start(bf16[96,512]{1,0:T(8,128)(2,1)S(1)} %get-tuple-element.72), channel_id=1, source_target_pairs={{0,4},{1,5},{2,6},{3,7},{4,8},{5,9},{6,10},{7,11},{8,12},{9,13},{1... | collective-permute-start | bytes 294920 | tf_op jit(solution)/shard_map/ppermute | solution.py:365
  83.2 17.6 %collective-permute-start.9 = (bf16[96,512]{1,0:T(8,128)(2,1)S(1)}, bf16[96,512]{1,0:T(8,128)(2,1)S(1)}, u32[]{:S(2)}, u32[]{:S(2)}) collective-permute-start(bf16[96,512]{1,0:T(8,128)(2,1)S(1)} %get-tuple-element.73), channel_id=1, source_target_pairs={{0,8},{1,9},{2,10},{3,11},{4,12},{5,13},{6,14},{7,15},{8,0},{9,1},... | collective-permute-start | bytes 294920 | tf_op jit(solution)/shard_map/ppermute | solution.py:365
  84.8 16.0 %collective-permute-start.10 = (bf16[96,512]{1,0:T(8,128)(2,1)S(1)}, bf16[96,512]{1,0:T(8,128)(2,1)S(1)}, u32[]{:S(2)}, u32[]{:S(2)}) collective-permute-start(bf16[96,512]{1,0:T(8,128)(2,1)S(1)} %get-tuple-element.74), channel_id=1, source_target_pairs={{0,12},{1,13},{2,14},{3,15},{4,0},{5,1},{6,2},{7,3},{8,4},{9,5},{1... | collective-permute-start | bytes 294920 | tf_op jit(solution)/shard_map/ppermute | solution.py:365
  87.6 11.4 %all-to-all-start.1 = ((bf16[16,2,512]{2,1,0:T(2,128)(2,1)}), bf16[16,2,512]{2,1,0:T(2,128)(2,1)S(1)}, u32[]{:S(2)}, u32[]{:S(2)}) async-start(bf16[16,2,512]{2,1,0:T(2,128)(2,1)} %get-tuple-element.66), calls=%async_computation.1 | async-start | bytes 65536 | tf_op jit(solution)/shard_map/all_to_all | solution.py:531
  91.1 7.9 %copy-start.3 = (f32[256,512]{1,0:T(8,128)S(1)}, f32[256,512]{1,0:T(8,128)}, u32[]{:S(2)}) copy-start(f32[256,512]{1,0:T(8,128)} %get-tuple-element.63.partial_ref) | copy-start | bytes 1572868
  91.1 7.9 %copy-start.6 = (s32[1,16,2]{1,2,0:T(2,128)S(1)}, s32[1,16,2]{1,2,0:T(2,128)}, u32[]{:S(2)}) copy-start(s32[1,16,2]{1,2,0:T(2,128)} %param.32) | copy-start | bytes 388
  (3 other events, 2.0 us)

commit v3 on v2

v3 whole, which is shorter than its diff:
```python
import functools

import jax
import jax.numpy as jnp
from jax import lax
from jax.experimental import pallas as pl
from jax.experimental.pallas import tpu as pltpu
from jax.sharding import PartitionSpec as P

NEAR = 64
EPSILON = 1e-05
TILE = 256
LANES = 128
F32 = jnp.float32
BF16 = jnp.bfloat16
MIB = 1024 * 1024

NN = (((1,), (0,)), ((), ()))
NT = (((1,), (1,)), ((), ()))
TN = (((0,), (0,)), ((), ()))


def dot(a, b, dims=NN):
    return lax.dot_general(a, b, dims, preferred_element_type=F32)


def sigmoid(x):
    return 0.5 * jnp.tanh(0.5 * x) + 0.5


def row_mean(x):
    return jnp.sum(x, axis=-1, keepdims=True) * (1.0 / x.shape[-1])


def ones_where(mask):
    return jnp.where(mask, 1.0, 0.0).astype(BF16)


def index_columns(idx_ref, step, tile):
    per = tile // LANES
    parts = []
    for j in range(per):
        row = idx_ref[pl.ds(step * per + j, 1), :]
        parts.append(jnp.transpose(jnp.broadcast_to(row, (LANES, LANES))))
    return jnp.concatenate(parts, axis=0)


def pick_columns(columns, width):
    lane = lax.broadcasted_iota(jnp.int32, columns.shape, 1)
    return [ones_where(columns == lane + c * LANES) for c in range(width // LANES)]


def pick_rows(idx_ref, step, tile, width):
    per = tile // LANES
    row = jnp.concatenate([idx_ref[pl.ds(step * per + j, 1), :] for j in range(per)], axis=1)
    return ones_where(lax.broadcasted_iota(jnp.int32, (width, tile), 0) == row)


def norm_forward(out):
    centred = out - row_mean(out)
    inverse = lax.rsqrt(row_mean(centred * centred) + EPSILON)
    return centred, inverse


def norm_backward(scaled, normed, inverse):
    return (
        inverse * (scaled - row_mean(scaled) - normed * row_mean(scaled * normed))
    ).astype(BF16)


def split_halves(bit, total_ref, at, rows, send_ref, keep_ref, offset):
    half = send_ref.shape[0]
    for q in range(half):
        there = pl.multiple_of((2 * q + 1 - bit) * rows, rows)
        here = pl.multiple_of((2 * q + bit) * rows, rows)
        send_ref[q, offset : offset + rows, :] = total_ref[pl.ds(at + there, rows), :].astype(BF16)
        keep_ref[q, offset : offset + rows, :] = total_ref[pl.ds(at + here, rows), :]


def fetch(pairs, sems):
    copies = []
    for at, (source, target) in enumerate(pairs):
        copies.append(pltpu.make_async_copy(source, target, sems.at[at]))
    for copy in copies:
        copy.start()
    return copies


def tile_pairs(source, target, tile):
    return [
        (source.at[pl.ds(at, tile)], target.at[pl.ds(at, tile)])
        for at in range(0, source.shape[0], tile)
    ]


def outgoing_kernel(index_hbm, node_hbm, far_ref, head_ref, tail_ref, index_ref, node_ref, sems):
    for copy in fetch([(index_hbm, index_ref), (node_hbm, node_ref)], sems):
        copy.wait()
    places, tiles = index_ref.shape[1], index_ref.shape[2]
    nodes = node_ref.shape[0]
    place = lax.broadcasted_iota(jnp.int32, (nodes, tiles), 0)
    for j in range(places):
        picks = ones_where(place == index_ref[0, j : j + 1, :])
        far_ref[:, j, :] = dot(picks, node_ref[...], TN).astype(BF16)
    head_ref[...] = node_ref[:NEAR, :]
    tail_ref[...] = node_ref[nodes - NEAR :, :]


def sender_table_index(raw, places, tiles, base):
    far = raw - base
    moved = base + lax.rem(far, places) * tiles + lax.div(far, places)
    return jnp.where(raw >= base, moved, raw)


def forward_kernel(
    tiles, places, fast,
    edge_hbm, w1_hbm, w2_hbm, nw1_hbm, nw2_hbm, node_hbm, ncot_hbm,
    sender_hbm, receiver_hbm, b1_hbm, b2_hbm, gain_hbm, nb1_hbm, nb2_hbm, ngain_hbm, count_hbm,
    lower_ref, upper_ref, far_ref,
    edge_ref, w1_ref, w2_ref, node_ref, receiver_ref, gain_ref,
    hidden_ref, slope_ref, normed_ref, inverse_ref, table_ref, moved_ref, dsum_ref, base_ref,
    gsend_ref, gkeep_ref,
    weights, summed, grads, nw1_ref, nw2_ref, ncot_ref, sender_ref,
    b1_ref, b2_ref, nb1_ref, nb2_ref, ngain_ref, count_ref, sems, edge_sems,
):
    here = lax.axis_index("tiles")
    edges, latent = edge_ref.shape
    nodes = node_ref.shape[0]
    rows = table_ref.shape[0]
    far_base = nodes + 2 * NEAR

    early = fetch(
        [
            (node_hbm, node_ref), (w1_hbm, w1_ref), (sender_hbm, sender_ref),
            (receiver_hbm, receiver_ref), (b1_hbm, b1_ref), (b2_hbm, b2_ref),
            (gain_hbm, gain_ref), (count_hbm, count_ref), (w2_hbm, w2_ref),
        ],
        sems,
    )
    edge_copies = fetch(tile_pairs(edge_hbm, edge_ref, TILE), edge_sems)
    late = fetch(
        [
            (nw1_hbm, nw1_ref), (nw2_hbm, nw2_ref), (ncot_hbm, ncot_ref),
            (nb1_hbm, nb1_ref), (nb2_hbm, nb2_ref), (ngain_hbm, ngain_ref),
        ],
        sems.at[pl.ds(len(early), 6)],
    )

    for copy in early:
        copy.wait()
    moved_ref[...] = sender_table_index(sender_ref[...], places, tiles, far_base)
    table_ref[:NEAR, :] = lower_ref[...]
    table_ref[NEAR : NEAR + nodes, :] = node_ref[...]
    table_ref[NEAR + nodes : far_base, :] = upper_ref[...]
    for j in range(places):
        table_ref[far_base + j * tiles : far_base + (j + 1) * tiles, :] = far_ref[:, j, :]
    used = far_base + places * tiles
    if used < rows:
        table_ref[used:, :] = jnp.zeros((rows - used, latent), BF16)
    weights[:latent, :] = w1_ref[:latent, :]
    weights[latent : latent + rows, :] = dot(
        table_ref[...], w1_ref[latent : 2 * latent, :]
    ).astype(BF16)
    weights[latent + rows :, :] = dot(node_ref[...], w1_ref[2 * latent :, :]).astype(BF16)

    for step in range(edges // TILE):
        edge_copies[step].wait()
        tile = slice(step * TILE, (step + 1) * TILE)
        senders = pick_columns(index_columns(moved_ref, step, TILE), rows)
        receivers = pick_columns(index_columns(receiver_ref, step, TILE), nodes)
        inputs = jnp.concatenate([edge_ref[tile, :]] + senders + receivers, axis=1)
        preact = dot(inputs, weights[...]) + b1_ref[...]
        sig = sigmoid(preact)
        hidden = (preact * sig).astype(BF16)
        hidden_ref[tile, :] = hidden
        slope_ref[tile, :] = (sig * (1.0 + preact * (1.0 - sig))).astype(BF16)
        centred, inverse = norm_forward(dot(hidden, w2_ref[...]) + b2_ref[...])
        position = step * TILE + lax.broadcasted_iota(jnp.int32, inverse.shape, 0)
        inverse = jnp.where(position < count_ref[here], inverse, 0.0)
        normed = centred * inverse
        normed_ref[tile, :] = normed
        inverse_ref[tile, :] = jnp.broadcast_to(inverse, (TILE, LANES))
        update = (normed * gain_ref[...]).astype(BF16)
        part = dot(pick_rows(receiver_ref, step, TILE, nodes), update)
        if step == 0:
            summed[...] = part
        else:
            summed[...] += part

    for copy in late:
        copy.wait()
    node_in = jnp.concatenate([node_ref[...], summed[...].astype(BF16)], axis=1)
    preact_n = dot(node_in, nw1_ref[...]) + nb1_ref[...]
    sig_n = sigmoid(preact_n)
    hidden_n = (preact_n * sig_n).astype(BF16)
    centred_n, inverse_n = norm_forward(dot(hidden_n, nw2_ref[...]) + nb2_ref[...])
    cot = ncot_ref[...].astype(F32)
    dout = norm_backward(cot * ngain_ref[...], centred_n * inverse_n, inverse_n)
    slope_n = sig_n * (1.0 + preact_n * (1.0 - sig_n))
    dpre = (dot(dout, nw2_ref[...], NT) * slope_n).astype(BF16)
    grads[: 2 * latent, :] = dot(node_in, dpre, TN)
    grads[2 * latent :, :] = dot(hidden_n, dout, TN)
    base_ref[...] = cot + dot(dpre, nw1_ref[:latent, :], NT)
    dsum_ref[...] = dot(dpre, nw1_ref[latent:, :], NT).astype(BF16)
    if fast:
        bit = lax.rem(here, 2)
        first = 2 * latent // tiles
        split_halves(bit, grads, 0, first, gsend_ref, gkeep_ref, 0)
        split_halves(bit, grads, 2 * latent, latent // tiles, gsend_ref, gkeep_ref, first)
    else:
        gkeep_ref[...] = grads[: 2 * latent, :]
        gsend_ref[...] = grads[2 * latent :, :]


def slope_kernel(
    tiles, fast,
    cot_hbm, receiver_ref, dsum_ref, hidden_ref, slope_ref, normed_ref, inverse_ref, w2_ref, gain_ref,
    cot_ref, dpre_ref, gsend_ref, gkeep_ref,
    grads, sems,
):
    here = lax.axis_index("tiles")
    edges, latent = cot_ref.shape
    nodes = dsum_ref.shape[0]
    copies = fetch(tile_pairs(cot_hbm, cot_ref, TILE), sems)

    for step in range(edges // TILE):
        copies[step].wait()
        tile = slice(step * TILE, (step + 1) * TILE)
        receivers = jnp.concatenate(
            pick_columns(index_columns(receiver_ref, step, TILE), nodes), axis=1
        )
        grad_update = cot_ref[tile, :].astype(F32) + dot(receivers, dsum_ref[...])
        inverse = inverse_ref[tile, :1]
        dout = norm_backward(grad_update * gain_ref[...], normed_ref[tile, :], inverse)
        dpre_ref[tile, :] = (
            dot(dout, w2_ref[...], NT) * slope_ref[tile, :].astype(F32)
        ).astype(BF16)
        part = dot(hidden_ref[tile, :], dout, TN)
        if step == 0:
            grads[...] = part
        else:
            grads[...] += part

    if fast:
        split_halves(lax.rem(here, 2), grads, 0, latent // tiles, gsend_ref, gkeep_ref, 0)
    else:
        gkeep_ref[...] = grads[...]
        gsend_ref[...] = jnp.zeros_like(gsend_ref)


def first_kernel(
    tiles, places, fast,
    dpre_ref, edge_ref, sender_ref, receiver_ref, table_ref, node_ref, w1_ref, base_ref,
    gsend_ref, gkeep_ref, lower_ref, upper_ref, far_ref, partial_ref,
    grads, sums,
):
    here = lax.axis_index("tiles")
    edges, latent = edge_ref.shape
    nodes = node_ref.shape[0]
    rows = table_ref.shape[0]

    for step in range(edges // TILE):
        tile = slice(step * TILE, (step + 1) * TILE)
        dpre = dpre_ref[tile, :]
        part = dot(edge_ref[tile, :], dpre, TN)
        picks = jnp.concatenate(
            [
                pick_rows(sender_ref, step, TILE, rows),
                pick_rows(receiver_ref, step, TILE, nodes),
            ],
            axis=0,
        )
        scattered = dot(picks, dpre)
        if step == 0:
            grads[:latent, :] = part
            sums[...] = scattered
        else:
            grads[:latent, :] += part
            sums[...] += scattered

    by_sender = sums[:rows, :].astype(BF16)
    by_receiver = sums[rows:, :].astype(BF16)
    grads[latent : 2 * latent, :] = dot(table_ref[...], by_sender, TN)
    grads[2 * latent :, :] = dot(node_ref[...], by_receiver, TN)
    if fast:
        split_halves(lax.rem(here, 2), grads, 0, 3 * latent // tiles, gsend_ref, gkeep_ref, 0)
    else:
        gkeep_ref[...] = grads[...]
        gsend_ref[...] = jnp.zeros_like(gsend_ref)
    back = dot(by_sender, w1_ref[latent : 2 * latent, :], NT)
    lower_ref[...] = back[:NEAR, :].astype(BF16)
    upper_ref[...] = back[NEAR + nodes : 2 * NEAR + nodes, :].astype(BF16)
    for j in range(places):
        at = 2 * NEAR + nodes + j * tiles
        far_ref[:, j, :] = back[at : at + tiles, :].astype(BF16)
    partial_ref[...] = (
        base_ref[...]
        + back[NEAR : NEAR + nodes, :]
        + dot(by_receiver, w1_ref[2 * latent :, :], NT)
    )


def edge_kernel(dpre_ref, cot_ref, w1_ref, out_hbm, out_ref, sems):
    edges, latent = cot_ref.shape
    copies = []
    for step in range(edges // TILE):
        tile = pl.ds(step * TILE, TILE)
        out_ref[tile, :] = (
            cot_ref[tile, :].astype(F32) + dot(dpre_ref[tile, :], w1_ref[:latent, :], NT)
        ).astype(BF16)
        copy = pltpu.make_async_copy(out_ref.at[tile], out_hbm.at[tile], sems.at[step])
        copy.start()
        copies.append(copy)
    for copy in copies:
        copy.wait()


def node_kernel(index_ref, partial_ref, below_ref, above_ref, far_ref, out_ref):
    places, tiles = index_ref.shape[1], index_ref.shape[2]
    nodes = partial_ref.shape[0]
    place = lax.broadcasted_iota(jnp.int32, (nodes, tiles), 0)
    total = partial_ref[...]
    for j in range(places):
        picks = ones_where(place == index_ref[0, j : j + 1, :])
        total = total + dot(picks, far_ref[:, j, :])
    out_ref[:NEAR, :] = (total[:NEAR, :] + below_ref[...].astype(F32)).astype(BF16)
    out_ref[NEAR : nodes - NEAR, :] = total[NEAR : nodes - NEAR, :].astype(BF16)
    out_ref[nodes - NEAR :, :] = (
        total[nodes - NEAR :, :] + above_ref[...].astype(F32)
    ).astype(BF16)


def halve_kernel(shift, count, *refs):
    keeps, gots = refs[:count], refs[count : 2 * count]
    send_ref, kept_ref = refs[2 * count :]
    bit = lax.rem(lax.div(lax.axis_index("tiles"), 2**shift), 2)
    at = 0
    for keep_ref, got_ref in zip(keeps, gots):
        rows = keep_ref.shape[1]
        for q in range(keep_ref.shape[0] // 2):
            there, here = 2 * q + 1 - bit, 2 * q + bit
            send_ref[q, at : at + rows, :] = (
                keep_ref[there] + got_ref[there].astype(F32)
            ).astype(BF16)
            kept_ref[q, at : at + rows, :] = keep_ref[here] + got_ref[here].astype(F32)
        at += rows


def spread_kernel(keep_ref, got_ref, own_ref, send_ref):
    place = lax.div(lax.axis_index("tiles"), 4)
    own_ref[...] = keep_ref[place] + got_ref[place].astype(F32)
    for q in range(keep_ref.shape[0]):
        send_ref[q] = (keep_ref[q] + got_ref[q].astype(F32)).astype(BF16)


def finish_kernel(own_ref, got_ref, *out_refs):
    count = got_ref.shape[0]
    place = lax.div(lax.axis_index("tiles"), 4)
    total = own_ref[...]
    for k in range(1, count):
        total = total + got_ref[lax.rem(place + k, count)].astype(F32)
    at = 0
    for out_ref in out_refs:
        out_ref[...] = total[at : at + out_ref.shape[0], :]
        at += out_ref.shape[0]


def shaped(shape, dtype):
    return jax.ShapeDtypeStruct(shape, dtype)


def in_hbm(*arrays):
    return [pltpu.with_memory_space_constraint(array, pltpu.HBM) for array in arrays]


def call(kernel, name, out_shape, args, hbm=0, scratch=(), out_specs=None, flops=0, limit=16):
    vmem = pl.BlockSpec(memory_space=pltpu.VMEM)
    return pl.pallas_call(
        kernel,
        in_specs=[pl.BlockSpec(memory_space=pltpu.HBM)] * hbm + [vmem] * (len(args) - hbm),
        out_specs=out_specs or [vmem] * len(out_shape),
        out_shape=out_shape,
        scratch_shapes=scratch,
        compiler_params=pltpu.CompilerParams(vmem_limit_bytes=limit * MIB),
        cost_estimate=pl.CostEstimate(flops=flops, bytes_accessed=flops // 400, transcendentals=0),
        name=name,
    )(*in_hbm(*args[:hbm]), *args[hbm:])


def swap(tiles, bit, send):
    return lax.ppermute(send, "tiles", [(i, i ^ bit) for i in range(tiles)])


def halve(keeps, gots):
    half, _, width = keeps[0].shape
    rows = sum(keep.shape[1] for keep in keeps)
    shape = (half // 2, rows, width)
    return call(
        functools.partial(halve_kernel, 1, len(keeps)),
        "halve",
        [pltpu.VMEM(shape, BF16), pltpu.VMEM(shape, F32)],
        [*keeps, *gots],
    )


def spread(keep, got):
    return call(
        spread_kernel,
        "spread",
        [pltpu.VMEM(keep.shape[1:], F32), pltpu.VMEM(keep.shape, BF16)],
        [keep, got],
    )


def exchange(tiles, send):
    groups = [[z * 4 + i for z in range(tiles // 4)] for i in range(4)]
    return lax.all_to_all(
        send, "tiles", split_axis=0, concat_axis=0, axis_index_groups=groups, tiled=True
    )


def finish(own, got, sizes):
    return call(
        finish_kernel, "finish", [shaped((size, own.shape[1]), F32) for size in sizes], [own, got]
    )


def shards(
    node_latent, edge_latent, node_cot, edge_cot,
    edge_w1, edge_b1, edge_w2, edge_b2, edge_gain,
    node_w1, node_b1, node_w2, node_b2, node_gain,
    send_index, edge_sender, edge_receiver, edge_count,
):
    tiles = lax.axis_size("tiles")
    nodes, latent = node_latent.shape
    edges = edge_latent.shape[0]
    places = send_index.shape[2]
    steps = edges // TILE
    used = nodes + 2 * NEAR + places * tiles
    rows = -(-used // LANES) * LANES
    fast = tiles == 16
    half = tiles // 2
    upward = [(i, i + 1) for i in range(tiles - 1)]
    downward = [(i + 1, i) for i in range(tiles - 1)]
    sender = edge_sender.reshape(edges // LANES, LANES)
    receiver = edge_receiver.reshape(edges // LANES, LANES)
    listed = jnp.swapaxes(send_index, 1, 2)
    row = lambda vector: vector.reshape(1, -1)
    vmem = pltpu.VMEM
    unit = 2 * edges * latent * latent

    if fast:
        grad_shapes = lambda count: [
            vmem((half, count // tiles, latent), BF16),
            vmem((half, count // tiles, latent), F32),
        ]
    else:
        grad_shapes = lambda count: [shaped((latent, latent), F32), shaped((count, latent), F32)]

    outgoing, head, tail = call(
        outgoing_kernel,
        "outgoing",
        [
            shaped((tiles, places, latent), BF16),
            shaped((NEAR, latent), BF16),
            shaped((NEAR, latent), BF16),
        ],
        [listed, node_latent],
        hbm=2,
        scratch=[vmem(listed.shape, jnp.int32), vmem((nodes, latent), BF16), pltpu.SemaphoreType.DMA((2,))],
    )
    lower = lax.ppermute(tail, "tiles", upward)
    upper = lax.ppermute(head, "tiles", downward)
    incoming = lax.all_to_all(outgoing, "tiles", split_axis=0, concat_axis=0, tiled=True)

    (
        edge_kept, w1_kept, w2_kept, node_kept, receiver_kept, gain_kept,
        hidden, slope, normed, inverse, table, moved, dsum, base, node_send, node_keep,
    ) = call(
        functools.partial(forward_kernel, tiles, places, fast),
        "forward",
        [
            vmem((edges, latent), BF16), vmem(edge_w1.shape, BF16), vmem(edge_w2.shape, BF16),
            vmem((nodes, latent), BF16), vmem(receiver.shape, jnp.int32), vmem((1, latent), F32),
            vmem((edges, latent), BF16), vmem((edges, latent), BF16), vmem((edges, latent), F32),
            vmem((edges, LANES), F32), vmem((rows, latent), BF16), vmem(sender.shape, jnp.int32),
            vmem((nodes, latent), BF16), vmem((nodes, latent), F32),
        ] + grad_shapes(3 * latent if fast else 2 * latent),
        [
            edge_latent, edge_w1, edge_w2, node_w1, node_w2, node_latent, node_cot,
            sender, receiver, row(edge_b1), row(edge_b2), row(edge_gain),
            row(node_b1), row(node_b2), row(node_gain), edge_count,
            lower, upper, incoming,
        ],
        hbm=16,
        scratch=[
            vmem((latent + rows + nodes, latent), BF16), vmem((nodes, latent), F32),
            vmem((3 * latent, latent), F32), vmem(node_w1.shape, BF16), vmem(node_w2.shape, BF16),
            vmem((nodes, latent), BF16), vmem(sender.shape, jnp.int32),
        ] + [vmem((1, latent), F32)] * 5 + [
            pltpu.SMEM(edge_count.shape, jnp.int32),
            pltpu.SemaphoreType.DMA((15,)), pltpu.SemaphoreType.DMA((steps,)),
        ],
        flops=7 * unit,
        limit=24,
    )

    cot_kept, dpre, second_send, second_keep = call(
        functools.partial(slope_kernel, tiles, fast),
        "slope",
        [vmem((edges, latent), BF16), vmem((edges, latent), BF16)] + grad_shapes(latent),
        [edge_cot, receiver_kept, dsum, hidden, slope, normed, inverse, w2_kept, gain_kept],
        hbm=1,
        scratch=[vmem((latent, latent), F32), pltpu.SemaphoreType.DMA((steps,))],
        flops=3 * unit,
    )
    if fast:
        send, chain = halve(
            [node_keep, second_keep],
            [swap(tiles, 1, node_send), swap(tiles, 1, second_send)],
        )
        dpre, send = lax.optimization_barrier((dpre, send))
        got = swap(tiles, 2, send)

    first_send, first_keep, to_lower, to_upper, to_far, partial = call(
        functools.partial(first_kernel, tiles, places, fast),
        "first",
        grad_shapes(3 * latent) + [
            shaped((NEAR, latent), BF16),
            shaped((NEAR, latent), BF16),
            shaped((tiles, places, latent), BF16),
            vmem((nodes, latent), F32),
        ],
        [dpre, edge_kept, moved, receiver_kept, table, node_kept, w1_kept, base],
        scratch=[vmem((3 * latent, latent), F32), vmem((rows + nodes, latent), F32)],
        flops=4 * unit,
    )

    (grad_edge,) = call(
        edge_kernel,
        "edge",
        [shaped((edges, latent), BF16)],
        [dpre, cot_kept, w1_kept],
        out_specs=[pl.BlockSpec(memory_space=pltpu.HBM)],
        scratch=[vmem((edges, latent), BF16), pltpu.SemaphoreType.DMA((steps,))],
        flops=2 * unit,
    )

    above = lax.ppermute(to_lower, "tiles", downward)
    below = lax.ppermute(to_upper, "tiles", upward)
    returned = lax.all_to_all(to_far, "tiles", split_axis=0, concat_axis=0, tiled=True)
    (grad_node,) = call(
        node_kernel,
        "node",
        [shaped((nodes, latent), BF16)],
        [listed, partial, below, above, returned],
    )

    if fast:
        send, late_chain = halve([first_keep], [swap(tiles, 1, first_send)])
        late_got = swap(tiles, 2, send)
        per = latent // tiles
        own, send = spread(chain, got)
        grad_node_w1, grad_node_w2, grad_edge_w2 = finish(
            own, exchange(tiles, send), [2 * per, per, per]
        )
        own, send = spread(late_chain, late_got)
        (grad_edge_w1,) = finish(own, exchange(tiles, send), [3 * per])
    else:
        scatter = functools.partial(
            lax.psum_scatter, axis_name="tiles", scatter_dimension=0, tiled=True
        )
        grad_node_w1, grad_node_w2 = scatter(node_keep), scatter(node_send)
        grad_edge_w1, grad_edge_w2 = scatter(first_keep), scatter(second_keep)
    return (grad_node, grad_edge, grad_edge_w1, grad_edge_w2, grad_node_w1, grad_node_w2)


def solution(mesh):
    split = P(("groups", "tiles"), None)
    return jax.shard_map(
        shards,
        mesh=mesh,
        in_specs=(split,) * 4
        + (P(),) * 10
        + (
            P(("groups", "tiles"), None, None),
            P(("groups", "tiles")),
            P(("groups", "tiles")),
            P("groups"),
        ),
        out_specs=(split,) * 6,
        check_vma=False,
    )
```

time: 102 us -> 92.2 us (0.904)
  Pallas kernels: 38.7 us -> 30.1 us
  starting transfers between devices: 24.3 us -> 18 us
  waiting for transfers between devices: 17.2 us -> 21.3 us
    ppermute x6 -> x0, starting transfers between devices: 12.8 us -> none  [exchange(): gots.append(lax.ppermute(send, 'tiles', pairs))]
    pallas_call x12, Pallas kernels: 38.7 us -> 30.1 us  [call(): pl.pallas_call(kernel, in_specs=[pl.BlockSpec(memory_space=pltpu.HBM)] *...]
    all_to_all x0 -> x2, starting transfers between devices: none -> 6.93 us  [exchange(): lax.all_to_all(send, 'tiles', split_axis=0, concat_axis=0, axis_index_gro...]
    all_to_all x0 -> x2, waiting for transfers between devices: none -> 3.96 us  [exchange(): lax.all_to_all(send, 'tiles', split_axis=0, concat_axis=0, axis_index_gro...]
    ppermute x5, waiting for transfers between devices: 13.9 us -> 16.5 us  [swap(): return lax.ppermute(send, 'tiles', [(i, i ^ bit) for i in range(tiles)])]
    all_to_all x1, waiting for transfers between devices: 3.32 us -> 0.83 us  [shards(): lax.all_to_all(to_far, 'tiles', split_axis=0, concat_axis=0, tiled=True)]
    unnamed x22 -> x24, local copies, waits for them, and re-layouts: 4.73 us -> 5.07 us
  transfers between devices with their start and end apart: 16 -> 12, of which waited for: 4 -> 6; matrix products, arithmetic and copies ran while one was open for 0% -> 0% of each run, Pallas kernels for 15% -> 17%
where the time goes in v3:
time: 92.2 us; the launch traced here: 91 us
  Pallas kernels  30.1 us (33%)
  waiting for transfers between devices  21.3 us (23%)
  starting transfers between devices  18 us (20%)
  blocking collectives  15.7 us (17%)
  local copies, waits for them, and re-layouts  5.07 us (5%)
    pallas_call x12, Pallas kernels, call(): pl.pallas_call(kernel, in_specs=[pl.BlockSpec(memory_space=pltpu.HBM)] *...  30.1 us
    ppermute x5, waiting for transfers between devices, swap(): return lax.ppermute(send, 'tiles', [(i, i ^ bit) for i in range(tiles)])  16.5 us
    all_to_all x1, blocking collectives, shards(): lax.all_to_all(outgoing, 'tiles', split_axis=0, concat_axis=0, tiled=True)  15.7 us
    all_to_all x2, starting transfers between devices, exchange(): lax.all_to_all(send, 'tiles', split_axis=0, concat_axis=0, axis_index_gro...  6.93 us
    unnamed x24, local copies, waits for them, and re-layouts  5.07 us
    all_to_all x2, waiting for transfers between devices, exchange(): lax.all_to_all(send, 'tiles', split_axis=0, concat_axis=0, axis_index_gro...  3.96 us
    all_to_all x1, starting transfers between devices, shards(): lax.all_to_all(to_far, 'tiles', split_axis=0, concat_axis=0, tiled=True)  3.5 us
    ppermute x1, starting transfers between devices, shards(): lower = lax.ppermute(tail, 'tiles', upward)  2.36 us
  transfers between devices with their start and end apart: 12, of which 6 were waited for; matrix products, arithmetic and copies ran while one was open for 0% of the time, Pallas kernels for 17%

profile of v3, /device:TPU:0, one launch (start us, length us, event | category | flops | bytes accessed | tf_op | source)
XLA Modules:
  0.0 91.0 jit_solution(5058761995780302674)
XLA Ops:
  0.6 1.2 %outgoing.1 = (bf16[16,2,512]{2,1,0:T(2,128)(2,1)S(1)}, bf16[64,512]{1,0:T(8,128)(2,1)S(1)}, bf16[64,512]{1,0:T(8,128)(2,1)S(1)}) custom-call(s32[1,2,16]{2,1,0:T(2,128)} %bitcast.9, bf16[256,512]{1,0:T(8,128)(2,1)} %node_hbm.3), custom_call_target="tpu_custom_call" | custom-call | tf_op jit(solution)/shard_map/outgoing/pallas_call | solution.py:378
  1.8 2.4 %collective-permute-start = (bf16[64,512]{1,0:T(8,128)(2,1)S(1)}, bf16[64,512]{1,0:T(8,128)(2,1)S(1)}, u32[]{:S(2)}, u32[]{:S(2)}) collective-permute-start(bf16[64,512]{1,0:T(8,128)(2,1)S(1)} %get-tuple-element.48), channel_id=1, source_target_pairs={{0,1},{1,2},{2,3},{3,4},{4,5},{5,6},{6,7},{7,8},{8,9},{9,10},{10,1... | collective-permute-start | bytes 196616 | tf_op jit(solution)/shard_map/ppermute | solution.py:472
  4.2 1.3 %collective-permute-start.1 = (bf16[64,512]{1,0:T(8,128)(2,1)S(1)}, bf16[64,512]{1,0:T(8,128)(2,1)S(1)}, u32[]{:S(2)}, u32[]{:S(2)}) collective-permute-start(bf16[64,512]{1,0:T(8,128)(2,1)S(1)} %get-tuple-element.49), channel_id=1, source_target_pairs={{1,0},{2,1},{3,2},{4,3},{5,4},{6,5},{7,6},{8,7},{9,8},{10,9},{11,1... | collective-permute-start | bytes 196616 | tf_op jit(solution)/shard_map/ppermute | solution.py:473
  5.5 15.7 %all_to_all.20.far_ref = bf16[16,2,512]{2,1,0:T(2,128)(2,1)S(1)} all-to-all(bf16[16,2,512]{2,1,0:T(2,128)(2,1)S(1)} %get-tuple-element.50), channel_id=1, replica_groups=mesh['groups'=2,'tiles'=16] {'tiles'}, dimensions={0} | all-to-all | bytes 65536 | tf_op jit(solution)/shard_map/all_to_all | solution.py:474
  21.2 11.9 %forward.1 = (bf16[1536,512]{1,0:T(8,128)(2,1)S(1)}, bf16[1536,512]{1,0:T(8,128)(2,1)S(1)}, bf16[512,512]{1,0:T(8,128)(2,1)S(1)}, bf16[256,512]{1,0:T(8,128)(2,1...) custom-call(bf16[1536,512]{1,0:T(8,128)(2,1)} %edge_hbm.1, ...), custom_call_target="tpu_custom_call" | custom-call | flops 5637144576 | bytes 14092861 | tf_op jit(solution)/shard_map/forward/pallas_call | solution.py:378
  33.3 5.4 %slope.1 = (bf16[1536,512]{1,0:T(8,128)(2,1)S(1)}, bf16[1536,512]{1,0:T(8,128)(2,1)S(1)}, bf16[8,32,512]{2,1,0:T(8,128)(2,1)S(1)}, f32[8,32,512]{2,1,0:T(8,128)S(1)}) custom-call(bf16[1536,512]{1,0:T(8,128)(2,1)} %cot_hbm.1, s32[12,128]{1,0:T(8,128)S(1)} %get-tuple-element.51.receiver_ref, bf16[256,512]{1,0:T(8,128)(2,1)S(1)} %get-tuple-element.52.dsum_ref, ...), custom_call_target="tpu_custom_call" | custom-call | flops 2415919104 | bytes 6039797 | tf_op jit(solution)/shard_map/slope/pallas_call | solution.py:378
  39.1 1.2 %collective-permute-done.3.refs_3_ = bf16[8,32,512]{2,1,0:T(8,128)(2,1)S(1)} collective-permute-done((bf16[8,32,512]{2,1,0:T(8,128)(2,1)S(1)}, bf16[8,32,512]{2,1,0:T(8,128)(2,1)S(1)}, u32[]{:S(2)}, u32[]{:S(2)}) %collective-permute-start.3) | collective-permute-done | bytes 262176 | tf_op jit(solution)/shard_map/ppermute | solution.py:391
  40.3 0.9 %halve.2 = (bf16[4,128,512]{2,1,0:T(8,128)(2,1)}, f32[4,128,512]{2,1,0:T(8,128)S(1)}) custom-call(f32[8,96,512]{2,1,0:T(8,128)S(1)} %get-tuple-element.60.refs_0_, f32[8,32,512]{2,1,0:T(8,128)S(1)} %get-tuple-element.61.refs_1_, bf16[8,96,512]{2,1,0:T(8,128)(2,1)S(1)} %collective-permute-done.2.refs_2_, bf16[8,32,512]{2,1,0:T(8,128)(2,1)S(1)} %collective-permute-done.3.refs_3_), custom_call_target="tpu_custom_call" | custom-call | tf_op jit(solution)/shard_map/halve/pallas_call | solution.py:378
  41.7 4.1 %first.1 = (bf16[8,96,512]{2,1,0:T(8,128)(2,1)}, f32[8,96,512]{2,1,0:T(8,128)S(1)}, bf16[64,512]{1,0:T(8,128)(2,1)S(1)}, bf16[64,512]{1,0:T(8,128)(2,1)S(1)}, bf...) custom-call(bf16[1536,512]{1,0:T(8,128)(2,1)S(1)} %get-tuple-element.65.dpre_ref, ...), custom_call_target="tpu_custom_call" | custom-call | flops 3221225472 | bytes 8053063 | tf_op jit(solution)/shard_map/first/pallas_call | solution.py:378
  47.4 3.5 %all-to-all-start.1 = ((bf16[16,2,512]{2,1,0:T(2,128)(2,1)}), bf16[16,2,512]{2,1,0:T(2,128)(2,1)S(1)}, u32[]{:S(2)}, u32[]{:S(2)}) async-start(bf16[16,2,512]{2,1,0:T(2,128)(2,1)} %get-tuple-element.75), calls=%async_computation.1 | async-start | bytes 65536 | tf_op jit(solution)/shard_map/all_to_all | solution.py:551
  50.9 4.9 %collective-permute-done.8.got_ref = bf16[4,128,512]{2,1,0:T(8,128)(2,1)S(1)} collective-permute-done((bf16[4,128,512]{2,1,0:T(8,128)(2,1)}, bf16[4,128,512]{2,1,0:T(8,128)(2,1)S(1)}, u32[]{:S(2)}, u32[]{:S(2)}) %collective-permute-start.8) | collective-permute-done | bytes 524320 | tf_op jit(solution)/shard_map/ppermute | solution.py:391
  56.6 0.8 all-to-all-done.1.far_ref
  57.5 3.5 %all-to-all-start.3 = ((bf16[4,128,512]{2,1,0:T(8,128)(2,1)}), bf16[4,128,512]{2,1,0:T(8,128)(2,1)S(1)}, u32[]{:S(2)}, u32[]{:S(2)}) async-start(bf16[4,128,512]{2,1,0:T(8,128)(2,1)} %copy-done.8), calls=%async_computation.3 | async-start | bytes 1048576 | tf_op jit(solution)/shard_map/all_to_all | solution.py:417
  61.0 1.3 %halve.3 = (bf16[4,96,512]{2,1,0:T(8,128)(2,1)S(1)}, f32[4,96,512]{2,1,0:T(8,128)S(1)}) custom-call(f32[8,96,512]{2,1,0:T(8,128)S(1)} %get-tuple-element.77.refs_0_, bf16[8,96,512]{2,1,0:T(8,128)(2,1)} %collective-permute-done.6.refs_1_), custom_call_target="tpu_custom_call" | custom-call | tf_op jit(solution)/shard_map/halve/pallas_call | solution.py:378
  62.6 10.4 %collective-permute-done.7.got_ref = bf16[4,96,512]{2,1,0:T(8,128)(2,1)S(1)} collective-permute-done((bf16[4,96,512]{2,1,0:T(8,128)(2,1)S(1)}, bf16[4,96,512]{2,1,0:T(8,128)(2,1)S(1)}, u32[]{:S(2)}, u32[]{:S(2)}) %collective-permute-start.7) | collective-permute-done | bytes 393248 | tf_op jit(solution)/shard_map/ppermute | solution.py:391
  73.8 1.7 %all-to-all-done.3.got_ref = bf16[4,128,512]{2,1,0:T(8,128)(2,1)S(1)} async-done(((bf16[4,128,512]{2,1,0:T(8,128)(2,1)}), bf16[4,128,512]{2,1,0:T(8,128)(2,1)S(1)}, u32[]{:S(2)}, u32[]{:S(2)}) %all-to-all-start.3) | async-done | bytes 524320 | tf_op jit(solution)/shard_map/all_to_all | solution.py:417
  75.5 3.5 %all-to-all-start.2 = ((bf16[4,96,512]{2,1,0:T(8,128)(2,1)}), bf16[4,96,512]{2,1,0:T(8,128)(2,1)S(1)}, u32[]{:S(2)}, u32[]{:S(2)}) async-start(bf16[4,96,512]{2,1,0:T(8,128)(2,1)} %get-tuple-element.82), calls=%async_computation.2 | async-start | bytes 786432 | tf_op jit(solution)/shard_map/all_to_all | solution.py:417
  79.0 1.3 %collective-permute-start.4 = (bf16[64,512]{1,0:T(8,128)(2,1)S(1)}, bf16[64,512]{1,0:T(8,128)(2,1)S(1)}, u32[]{:S(2)}, u32[]{:S(2)}) collective-permute-start(bf16[64,512]{1,0:T(8,128)(2,1)S(1)} %copy-done.11), channel_id=1, source_target_pairs={{0,1},{1,2},{2,3},{3,4},{4,5},{5,6},{6,7},{7,8},{8,9},{9,10},{10,1... | collective-permute-start | bytes 196616 | tf_op jit(solution)/shard_map/ppermute | solution.py:550
  80.3 1.3 %collective-permute-start.5 = (bf16[64,512]{1,0:T(8,128)(2,1)S(1)}, bf16[64,512]{1,0:T(8,128)(2,1)S(1)}, u32[]{:S(2)}, u32[]{:S(2)}) collective-permute-start(bf16[64,512]{1,0:T(8,128)(2,1)S(1)} %get-tuple-element.74), channel_id=1, source_target_pairs={{1,0},{2,1},{3,2},{4,3},{5,4},{6,5},{7,6},{8,7},{9,8},{10,9},{11,1... | collective-permute-start | bytes 196616 | tf_op jit(solution)/shard_map/ppermute | solution.py:549
  81.6 1.4 %copy-done.3 = bf16[1536,512]{1,0:T(8,128)(2,1)S(1)} copy-done((bf16[1536,512]{1,0:T(8,128)(2,1)S(1)}, bf16[1536,512]{1,0:T(8,128)(2,1)}, u32[]{:S(2)}) %copy-start.3) | copy-done | bytes 1572888
  83.0 1.4 %copy-done.5 = bf16[1536,512]{1,0:T(8,128)(2,1)S(1)} copy-done((bf16[1536,512]{1,0:T(8,128)(2,1)S(1)}, bf16[1536,512]{1,0:T(8,128)(2,1)}, u32[]{:S(2)}) %copy-start.5) | copy-done | bytes 1572888
  84.4 1.8 %edge.1 = bf16[1536,512]{1,0:T(8,128)(2,1)} custom-call(bf16[1536,512]{1,0:T(8,128)(2,1)S(1)} %copy-done.5, bf16[1536,512]{1,0:T(8,128)(2,1)S(1)} %copy-done.3, bf16[1536,512]{1,0:T(8,128)(2,1)S(1)} %copy-done.1), custom_call_target="tpu_custom_call" | custom-call | flops 1610612736 | bytes 4026531 | tf_op jit(solution)/shard_map/edge/pallas_call | solution.py:378
  86.3 1.0 %node.1 = bf16[256,512]{1,0:T(8,128)(2,1)} custom-call(s32[1,2,16]{2,1,0:T(2,128)S(1)} %bitcast.10, f32[256,512]{1,0:T(8,128)S(1)} %copy-done.7, bf16[64,512]{1,0:T(8,128)(2,1)S(1)} %collective-permute-done.4.below_ref, bf16[64,512]{1,0:T(8,128)(2,1)S(1)} %collective-permute-done.5.above_ref, bf16[16,2,512]{2,1,0:T(2,128)(2,1)S(1)} %all-to-all-done.1.far_ref), custom_call_target="tpu_custom_call" | custom-call | tf_op jit(solution)/shard_map/node/pallas_call | solution.py:378
  88.0 2.3 %all-to-all-done.2.got_ref = bf16[4,96,512]{2,1,0:T(8,128)(2,1)S(1)} async-done(((bf16[4,96,512]{2,1,0:T(8,128)(2,1)}), bf16[4,96,512]{2,1,0:T(8,128)(2,1)S(1)}, u32[]{:S(2)}, u32[]{:S(2)}) %all-to-all-start.2) | async-done | bytes 393248 | tf_op jit(solution)/shard_map/all_to_all | solution.py:417
  (37 shorter events, 6.0 us)
Async XLA Ops:
  1.8 19.4 %collective-permute-start = (bf16[64,512]{1,0:T(8,128)(2,1)S(1)}, bf16[64,512]{1,0:T(8,128)(2,1)S(1)}, u32[]{:S(2)}, u32[]{:S(2)}) collective-permute-start(bf16[64,512]{1,0:T(8,128)(2,1)S(1)} %get-tuple-element.48), channel_id=1, source_target_pairs={{0,1},{1,2},{2,3},{3,4},{4,5},{5,6},{6,7},{7,8},{8,9},{9,10},{10,1... | collective-permute-start | bytes 196616 | tf_op jit(solution)/shard_map/ppermute | solution.py:472
  4.2 17.0 %collective-permute-start.1 = (bf16[64,512]{1,0:T(8,128)(2,1)S(1)}, bf16[64,512]{1,0:T(8,128)(2,1)S(1)}, u32[]{:S(2)}, u32[]{:S(2)}) collective-permute-start(bf16[64,512]{1,0:T(8,128)(2,1)S(1)} %get-tuple-element.49), channel_id=1, source_target_pairs={{1,0},{2,1},{3,2},{4,3},{5,4},{6,5},{7,6},{8,7},{9,8},{10,9},{11,1... | collective-permute-start | bytes 196616 | tf_op jit(solution)/shard_map/ppermute | solution.py:473
  33.2 8.6 %copy-start = (bf16[1536,512]{1,0:T(8,128)(2,1)}, bf16[1536,512]{1,0:T(8,128)(2,1)S(1)}, u32[]{:S(2)}) copy-start(bf16[1536,512]{1,0:T(8,128)(2,1)S(1)} %get-tuple-element.70.w1_ref) | copy-start | bytes 4718596
  33.2 7.2 %collective-permute-start.2 = (bf16[8,96,512]{2,1,0:T(8,128)(2,1)S(1)}, bf16[8,96,512]{2,1,0:T(8,128)(2,1)S(1)}, u32[]{:S(2)}, u32[]{:S(2)}) collective-permute-start(bf16[8,96,512]{2,1,0:T(8,128)(2,1)S(1)} %get-tuple-element.62), channel_id=1, source_target_pairs={{0,1},{1,0},{2,3},{3,2},{4,5},{5,4},{6,7},{7,6},{8,9},{9,8},{10,11... | collective-permute-start | bytes 2359304 | tf_op jit(solution)/shard_map/ppermute | solution.py:391
  38.7 2.6 %copy-start.2 = (bf16[1536,512]{1,0:T(8,128)(2,1)}, bf16[1536,512]{1,0:T(8,128)(2,1)S(1)}, u32[]{:S(2)}) copy-start(bf16[1536,512]{1,0:T(8,128)(2,1)S(1)} %get-tuple-element.76.cot_ref) | copy-start | bytes 4718596
  38.7 3.0 %copy-start.4 = (bf16[1536,512]{1,0:T(8,128)(2,1)}, bf16[1536,512]{1,0:T(8,128)(2,1)S(1)}, u32[]{:S(2)}) copy-start(bf16[1536,512]{1,0:T(8,128)(2,1)S(1)} %get-tuple-element.65.dpre_ref) | copy-start | bytes 4718596
  38.7 1.6 %collective-permute-start.3 = (bf16[8,32,512]{2,1,0:T(8,128)(2,1)S(1)}, bf16[8,32,512]{2,1,0:T(8,128)(2,1)S(1)}, u32[]{:S(2)}, u32[]{:S(2)}) collective-permute-start(bf16[8,32,512]{2,1,0:T(8,128)(2,1)S(1)} %get-tuple-element.63), channel_id=1, source_target_pairs={{0,1},{1,0},{2,3},{3,2},{4,5},{5,4},{6,7},{7,6},{8,9},{9,8},{10,11... | collective-permute-start | bytes 786440 | tf_op jit(solution)/shard_map/ppermute | solution.py:391
  41.3 14.5 %collective-permute-start.8 = (bf16[4,128,512]{2,1,0:T(8,128)(2,1)}, bf16[4,128,512]{2,1,0:T(8,128)(2,1)S(1)}, u32[]{:S(2)}, u32[]{:S(2)}) collective-permute-start(bf16[4,128,512]{2,1,0:T(8,128)(2,1)} %get-tuple-element.84), channel_id=1, source_target_pairs={{0,2},{1,3},{2,0},{3,1},{4,6},{5,7},{6,4},{7,5},{8,10},{9,11},{10,... | collective-permute-start | bytes 1572872 | tf_op jit(solution)/shard_map/ppermute | solution.py:391
  45.9 0.8 copy-start.6
  46.7 0.6 copy-start.10
  47.3 13.6 %collective-permute-start.6 = (bf16[8,96,512]{2,1,0:T(8,128)(2,1)}, bf16[8,96,512]{2,1,0:T(8,128)(2,1)}, u32[]{:S(2)}, u32[]{:S(2)}) collective-permute-start(bf16[8,96,512]{2,1,0:T(8,128)(2,1)} %get-tuple-element.78), channel_id=1, source_target_pairs={{0,1},{1,0},{2,3},{3,2},{4,5},{5,4},{6,7},{7,6},{8,9},{9,8},{10,11... | collective-permute-start | bytes 2359304 | tf_op jit(solution)/shard_map/ppermute | solution.py:391
  47.4 10.1 %all-to-all-start.1 = ((bf16[16,2,512]{2,1,0:T(2,128)(2,1)}), bf16[16,2,512]{2,1,0:T(2,128)(2,1)S(1)}, u32[]{:S(2)}, u32[]{:S(2)}) async-start(bf16[16,2,512]{2,1,0:T(2,128)(2,1)} %get-tuple-element.75), calls=%async_computation.1 | async-start | bytes 65536 | tf_op jit(solution)/shard_map/all_to_all | solution.py:551
  55.8 0.8 copy-start.8
  57.5 18.1 %all-to-all-start.3 = ((bf16[4,128,512]{2,1,0:T(8,128)(2,1)}), bf16[4,128,512]{2,1,0:T(8,128)(2,1)S(1)}, u32[]{:S(2)}, u32[]{:S(2)}) async-start(bf16[4,128,512]{2,1,0:T(8,128)(2,1)} %copy-done.8), calls=%async_computation.3 | async-start | bytes 1048576 | tf_op jit(solution)/shard_map/all_to_all | solution.py:417
  62.2 16.8 %copy-start.11 = (bf16[64,512]{1,0:T(8,128)(2,1)S(1)}, bf16[64,512]{1,0:T(8,128)(2,1)}, u32[]{:S(2)}) copy-start(bf16[64,512]{1,0:T(8,128)(2,1)} %copy-done.10) | copy-start | bytes 196612
  62.2 19.4 %copy-start.1 = (bf16[1536,512]{1,0:T(8,128)(2,1)S(1)}, bf16[1536,512]{1,0:T(8,128)(2,1)}, u32[]{:S(2)}) copy-start(bf16[1536,512]{1,0:T(8,128)(2,1)} %copy-done) | copy-start | bytes 4718596
  62.2 10.8 %collective-permute-start.7 = (bf16[4,96,512]{2,1,0:T(8,128)(2,1)S(1)}, bf16[4,96,512]{2,1,0:T(8,128)(2,1)S(1)}, u32[]{:S(2)}, u32[]{:S(2)}) collective-permute-start(bf16[4,96,512]{2,1,0:T(8,128)(2,1)S(1)} %get-tuple-element.80), channel_id=1, source_target_pairs={{0,2},{1,3},{2,0},{3,1},{4,6},{5,7},{6,4},{7,5},{8,10},{9,11},{10,... | collective-permute-start | bytes 1179656 | tf_op jit(solution)/shard_map/ppermute | solution.py:391
  75.5 14.7 %all-to-all-start.2 = ((bf16[4,96,512]{2,1,0:T(8,128)(2,1)}), bf16[4,96,512]{2,1,0:T(8,128)(2,1)S(1)}, u32[]{:S(2)}, u32[]{:S(2)}) async-start(bf16[4,96,512]{2,1,0:T(8,128)(2,1)} %get-tuple-element.82), calls=%async_computation.2 | async-start | bytes 786432 | tf_op jit(solution)/shard_map/all_to_all | solution.py:417
  79.0 7.2 %collective-permute-start.4 = (bf16[64,512]{1,0:T(8,128)(2,1)S(1)}, bf16[64,512]{1,0:T(8,128)(2,1)S(1)}, u32[]{:S(2)}, u32[]{:S(2)}) collective-permute-start(bf16[64,512]{1,0:T(8,128)(2,1)S(1)} %copy-done.11), channel_id=1, source_target_pairs={{0,1},{1,2},{2,3},{3,4},{4,5},{5,6},{6,7},{7,8},{8,9},{9,10},{10,1... | collective-permute-start | bytes 196616 | tf_op jit(solution)/shard_map/ppermute | solution.py:550
  80.3 5.9 %collective-permute-start.5 = (bf16[64,512]{1,0:T(8,128)(2,1)S(1)}, bf16[64,512]{1,0:T(8,128)(2,1)S(1)}, u32[]{:S(2)}, u32[]{:S(2)}) collective-permute-start(bf16[64,512]{1,0:T(8,128)(2,1)S(1)} %get-tuple-element.74), channel_id=1, source_target_pairs={{1,0},{2,1},{3,2},{4,3},{5,4},{6,5},{7,6},{8,7},{9,8},{10,9},{11,1... | collective-permute-start | bytes 196616 | tf_op jit(solution)/shard_map/ppermute | solution.py:549
  81.6 1.4 %copy-start.3 = (bf16[1536,512]{1,0:T(8,128)(2,1)S(1)}, bf16[1536,512]{1,0:T(8,128)(2,1)}, u32[]{:S(2)}) copy-start(bf16[1536,512]{1,0:T(8,128)(2,1)} %copy-done.2) | copy-start | bytes 4718596
  83.0 1.4 %copy-start.5 = (bf16[1536,512]{1,0:T(8,128)(2,1)S(1)}, bf16[1536,512]{1,0:T(8,128)(2,1)}, u32[]{:S(2)}) copy-start(bf16[1536,512]{1,0:T(8,128)(2,1)} %copy-done.4) | copy-start | bytes 4718596
  84.4 1.8 %copy-start.7 = (f32[256,512]{1,0:T(8,128)S(1)}, f32[256,512]{1,0:T(8,128)}, u32[]{:S(2)}) copy-start(f32[256,512]{1,0:T(8,128)} %copy-done.6) | copy-start | bytes 1572868
  84.4 1.8 %copy-start.9 = (s32[1,16,2]{1,2,0:T(2,128)S(1)}, s32[1,16,2]{1,2,0:T(2,128)}, u32[]{:S(2)}) copy-start(s32[1,16,2]{1,2,0:T(2,128)} %param.32) | copy-start | bytes 388

commit v4 on v3

--- a/solution.py
+++ b/solution.py
@@ -45,9 +45,9 @@
     return jnp.concatenate(parts, axis=0)
 
 
-def pick_columns(columns, width):
+def pick_columns(columns, start, stop):
     lane = lax.broadcasted_iota(jnp.int32, columns.shape, 1)
-    return [ones_where(columns == lane + c * LANES) for c in range(width // LANES)]
+    return [ones_where(columns == lane + at) for at in range(start, stop, LANES)]
 
 
 def pick_rows(idx_ref, step, tile, width):
@@ -68,13 +68,13 @@
     ).astype(BF16)
 
 
-def split_halves(bit, total_ref, at, rows, send_ref, keep_ref, offset):
+def split_halves(bit, total_ref, at, block, first, rows, send_ref, keep_ref, offset):
     half = send_ref.shape[0]
     for q in range(half):
-        there = pl.multiple_of((2 * q + 1 - bit) * rows, rows)
-        here = pl.multiple_of((2 * q + bit) * rows, rows)
-        send_ref[q, offset : offset + rows, :] = total_ref[pl.ds(at + there, rows), :].astype(BF16)
-        keep_ref[q, offset : offset + rows, :] = total_ref[pl.ds(at + here, rows), :]
+        there = pl.multiple_of(at + first + (2 * q + 1 - bit) * block, 32)
+        here = pl.multiple_of(at + first + (2 * q + bit) * block, 32)
+        send_ref[q, offset : offset + rows, :] = total_ref[pl.ds(there, rows), :].astype(BF16)
+        keep_ref[q, offset : offset + rows, :] = total_ref[pl.ds(here, rows), :]
 
 
 def fetch(pairs, sems):
@@ -106,38 +106,68 @@
     tail_ref[...] = node_ref[nodes - NEAR :, :]
 
 
-def sender_table_index(raw, places, tiles, base):
-    far = raw - base
-    moved = base + lax.rem(far, places) * tiles + lax.div(far, places)
-    return jnp.where(raw >= base, moved, raw)
+def table_index(raw, places, tiles, nodes):
+    far = raw - (nodes + 2 * NEAR)
+    far = nodes + 2 * NEAR + lax.rem(far, places) * tiles + lax.div(far, places)
+    rim = jnp.where(raw < NEAR, raw + nodes, raw)
+    own = jnp.where((raw >= NEAR) & (raw < NEAR + nodes), raw - NEAR, rim)
+    return jnp.where(raw >= nodes + 2 * NEAR, far, own)
+
+
+def prepare_kernel(
+    tiles, places,
+    node_hbm, w1_hbm, sender_hbm, receiver_hbm, b1_hbm, edge_hbm,
+    edge_ref, w1_ref, node_ref, receiver_ref, moved_ref, partial_ref,
+    weights, sender_ref, b1_ref, sems, edge_sems,
+):
+    edges, latent = edge_ref.shape
+    nodes = node_ref.shape[0]
+    copies = fetch(
+        [
+            (node_hbm, node_ref), (w1_hbm, w1_ref), (sender_hbm, sender_ref),
+            (receiver_hbm, receiver_ref), (b1_hbm, b1_ref),
+        ],
+        sems,
+    )
+    edge_copies = fetch(tile_pairs(edge_hbm, edge_ref, edges // 2), edge_sems)
+    for copy in copies:
+        copy.wait()
+    moved_ref[...] = table_index(sender_ref[...], places, tiles, nodes)
+    weights[:latent, :] = w1_ref[:latent, :]
+    weights[latent : latent + nodes, :] = dot(
+        node_ref[...], w1_ref[latent : 2 * latent, :]
+    ).astype(BF16)
+    weights[latent + nodes :, :] = dot(node_ref[...], w1_ref[2 * latent :, :]).astype(BF16)
+    for copy in edge_copies:
+        copy.wait()
+    for step in range(edges // TILE):
+        tile = slice(step * TILE, (step + 1) * TILE)
+        senders = pick_columns(index_columns(moved_ref, step, TILE), 0, nodes)
+        receivers = pick_columns(index_columns(receiver_ref, step, TILE), 0, nodes)
+        inputs = jnp.concatenate([edge_ref[tile, :]] + senders + receivers, axis=1)
+        partial_ref[tile, :] = dot(inputs, weights[...]) + b1_ref[...]
 
 
 def forward_kernel(
     tiles, places, fast,
-    edge_hbm, w1_hbm, w2_hbm, nw1_hbm, nw2_hbm, node_hbm, ncot_hbm,
-    sender_hbm, receiver_hbm, b1_hbm, b2_hbm, gain_hbm, nb1_hbm, nb2_hbm, ngain_hbm, count_hbm,
-    lower_ref, upper_ref, far_ref,
-    edge_ref, w1_ref, w2_ref, node_ref, receiver_ref, gain_ref,
-    hidden_ref, slope_ref, normed_ref, inverse_ref, table_ref, moved_ref, dsum_ref, base_ref,
+    w2_hbm, nw1_hbm, nw2_hbm, ncot_hbm,
+    b2_hbm, gain_hbm, nb1_hbm, nb2_hbm, ngain_hbm, count_hbm,
+    lower_ref, upper_ref, far_ref, partial_ref, w1_ref, node_ref, receiver_ref, moved_ref,
+    w2_ref, gain_ref,
+    hidden_ref, slope_ref, normed_ref, inverse_ref, table_ref, dsum_ref, base_ref,
     gsend_ref, gkeep_ref,
-    weights, summed, grads, nw1_ref, nw2_ref, ncot_ref, sender_ref,
-    b1_ref, b2_ref, nb1_ref, nb2_ref, ngain_ref, count_ref, sems, edge_sems,
+    weights, summed, grads, nw1_ref, nw2_ref, ncot_ref,
+    b2_ref, nb1_ref, nb2_ref, ngain_ref, count_ref, sems,
 ):
     here = lax.axis_index("tiles")
-    edges, latent = edge_ref.shape
+    edges, latent = hidden_ref.shape
     nodes = node_ref.shape[0]
     rows = table_ref.shape[0]
-    far_base = nodes + 2 * NEAR
+    steps = edges // TILE
 
     early = fetch(
-        [
-            (node_hbm, node_ref), (w1_hbm, w1_ref), (sender_hbm, sender_ref),
-            (receiver_hbm, receiver_ref), (b1_hbm, b1_ref), (b2_hbm, b2_ref),
-            (gain_hbm, gain_ref), (count_hbm, count_ref), (w2_hbm, w2_ref),
-        ],
-        sems,
-    )
-    edge_copies = fetch(tile_pairs(edge_hbm, edge_ref, TILE), edge_sems)
+        [(count_hbm, count_ref), (b2_hbm, b2_ref), (gain_hbm, gain_ref), (w2_hbm, w2_ref)], sems
+    )
     late = fetch(
         [
             (nw1_hbm, nw1_ref), (nw2_hbm, nw2_ref), (ncot_hbm, ncot_ref),
@@ -146,37 +176,33 @@
         sems.at[pl.ds(len(early), 6)],
     )
 
+    table_ref[:nodes, :] = node_ref[...]
+    table_ref[nodes : nodes + NEAR, :] = lower_ref[...]
+    table_ref[nodes + NEAR : nodes + 2 * NEAR, :] = upper_ref[...]
+    for j in range(places):
+        at = nodes + 2 * NEAR + j * tiles
+        table_ref[at : at + tiles, :] = far_ref[:, j, :]
+    used = nodes + 2 * NEAR + places * tiles
+    if used < rows:
+        table_ref[used:, :] = jnp.zeros((rows - used, latent), BF16)
+    weights[...] = dot(table_ref[nodes:, :], w1_ref[latent : 2 * latent, :]).astype(BF16)
     for copy in early:
         copy.wait()
-    moved_ref[...] = sender_table_index(sender_ref[...], places, tiles, far_base)
-    table_ref[:NEAR, :] = lower_ref[...]
-    table_ref[NEAR : NEAR + nodes, :] = node_ref[...]
-    table_ref[NEAR + nodes : far_base, :] = upper_ref[...]
-    for j in range(places):
-        table_ref[far_base + j * tiles : far_base + (j + 1) * tiles, :] = far_ref[:, j, :]
-    used = far_base + places * tiles
-    if used < rows:
-        table_ref[used:, :] = jnp.zeros((rows - used, latent), BF16)
-    weights[:latent, :] = w1_ref[:latent, :]
-    weights[latent : latent + rows, :] = dot(
-        table_ref[...], w1_ref[latent : 2 * latent, :]
-    ).astype(BF16)
-    weights[latent + rows :, :] = dot(node_ref[...], w1_ref[2 * latent :, :]).astype(BF16)
-
-    for step in range(edges // TILE):
-        edge_copies[step].wait()
+    live = count_ref[here]
+
+    def activate(step):
         tile = slice(step * TILE, (step + 1) * TILE)
-        senders = pick_columns(index_columns(moved_ref, step, TILE), rows)
-        receivers = pick_columns(index_columns(receiver_ref, step, TILE), nodes)
-        inputs = jnp.concatenate([edge_ref[tile, :]] + senders + receivers, axis=1)
-        preact = dot(inputs, weights[...]) + b1_ref[...]
+        senders = pick_columns(index_columns(moved_ref, step, TILE), nodes, rows)
+        preact = partial_ref[tile, :] + dot(jnp.concatenate(senders, axis=1), weights[...])
         sig = sigmoid(preact)
-        hidden = (preact * sig).astype(BF16)
-        hidden_ref[tile, :] = hidden
         slope_ref[tile, :] = (sig * (1.0 + preact * (1.0 - sig))).astype(BF16)
-        centred, inverse = norm_forward(dot(hidden, w2_ref[...]) + b2_ref[...])
+        hidden_ref[tile, :] = (preact * sig).astype(BF16)
+
+    def normalize(step):
+        tile = slice(step * TILE, (step + 1) * TILE)
+        centred, inverse = norm_forward(dot(hidden_ref[tile, :], w2_ref[...]) + b2_ref[...])
         position = step * TILE + lax.broadcasted_iota(jnp.int32, inverse.shape, 0)
-        inverse = jnp.where(position < count_ref[here], inverse, 0.0)
+        inverse = jnp.where(position < live, inverse, 0.0)
         normed = centred * inverse
         normed_ref[tile, :] = normed
         inverse_ref[tile, :] = jnp.broadcast_to(inverse, (TILE, LANES))
@@ -186,6 +212,12 @@
             summed[...] = part
         else:
             summed[...] += part
+
+    for step in range(steps + 1):
+        if step < steps:
+            activate(step)
+        if step > 0:
+            normalize(step - 1)
 
     for copy in late:
         copy.wait()
@@ -205,8 +237,9 @@
     if fast:
         bit = lax.rem(here, 2)
         first = 2 * latent // tiles
-        split_halves(bit, grads, 0, first, gsend_ref, gkeep_ref, 0)
-        split_halves(bit, grads, 2 * latent, latent // tiles, gsend_ref, gkeep_ref, first)
+        split_halves(bit, grads, 0, first, 0, first, gsend_ref, gkeep_ref, 0)
+        second = latent // tiles
+        split_halves(bit, grads, 2 * latent, second, 0, second, gsend_ref, gkeep_ref, first)
     else:
         gkeep_ref[...] = grads[: 2 * latent, :]
         gsend_ref[...] = grads[2 * latent :, :]
@@ -216,33 +249,45 @@
     tiles, fast,
     cot_hbm, receiver_ref, dsum_ref, hidden_ref, slope_ref, normed_ref, inverse_ref, w2_ref, gain_ref,
     cot_ref, dpre_ref, gsend_ref, gkeep_ref,
-    grads, sems,
+    grads, dout, sems,
 ):
     here = lax.axis_index("tiles")
     edges, latent = cot_ref.shape
     nodes = dsum_ref.shape[0]
-    copies = fetch(tile_pairs(cot_hbm, cot_ref, TILE), sems)
-
-    for step in range(edges // TILE):
-        copies[step].wait()
+    copies = fetch(tile_pairs(cot_hbm, cot_ref, edges // 2), sems)
+    steps = edges // TILE
+    for copy in copies:
+        copy.wait()
+
+    def outer(step):
         tile = slice(step * TILE, (step + 1) * TILE)
         receivers = jnp.concatenate(
-            pick_columns(index_columns(receiver_ref, step, TILE), nodes), axis=1
+            pick_columns(index_columns(receiver_ref, step, TILE), 0, nodes), axis=1
         )
         grad_update = cot_ref[tile, :].astype(F32) + dot(receivers, dsum_ref[...])
         inverse = inverse_ref[tile, :1]
-        dout = norm_backward(grad_update * gain_ref[...], normed_ref[tile, :], inverse)
+        dout[tile, :] = norm_backward(grad_update * gain_ref[...], normed_ref[tile, :], inverse)
+
+    def inner(step):
+        tile = slice(step * TILE, (step + 1) * TILE)
         dpre_ref[tile, :] = (
-            dot(dout, w2_ref[...], NT) * slope_ref[tile, :].astype(F32)
+            dot(dout[tile, :], w2_ref[...], NT) * slope_ref[tile, :].astype(F32)
         ).astype(BF16)
-        part = dot(hidden_ref[tile, :], dout, TN)
+        part = dot(hidden_ref[tile, :], dout[tile, :], TN)
         if step == 0:
             grads[...] = part
         else:
             grads[...] += part
 
+    for step in range(steps + 1):
+        if step < steps:
+            outer(step)
+        if step > 0:
+            inner(step - 1)
+
     if fast:
-        split_halves(lax.rem(here, 2), grads, 0, latent // tiles, gsend_ref, gkeep_ref, 0)
+        rows = latent // tiles
+        split_halves(lax.rem(here, 2), grads, 0, rows, 0, rows, gsend_ref, gkeep_ref, 0)
     else:
         gkeep_ref[...] = grads[...]
         gsend_ref[...] = jnp.zeros_like(gsend_ref)
@@ -251,9 +296,10 @@
 def first_kernel(
     tiles, places, fast,
     dpre_ref, edge_ref, sender_ref, receiver_ref, table_ref, node_ref, w1_ref, base_ref,
-    gsend_ref, gkeep_ref, lower_ref, upper_ref, far_ref, partial_ref,
-    grads, sums,
+    *refs,
 ):
+    out_refs, (grads, sums) = refs[:-2], refs[-2:]
+    lower_ref, upper_ref, far_ref, partial_ref = out_refs[:4]
     here = lax.axis_index("tiles")
     edges, latent = edge_ref.shape
     nodes = node_ref.shape[0]
@@ -283,20 +329,23 @@
     grads[latent : 2 * latent, :] = dot(table_ref[...], by_sender, TN)
     grads[2 * latent :, :] = dot(node_ref[...], by_receiver, TN)
     if fast:
-        split_halves(lax.rem(here, 2), grads, 0, 3 * latent // tiles, gsend_ref, gkeep_ref, 0)
+        bit = lax.rem(here, 2)
+        block = 3 * latent // tiles
+        at = 0
+        for send_ref, keep_ref in (out_refs[4:6], out_refs[6:8]):
+            part = send_ref.shape[1]
+            split_halves(bit, grads, 0, block, at, part, send_ref, keep_ref, 0)
+            at += part
     else:
-        gkeep_ref[...] = grads[...]
-        gsend_ref[...] = jnp.zeros_like(gsend_ref)
+        out_refs[4][...] = grads[...]
     back = dot(by_sender, w1_ref[latent : 2 * latent, :], NT)
-    lower_ref[...] = back[:NEAR, :].astype(BF16)
-    upper_ref[...] = back[NEAR + nodes : 2 * NEAR + nodes, :].astype(BF16)
+    lower_ref[...] = back[nodes : nodes + NEAR, :].astype(BF16)
+    upper_ref[...] = back[nodes + NEAR : nodes + 2 * NEAR, :].astype(BF16)
     for j in range(places):
         at = 2 * NEAR + nodes + j * tiles
         far_ref[:, j, :] = back[at : at + tiles, :].astype(BF16)
     partial_ref[...] = (
-        base_ref[...]
-        + back[NEAR : NEAR + nodes, :]
-        + dot(by_receiver, w1_ref[2 * latent :, :], NT)
+        base_ref[...] + back[:nodes, :] + dot(by_receiver, w1_ref[2 * latent :, :], NT)
     )
 
 
@@ -346,23 +395,18 @@
         at += rows
 
 
-def spread_kernel(keep_ref, got_ref, own_ref, send_ref):
-    place = lax.div(lax.axis_index("tiles"), 4)
-    own_ref[...] = keep_ref[place] + got_ref[place].astype(F32)
-    for q in range(keep_ref.shape[0]):
-        send_ref[q] = (keep_ref[q] + got_ref[q].astype(F32)).astype(BF16)
-
-
-def finish_kernel(own_ref, got_ref, *out_refs):
-    count = got_ref.shape[0]
-    place = lax.div(lax.axis_index("tiles"), 4)
-    total = own_ref[...]
-    for k in range(1, count):
-        total = total + got_ref[lax.rem(place + k, count)].astype(F32)
-    at = 0
-    for out_ref in out_refs:
-        out_ref[...] = total[at : at + out_ref.shape[0], :]
-        at += out_ref.shape[0]
+def finish_kernel(count, splits, *refs):
+    out_refs = refs[2 * count :]
+    rows = [0] * len(out_refs)
+    for keep_ref, got_ref, parts in zip(refs[:count], refs[count : 2 * count], splits):
+        at = 0
+        for which, size in parts:
+            first = rows[which]
+            out_refs[which][first : first + size, :] = keep_ref[0, at : at + size, :] + got_ref[
+                0, at : at + size, :
+            ].astype(F32)
+            at += size
+            rows[which] += size
 
 
 def shaped(shape, dtype):
@@ -391,38 +435,29 @@
     return lax.ppermute(send, "tiles", [(i, i ^ bit) for i in range(tiles)])
 
 
-def halve(keeps, gots):
+def halve(shift, keeps, gots):
     half, _, width = keeps[0].shape
     rows = sum(keep.shape[1] for keep in keeps)
     shape = (half // 2, rows, width)
     return call(
-        functools.partial(halve_kernel, 1, len(keeps)),
+        functools.partial(halve_kernel, shift, len(keeps)),
         "halve",
         [pltpu.VMEM(shape, BF16), pltpu.VMEM(shape, F32)],
         [*keeps, *gots],
     )
 
 
-def spread(keep, got):
+def finish(keeps, gots, splits, sizes):
     return call(
-        spread_kernel,
-        "spread",
-        [pltpu.VMEM(keep.shape[1:], F32), pltpu.VMEM(keep.shape, BF16)],
-        [keep, got],
-    )
-
-
-def exchange(tiles, send):
-    groups = [[z * 4 + i for z in range(tiles // 4)] for i in range(4)]
-    return lax.all_to_all(
-        send, "tiles", split_axis=0, concat_axis=0, axis_index_groups=groups, tiled=True
-    )
-
-
-def finish(own, got, sizes):
-    return call(
-        finish_kernel, "finish", [shaped((size, own.shape[1]), F32) for size in sizes], [own, got]
-    )
+        functools.partial(finish_kernel, len(keeps), splits),
+        "finish",
+        [shaped((size, keeps[0].shape[-1]), F32) for size in sizes],
+        [*keeps, *gots],
+    )
+
+
+def after(value, *others):
+    return lax.optimization_barrier((value, *others))[0]
 
 
 def shards(
@@ -473,36 +508,49 @@
     upper = lax.ppermute(head, "tiles", downward)
     incoming = lax.all_to_all(outgoing, "tiles", split_axis=0, concat_axis=0, tiled=True)
 
+    edge_kept, w1_kept, node_kept, receiver_kept, moved, preact = call(
+        functools.partial(prepare_kernel, tiles, places),
+        "prepare",
+        [
+            vmem((edges, latent), BF16), vmem(edge_w1.shape, BF16), vmem((nodes, latent), BF16),
+            vmem(receiver.shape, jnp.int32), vmem(sender.shape, jnp.int32),
+            vmem((edges, latent), F32),
+        ],
+        [node_latent, edge_w1, after(sender, outgoing), receiver, row(edge_b1), edge_latent],
+        hbm=6,
+        scratch=[
+            vmem((latent + 2 * nodes, latent), BF16), vmem(sender.shape, jnp.int32),
+            vmem((1, latent), F32), pltpu.SemaphoreType.DMA((5,)), pltpu.SemaphoreType.DMA((2,)),
+        ],
+        flops=3 * unit,
+    )
+
     (
-        edge_kept, w1_kept, w2_kept, node_kept, receiver_kept, gain_kept,
-        hidden, slope, normed, inverse, table, moved, dsum, base, node_send, node_keep,
+        w2_kept, gain_kept,
+        hidden, slope, normed, inverse, table, dsum, base, node_send, node_keep,
     ) = call(
         functools.partial(forward_kernel, tiles, places, fast),
         "forward",
         [
-            vmem((edges, latent), BF16), vmem(edge_w1.shape, BF16), vmem(edge_w2.shape, BF16),
-            vmem((nodes, latent), BF16), vmem(receiver.shape, jnp.int32), vmem((1, latent), F32),
+            vmem(edge_w2.shape, BF16), vmem((1, latent), F32),
             vmem((edges, latent), BF16), vmem((edges, latent), BF16), vmem((edges, latent), F32),
-            vmem((edges, LANES), F32), vmem((rows, latent), BF16), vmem(sender.shape, jnp.int32),
+            vmem((edges, LANES), F32), vmem((rows, latent), BF16),
             vmem((nodes, latent), BF16), vmem((nodes, latent), F32),
         ] + grad_shapes(3 * latent if fast else 2 * latent),
         [
-            edge_latent, edge_w1, edge_w2, node_w1, node_w2, node_latent, node_cot,
-            sender, receiver, row(edge_b1), row(edge_b2), row(edge_gain),
-            row(node_b1), row(node_b2), row(node_gain), edge_count,
-            lower, upper, incoming,
-        ],
-        hbm=16,
+            edge_w2, node_w1, node_w2, node_cot,
+            row(edge_b2), row(edge_gain), row(node_b1), row(node_b2), row(node_gain), edge_count,
+            lower, upper, incoming, preact, w1_kept, node_kept, receiver_kept, moved,
+        ],
+        hbm=10,
         scratch=[
-            vmem((latent + rows + nodes, latent), BF16), vmem((nodes, latent), F32),
+            vmem((rows - nodes, latent), BF16), vmem((nodes, latent), F32),
             vmem((3 * latent, latent), F32), vmem(node_w1.shape, BF16), vmem(node_w2.shape, BF16),
-            vmem((nodes, latent), BF16), vmem(sender.shape, jnp.int32),
-        ] + [vmem((1, latent), F32)] * 5 + [
-            pltpu.SMEM(edge_count.shape, jnp.int32),
-            pltpu.SemaphoreType.DMA((15,)), pltpu.SemaphoreType.DMA((steps,)),
-        ],
-        flops=7 * unit,
-        limit=24,
+            vmem((nodes, latent), BF16),
+        ] + [vmem((1, latent), F32)] * 4 + [
+            pltpu.SMEM(edge_count.shape, jnp.int32), pltpu.SemaphoreType.DMA((10,)),
+        ],
+        flops=5 * unit,
     )
 
     cot_kept, dpre, second_send, second_keep = call(
@@ -511,26 +559,33 @@
         [vmem((edges, latent), BF16), vmem((edges, latent), BF16)] + grad_shapes(latent),
         [edge_cot, receiver_kept, dsum, hidden, slope, normed, inverse, w2_kept, gain_kept],
         hbm=1,
-        scratch=[vmem((latent, latent), F32), pltpu.SemaphoreType.DMA((steps,))],
+        scratch=[
+            vmem((latent, latent), F32), vmem((edges, latent), BF16), pltpu.SemaphoreType.DMA((2,)),
+        ],
         flops=3 * unit,
     )
     if fast:
-        send, chain = halve(
-            [node_keep, second_keep],
-            [swap(tiles, 1, node_send), swap(tiles, 1, second_send)],
-        )
-        dpre, send = lax.optimization_barrier((dpre, send))
+        send, chain = halve(1, [node_keep], [swap(tiles, 1, node_send)])
+        dpre = after(dpre, send)
         got = swap(tiles, 2, send)
-
-    first_send, first_keep, to_lower, to_upper, to_far, partial = call(
+        got_second = swap(tiles, 1, second_send)
+
+    per = latent // tiles
+    to_lower, to_upper, to_far, partial, *first = call(
         functools.partial(first_kernel, tiles, places, fast),
         "first",
-        grad_shapes(3 * latent) + [
-            shaped((NEAR, latent), BF16),
-            shaped((NEAR, latent), BF16),
+        [
+            vmem((NEAR, latent), BF16),
+            vmem((NEAR, latent), BF16),
             shaped((tiles, places, latent), BF16),
             vmem((nodes, latent), F32),
-        ],
+        ] + (
+            [
+                vmem((half, 2 * per, latent), BF16), vmem((half, 2 * per, latent), F32),
+                vmem((half, per, latent), BF16), vmem((half, per, latent), F32),
+            ]
+            if fast else [shaped((3 * latent, latent), F32)]
+        ),
         [dpre, edge_kept, moved, receiver_kept, table, node_kept, w1_kept, base],
         scratch=[vmem((3 * latent, latent), F32), vmem((rows + nodes, latent), F32)],
         flops=4 * unit,
@@ -540,11 +595,23 @@
         edge_kernel,
         "edge",
         [shaped((edges, latent), BF16)],
-        [dpre, cot_kept, w1_kept],
+        [after(dpre, partial), cot_kept, w1_kept],
         out_specs=[pl.BlockSpec(memory_space=pltpu.HBM)],
         scratch=[vmem((edges, latent), BF16), pltpu.SemaphoreType.DMA((steps,))],
         flops=2 * unit,
     )
+
+    if fast:
+        send_a, keep_a, send_b, keep_b = first
+        send_a, chain_a = halve(1, [after(keep_a, grad_edge)], [swap(tiles, 1, send_a)])
+        got_a = swap(tiles, 2, send_a)
+        send_b, chain_b = halve(
+            1, [after(keep_b, send_a), second_keep], [swap(tiles, 1, send_b), got_second]
+        )
+        got_b = swap(tiles, 2, send_b)
+        send, chain = halve(2, [after(chain, send_b)], [got])
+        got = swap(tiles, 4, send)
+        to_far, to_lower, to_upper = lax.optimization_barrier((to_far, to_lower, to_upper, send))[:3]
 
     above = lax.ppermute(to_lower, "tiles", downward)
     below = lax.ppermute(to_upper, "tiles", upward)
@@ -557,21 +624,28 @@
     )
 
     if fast:
-        send, late_chain = halve([first_keep], [swap(tiles, 1, first_send)])
-        late_got = swap(tiles, 2, send)
-        per = latent // tiles
-        own, send = spread(chain, got)
-        grad_node_w1, grad_node_w2, grad_edge_w2 = finish(
-            own, exchange(tiles, send), [2 * per, per, per]
+        send, chain = halve(3, [chain], [got])
+        got = swap(tiles, 8, send)
+        send_a, chain_a = halve(2, [after(chain_a, send)], [got_a])
+        got_a = swap(tiles, 4, send_a)
+        send_a, chain_a = halve(3, [chain_a], [got_a])
+        got_a = swap(tiles, 8, send_a)
+        send_b, chain_b = halve(2, [after(chain_b, send_a)], [got_b])
+        got_b = swap(tiles, 4, send_b)
+        grad_node_w1, grad_node_w2 = finish(
+            [chain], [got], [[(0, 2 * per), (1, per)]], [2 * per, per]
         )
-        own, send = spread(late_chain, late_got)
-        (grad_edge_w1,) = finish(own, exchange(tiles, send), [3 * per])
+        send_b, chain_b = halve(3, [chain_b], [got_b])
+        got_b = swap(tiles, 8, send_b)
+        grad_edge_w1, grad_edge_w2 = finish(
+            [chain_a, chain_b], [got_a, got_b], [[(0, 2 * per)], [(0, per), (1, per)]], [3 * per, per]
+        )
     else:
         scatter = functools.partial(
             lax.psum_scatter, axis_name="tiles", scatter_dimension=0, tiled=True
         )
         grad_node_w1, grad_node_w2 = scatter(node_keep), scatter(node_send)
-        grad_edge_w1, grad_edge_w2 = scatter(first_keep), scatter(second_keep)
+        grad_edge_w1, grad_edge_w2 = scatter(first[0]), scatter(second_keep)
     return (grad_node, grad_edge, grad_edge_w1, grad_edge_w2, grad_node_w1, grad_node_w2)
 
 

time: 92.2 us -> 91.7 us (level)
  starting transfers between devices: 18 us -> 33.4 us
  waiting for transfers between devices: 21.3 us -> 13.3 us
  blocking collectives: 15.7 us -> 10.7 us
  Pallas kernels: 30.1 us -> 27.1 us
    ppermute x5 -> x13, starting transfers between devices: 1.34 us -> 19.8 us  [swap(): return lax.ppermute(send, 'tiles', [(i, i ^ bit) for i in range(tiles)])]
    all_to_all x1, blocking collectives: 15.7 us -> 10.7 us  [shards(): lax.all_to_all(to_far, 'tiles', split_axis=0, concat_axis=0, tiled=True)]
    all_to_all x3 -> x1, waiting for transfers between devices: 4.79 us -> 0.01 us  [shards(): lax.all_to_all(outgoing, 'tiles', split_axis=0, concat_axis=0, tiled=True)]
    ppermute x5 -> x13, waiting for transfers between devices: 16.5 us -> 13.3 us  [swap(): return lax.ppermute(send, 'tiles', [(i, i ^ bit) for i in range(tiles)])]
    all_to_all x3 -> x1, starting transfers between devices: 10.4 us -> 7.37 us  [shards(): lax.all_to_all(outgoing, 'tiles', split_axis=0, concat_axis=0, tiled=True)]
    pallas_call x12 -> x18, Pallas kernels: 30.1 us -> 27.1 us  [call(): pl.pallas_call(kernel, in_specs=[pl.BlockSpec(memory_space=pltpu.HBM)] *...]
    unnamed x24 -> x12, local copies, waits for them, and re-layouts: 5.07 us -> 5.9 us
  transfers between devices with their start and end apart: 12 -> 18, of which waited for: 6 -> 3; matrix products, arithmetic and copies ran while one was open for 0% -> 0% of each run, Pallas kernels for 17% -> 14%
where the time goes in v4:
time: 91.7 us; the launch traced here: 91.2 us
  starting transfers between devices  33.4 us (36%)
  Pallas kernels  27.1 us (30%)
  waiting for transfers between devices  13.3 us (15%)
  blocking collectives  10.7 us (12%)
  local copies, waits for them, and re-layouts  5.9 us (6%)
    pallas_call x18, Pallas kernels, call(): pl.pallas_call(kernel, in_specs=[pl.BlockSpec(memory_space=pltpu.HBM)] *...  27.1 us
    ppermute x13, starting transfers between devices, swap(): return lax.ppermute(send, 'tiles', [(i, i ^ bit) for i in range(tiles)])  19.8 us
    ppermute x13, waiting for transfers between devices, swap(): return lax.ppermute(send, 'tiles', [(i, i ^ bit) for i in range(tiles)])  13.3 us
    all_to_all x1, blocking collectives, shards(): lax.all_to_all(to_far, 'tiles', split_axis=0, concat_axis=0, tiled=True)  10.7 us
    all_to_all x1, starting transfers between devices, shards(): lax.all_to_all(outgoing, 'tiles', split_axis=0, concat_axis=0, tiled=True)  7.37 us
    unnamed x12, local copies, waits for them, and re-layouts  5.9 us
    ppermute x1, starting transfers between devices, shards(): lower = lax.ppermute(tail, 'tiles', upward)  2.31 us
  transfers between devices with their start and end apart: 18, of which 3 were waited for; matrix products, arithmetic and copies ran while one was open for 0% of the time, Pallas kernels for 14%

profile of v4, /device:TPU:0, one launch (start us, length us, event | category | flops | bytes accessed | tf_op | source)
XLA Modules:
  0.0 91.2 jit_solution(69875201935674571)
XLA Ops:
  0.6 1.8 %outgoing.1 = (bf16[16,2,512]{2,1,0:T(2,128)(2,1)}, bf16[64,512]{1,0:T(8,128)(2,1)S(1)}, bf16[64,512]{1,0:T(8,128)(2,1)S(1)}) custom-call(s32[1,2,16]{2,1,0:T(2,128)} %bitcast.9, bf16[256,512]{1,0:T(8,128)(2,1)} %node_hbm.3), custom_call_target="tpu_custom_call" | custom-call | tf_op jit(solution)/shard_map/outgoing/pallas_call | solution.py:422
  2.5 7.4 %all-to-all-start = ((bf16[16,2,512]{2,1,0:T(2,128)(2,1)}), bf16[16,2,512]{2,1,0:T(2,128)(2,1)S(1)}, u32[]{:S(2)}, u32[]{:S(2)}) async-start(bf16[16,2,512]{2,1,0:T(2,128)(2,1)} %get-tuple-element.71), calls=%async_computation | async-start | bytes 65536 | tf_op jit(solution)/shard_map/all_to_all | solution.py:509
  9.8 2.3 %collective-permute-start = (bf16[64,512]{1,0:T(8,128)(2,1)S(1)}, bf16[64,512]{1,0:T(8,128)(2,1)S(1)}, u32[]{:S(2)}, u32[]{:S(2)}) collective-permute-start(bf16[64,512]{1,0:T(8,128)(2,1)S(1)} %get-tuple-element.74), channel_id=1, source_target_pairs={{0,1},{1,2},{2,3},{3,4},{4,5},{5,6},{6,7},{7,8},{8,9},{9,10},{10,1... | collective-permute-start | bytes 196616 | tf_op jit(solution)/shard_map/ppermute | solution.py:507
  12.2 1.3 %collective-permute-start.1 = (bf16[64,512]{1,0:T(8,128)(2,1)S(1)}, bf16[64,512]{1,0:T(8,128)(2,1)S(1)}, u32[]{:S(2)}, u32[]{:S(2)}) collective-permute-start(bf16[64,512]{1,0:T(8,128)(2,1)S(1)} %get-tuple-element.75), channel_id=1, source_target_pairs={{1,0},{2,1},{3,2},{4,3},{5,4},{6,5},{7,6},{8,7},{9,8},{10,9},{11,1... | collective-permute-start | bytes 196616 | tf_op jit(solution)/shard_map/ppermute | solution.py:508
  13.5 3.9 %prepare.1 = (bf16[1536,512]{1,0:T(8,128)(2,1)S(1)}, bf16[1536,512]{1,0:T(8,128)(2,1)S(1)}, bf16[256,512]{1,0:T(8,128)(2,1)S(1)}, s32[12,128]{1,0:T(8,128)S(1)},...) custom-call(bf16[256,512]{1,0:T(8,128)(2,1)} %node_hbm.3, bf16[1536,512]{1,0:T(8,128)(2,1)} %w1_hbm.1, ...), custom_call_target="tpu_custom_call" | custom-call | flops 2415919104 | bytes 6039797 | tf_op jit(solution)/shard_map/prepare/pallas_call | solution.py:422
  17.4 1.6 %copy-done.1 = f32[1536,512]{1,0:T(8,128)} copy-done((f32[1536,512]{1,0:T(8,128)}, f32[1536,512]{1,0:T(8,128)S(1)}, u32[]{:S(2)}) %copy-start.1) | copy-done | bytes 3145752
  19.7 1.9 %copy-done.2 = f32[1536,512]{1,0:T(8,128)S(1)} copy-done((f32[1536,512]{1,0:T(8,128)S(1)}, f32[1536,512]{1,0:T(8,128)}, u32[]{:S(2)}) %copy-start.2) | copy-done | bytes 3145752
  22.5 8.0 %forward.1 = (bf16[512,512]{1,0:T(8,128)(2,1)S(1)}, f32[1,512]{1,0:T(1,128)S(1)}, bf16[1536,512]{1,0:T(8,128)(2,1)S(1)}, bf16[1536,512]{1,0:T(8,128)(2,1)S(1)}, ...) custom-call(bf16[512,512]{1,0:T(8,128)(2,1)} %w2_hbm.1, ...), custom_call_target="tpu_custom_call" | custom-call | flops 4026531840 | bytes 10066329 | tf_op jit(solution)/shard_map/forward/pallas_call | solution.py:422
  30.5 2.3 %collective-permute-start.2 = (bf16[8,96,512]{2,1,0:T(8,128)(2,1)S(1)}, bf16[8,96,512]{2,1,0:T(8,128)(2,1)S(1)}, u32[]{:S(2)}, u32[]{:S(2)}) collective-permute-start(bf16[8,96,512]{2,1,0:T(8,128)(2,1)S(1)} %get-tuple-element.89), channel_id=1, source_target_pairs={{0,1},{1,0},{2,3},{3,2},{4,5},{5,4},{6,7},{7,6},{8,9},{9,8},{10,11... | collective-permute-start | bytes 2359304 | tf_op jit(solution)/shard_map/ppermute | solution.py:435
  32.9 4.8 %slope.1 = (bf16[1536,512]{1,0:T(8,128)(2,1)S(1)}, bf16[1536,512]{1,0:T(8,128)(2,1)S(1)}, bf16[8,32,512]{2,1,0:T(8,128)(2,1)S(1)}, f32[8,32,512]{2,1,0:T(8,128)S(1)}) custom-call(bf16[1536,512]{1,0:T(8,128)(2,1)} %cot_hbm.1, s32[12,128]{1,0:T(8,128)S(1)} %get-tuple-element.73.receiver_ref, bf16[256,512]{1,0:T(8,128)(2,1)S(1)} %get-tuple-element.80.dsum_ref, ...), custom_call_target="tpu_custom_call" | custom-call | flops 2415919104 | bytes 6039797 | tf_op jit(solution)/shard_map/slope/pallas_call | solution.py:422
  38.6 3.7 %first.1 = (bf16[64,512]{1,0:T(8,128)(2,1)S(1)}, bf16[64,512]{1,0:T(8,128)(2,1)S(1)}, bf16[16,2,512]{2,1,0:T(2,128)(2,1)S(1)}, f32[256,512]{1,0:T(8,128)S(1)}, b...) custom-call(bf16[1536,512]{1,0:T(8,128)(2,1)S(1)} %get-tuple-element, ...), custom_call_target="tpu_custom_call" | custom-call | flops 3221225472 | bytes 8053063 | tf_op jit(solution)/shard_map/first/pallas_call | solution.py:422
  42.4 2.1 %collective-permute-start.6 = (bf16[4,96,512]{2,1,0:T(8,128)(2,1)S(1)}, bf16[4,96,512]{2,1,0:T(8,128)(2,1)S(1)}, u32[]{:S(2)}, u32[]{:S(2)}) collective-permute-start(bf16[4,96,512]{2,1,0:T(8,128)(2,1)S(1)} %get-tuple-element.90), channel_id=1, source_target_pairs={{0,2},{1,3},{2,0},{3,1},{4,6},{5,7},{6,4},{7,5},{8,10},{9,11},{10,... | collective-permute-start | bytes 1179656 | tf_op jit(solution)/shard_map/ppermute | solution.py:435
  45.0 1.8 %edge.1 = bf16[1536,512]{1,0:T(8,128)(2,1)} custom-call(bf16[1536,512]{1,0:T(8,128)(2,1)S(1)} %get-tuple-element.102.dpre_ref, bf16[1536,512]{1,0:T(8,128)(2,1)S(1)} %get-tuple-element.103.cot_ref, bf16[1536,512]{1,0:T(8,128)(2,1)S(1)} %get-tuple-element.77.w1_ref), custom_call_target="tpu_custom_call" | custom-call | flops 1610612736 | bytes 4026531 | tf_op jit(solution)/shard_map/edge/pallas_call | solution.py:422
  47.2 7.2 %collective-permute-done.6.refs_1_ = bf16[4,96,512]{2,1,0:T(8,128)(2,1)S(1)} collective-permute-done((bf16[4,96,512]{2,1,0:T(8,128)(2,1)S(1)}, bf16[4,96,512]{2,1,0:T(8,128)(2,1)S(1)}, u32[]{:S(2)}, u32[]{:S(2)}) %collective-permute-start.6) | collective-permute-done | bytes 393248 | tf_op jit(solution)/shard_map/ppermute | solution.py:435
  54.5 3.0 %collective-permute-start.9 = (bf16[2,96,512]{2,1,0:T(8,128)(2,1)S(1)}, bf16[2,96,512]{2,1,0:T(8,128)(2,1)S(1)}, u32[]{:S(2)}, u32[]{:S(2)}) collective-permute-start(bf16[2,96,512]{2,1,0:T(8,128)(2,1)S(1)} %get-tuple-element.113), channel_id=1, source_target_pairs={{0,4},{1,5},{2,6},{3,7},{4,0},{5,1},{6,2},{7,3},{8,12},{9,13},{10,... | collective-permute-start | bytes 589832 | tf_op jit(solution)/shard_map/ppermute | solution.py:435
  58.1 3.1 %collective-permute-done.9.refs_1_ = bf16[2,96,512]{2,1,0:T(8,128)(2,1)S(1)} collective-permute-done((bf16[2,96,512]{2,1,0:T(8,128)(2,1)S(1)}, bf16[2,96,512]{2,1,0:T(8,128)(2,1)S(1)}, u32[]{:S(2)}, u32[]{:S(2)}) %collective-permute-start.9) | collective-permute-done | bytes 196640 | tf_op jit(solution)/shard_map/ppermute | solution.py:435
  61.3 2.1 %collective-permute-start.11 = (bf16[2,64,512]{2,1,0:T(8,128)(2,1)S(1)}, bf16[2,64,512]{2,1,0:T(8,128)(2,1)S(1)}, u32[]{:S(2)}, u32[]{:S(2)}) collective-permute-start(bf16[2,64,512]{2,1,0:T(8,128)(2,1)S(1)} %get-tuple-element.122), channel_id=1, source_target_pairs={{0,4},{1,5},{2,6},{3,7},{4,0},{5,1},{6,2},{7,3},{8,12},{9,13},{10,... | collective-permute-start | bytes 393224 | tf_op jit(solution)/shard_map/ppermute | solution.py:435
  63.3 2.9 %collective-permute-done.11.refs_1_ = bf16[2,64,512]{2,1,0:T(8,128)(2,1)S(1)} collective-permute-done((bf16[2,64,512]{2,1,0:T(8,128)(2,1)S(1)}, bf16[2,64,512]{2,1,0:T(8,128)(2,1)S(1)}, u32[]{:S(2)}, u32[]{:S(2)}) %collective-permute-start.11) | collective-permute-done | bytes 131104 | tf_op jit(solution)/shard_map/ppermute | solution.py:435
  66.4 2.1 %collective-permute-start.13 = (bf16[2,64,512]{2,1,0:T(8,128)(2,1)S(1)}, bf16[2,64,512]{2,1,0:T(8,128)(2,1)S(1)}, u32[]{:S(2)}, u32[]{:S(2)}) collective-permute-start(bf16[2,64,512]{2,1,0:T(8,128)(2,1)S(1)} %get-tuple-element.128), channel_id=1, source_target_pairs={{0,4},{1,5},{2,6},{3,7},{4,0},{5,1},{6,2},{7,3},{8,12},{9,13},{10,... | collective-permute-start | bytes 393224 | tf_op jit(solution)/shard_map/ppermute | solution.py:435
  68.5 2.4 %collective-permute-start.16 = (bf16[1,96,512]{2,1,0:T(8,128)(2,1)S(1)}, bf16[1,96,512]{2,1,0:T(8,128)(2,1)S(1)}, u32[]{:S(2)}, u32[]{:S(2)}) collective-permute-start(bf16[1,96,512]{2,1,0:T(8,128)(2,1)S(1)} %get-tuple-element.119), channel_id=1, source_target_pairs={{0,8},{1,9},{2,10},{3,11},{4,12},{5,13},{6,14},{7,15},{8,0},{9,1},... | collective-permute-start | bytes 294920 | tf_op jit(solution)/shard_map/ppermute | solution.py:435
  70.8 1.3 %collective-permute-start.7 = (bf16[64,512]{1,0:T(8,128)(2,1)S(1)}, bf16[64,512]{1,0:T(8,128)(2,1)S(1)}, u32[]{:S(2)}, u32[]{:S(2)}) collective-permute-start(bf16[64,512]{1,0:T(8,128)(2,1)S(1)} %get-tuple-element.114), channel_id=1, source_target_pairs={{0,1},{1,2},{2,3},{3,4},{4,5},{5,6},{6,7},{7,8},{8,9},{9,10},{10,1... | collective-permute-start | bytes 196616 | tf_op jit(solution)/shard_map/ppermute | solution.py:617
  72.1 1.3 %collective-permute-start.8 = (bf16[64,512]{1,0:T(8,128)(2,1)S(1)}, bf16[64,512]{1,0:T(8,128)(2,1)S(1)}, u32[]{:S(2)}, u32[]{:S(2)}) collective-permute-start(bf16[64,512]{1,0:T(8,128)(2,1)S(1)} %get-tuple-element.115), channel_id=1, source_target_pairs={{1,0},{2,1},{3,2},{4,3},{5,4},{6,5},{7,6},{8,7},{9,8},{10,9},{11,1... | collective-permute-start | bytes 196616 | tf_op jit(solution)/shard_map/ppermute | solution.py:616
  73.4 4.5 %collective-permute-start.14 = (bf16[1,64,512]{2,1,0:T(8,128)(2,1)S(1)}, bf16[1,64,512]{2,1,0:T(8,128)(2,1)S(1)}, u32[]{:S(2)}, u32[]{:S(2)}) collective-permute-start(bf16[1,64,512]{2,1,0:T(8,128)(2,1)S(1)} %get-tuple-element.125), channel_id=1, source_target_pairs={{0,8},{1,9},{2,10},{3,11},{4,12},{5,13},{6,14},{7,15},{8,0},{9,1},... | collective-permute-start | bytes 196616 | tf_op jit(solution)/shard_map/ppermute | solution.py:435
  78.1 10.7 %all_to_all.10.far_ref = bf16[16,2,512]{2,1,0:T(2,128)(2,1)S(1)} all-to-all(bf16[16,2,512]{2,1,0:T(2,128)(2,1)S(1)} %get-tuple-element.116), channel_id=1, replica_groups=mesh['groups'=2,'tiles'=16] {'tiles'}, dimensions={0} | all-to-all | bytes 65536 | tf_op jit(solution)/shard_map/all_to_all | solution.py:618
  (43 shorter events, 6.9 us)
Async XLA Ops:
  2.5 17.2 %all-to-all-start = ((bf16[16,2,512]{2,1,0:T(2,128)(2,1)}), bf16[16,2,512]{2,1,0:T(2,128)(2,1)S(1)}, u32[]{:S(2)}, u32[]{:S(2)}) async-start(bf16[16,2,512]{2,1,0:T(2,128)(2,1)} %get-tuple-element.71), calls=%async_computation | async-start | bytes 65536 | tf_op jit(solution)/shard_map/all_to_all | solution.py:509
  9.8 9.8 %collective-permute-start = (bf16[64,512]{1,0:T(8,128)(2,1)S(1)}, bf16[64,512]{1,0:T(8,128)(2,1)S(1)}, u32[]{:S(2)}, u32[]{:S(2)}) collective-permute-start(bf16[64,512]{1,0:T(8,128)(2,1)S(1)} %get-tuple-element.74), channel_id=1, source_target_pairs={{0,1},{1,2},{2,3},{3,4},{4,5},{5,6},{6,7},{7,8},{8,9},{9,10},{10,1... | collective-permute-start | bytes 196616 | tf_op jit(solution)/shard_map/ppermute | solution.py:507
  12.2 7.5 %collective-permute-start.1 = (bf16[64,512]{1,0:T(8,128)(2,1)S(1)}, bf16[64,512]{1,0:T(8,128)(2,1)S(1)}, u32[]{:S(2)}, u32[]{:S(2)}) collective-permute-start(bf16[64,512]{1,0:T(8,128)(2,1)S(1)} %get-tuple-element.75), channel_id=1, source_target_pairs={{1,0},{2,1},{3,2},{4,3},{5,4},{6,5},{7,6},{8,7},{9,8},{10,9},{11,1... | collective-permute-start | bytes 196616 | tf_op jit(solution)/shard_map/ppermute | solution.py:508
  17.3 1.6 %copy-start.1 = (f32[1536,512]{1,0:T(8,128)}, f32[1536,512]{1,0:T(8,128)S(1)}, u32[]{:S(2)}) copy-start(f32[1536,512]{1,0:T(8,128)S(1)} %get-tuple-element.76.partial_ref) | copy-start | bytes 9437188
  19.0 0.7 copy-start.3
  19.7 1.9 %copy-start.2 = (f32[1536,512]{1,0:T(8,128)S(1)}, f32[1536,512]{1,0:T(8,128)}, u32[]{:S(2)}) copy-start(f32[1536,512]{1,0:T(8,128)} %copy-done.1) | copy-start | bytes 9437188
  21.6 0.9 %copy-start.4 = (bf16[256,512]{1,0:T(8,128)(2,1)S(1)}, bf16[256,512]{1,0:T(8,128)(2,1)}, u32[]{:S(2)}) copy-start(bf16[256,512]{1,0:T(8,128)(2,1)} %copy-done.3) | copy-start | bytes 786436
  30.5 7.1 %collective-permute-start.2 = (bf16[8,96,512]{2,1,0:T(8,128)(2,1)S(1)}, bf16[8,96,512]{2,1,0:T(8,128)(2,1)S(1)}, u32[]{:S(2)}, u32[]{:S(2)}) collective-permute-start(bf16[8,96,512]{2,1,0:T(8,128)(2,1)S(1)} %get-tuple-element.89), channel_id=1, source_target_pairs={{0,1},{1,0},{2,3},{3,2},{4,5},{5,4},{6,7},{7,6},{8,9},{9,8},{10,11... | collective-permute-start | bytes 2359304 | tf_op jit(solution)/shard_map/ppermute | solution.py:435
  37.6 1.0 %copy-start.5 = (bf16[256,512]{1,0:T(8,128)(2,1)S(1)}, bf16[256,512]{1,0:T(8,128)(2,1)}, u32[]{:S(2)}) copy-start(bf16[256,512]{1,0:T(8,128)(2,1)} %copy-done.3) | copy-start | bytes 786436
  42.3 4.6 %collective-permute-start.3 = (bf16[8,64,512]{2,1,0:T(8,128)(2,1)S(1)}, bf16[8,64,512]{2,1,0:T(8,128)(2,1)S(1)}, u32[]{:S(2)}, u32[]{:S(2)}) collective-permute-start(bf16[8,64,512]{2,1,0:T(8,128)(2,1)S(1)} %get-tuple-element.105), channel_id=1, source_target_pairs={{0,1},{1,0},{2,3},{3,2},{4,5},{5,4},{6,7},{7,6},{8,9},{9,8},{10,11... | collective-permute-start | bytes 1572872 | tf_op jit(solution)/shard_map/ppermute | solution.py:435
  42.4 12.0 %collective-permute-start.6 = (bf16[4,96,512]{2,1,0:T(8,128)(2,1)S(1)}, bf16[4,96,512]{2,1,0:T(8,128)(2,1)S(1)}, u32[]{:S(2)}, u32[]{:S(2)}) collective-permute-start(bf16[4,96,512]{2,1,0:T(8,128)(2,1)S(1)} %get-tuple-element.90), channel_id=1, source_target_pairs={{0,2},{1,3},{2,0},{3,1},{4,6},{5,7},{6,4},{7,5},{8,10},{9,11},{10,... | collective-permute-start | bytes 1179656 | tf_op jit(solution)/shard_map/ppermute | solution.py:435
  44.5 2.6 %collective-permute-start.5 = (bf16[8,32,512]{2,1,0:T(8,128)(2,1)S(1)}, bf16[8,32,512]{2,1,0:T(8,128)(2,1)S(1)}, u32[]{:S(2)}, u32[]{:S(2)}) collective-permute-start(bf16[8,32,512]{2,1,0:T(8,128)(2,1)S(1)} %get-tuple-element.110), channel_id=1, source_target_pairs={{0,1},{1,0},{2,3},{3,2},{4,5},{5,4},{6,7},{7,6},{8,9},{9,8},{10,11... | collective-permute-start | bytes 786440 | tf_op jit(solution)/shard_map/ppermute | solution.py:435
  44.5 2.6 %collective-permute-start.4 = (bf16[8,32,512]{2,1,0:T(8,128)(2,1)S(1)}, bf16[8,32,512]{2,1,0:T(8,128)(2,1)S(1)}, u32[]{:S(2)}, u32[]{:S(2)}) collective-permute-start(bf16[8,32,512]{2,1,0:T(8,128)(2,1)S(1)} %get-tuple-element.109), channel_id=1, source_target_pairs={{0,1},{1,0},{2,3},{3,2},{4,5},{5,4},{6,7},{7,6},{8,9},{9,8},{10,11... | collective-permute-start | bytes 786440 | tf_op jit(solution)/shard_map/ppermute | solution.py:435
  47.0 14.2 %collective-permute-start.10 = (bf16[4,64,512]{2,1,0:T(8,128)(2,1)S(1)}, bf16[4,64,512]{2,1,0:T(8,128)(2,1)S(1)}, u32[]{:S(2)}, u32[]{:S(2)}) collective-permute-start(bf16[4,64,512]{2,1,0:T(8,128)(2,1)S(1)} %get-tuple-element.106), channel_id=1, source_target_pairs={{0,2},{1,3},{2,0},{3,1},{4,6},{5,7},{6,4},{7,5},{8,10},{9,11},{10,... | collective-permute-start | bytes 786440 | tf_op jit(solution)/shard_map/ppermute | solution.py:435
  54.5 34.3 %copy-start = (s32[1,16,2]{1,2,0:T(2,128)S(1)}, s32[1,16,2]{1,2,0:T(2,128)}, u32[]{:S(2)}) copy-start(s32[1,16,2]{1,2,0:T(2,128)} %param.32) | copy-start | bytes 388
  54.5 6.6 %collective-permute-start.9 = (bf16[2,96,512]{2,1,0:T(8,128)(2,1)S(1)}, bf16[2,96,512]{2,1,0:T(8,128)(2,1)S(1)}, u32[]{:S(2)}, u32[]{:S(2)}) collective-permute-start(bf16[2,96,512]{2,1,0:T(8,128)(2,1)S(1)} %get-tuple-element.113), channel_id=1, source_target_pairs={{0,4},{1,5},{2,6},{3,7},{4,0},{5,1},{6,2},{7,3},{8,12},{9,13},{10,... | collective-permute-start | bytes 589832 | tf_op jit(solution)/shard_map/ppermute | solution.py:435
  57.5 8.8 %collective-permute-start.12 = (bf16[4,64,512]{2,1,0:T(8,128)(2,1)S(1)}, bf16[4,64,512]{2,1,0:T(8,128)(2,1)S(1)}, u32[]{:S(2)}, u32[]{:S(2)}) collective-permute-start(bf16[4,64,512]{2,1,0:T(8,128)(2,1)S(1)} %get-tuple-element.111), channel_id=1, source_target_pairs={{0,2},{1,3},{2,0},{3,1},{4,6},{5,7},{6,4},{7,5},{8,10},{9,11},{10,... | collective-permute-start | bytes 786440 | tf_op jit(solution)/shard_map/ppermute | solution.py:435
  61.3 5.0 %collective-permute-start.11 = (bf16[2,64,512]{2,1,0:T(8,128)(2,1)S(1)}, bf16[2,64,512]{2,1,0:T(8,128)(2,1)S(1)}, u32[]{:S(2)}, u32[]{:S(2)}) collective-permute-start(bf16[2,64,512]{2,1,0:T(8,128)(2,1)S(1)} %get-tuple-element.122), channel_id=1, source_target_pairs={{0,4},{1,5},{2,6},{3,7},{4,0},{5,1},{6,2},{7,3},{8,12},{9,13},{10,... | collective-permute-start | bytes 393224 | tf_op jit(solution)/shard_map/ppermute | solution.py:435
  66.4 11.5 %collective-permute-start.13 = (bf16[2,64,512]{2,1,0:T(8,128)(2,1)S(1)}, bf16[2,64,512]{2,1,0:T(8,128)(2,1)S(1)}, u32[]{:S(2)}, u32[]{:S(2)}) collective-permute-start(bf16[2,64,512]{2,1,0:T(8,128)(2,1)S(1)} %get-tuple-element.128), channel_id=1, source_target_pairs={{0,4},{1,5},{2,6},{3,7},{4,0},{5,1},{6,2},{7,3},{8,12},{9,13},{10,... | collective-permute-start | bytes 393224 | tf_op jit(solution)/shard_map/ppermute | solution.py:435
  68.5 21.4 %collective-permute-start.16 = (bf16[1,96,512]{2,1,0:T(8,128)(2,1)S(1)}, bf16[1,96,512]{2,1,0:T(8,128)(2,1)S(1)}, u32[]{:S(2)}, u32[]{:S(2)}) collective-permute-start(bf16[1,96,512]{2,1,0:T(8,128)(2,1)S(1)} %get-tuple-element.119), channel_id=1, source_target_pairs={{0,8},{1,9},{2,10},{3,11},{4,12},{5,13},{6,14},{7,15},{8,0},{9,1},... | collective-permute-start | bytes 294920 | tf_op jit(solution)/shard_map/ppermute | solution.py:435
  70.8 17.9 %collective-permute-start.7 = (bf16[64,512]{1,0:T(8,128)(2,1)S(1)}, bf16[64,512]{1,0:T(8,128)(2,1)S(1)}, u32[]{:S(2)}, u32[]{:S(2)}) collective-permute-start(bf16[64,512]{1,0:T(8,128)(2,1)S(1)} %get-tuple-element.114), channel_id=1, source_target_pairs={{0,1},{1,2},{2,3},{3,4},{4,5},{5,6},{6,7},{7,8},{8,9},{9,10},{10,1... | collective-permute-start | bytes 196616 | tf_op jit(solution)/shard_map/ppermute | solution.py:617
  72.1 16.7 %collective-permute-start.8 = (bf16[64,512]{1,0:T(8,128)(2,1)S(1)}, bf16[64,512]{1,0:T(8,128)(2,1)S(1)}, u32[]{:S(2)}, u32[]{:S(2)}) collective-permute-start(bf16[64,512]{1,0:T(8,128)(2,1)S(1)} %get-tuple-element.115), channel_id=1, source_target_pairs={{1,0},{2,1},{3,2},{4,3},{5,4},{6,5},{7,6},{8,7},{9,8},{10,9},{11,1... | collective-permute-start | bytes 196616 | tf_op jit(solution)/shard_map/ppermute | solution.py:616
  73.4 17.1 %collective-permute-start.14 = (bf16[1,64,512]{2,1,0:T(8,128)(2,1)S(1)}, bf16[1,64,512]{2,1,0:T(8,128)(2,1)S(1)}, u32[]{:S(2)}, u32[]{:S(2)}) collective-permute-start(bf16[1,64,512]{2,1,0:T(8,128)(2,1)S(1)} %get-tuple-element.125), channel_id=1, source_target_pairs={{0,8},{1,9},{2,10},{3,11},{4,12},{5,13},{6,14},{7,15},{8,0},{9,1},... | collective-permute-start | bytes 196616 | tf_op jit(solution)/shard_map/ppermute | solution.py:435
  78.0 12.6 %collective-permute-start.15 = (bf16[1,64,512]{2,1,0:T(8,128)(2,1)S(1)}, bf16[1,64,512]{2,1,0:T(8,128)(2,1)S(1)}, u32[]{:S(2)}, u32[]{:S(2)}) collective-permute-start(bf16[1,64,512]{2,1,0:T(8,128)(2,1)S(1)} %get-tuple-element.130), channel_id=1, source_target_pairs={{0,8},{1,9},{2,10},{3,11},{4,12},{5,13},{6,14},{7,15},{8,0},{9,1},... | collective-permute-start | bytes 196616 | tf_op jit(solution)/shard_map/ppermute | solution.py:435

commit v5 on v4

--- a/solution.py
+++ b/solution.py
@@ -69,11 +69,12 @@
 
 
 def split_halves(bit, total_ref, at, block, first, rows, send_ref, keep_ref, offset):
-    half = send_ref.shape[0]
+    half, size = keep_ref.shape[:2]
     for q in range(half):
         there = pl.multiple_of(at + first + (2 * q + 1 - bit) * block, 32)
         here = pl.multiple_of(at + first + (2 * q + bit) * block, 32)
-        send_ref[q, offset : offset + rows, :] = total_ref[pl.ds(there, rows), :].astype(BF16)
+        to = q * size + offset
+        send_ref[to : to + rows, :] = total_ref[pl.ds(there, rows), :].astype(BF16)
         keep_ref[q, offset : offset + rows, :] = total_ref[pl.ds(here, rows), :]
 
 
@@ -93,57 +94,110 @@
     ]
 
 
-def outgoing_kernel(index_hbm, node_hbm, far_ref, head_ref, tail_ref, index_ref, node_ref, sems):
+def slot_owner(origin, shape, dim, places):
+    row = lax.broadcasted_iota(jnp.int32, shape, dim)
+    return lax.div(row, places) ^ origin, lax.rem(row, places)
+
+
+def bit_slots(bit, shape, places):
+    row = lax.broadcasted_iota(jnp.int32, shape, 0)
+    column = lax.broadcasted_iota(jnp.int32, shape, 1)
+    slot, place = lax.div(column, places), lax.rem(column, places)
+    rank = ((slot >> (bit + 1)) << bit) | (slot & (2**bit - 1))
+    return ((slot >> bit) & 1 == 1) & (rank * places + place == row)
+
+
+def slots_out(bit, slots, places):
+    rows = slots.shape[0]
+    return dot(ones_where(bit_slots(bit, (rows // 2, rows), places)), slots).astype(BF16)
+
+
+def slots_in(bit, slots, got, places):
+    rows = slots.shape[0]
+    row = lax.broadcasted_iota(jnp.int32, (rows, rows), 0)
+    column = lax.broadcasted_iota(jnp.int32, (rows, rows), 1)
+    kept = (row == column) & ((lax.div(column, places) >> bit) & 1 == 0)
+    moved = ones_where(bit_slots(bit, (rows // 2, rows), places))
+    return (dot(ones_where(kept), slots) + dot(moved, got, TN)).astype(BF16)
+
+
+def outgoing_kernel(
+    fast, index_hbm, node_hbm, slots_ref, send_ref, head_ref, tail_ref, index_ref, node_ref, sems
+):
     for copy in fetch([(index_hbm, index_ref), (node_hbm, node_ref)], sems):
         copy.wait()
     places, tiles = index_ref.shape[1], index_ref.shape[2]
-    nodes = node_ref.shape[0]
+    nodes, latent = node_ref.shape
+    origin = lax.axis_index("tiles") if fast else 0
     place = lax.broadcasted_iota(jnp.int32, (nodes, tiles), 0)
+    owner, at = slot_owner(origin, (places * tiles, tiles), 0, places)
+    column = lax.broadcasted_iota(jnp.int32, (places * tiles, tiles), 1)
+    slots = jnp.zeros((places * tiles, latent), F32)
     for j in range(places):
         picks = ones_where(place == index_ref[0, j : j + 1, :])
-        far_ref[:, j, :] = dot(picks, node_ref[...], TN).astype(BF16)
+        listed = dot(picks, node_ref[...], TN).astype(BF16)
+        slots += dot(ones_where((owner == column) & (at == j)), listed)
+    slots = slots.astype(BF16)
+    slots_ref[...] = slots
+    send_ref[...] = slots_out(0, slots, places) if fast else jnp.zeros_like(send_ref)
     head_ref[...] = node_ref[:NEAR, :]
     tail_ref[...] = node_ref[nodes - NEAR :, :]
 
 
-def table_index(raw, places, tiles, nodes):
+def shuffle_kernel(bit, places, slots_ref, got_ref, moved_ref, send_ref):
+    slots = slots_in(bit, slots_ref[...], got_ref[...], places)
+    moved_ref[...] = slots
+    send_ref[...] = slots_out(bit + 1, slots, places)
+
+
+def table_index(raw, origin, places, nodes):
     far = raw - (nodes + 2 * NEAR)
-    far = nodes + 2 * NEAR + lax.rem(far, places) * tiles + lax.div(far, places)
+    owner = lax.div(far, places) ^ origin
+    far = nodes + 2 * NEAR + owner * places + lax.rem(far, places)
     rim = jnp.where(raw < NEAR, raw + nodes, raw)
     own = jnp.where((raw >= NEAR) & (raw < NEAR + nodes), raw - NEAR, rim)
     return jnp.where(raw >= nodes + 2 * NEAR, far, own)
 
 
-def prepare_kernel(
-    tiles, places,
-    node_hbm, w1_hbm, sender_hbm, receiver_hbm, b1_hbm, edge_hbm,
-    edge_ref, w1_ref, node_ref, receiver_ref, moved_ref, partial_ref,
-    weights, sender_ref, b1_ref, sems, edge_sems,
+def weights_kernel(
+    places, fast,
+    node_hbm, w1_hbm, sender_hbm, receiver_hbm,
+    w1_ref, node_ref, receiver_ref, moved_ref, weights,
+    sender_ref, sems,
 ):
-    edges, latent = edge_ref.shape
+    latent = node_ref.shape[1]
     nodes = node_ref.shape[0]
     copies = fetch(
         [
             (node_hbm, node_ref), (w1_hbm, w1_ref), (sender_hbm, sender_ref),
-            (receiver_hbm, receiver_ref), (b1_hbm, b1_ref),
+            (receiver_hbm, receiver_ref),
         ],
         sems,
     )
-    edge_copies = fetch(tile_pairs(edge_hbm, edge_ref, edges // 2), edge_sems)
     for copy in copies:
         copy.wait()
-    moved_ref[...] = table_index(sender_ref[...], places, tiles, nodes)
+    origin = lax.axis_index("tiles") if fast else 0
+    moved_ref[...] = table_index(sender_ref[...], origin, places, nodes)
     weights[:latent, :] = w1_ref[:latent, :]
     weights[latent : latent + nodes, :] = dot(
         node_ref[...], w1_ref[latent : 2 * latent, :]
     ).astype(BF16)
     weights[latent + nodes :, :] = dot(node_ref[...], w1_ref[2 * latent :, :]).astype(BF16)
-    for copy in edge_copies:
+
+
+def prepare_kernel(
+    first, b1_hbm, edge_hbm, moved_ref, receiver_ref, weights, edge_ref, partial_ref,
+    b1_ref, sems,
+):
+    edges, latent = edge_ref.shape
+    nodes = weights.shape[0] - latent >> 1
+    start = pl.ds(first * TILE, edges)
+    for copy in fetch([(b1_hbm, b1_ref), (edge_hbm.at[start], edge_ref)], sems):
         copy.wait()
     for step in range(edges // TILE):
         tile = slice(step * TILE, (step + 1) * TILE)
-        senders = pick_columns(index_columns(moved_ref, step, TILE), 0, nodes)
-        receivers = pick_columns(index_columns(receiver_ref, step, TILE), 0, nodes)
+        senders = pick_columns(index_columns(moved_ref, first + step, TILE), 0, nodes)
+        receivers = pick_columns(index_columns(receiver_ref, first + step, TILE), 0, nodes)
         inputs = jnp.concatenate([edge_ref[tile, :]] + senders + receivers, axis=1)
         partial_ref[tile, :] = dot(inputs, weights[...]) + b1_ref[...]
 
@@ -152,7 +206,8 @@
     tiles, places, fast,
     w2_hbm, nw1_hbm, nw2_hbm, ncot_hbm,
     b2_hbm, gain_hbm, nb1_hbm, nb2_hbm, ngain_hbm, count_hbm,
-    lower_ref, upper_ref, far_ref, partial_ref, w1_ref, node_ref, receiver_ref, moved_ref,
+    lower_ref, upper_ref, slots_ref, got_ref, early_ref, later_ref,
+    w1_ref, node_ref, receiver_ref, moved_ref,
     w2_ref, gain_ref,
     hidden_ref, slope_ref, normed_ref, inverse_ref, table_ref, dsum_ref, base_ref,
     gsend_ref, gkeep_ref,
@@ -179,9 +234,10 @@
     table_ref[:nodes, :] = node_ref[...]
     table_ref[nodes : nodes + NEAR, :] = lower_ref[...]
     table_ref[nodes + NEAR : nodes + 2 * NEAR, :] = upper_ref[...]
-    for j in range(places):
-        at = nodes + 2 * NEAR + j * tiles
-        table_ref[at : at + tiles, :] = far_ref[:, j, :]
+    slots = slots_ref[...]
+    if fast:
+        slots = slots_in(3, slots, got_ref[...], places)
+    table_ref[nodes + 2 * NEAR : nodes + 2 * NEAR + places * tiles, :] = slots
     used = nodes + 2 * NEAR + places * tiles
     if used < rows:
         table_ref[used:, :] = jnp.zeros((rows - used, latent), BF16)
@@ -193,7 +249,12 @@
     def activate(step):
         tile = slice(step * TILE, (step + 1) * TILE)
         senders = pick_columns(index_columns(moved_ref, step, TILE), nodes, rows)
-        preact = partial_ref[tile, :] + dot(jnp.concatenate(senders, axis=1), weights[...])
+        part = early_ref.shape[0]
+        if step * TILE < part:
+            known = early_ref[tile, :]
+        else:
+            known = later_ref[step * TILE - part : (step + 1) * TILE - part, :]
+        preact = known + dot(jnp.concatenate(senders, axis=1), weights[...])
         sig = sigmoid(preact)
         slope_ref[tile, :] = (sig * (1.0 + preact * (1.0 - sig))).astype(BF16)
         hidden_ref[tile, :] = (preact * sig).astype(BF16)
@@ -295,20 +356,25 @@
 
 def first_kernel(
     tiles, places, fast,
-    dpre_ref, edge_ref, sender_ref, receiver_ref, table_ref, node_ref, w1_ref, base_ref,
+    dpre_ref, early_ref, later_ref, sender_ref, receiver_ref, table_ref, node_ref, w1_ref, base_ref,
     *refs,
 ):
     out_refs, (grads, sums) = refs[:-2], refs[-2:]
     lower_ref, upper_ref, far_ref, partial_ref = out_refs[:4]
     here = lax.axis_index("tiles")
-    edges, latent = edge_ref.shape
+    edges, latent = dpre_ref.shape
     nodes = node_ref.shape[0]
     rows = table_ref.shape[0]
+    early = early_ref.shape[0]
 
     for step in range(edges // TILE):
         tile = slice(step * TILE, (step + 1) * TILE)
         dpre = dpre_ref[tile, :]
-        part = dot(edge_ref[tile, :], dpre, TN)
+        if step * TILE < early:
+            edge = early_ref[tile, :]
+        else:
+            edge = later_ref[step * TILE - early : (step + 1) * TILE - early, :]
+        part = dot(edge, dpre, TN)
         picks = jnp.concatenate(
             [
                 pick_rows(sender_ref, step, TILE, rows),
@@ -328,22 +394,22 @@
     by_receiver = sums[rows:, :].astype(BF16)
     grads[latent : 2 * latent, :] = dot(table_ref[...], by_sender, TN)
     grads[2 * latent :, :] = dot(node_ref[...], by_receiver, TN)
+    back = dot(by_sender, w1_ref[latent : 2 * latent, :], NT)
+    far = back[nodes + 2 * NEAR : nodes + 2 * NEAR + places * tiles, :].astype(BF16)
+    far_ref[...] = far
     if fast:
         bit = lax.rem(here, 2)
         block = 3 * latent // tiles
         at = 0
         for send_ref, keep_ref in (out_refs[4:6], out_refs[6:8]):
-            part = send_ref.shape[1]
+            part = keep_ref.shape[1]
             split_halves(bit, grads, 0, block, at, part, send_ref, keep_ref, 0)
             at += part
+        out_refs[4][tiles // 2 * out_refs[5].shape[1] :, :] = slots_out(0, far, places)
     else:
         out_refs[4][...] = grads[...]
-    back = dot(by_sender, w1_ref[latent : 2 * latent, :], NT)
     lower_ref[...] = back[nodes : nodes + NEAR, :].astype(BF16)
     upper_ref[...] = back[nodes + NEAR : nodes + 2 * NEAR, :].astype(BF16)
-    for j in range(places):
-        at = 2 * NEAR + nodes + j * tiles
-        far_ref[:, j, :] = back[at : at + tiles, :].astype(BF16)
     partial_ref[...] = (
         base_ref[...] + back[:nodes, :] + dot(by_receiver, w1_ref[2 * latent :, :], NT)
     )
@@ -364,14 +430,23 @@
         copy.wait()
 
 
-def node_kernel(index_ref, partial_ref, below_ref, above_ref, far_ref, out_ref):
+def node_kernel(fast, index_ref, partial_ref, below_ref, above_ref, slots_ref, *refs):
+    out_ref = refs[-1]
     places, tiles = index_ref.shape[1], index_ref.shape[2]
     nodes = partial_ref.shape[0]
+    origin = lax.axis_index("tiles") if fast else 0
+    slots = slots_ref[...]
+    if fast:
+        got_ref = refs[0]
+        slots = slots_in(3, slots, got_ref[got_ref.shape[0] - slots.shape[0] // 2 :, :], places)
     place = lax.broadcasted_iota(jnp.int32, (nodes, tiles), 0)
+    owner, at = slot_owner(origin, (tiles, places * tiles), 1, places)
+    row = lax.broadcasted_iota(jnp.int32, (tiles, places * tiles), 0)
     total = partial_ref[...]
     for j in range(places):
         picks = ones_where(place == index_ref[0, j : j + 1, :])
-        total = total + dot(picks, far_ref[:, j, :])
+        far = dot(ones_where((owner == row) & (at == j)), slots).astype(BF16)
+        total = total + dot(picks, far)
     out_ref[:NEAR, :] = (total[:NEAR, :] + below_ref[...].astype(F32)).astype(BF16)
     out_ref[NEAR : nodes - NEAR, :] = total[NEAR : nodes - NEAR, :].astype(BF16)
     out_ref[nodes - NEAR :, :] = (
@@ -379,20 +454,30 @@
     ).astype(BF16)
 
 
-def halve_kernel(shift, count, *refs):
+def halve_kernel(shift, count, places, *refs):
     keeps, gots = refs[:count], refs[count : 2 * count]
-    send_ref, kept_ref = refs[2 * count :]
+    rest = refs[2 * count :]
+    send_ref, kept_ref = rest[-2:] if not places else rest[-3:-1]
+    size = kept_ref.shape[1]
     bit = lax.rem(lax.div(lax.axis_index("tiles"), 2**shift), 2)
     at = 0
     for keep_ref, got_ref in zip(keeps, gots):
-        rows = keep_ref.shape[1]
-        for q in range(keep_ref.shape[0] // 2):
+        blocks, rows = keep_ref.shape[:2]
+        for q in range(blocks // 2):
             there, here = 2 * q + 1 - bit, 2 * q + bit
-            send_ref[q, at : at + rows, :] = (
-                keep_ref[there] + got_ref[there].astype(F32)
-            ).astype(BF16)
-            kept_ref[q, at : at + rows, :] = keep_ref[here] + got_ref[here].astype(F32)
+            got_there = got_ref[pl.ds(pl.multiple_of(there * rows, 32), rows), :].astype(F32)
+            got_here = got_ref[pl.ds(pl.multiple_of(here * rows, 32), rows), :].astype(F32)
+            to = q * size + at
+            send_ref[to : to + rows, :] = (keep_ref[there] + got_there).astype(BF16)
+            kept_ref[q, at : at + rows, :] = keep_ref[here] + got_here
         at += rows
+    if places:
+        slots_ref, moved_ref = rest[0], rest[-1]
+        half = slots_ref.shape[0] // 2
+        got_ref = gots[0]
+        slots = slots_in(shift - 1, slots_ref[...], got_ref[got_ref.shape[0] - half :, :], places)
+        moved_ref[...] = slots
+        send_ref[send_ref.shape[0] - half :, :] = slots_out(shift, slots, places)
 
 
 def finish_kernel(count, splits, *refs):
@@ -402,9 +487,9 @@
         at = 0
         for which, size in parts:
             first = rows[which]
-            out_refs[which][first : first + size, :] = keep_ref[0, at : at + size, :] + got_ref[
-                0, at : at + size, :
-            ].astype(F32)
+            out_refs[which][first : first + size, :] = (
+                keep_ref[0, at : at + size, :] + got_ref[at : at + size, :].astype(F32)
+            )
             at += size
             rows[which] += size
 
@@ -417,7 +502,7 @@
     return [pltpu.with_memory_space_constraint(array, pltpu.HBM) for array in arrays]
 
 
-def call(kernel, name, out_shape, args, hbm=0, scratch=(), out_specs=None, flops=0, limit=16):
+def call(kernel, name, out_shape, args, hbm=0, scratch=(), out_specs=None, limit=16):
     vmem = pl.BlockSpec(memory_space=pltpu.VMEM)
     return pl.pallas_call(
         kernel,
@@ -426,7 +511,6 @@
         out_shape=out_shape,
         scratch_shapes=scratch,
         compiler_params=pltpu.CompilerParams(vmem_limit_bytes=limit * MIB),
-        cost_estimate=pl.CostEstimate(flops=flops, bytes_accessed=flops // 400, transcendentals=0),
         name=name,
     )(*in_hbm(*args[:hbm]), *args[hbm:])
 
@@ -435,15 +519,17 @@
     return lax.ppermute(send, "tiles", [(i, i ^ bit) for i in range(tiles)])
 
 
-def halve(shift, keeps, gots):
+def halve(shift, keeps, gots, slots=None, places=0):
     half, _, width = keeps[0].shape
     rows = sum(keep.shape[1] for keep in keeps)
-    shape = (half // 2, rows, width)
+    extra = [] if slots is None else [slots]
+    sent = half // 2 * rows + sum(slots.shape[0] // 2 for slots in extra)
     return call(
-        functools.partial(halve_kernel, shift, len(keeps)),
+        functools.partial(halve_kernel, shift, len(keeps), places),
         "halve",
-        [pltpu.VMEM(shape, BF16), pltpu.VMEM(shape, F32)],
-        [*keeps, *gots],
+        [pltpu.VMEM((sent, width), BF16), pltpu.VMEM((half // 2, rows, width), F32)]
+        + [pltpu.VMEM(slots.shape, BF16) for slots in extra],
+        [*keeps, *gots, *extra],
     )
 
 
@@ -482,23 +568,23 @@
     listed = jnp.swapaxes(send_index, 1, 2)
     row = lambda vector: vector.reshape(1, -1)
     vmem = pltpu.VMEM
-    unit = 2 * edges * latent * latent
 
     if fast:
         grad_shapes = lambda count: [
-            vmem((half, count // tiles, latent), BF16),
+            vmem((count // 2, latent), BF16),
             vmem((half, count // tiles, latent), F32),
         ]
     else:
         grad_shapes = lambda count: [shaped((latent, latent), F32), shaped((count, latent), F32)]
 
-    outgoing, head, tail = call(
-        outgoing_kernel,
+    outgoing, send, head, tail = call(
+        functools.partial(outgoing_kernel, fast),
         "outgoing",
         [
-            shaped((tiles, places, latent), BF16),
-            shaped((NEAR, latent), BF16),
-            shaped((NEAR, latent), BF16),
+            vmem((tiles * places, latent), BF16) if fast else shaped((tiles * places, latent), BF16),
+            vmem((tiles * places // 2, latent), BF16),
+            vmem((NEAR, latent), BF16),
+            vmem((NEAR, latent), BF16),
         ],
         [listed, node_latent],
         hbm=2,
@@ -506,24 +592,52 @@
     )
     lower = lax.ppermute(tail, "tiles", upward)
     upper = lax.ppermute(head, "tiles", downward)
-    incoming = lax.all_to_all(outgoing, "tiles", split_axis=0, concat_axis=0, tiled=True)
-
-    edge_kept, w1_kept, node_kept, receiver_kept, moved, preact = call(
-        functools.partial(prepare_kernel, tiles, places),
-        "prepare",
+    w1_kept, node_kept, receiver_kept, moved, weights = call(
+        functools.partial(weights_kernel, places, fast),
+        "weights",
         [
-            vmem((edges, latent), BF16), vmem(edge_w1.shape, BF16), vmem((nodes, latent), BF16),
+            vmem(edge_w1.shape, BF16), vmem((nodes, latent), BF16),
             vmem(receiver.shape, jnp.int32), vmem(sender.shape, jnp.int32),
-            vmem((edges, latent), F32),
+            vmem((latent + 2 * nodes, latent), BF16),
         ],
-        [node_latent, edge_w1, after(sender, outgoing), receiver, row(edge_b1), edge_latent],
-        hbm=6,
-        scratch=[
-            vmem((latent + 2 * nodes, latent), BF16), vmem(sender.shape, jnp.int32),
-            vmem((1, latent), F32), pltpu.SemaphoreType.DMA((5,)), pltpu.SemaphoreType.DMA((2,)),
-        ],
-        flops=3 * unit,
-    )
+        [node_latent, edge_w1, after(sender, send), receiver],
+        hbm=4,
+        scratch=[vmem(sender.shape, jnp.int32), pltpu.SemaphoreType.DMA((4,))],
+    )
+
+    def prepare(first, moved):
+        return call(
+            functools.partial(prepare_kernel, first),
+            "prepare",
+            [vmem((edges // 2, latent), BF16), vmem((edges // 2, latent), F32)],
+            [row(edge_b1), edge_latent, moved, receiver_kept, weights],
+            hbm=2,
+            scratch=[vmem((1, latent), F32), pltpu.SemaphoreType.DMA((2,))],
+        )
+
+    def shuffle(bit, slots, got):
+        return call(
+            functools.partial(shuffle_kernel, bit, places),
+            "shuffle",
+            [vmem(slots.shape, BF16), vmem(got.shape, BF16)],
+            [slots, got],
+        )
+
+    if fast:
+        got = swap(tiles, 1, send)
+        slots, send = shuffle(0, after(outgoing, moved), got)
+        got = swap(tiles, 2, send)
+        edge_early, early = prepare(0, after(moved, send))
+        slots, send = shuffle(1, after(slots, early), got)
+        got = swap(tiles, 4, send)
+        edge_later, later = prepare(steps // 2, after(moved, send))
+        slots, send = shuffle(2, after(slots, later), got)
+        got = swap(tiles, 8, send)
+    else:
+        edge_early, early = prepare(0, moved)
+        edge_later, later = prepare(steps // 2, moved)
+        slots = lax.all_to_all(outgoing, "tiles", split_axis=0, concat_axis=0, tiled=True)
+        got = slots
 
     (
         w2_kept, gain_kept,
@@ -540,7 +654,7 @@
         [
             edge_w2, node_w1, node_w2, node_cot,
             row(edge_b2), row(edge_gain), row(node_b1), row(node_b2), row(node_gain), edge_count,
-            lower, upper, incoming, preact, w1_kept, node_kept, receiver_kept, moved,
+            lower, upper, slots, got, early, later, w1_kept, node_kept, receiver_kept, moved,
         ],
         hbm=10,
         scratch=[
@@ -550,7 +664,6 @@
         ] + [vmem((1, latent), F32)] * 4 + [
             pltpu.SMEM(edge_count.shape, jnp.int32), pltpu.SemaphoreType.DMA((10,)),
         ],
-        flops=5 * unit,
     )
 
     cot_kept, dpre, second_send, second_keep = call(
@@ -562,7 +675,6 @@
         scratch=[
             vmem((latent, latent), F32), vmem((edges, latent), BF16), pltpu.SemaphoreType.DMA((2,)),
         ],
-        flops=3 * unit,
     )
     if fast:
         send, chain = halve(1, [node_keep], [swap(tiles, 1, node_send)])
@@ -577,18 +689,18 @@
         [
             vmem((NEAR, latent), BF16),
             vmem((NEAR, latent), BF16),
-            shaped((tiles, places, latent), BF16),
+            vmem((tiles * places, latent), BF16) if fast else shaped((tiles * places, latent), BF16),
             vmem((nodes, latent), F32),
         ] + (
             [
-                vmem((half, 2 * per, latent), BF16), vmem((half, 2 * per, latent), F32),
-                vmem((half, per, latent), BF16), vmem((half, per, latent), F32),
+                vmem((2 * half * per + tiles * places // 2, latent), BF16),
+                vmem((half, 2 * per, latent), F32),
+                vmem((half * per, latent), BF16), vmem((half, per, latent), F32),
             ]
             if fast else [shaped((3 * latent, latent), F32)]
         ),
-        [dpre, edge_kept, moved, receiver_kept, table, node_kept, w1_kept, base],
+        [dpre, edge_early, edge_later, moved, receiver_kept, table, node_kept, w1_kept, base],
         scratch=[vmem((3 * latent, latent), F32), vmem((rows + nodes, latent), F32)],
-        flops=4 * unit,
     )
 
     (grad_edge,) = call(
@@ -598,38 +710,32 @@
         [after(dpre, partial), cot_kept, w1_kept],
         out_specs=[pl.BlockSpec(memory_space=pltpu.HBM)],
         scratch=[vmem((edges, latent), BF16), pltpu.SemaphoreType.DMA((steps,))],
-        flops=2 * unit,
     )
 
     if fast:
         send_a, keep_a, send_b, keep_b = first
-        send_a, chain_a = halve(1, [after(keep_a, grad_edge)], [swap(tiles, 1, send_a)])
+        send_a, chain_a, slots = halve(
+            1, [after(keep_a, grad_edge)], [swap(tiles, 1, send_a)], to_far, places
+        )
         got_a = swap(tiles, 2, send_a)
         send_b, chain_b = halve(
             1, [after(keep_b, send_a), second_keep], [swap(tiles, 1, send_b), got_second]
         )
         got_b = swap(tiles, 2, send_b)
+        to_lower, to_upper = lax.optimization_barrier((to_lower, to_upper, send_b))[:2]
         send, chain = halve(2, [after(chain, send_b)], [got])
         got = swap(tiles, 4, send)
-        to_far, to_lower, to_upper = lax.optimization_barrier((to_far, to_lower, to_upper, send))[:3]
 
     above = lax.ppermute(to_lower, "tiles", downward)
     below = lax.ppermute(to_upper, "tiles", upward)
-    returned = lax.all_to_all(to_far, "tiles", split_axis=0, concat_axis=0, tiled=True)
-    (grad_node,) = call(
-        node_kernel,
-        "node",
-        [shaped((nodes, latent), BF16)],
-        [listed, partial, below, above, returned],
-    )
-
     if fast:
         send, chain = halve(3, [chain], [got])
         got = swap(tiles, 8, send)
-        send_a, chain_a = halve(2, [after(chain_a, send)], [got_a])
+        send_a, chain_a, slots = halve(2, [after(chain_a, send)], [got_a], slots, places)
         got_a = swap(tiles, 4, send_a)
-        send_a, chain_a = halve(3, [chain_a], [got_a])
+        send_a, chain_a, slots = halve(3, [chain_a], [got_a], slots, places)
         got_a = swap(tiles, 8, send_a)
+        returned = [slots, got_a]
         send_b, chain_b = halve(2, [after(chain_b, send_a)], [got_b])
         got_b = swap(tiles, 4, send_b)
         grad_node_w1, grad_node_w2 = finish(
@@ -641,11 +747,18 @@
             [chain_a, chain_b], [got_a, got_b], [[(0, 2 * per)], [(0, per), (1, per)]], [3 * per, per]
         )
     else:
+        returned = [lax.all_to_all(to_far, "tiles", split_axis=0, concat_axis=0, tiled=True)]
         scatter = functools.partial(
             lax.psum_scatter, axis_name="tiles", scatter_dimension=0, tiled=True
         )
         grad_node_w1, grad_node_w2 = scatter(node_keep), scatter(node_send)
         grad_edge_w1, grad_edge_w2 = scatter(first[0]), scatter(second_keep)
+    (grad_node,) = call(
+        functools.partial(node_kernel, fast),
+        "node",
+        [shaped((nodes, latent), BF16)],
+        [listed, partial, below, above, *returned],
+    )
     return (grad_node, grad_edge, grad_edge_w1, grad_edge_w2, grad_node_w1, grad_node_w2)
 
 

time: 91.7 us -> 85 us (0.927)
  blocking collectives: 10.7 us -> 0 us
  local copies, waits for them, and re-layouts: 5.9 us -> 0.01 us
  waiting for transfers between devices: 13.3 us -> 17.8 us
  Pallas kernels: 27.1 us -> 31.5 us
  starting transfers between devices: 33.4 us -> 34.6 us
    all_to_all x1 -> x0, blocking collectives: 10.7 us -> none  [shards(): lax.all_to_all(to_far, 'tiles', split_axis=0, concat_axis=0, tiled=True)]
    ppermute x13 -> x17, starting transfers between devices: 19.8 us -> 28.7 us  [swap(): return lax.ppermute(send, 'tiles', [(i, i ^ bit) for i in range(tiles)])]
    all_to_all x1 -> x0, starting transfers between devices: 7.37 us -> none  [shards(): lax.all_to_all(outgoing, 'tiles', split_axis=0, concat_axis=0, tiled=True)]
    unnamed x12 -> x2, local copies, waits for them, and re-layouts: 5.9 us -> 0.01 us
    ppermute x13 -> x17, waiting for transfers between devices: 13.3 us -> 17.8 us  [swap(): return lax.ppermute(send, 'tiles', [(i, i ^ bit) for i in range(tiles)])]
    pallas_call x18 -> x23, Pallas kernels: 27.1 us -> 31.5 us  [call(): pl.pallas_call(kernel, in_specs=[pl.BlockSpec(memory_space=pltpu.HBM)] *...]
  transfers between devices with their start and end apart: 18 -> 21, of which waited for: 3 -> 6; matrix products, arithmetic and copies ran while one was open for 0% -> 0% of each run, Pallas kernels for 14% -> 20%
where the time goes in v5:
time: 85 us; the launch traced here: 84.7 us
  starting transfers between devices  34.6 us (41%)
  Pallas kernels  31.5 us (37%)
  waiting for transfers between devices  17.8 us (21%)
    pallas_call x23, Pallas kernels, call(): pl.pallas_call(kernel, in_specs=[pl.BlockSpec(memory_space=pltpu.HBM)] *...  31.5 us
    ppermute x17, starting transfers between devices, swap(): return lax.ppermute(send, 'tiles', [(i, i ^ bit) for i in range(tiles)])  28.7 us
    ppermute x17, waiting for transfers between devices, swap(): return lax.ppermute(send, 'tiles', [(i, i ^ bit) for i in range(tiles)])  17.8 us
    ppermute x1, starting transfers between devices, shards(): lower = lax.ppermute(tail, 'tiles', upward)  1.95 us
  transfers between devices with their start and end apart: 21, of which 6 were waited for; matrix products, arithmetic and copies ran while one was open for 0% of the time, Pallas kernels for 20%

profile of v5, /device:TPU:0, one launch (start us, length us, event | category | flops | bytes accessed | tf_op | source)
XLA Modules:
  0.0 84.7 jit_solution(9486691776908445994)
XLA Ops:
  0.6 1.5 %outgoing.1 = (bf16[32,512]{1,0:T(8,128)(2,1)S(1)}, bf16[16,512]{1,0:T(8,128)(2,1)S(1)}, bf16[64,512]{1,0:T(8,128)(2,1)S(1)}, bf16[64,512]{1,0:T(8,128)(2,1)S(1)}) custom-call(s32[1,2,16]{2,1,0:T(2,128)} %bitcast.9, bf16[256,512]{1,0:T(8,128)(2,1)} %node_hbm.3), custom_call_target="tpu_custom_call" | custom-call | tf_op jit(solution)/shard_map/outgoing/pallas_call | solution.py:507
  2.6 2.0 %collective-permute-start = (bf16[64,512]{1,0:T(8,128)(2,1)S(1)}, bf16[64,512]{1,0:T(8,128)(2,1)S(1)}, u32[]{:S(2)}, u32[]{:S(2)}) collective-permute-start(bf16[64,512]{1,0:T(8,128)(2,1)S(1)} %get-tuple-element.91), channel_id=1, source_target_pairs={{0,1},{1,2},{2,3},{3,4},{4,5},{5,6},{6,7},{7,8},{8,9},{9,10},{10,1... | collective-permute-start | bytes 196616 | tf_op jit(solution)/shard_map/ppermute | solution.py:593
  5.9 2.0 %weights.1 = (bf16[1536,512]{1,0:T(8,128)(2,1)S(1)}, bf16[256,512]{1,0:T(8,128)(2,1)S(1)}, s32[12,128]{1,0:T(8,128)S(1)}, s32[12,128]{1,0:T(8,128)S(1)}, bf16[1024,512]{1,0:T(8,128)(2,1)S(1)}) custom-call(bf16[256,512]{1,0:T(8,128)(2,1)} %node_hbm.3, bf16[1536,512]{1,0:T(8,128)(2,1)} %w1_hbm.1, s32[12,128]{1,0:T(8,128)} %bitcast.11, s32[12,128]{1,0:T(8,128)} %bitcast.12), custom_call_target="tpu_custom_call" | custom-call | tf_op jit(solution)/shard_map/weights/pallas_call | solution.py:507
  8.2 4.8 %collective-permute-start.3 = (bf16[16,512]{1,0:T(8,128)(2,1)S(1)}, bf16[16,512]{1,0:T(8,128)(2,1)S(1)}, u32[]{:S(2)}, u32[]{:S(2)}) collective-permute-start(bf16[16,512]{1,0:T(8,128)(2,1)S(1)} %get-tuple-element.97), channel_id=1, source_target_pairs={{0,2},{1,3},{2,0},{3,1},{4,6},{5,7},{6,4},{7,5},{8,10},{9,11},{10,... | collective-permute-start | bytes 49160 | tf_op jit(solution)/shard_map/ppermute | solution.py:519
  13.1 2.2 %prepare.2 = (bf16[768,512]{1,0:T(8,128)(2,1)S(1)}, f32[768,512]{1,0:T(8,128)S(1)}) custom-call(f32[1,512]{1,0:T(1,128)} %bitcast.13, bf16[1536,512]{1,0:T(8,128)(2,1)} %edge_hbm.3, s32[12,128]{1,0:T(8,128)S(1)} %get-tuple-element.104.moved_ref.sender_ref, s32[12,128]{1,0:T(8,128)S(1)} %get-tuple-element.90.receiver_ref, ...), custom_call_target="tpu_custom_call" | custom-call | tf_op jit(solution)/shard_map/prepare/pallas_call | solution.py:507
  15.5 2.6 %collective-permute-start.4 = (bf16[16,512]{1,0:T(8,128)(2,1)S(1)}, bf16[16,512]{1,0:T(8,128)(2,1)S(1)}, u32[]{:S(2)}, u32[]{:S(2)}) collective-permute-start(bf16[16,512]{1,0:T(8,128)(2,1)S(1)} %get-tuple-element.103), channel_id=1, source_target_pairs={{0,4},{1,5},{2,6},{3,7},{4,0},{5,1},{6,2},{7,3},{8,12},{9,13},{10,... | collective-permute-start | bytes 49160 | tf_op jit(solution)/shard_map/ppermute | solution.py:519
  18.1 2.1 %prepare.3 = (bf16[768,512]{1,0:T(8,128)(2,1)S(1)}, f32[768,512]{1,0:T(8,128)S(1)}) custom-call(f32[1,512]{1,0:T(1,128)} %bitcast.14, bf16[1536,512]{1,0:T(8,128)(2,1)} %edge_hbm.3, s32[12,128]{1,0:T(8,128)S(1)} %get-tuple-element.104.moved_ref.sender_ref, s32[12,128]{1,0:T(8,128)S(1)} %get-tuple-element.90.receiver_ref, ...), custom_call_target="tpu_custom_call" | custom-call | tf_op jit(solution)/shard_map/prepare/pallas_call | solution.py:507
  20.6 2.6 %collective-permute-start.5 = (bf16[16,512]{1,0:T(8,128)(2,1)S(1)}, bf16[16,512]{1,0:T(8,128)(2,1)S(1)}, u32[]{:S(2)}, u32[]{:S(2)}) collective-permute-start(bf16[16,512]{1,0:T(8,128)(2,1)S(1)} %get-tuple-element.108), channel_id=1, source_target_pairs={{0,8},{1,9},{2,10},{3,11},{4,12},{5,13},{6,14},{7,15},{8,0},{9,1},... | collective-permute-start | bytes 49160 | tf_op jit(solution)/shard_map/ppermute | solution.py:519
  23.2 2.0 %collective-permute-done.5.got_ref = bf16[16,512]{1,0:T(8,128)(2,1)S(1)} collective-permute-done((bf16[16,512]{1,0:T(8,128)(2,1)S(1)}, bf16[16,512]{1,0:T(8,128)(2,1)S(1)}, u32[]{:S(2)}, u32[]{:S(2)}) %collective-permute-start.5) | collective-permute-done | bytes 16416 | tf_op jit(solution)/shard_map/ppermute | solution.py:519
  25.2 8.1 %forward.1 = (bf16[512,512]{1,0:T(8,128)(2,1)S(1)}, f32[1,512]{1,0:T(1,128)S(1)}, bf16[1536,512]{1,0:T(8,128)(2,1)S(1)}, bf16[1536,512]{1,0:T(8,128)(2,1)S(1)}, ...) custom-call(bf16[512,512]{1,0:T(8,128)(2,1)} %w2_hbm.1, ...), custom_call_target="tpu_custom_call" | custom-call | tf_op jit(solution)/shard_map/forward/pallas_call | solution.py:507
  33.4 4.7 %slope.1 = (bf16[1536,512]{1,0:T(8,128)(2,1)S(1)}, bf16[1536,512]{1,0:T(8,128)(2,1)S(1)}, bf16[256,512]{1,0:T(8,128)(2,1)S(1)}, f32[8,32,512]{2,1,0:T(8,128)S(1)}) custom-call(bf16[1536,512]{1,0:T(8,128)(2,1)} %cot_hbm.1, s32[12,128]{1,0:T(8,128)S(1)} %get-tuple-element.90.receiver_ref, bf16[256,512]{1,0:T(8,128)(2,1)S(1)} %get-tuple-element.111.dsum_ref, ...), custom_call_target="tpu_custom_call" | custom-call | tf_op jit(solution)/shard_map/slope/pallas_call | solution.py:507
  38.3 3.9 %first.1 = (bf16[64,512]{1,0:T(8,128)(2,1)S(1)}, bf16[64,512]{1,0:T(8,128)(2,1)S(1)}, bf16[32,512]{1,0:T(8,128)(2,1)S(1)}, f32[256,512]{1,0:T(8,128)S(1)}, bf16[...) custom-call(bf16[1536,512]{1,0:T(8,128)(2,1)S(1)} %get-tuple-element, ...), custom_call_target="tpu_custom_call" | custom-call | tf_op jit(solution)/shard_map/first/pallas_call | solution.py:507
  44.0 1.8 %edge.1 = bf16[1536,512]{1,0:T(8,128)(2,1)} custom-call(bf16[1536,512]{1,0:T(8,128)(2,1)S(1)} %get-tuple-element.132.dpre_ref, bf16[1536,512]{1,0:T(8,128)(2,1)S(1)} %get-tuple-element.133.cot_ref, bf16[1536,512]{1,0:T(8,128)(2,1)S(1)} %get-tuple-element.109.w1_ref), custom_call_target="tpu_custom_call" | custom-call | tf_op jit(solution)/shard_map/edge/pallas_call | solution.py:507
  46.2 1.4 %collective-permute-start.14 = (bf16[272,512]{1,0:T(8,128)(2,1)S(1)}, bf16[272,512]{1,0:T(8,128)(2,1)S(1)}, u32[]{:S(2)}, u32[]{:S(2)}) collective-permute-start(bf16[272,512]{1,0:T(8,128)(2,1)S(1)} %get-tuple-element.137), channel_id=1, source_target_pairs={{0,2},{1,3},{2,0},{3,1},{4,6},{5,7},{6,4},{7,5},{8,10},{9,11},{10,... | collective-permute-start | bytes 835592 | tf_op jit(solution)/shard_map/ppermute | solution.py:519
  47.7 7.1 %collective-permute-done.12.refs_1_ = bf16[384,512]{1,0:T(8,128)(2,1)S(1)} collective-permute-done((bf16[384,512]{1,0:T(8,128)(2,1)S(1)}, bf16[384,512]{1,0:T(8,128)(2,1)S(1)}, u32[]{:S(2)}, u32[]{:S(2)}) %collective-permute-start.12) | collective-permute-done | bytes 393248 | tf_op jit(solution)/shard_map/ppermute | solution.py:519
  54.9 1.6 %collective-permute-start.13 = (bf16[192,512]{1,0:T(8,128)(2,1)S(1)}, bf16[192,512]{1,0:T(8,128)(2,1)S(1)}, u32[]{:S(2)}, u32[]{:S(2)}) collective-permute-start(bf16[192,512]{1,0:T(8,128)(2,1)S(1)} %get-tuple-element.149), channel_id=1, source_target_pairs={{0,4},{1,5},{2,6},{3,7},{4,0},{5,1},{6,2},{7,3},{8,12},{9,13},{10,... | collective-permute-start | bytes 589832 | tf_op jit(solution)/shard_map/ppermute | solution.py:519
  57.1 3.5 %collective-permute-done.13.refs_1_ = bf16[192,512]{1,0:T(8,128)(2,1)S(1)} collective-permute-done((bf16[192,512]{1,0:T(8,128)(2,1)S(1)}, bf16[192,512]{1,0:T(8,128)(2,1)S(1)}, u32[]{:S(2)}, u32[]{:S(2)}) %collective-permute-start.13) | collective-permute-done | bytes 196640 | tf_op jit(solution)/shard_map/ppermute | solution.py:519
  61.1 1.6 %collective-permute-start.15 = (bf16[144,512]{1,0:T(8,128)(2,1)S(1)}, bf16[144,512]{1,0:T(8,128)(2,1)S(1)}, u32[]{:S(2)}, u32[]{:S(2)}) collective-permute-start(bf16[144,512]{1,0:T(8,128)(2,1)S(1)} %get-tuple-element.154), channel_id=1, source_target_pairs={{0,4},{1,5},{2,6},{3,7},{4,0},{5,1},{6,2},{7,3},{8,12},{9,13},{10,... | collective-permute-start | bytes 442376 | tf_op jit(solution)/shard_map/ppermute | solution.py:519
  62.7 3.6 %collective-permute-done.15.refs_1_ = bf16[144,512]{1,0:T(8,128)(2,1)S(1)} collective-permute-done((bf16[144,512]{1,0:T(8,128)(2,1)S(1)}, bf16[144,512]{1,0:T(8,128)(2,1)S(1)}, u32[]{:S(2)}, u32[]{:S(2)}) %collective-permute-start.15) | collective-permute-done | bytes 147488 | tf_op jit(solution)/shard_map/ppermute | solution.py:519
  66.7 1.6 %collective-permute-start.18 = (bf16[128,512]{1,0:T(8,128)(2,1)S(1)}, bf16[128,512]{1,0:T(8,128)(2,1)S(1)}, u32[]{:S(2)}, u32[]{:S(2)}) collective-permute-start(bf16[128,512]{1,0:T(8,128)(2,1)S(1)} %get-tuple-element.162), channel_id=1, source_target_pairs={{0,4},{1,5},{2,6},{3,7},{4,0},{5,1},{6,2},{7,3},{8,12},{9,13},{10,... | collective-permute-start | bytes 393224 | tf_op jit(solution)/shard_map/ppermute | solution.py:519
  68.3 2.6 %collective-permute-start.20 = (bf16[96,512]{1,0:T(8,128)(2,1)S(1)}, bf16[96,512]{1,0:T(8,128)(2,1)S(1)}, u32[]{:S(2)}, u32[]{:S(2)}) collective-permute-start(bf16[96,512]{1,0:T(8,128)(2,1)S(1)} %get-tuple-element.150), channel_id=1, source_target_pairs={{0,8},{1,9},{2,10},{3,11},{4,12},{5,13},{6,14},{7,15},{8,0},{9,1},... | collective-permute-start | bytes 294920 | tf_op jit(solution)/shard_map/ppermute | solution.py:519
  73.9 6.6 %collective-permute-start.19 = (bf16[64,512]{1,0:T(8,128)(2,1)S(1)}, bf16[64,512]{1,0:T(8,128)(2,1)S(1)}, u32[]{:S(2)}, u32[]{:S(2)}) collective-permute-start(bf16[64,512]{1,0:T(8,128)(2,1)S(1)} %get-tuple-element.164), channel_id=1, source_target_pairs={{0,8},{1,9},{2,10},{3,11},{4,12},{5,13},{6,14},{7,15},{8,0},{9,1},... | collective-permute-start | bytes 196616 | tf_op jit(solution)/shard_map/ppermute | solution.py:519
  81.2 1.4 %node.1 = bf16[256,512]{1,0:T(8,128)(2,1)} custom-call(s32[1,2,16]{2,1,0:T(2,128)S(1)} %bitcast.10, f32[256,512]{1,0:T(8,128)S(1)} %get-tuple-element.127.partial_ref, bf16[64,512]{1,0:T(8,128)(2,1)S(1)} %collective-permute-done.10.below_ref, bf16[64,512]{1,0:T(8,128)(2,1)S(1)} %collective-permute-done.11.above_ref, ...), custom_call_target="tpu_custom_call" | custom-call | tf_op jit(solution)/shard_map/node/pallas_call | solution.py:507
  82.6 1.4 %collective-permute-done.19.refs_3_ = bf16[64,512]{1,0:T(8,128)(2,1)S(1)} collective-permute-done((bf16[64,512]{1,0:T(8,128)(2,1)S(1)}, bf16[64,512]{1,0:T(8,128)(2,1)S(1)}, u32[]{:S(2)}, u32[]{:S(2)}) %collective-permute-start.19) | collective-permute-done | bytes 65568 | tf_op jit(solution)/shard_map/ppermute | solution.py:519
  (43 shorter events, 10.9 us)
Async XLA Ops:
  2.1 5.8 %collective-permute-start.2 = (bf16[16,512]{1,0:T(8,128)(2,1)S(1)}, bf16[16,512]{1,0:T(8,128)(2,1)S(1)}, u32[]{:S(2)}, u32[]{:S(2)}) collective-permute-start(bf16[16,512]{1,0:T(8,128)(2,1)S(1)} %get-tuple-element.88), channel_id=1, source_target_pairs={{0,1},{1,0},{2,3},{3,2},{4,5},{5,4},{6,7},{7,6},{8,9},{9,8},{10,11... | collective-permute-start | bytes 49160 | tf_op jit(solution)/shard_map/ppermute | solution.py:519
  2.6 22.6 %collective-permute-start = (bf16[64,512]{1,0:T(8,128)(2,1)S(1)}, bf16[64,512]{1,0:T(8,128)(2,1)S(1)}, u32[]{:S(2)}, u32[]{:S(2)}) collective-permute-start(bf16[64,512]{1,0:T(8,128)(2,1)S(1)} %get-tuple-element.91), channel_id=1, source_target_pairs={{0,1},{1,2},{2,3},{3,4},{4,5},{5,6},{6,7},{7,8},{8,9},{9,10},{10,1... | collective-permute-start | bytes 196616 | tf_op jit(solution)/shard_map/ppermute | solution.py:593
  4.6 20.7 %collective-permute-start.1 = (bf16[64,512]{1,0:T(8,128)(2,1)S(1)}, bf16[64,512]{1,0:T(8,128)(2,1)S(1)}, u32[]{:S(2)}, u32[]{:S(2)}) collective-permute-start(bf16[64,512]{1,0:T(8,128)(2,1)S(1)} %get-tuple-element.92), channel_id=1, source_target_pairs={{1,0},{2,1},{3,2},{4,3},{5,4},{6,5},{7,6},{8,7},{9,8},{10,9},{11,1... | collective-permute-start | bytes 196616 | tf_op jit(solution)/shard_map/ppermute | solution.py:594
  8.2 7.0 %collective-permute-start.3 = (bf16[16,512]{1,0:T(8,128)(2,1)S(1)}, bf16[16,512]{1,0:T(8,128)(2,1)S(1)}, u32[]{:S(2)}, u32[]{:S(2)}) collective-permute-start(bf16[16,512]{1,0:T(8,128)(2,1)S(1)} %get-tuple-element.97), channel_id=1, source_target_pairs={{0,2},{1,3},{2,0},{3,1},{4,6},{5,7},{6,4},{7,5},{8,10},{9,11},{10,... | collective-permute-start | bytes 49160 | tf_op jit(solution)/shard_map/ppermute | solution.py:519
  15.5 4.7 %collective-permute-start.4 = (bf16[16,512]{1,0:T(8,128)(2,1)S(1)}, bf16[16,512]{1,0:T(8,128)(2,1)S(1)}, u32[]{:S(2)}, u32[]{:S(2)}) collective-permute-start(bf16[16,512]{1,0:T(8,128)(2,1)S(1)} %get-tuple-element.103), channel_id=1, source_target_pairs={{0,4},{1,5},{2,6},{3,7},{4,0},{5,1},{6,2},{7,3},{8,12},{9,13},{10,... | collective-permute-start | bytes 49160 | tf_op jit(solution)/shard_map/ppermute | solution.py:519
  20.6 4.7 %collective-permute-start.5 = (bf16[16,512]{1,0:T(8,128)(2,1)S(1)}, bf16[16,512]{1,0:T(8,128)(2,1)S(1)}, u32[]{:S(2)}, u32[]{:S(2)}) collective-permute-start(bf16[16,512]{1,0:T(8,128)(2,1)S(1)} %get-tuple-element.108), channel_id=1, source_target_pairs={{0,8},{1,9},{2,10},{3,11},{4,12},{5,13},{6,14},{7,15},{8,0},{9,1},... | collective-permute-start | bytes 49160 | tf_op jit(solution)/shard_map/ppermute | solution.py:519
  33.4 4.8 %collective-permute-start.6 = (bf16[768,512]{1,0:T(8,128)(2,1)S(1)}, bf16[768,512]{1,0:T(8,128)(2,1)S(1)}, u32[]{:S(2)}, u32[]{:S(2)}) collective-permute-start(bf16[768,512]{1,0:T(8,128)(2,1)S(1)} %get-tuple-element.120), channel_id=1, source_target_pairs={{0,1},{1,0},{2,3},{3,2},{4,5},{5,4},{6,7},{7,6},{8,9},{9,8},{10,11... | collective-permute-start | bytes 2359304 | tf_op jit(solution)/shard_map/ppermute | solution.py:519
  42.3 3.6 %collective-permute-start.7 = (bf16[528,512]{1,0:T(8,128)(2,1)S(1)}, bf16[528,512]{1,0:T(8,128)(2,1)S(1)}, u32[]{:S(2)}, u32[]{:S(2)}) collective-permute-start(bf16[528,512]{1,0:T(8,128)(2,1)S(1)} %get-tuple-element.135), channel_id=1, source_target_pairs={{0,1},{1,0},{2,3},{3,2},{4,5},{5,4},{6,7},{7,6},{8,9},{9,8},{10,11... | collective-permute-start | bytes 1622024 | tf_op jit(solution)/shard_map/ppermute | solution.py:519
  42.9 12.0 %collective-permute-start.12 = (bf16[384,512]{1,0:T(8,128)(2,1)S(1)}, bf16[384,512]{1,0:T(8,128)(2,1)S(1)}, u32[]{:S(2)}, u32[]{:S(2)}) collective-permute-start(bf16[384,512]{1,0:T(8,128)(2,1)S(1)} %get-tuple-element.121), channel_id=1, source_target_pairs={{0,2},{1,3},{2,0},{3,1},{4,6},{5,7},{6,4},{7,5},{8,10},{9,11},{10,... | collective-permute-start | bytes 1179656 | tf_op jit(solution)/shard_map/ppermute | solution.py:519
  43.5 4.1 %collective-permute-start.9 = (bf16[256,512]{1,0:T(8,128)(2,1)S(1)}, bf16[256,512]{1,0:T(8,128)(2,1)S(1)}, u32[]{:S(2)}, u32[]{:S(2)}) collective-permute-start(bf16[256,512]{1,0:T(8,128)(2,1)S(1)} %get-tuple-element.141), channel_id=1, source_target_pairs={{0,1},{1,0},{2,3},{3,2},{4,5},{5,4},{6,7},{7,6},{8,9},{9,8},{10,11... | collective-permute-start | bytes 786440 | tf_op jit(solution)/shard_map/ppermute | solution.py:519
  43.5 4.1 %collective-permute-start.8 = (bf16[256,512]{1,0:T(8,128)(2,1)S(1)}, bf16[256,512]{1,0:T(8,128)(2,1)S(1)}, u32[]{:S(2)}, u32[]{:S(2)}) collective-permute-start(bf16[256,512]{1,0:T(8,128)(2,1)S(1)} %get-tuple-element.140), channel_id=1, source_target_pairs={{0,1},{1,0},{2,3},{3,2},{4,5},{5,4},{6,7},{7,6},{8,9},{9,8},{10,11... | collective-permute-start | bytes 786440 | tf_op jit(solution)/shard_map/ppermute | solution.py:519
  46.2 14.6 %collective-permute-start.14 = (bf16[272,512]{1,0:T(8,128)(2,1)S(1)}, bf16[272,512]{1,0:T(8,128)(2,1)S(1)}, u32[]{:S(2)}, u32[]{:S(2)}) collective-permute-start(bf16[272,512]{1,0:T(8,128)(2,1)S(1)} %get-tuple-element.137), channel_id=1, source_target_pairs={{0,2},{1,3},{2,0},{3,1},{4,6},{5,7},{6,4},{7,5},{8,10},{9,11},{10,... | collective-permute-start | bytes 835592 | tf_op jit(solution)/shard_map/ppermute | solution.py:519
  54.9 5.7 %collective-permute-start.13 = (bf16[192,512]{1,0:T(8,128)(2,1)S(1)}, bf16[192,512]{1,0:T(8,128)(2,1)S(1)}, u32[]{:S(2)}, u32[]{:S(2)}) collective-permute-start(bf16[192,512]{1,0:T(8,128)(2,1)S(1)} %get-tuple-element.149), channel_id=1, source_target_pairs={{0,4},{1,5},{2,6},{3,7},{4,0},{5,1},{6,2},{7,3},{8,12},{9,13},{10,... | collective-permute-start | bytes 589832 | tf_op jit(solution)/shard_map/ppermute | solution.py:519
  56.5 10.0 %collective-permute-start.17 = (bf16[256,512]{1,0:T(8,128)(2,1)S(1)}, bf16[256,512]{1,0:T(8,128)(2,1)S(1)}, u32[]{:S(2)}, u32[]{:S(2)}) collective-permute-start(bf16[256,512]{1,0:T(8,128)(2,1)S(1)} %get-tuple-element.142), channel_id=1, source_target_pairs={{0,2},{1,3},{2,0},{3,1},{4,6},{5,7},{6,4},{7,5},{8,10},{9,11},{10,... | collective-permute-start | bytes 786440 | tf_op jit(solution)/shard_map/ppermute | solution.py:519
  60.6 20.5 %copy-start = (s32[1,16,2]{1,2,0:T(2,128)S(1)}, s32[1,16,2]{1,2,0:T(2,128)}, u32[]{:S(2)}) copy-start(s32[1,16,2]{1,2,0:T(2,128)} %param.32) | copy-start | bytes 388
  61.1 5.2 %collective-permute-start.15 = (bf16[144,512]{1,0:T(8,128)(2,1)S(1)}, bf16[144,512]{1,0:T(8,128)(2,1)S(1)}, u32[]{:S(2)}, u32[]{:S(2)}) collective-permute-start(bf16[144,512]{1,0:T(8,128)(2,1)S(1)} %get-tuple-element.154), channel_id=1, source_target_pairs={{0,4},{1,5},{2,6},{3,7},{4,0},{5,1},{6,2},{7,3},{8,12},{9,13},{10,... | collective-permute-start | bytes 442376 | tf_op jit(solution)/shard_map/ppermute | solution.py:519
  66.7 7.2 %collective-permute-start.18 = (bf16[128,512]{1,0:T(8,128)(2,1)S(1)}, bf16[128,512]{1,0:T(8,128)(2,1)S(1)}, u32[]{:S(2)}, u32[]{:S(2)}) collective-permute-start(bf16[128,512]{1,0:T(8,128)(2,1)S(1)} %get-tuple-element.162), channel_id=1, source_target_pairs={{0,4},{1,5},{2,6},{3,7},{4,0},{5,1},{6,2},{7,3},{8,12},{9,13},{10,... | collective-permute-start | bytes 393224 | tf_op jit(solution)/shard_map/ppermute | solution.py:519
  68.3 12.2 %collective-permute-start.20 = (bf16[96,512]{1,0:T(8,128)(2,1)S(1)}, bf16[96,512]{1,0:T(8,128)(2,1)S(1)}, u32[]{:S(2)}, u32[]{:S(2)}) collective-permute-start(bf16[96,512]{1,0:T(8,128)(2,1)S(1)} %get-tuple-element.150), channel_id=1, source_target_pairs={{0,8},{1,9},{2,10},{3,11},{4,12},{5,13},{6,14},{7,15},{8,0},{9,1},... | collective-permute-start | bytes 294920 | tf_op jit(solution)/shard_map/ppermute | solution.py:519
  70.9 10.2 %collective-permute-start.16 = (bf16[80,512]{1,0:T(8,128)(2,1)S(1)}, bf16[80,512]{1,0:T(8,128)(2,1)S(1)}, u32[]{:S(2)}, u32[]{:S(2)}) collective-permute-start(bf16[80,512]{1,0:T(8,128)(2,1)S(1)} %get-tuple-element.157), channel_id=1, source_target_pairs={{0,8},{1,9},{2,10},{3,11},{4,12},{5,13},{6,14},{7,15},{8,0},{9,1},... | collective-permute-start | bytes 245768 | tf_op jit(solution)/shard_map/ppermute | solution.py:519
  71.2 9.9 %collective-permute-start.10 = (bf16[64,512]{1,0:T(8,128)(2,1)S(1)}, bf16[64,512]{1,0:T(8,128)(2,1)S(1)}, u32[]{:S(2)}, u32[]{:S(2)}) collective-permute-start(bf16[64,512]{1,0:T(8,128)(2,1)S(1)} %get-tuple-element.143), channel_id=1, source_target_pairs={{0,1},{1,2},{2,3},{3,4},{4,5},{5,6},{6,7},{7,8},{8,9},{9,10},{10,1... | collective-permute-start | bytes 196616 | tf_op jit(solution)/shard_map/ppermute | solution.py:730
  72.5 8.6 %collective-permute-start.11 = (bf16[64,512]{1,0:T(8,128)(2,1)S(1)}, bf16[64,512]{1,0:T(8,128)(2,1)S(1)}, u32[]{:S(2)}, u32[]{:S(2)}) collective-permute-start(bf16[64,512]{1,0:T(8,128)(2,1)S(1)} %get-tuple-element.144), channel_id=1, source_target_pairs={{1,0},{2,1},{3,2},{4,3},{5,4},{6,5},{7,6},{8,7},{9,8},{10,9},{11,1... | collective-permute-start | bytes 196616 | tf_op jit(solution)/shard_map/ppermute | solution.py:729
  73.9 10.1 %collective-permute-start.19 = (bf16[64,512]{1,0:T(8,128)(2,1)S(1)}, bf16[64,512]{1,0:T(8,128)(2,1)S(1)}, u32[]{:S(2)}, u32[]{:S(2)}) collective-permute-start(bf16[64,512]{1,0:T(8,128)(2,1)S(1)} %get-tuple-element.164), channel_id=1, source_target_pairs={{0,8},{1,9},{2,10},{3,11},{4,12},{5,13},{6,14},{7,15},{8,0},{9,1},... | collective-permute-start | bytes 196616 | tf_op jit(solution)/shard_map/ppermute | solution.py:519

commit v6 on v5

--- a/solution.py
+++ b/solution.py
@@ -14,6 +14,7 @@
 F32 = jnp.float32
 BF16 = jnp.bfloat16
 MIB = 1024 * 1024
+AHEAD = 10**10
 
 NN = (((1,), (0,)), ((), ()))
 NT = (((1,), (1,)), ((), ()))
@@ -139,7 +140,7 @@
         slots += dot(ones_where((owner == column) & (at == j)), listed)
     slots = slots.astype(BF16)
     slots_ref[...] = slots
-    send_ref[...] = slots_out(0, slots, places) if fast else jnp.zeros_like(send_ref)
+    send_ref[...] = slots_out(3, slots, places) if fast else jnp.zeros_like(send_ref)
     head_ref[...] = node_ref[:NEAR, :]
     tail_ref[...] = node_ref[nodes - NEAR :, :]
 
@@ -147,7 +148,7 @@
 def shuffle_kernel(bit, places, slots_ref, got_ref, moved_ref, send_ref):
     slots = slots_in(bit, slots_ref[...], got_ref[...], places)
     moved_ref[...] = slots
-    send_ref[...] = slots_out(bit + 1, slots, places)
+    send_ref[...] = slots_out(bit - 1, slots, places)
 
 
 def table_index(raw, origin, places, nodes):
@@ -236,7 +237,7 @@
     table_ref[nodes + NEAR : nodes + 2 * NEAR, :] = upper_ref[...]
     slots = slots_ref[...]
     if fast:
-        slots = slots_in(3, slots, got_ref[...], places)
+        slots = slots_in(0, slots, got_ref[...], places)
     table_ref[nodes + 2 * NEAR : nodes + 2 * NEAR + places * tiles, :] = slots
     used = nodes + 2 * NEAR + places * tiles
     if used < rows:
@@ -502,7 +503,7 @@
     return [pltpu.with_memory_space_constraint(array, pltpu.HBM) for array in arrays]
 
 
-def call(kernel, name, out_shape, args, hbm=0, scratch=(), out_specs=None, limit=16):
+def call(kernel, name, out_shape, args, hbm=0, scratch=(), out_specs=None, flops=0):
     vmem = pl.BlockSpec(memory_space=pltpu.VMEM)
     return pl.pallas_call(
         kernel,
@@ -510,7 +511,8 @@
         out_specs=out_specs or [vmem] * len(out_shape),
         out_shape=out_shape,
         scratch_shapes=scratch,
-        compiler_params=pltpu.CompilerParams(vmem_limit_bytes=limit * MIB),
+        compiler_params=pltpu.CompilerParams(vmem_limit_bytes=16 * MIB),
+        cost_estimate=pl.CostEstimate(flops=flops, bytes_accessed=flops // 100, transcendentals=0),
         name=name,
     )(*in_hbm(*args[:hbm]), *args[hbm:])
 
@@ -519,7 +521,7 @@
     return lax.ppermute(send, "tiles", [(i, i ^ bit) for i in range(tiles)])
 
 
-def halve(shift, keeps, gots, slots=None, places=0):
+def halve(shift, keeps, gots, slots=None, places=0, flops=0):
     half, _, width = keeps[0].shape
     rows = sum(keep.shape[1] for keep in keeps)
     extra = [] if slots is None else [slots]
@@ -530,6 +532,7 @@
         [pltpu.VMEM((sent, width), BF16), pltpu.VMEM((half // 2, rows, width), F32)]
         + [pltpu.VMEM(slots.shape, BF16) for slots in extra],
         [*keeps, *gots, *extra],
+        flops=flops,
     )
 
 
@@ -590,6 +593,8 @@
         hbm=2,
         scratch=[vmem(listed.shape, jnp.int32), vmem((nodes, latent), BF16), pltpu.SemaphoreType.DMA((2,))],
     )
+    if fast:
+        far_got = swap(tiles, 8, send)
     lower = lax.ppermute(tail, "tiles", upward)
     upper = lax.ppermute(head, "tiles", downward)
     w1_kept, node_kept, receiver_kept, moved, weights = call(
@@ -624,15 +629,14 @@
         )
 
     if fast:
+        slots, send = shuffle(3, after(outgoing, moved), far_got)
+        got = swap(tiles, 4, send)
+        edge_early, early = prepare(0, after(moved, send))
+        slots, send = shuffle(2, after(slots, early), got)
+        got = swap(tiles, 2, send)
+        edge_later, later = prepare(steps // 2, after(moved, send))
+        slots, send = shuffle(1, after(slots, later), got)
         got = swap(tiles, 1, send)
-        slots, send = shuffle(0, after(outgoing, moved), got)
-        got = swap(tiles, 2, send)
-        edge_early, early = prepare(0, after(moved, send))
-        slots, send = shuffle(1, after(slots, early), got)
-        got = swap(tiles, 4, send)
-        edge_later, later = prepare(steps // 2, after(moved, send))
-        slots, send = shuffle(2, after(slots, later), got)
-        got = swap(tiles, 8, send)
     else:
         edge_early, early = prepare(0, moved)
         edge_later, later = prepare(steps // 2, moved)
@@ -677,10 +681,20 @@
         ],
     )
     if fast:
-        send, chain = halve(1, [node_keep], [swap(tiles, 1, node_send)])
+        send, chain = halve(1, [after(node_keep, dpre)], [swap(tiles, 1, node_send)])
         dpre = after(dpre, send)
         got = swap(tiles, 2, send)
         got_second = swap(tiles, 1, second_send)
+
+    (grad_edge,) = call(
+        edge_kernel,
+        "edge",
+        [shaped((edges, latent), BF16)],
+        [dpre, cot_kept, w1_kept],
+        out_specs=[pl.BlockSpec(memory_space=pltpu.HBM)],
+        scratch=[vmem((edges, latent), BF16), pltpu.SemaphoreType.DMA((steps,))],
+    )
+    dpre = after(dpre, grad_edge)
 
     per = latent // tiles
     to_lower, to_upper, to_far, partial, *first = call(
@@ -703,19 +717,12 @@
         scratch=[vmem((3 * latent, latent), F32), vmem((rows + nodes, latent), F32)],
     )
 
-    (grad_edge,) = call(
-        edge_kernel,
-        "edge",
-        [shaped((edges, latent), BF16)],
-        [after(dpre, partial), cot_kept, w1_kept],
-        out_specs=[pl.BlockSpec(memory_space=pltpu.HBM)],
-        scratch=[vmem((edges, latent), BF16), pltpu.SemaphoreType.DMA((steps,))],
-    )
-
     if fast:
         send_a, keep_a, send_b, keep_b = first
+        send, chain = halve(2, [after(chain, partial)], [got], flops=AHEAD)
+        got = swap(tiles, 4, send)
         send_a, chain_a, slots = halve(
-            1, [after(keep_a, grad_edge)], [swap(tiles, 1, send_a)], to_far, places
+            1, [after(keep_a, send)], [swap(tiles, 1, send_a)], to_far, places
         )
         got_a = swap(tiles, 2, send_a)
         send_b, chain_b = halve(
@@ -723,28 +730,27 @@
         )
         got_b = swap(tiles, 2, send_b)
         to_lower, to_upper = lax.optimization_barrier((to_lower, to_upper, send_b))[:2]
-        send, chain = halve(2, [after(chain, send_b)], [got])
-        got = swap(tiles, 4, send)
 
     above = lax.ppermute(to_lower, "tiles", downward)
     below = lax.ppermute(to_upper, "tiles", upward)
     if fast:
         send, chain = halve(3, [chain], [got])
         got = swap(tiles, 8, send)
-        send_a, chain_a, slots = halve(2, [after(chain_a, send)], [got_a], slots, places)
+        chain_a = lax.optimization_barrier((chain_a, send, above, below))[0]
+        send_a, chain_a, slots = halve(2, [chain_a], [got_a], slots, places, AHEAD)
         got_a = swap(tiles, 4, send_a)
         send_a, chain_a, slots = halve(3, [chain_a], [got_a], slots, places)
         got_a = swap(tiles, 8, send_a)
-        returned = [slots, got_a]
-        send_b, chain_b = halve(2, [after(chain_b, send_a)], [got_b])
+        send_b, chain_b = halve(2, [after(chain_b, send_a, got)], [got_b])
         got_b = swap(tiles, 4, send_b)
-        grad_node_w1, grad_node_w2 = finish(
-            [chain], [got], [[(0, 2 * per), (1, per)]], [2 * per, per]
-        )
         send_b, chain_b = halve(3, [chain_b], [got_b])
         got_b = swap(tiles, 8, send_b)
-        grad_edge_w1, grad_edge_w2 = finish(
-            [chain_a, chain_b], [got_a, got_b], [[(0, 2 * per)], [(0, per), (1, per)]], [3 * per, per]
+        returned = [slots, got_a]
+        grad_edge_w1, grad_edge_w2, grad_node_w1, grad_node_w2 = finish(
+            [chain, chain_a, chain_b],
+            [got, got_a, got_b],
+            [[(2, 2 * per), (3, per)], [(0, 2 * per)], [(0, per), (1, per)]],
+            [3 * per, per, 2 * per, per],
         )
     else:
         returned = [lax.all_to_all(to_far, "tiles", split_axis=0, concat_axis=0, tiled=True)]

time: 85 us -> 83.3 us (0.980)
  starting transfers between devices: 34.6 us -> 26.7 us
  waiting for transfers between devices: 17.8 us -> 24.6 us
    ppermute x17, starting transfers between devices: 28.7 us -> 21.3 us  [swap(): return lax.ppermute(send, 'tiles', [(i, i ^ bit) for i in range(tiles)])]
    ppermute x17, waiting for transfers between devices: 17.8 us -> 24.6 us  [swap(): return lax.ppermute(send, 'tiles', [(i, i ^ bit) for i in range(tiles)])]
    pallas_call x23 -> x22, Pallas kernels: 31.5 us -> 30.8 us  [call(): pl.pallas_call(kernel, in_specs=[pl.BlockSpec(memory_space=pltpu.HBM)] *...]
  transfers between devices with their start and end apart: 21 -> 21, of which waited for: 6 -> 7; matrix products, arithmetic and copies ran while one was open for 0% -> 0% of each run, Pallas kernels for 20% -> 24%
where the time goes in v6:
time: 83.3 us; the launch traced here: 83 us
  Pallas kernels  30.8 us (37%)
  starting transfers between devices  26.7 us (32%)
  waiting for transfers between devices  24.6 us (30%)
  between operations  0.88 us (1%)
    pallas_call x22, Pallas kernels, call(): pl.pallas_call(kernel, in_specs=[pl.BlockSpec(memory_space=pltpu.HBM)] *...  30.8 us
    ppermute x17, waiting for transfers between devices, swap(): return lax.ppermute(send, 'tiles', [(i, i ^ bit) for i in range(tiles)])  24.6 us
    ppermute x17, starting transfers between devices, swap(): return lax.ppermute(send, 'tiles', [(i, i ^ bit) for i in range(tiles)])  21.3 us
  transfers between devices with their start and end apart: 21, of which 7 were waited for; matrix products, arithmetic and copies ran while one was open for 0% of the time, Pallas kernels for 24%

profile of v6, /device:TPU:0, one launch (start us, length us, event | category | flops | bytes accessed | tf_op | source)
XLA Modules:
  0.0 83.0 jit_solution(17877338824041553118)
XLA Ops:
  0.6 1.5 %outgoing.1 = (bf16[32,512]{1,0:T(8,128)(2,1)S(1)}, bf16[16,512]{1,0:T(8,128)(2,1)S(1)}, bf16[64,512]{1,0:T(8,128)(2,1)S(1)}, bf16[64,512]{1,0:T(8,128)(2,1)S(1)}) custom-call(s32[1,2,16]{2,1,0:T(2,128)} %bitcast.9, bf16[256,512]{1,0:T(8,128)(2,1)} %node_hbm.3), custom_call_target="tpu_custom_call" | custom-call | tf_op jit(solution)/shard_map/outgoing/pallas_call | solution.py:508
  2.1 4.1 %collective-permute-start.2 = (bf16[16,512]{1,0:T(8,128)(2,1)S(1)}, bf16[16,512]{1,0:T(8,128)(2,1)S(1)}, u32[]{:S(2)}, u32[]{:S(2)}) collective-permute-start(bf16[16,512]{1,0:T(8,128)(2,1)S(1)} %get-tuple-element.89), channel_id=1, source_target_pairs={{0,8},{1,9},{2,10},{3,11},{4,12},{5,13},{6,14},{7,15},{8,0},{9,1},... | collective-permute-start | bytes 49160 | tf_op jit(solution)/shard_map/ppermute | solution.py:521
  6.2 1.4 %collective-permute-start = (bf16[64,512]{1,0:T(8,128)(2,1)S(1)}, bf16[64,512]{1,0:T(8,128)(2,1)S(1)}, u32[]{:S(2)}, u32[]{:S(2)}) collective-permute-start(bf16[64,512]{1,0:T(8,128)(2,1)S(1)} %get-tuple-element.92), channel_id=1, source_target_pairs={{0,1},{1,2},{2,3},{3,4},{4,5},{5,6},{6,7},{7,8},{8,9},{9,10},{10,1... | collective-permute-start | bytes 196616 | tf_op jit(solution)/shard_map/ppermute | solution.py:598
  7.7 1.3 %collective-permute-start.1 = (bf16[64,512]{1,0:T(8,128)(2,1)S(1)}, bf16[64,512]{1,0:T(8,128)(2,1)S(1)}, u32[]{:S(2)}, u32[]{:S(2)}) collective-permute-start(bf16[64,512]{1,0:T(8,128)(2,1)S(1)} %get-tuple-element.93), channel_id=1, source_target_pairs={{1,0},{2,1},{3,2},{4,3},{5,4},{6,5},{7,6},{8,7},{9,8},{10,9},{11,1... | collective-permute-start | bytes 196616 | tf_op jit(solution)/shard_map/ppermute | solution.py:599
  9.0 2.0 %weights.1 = (bf16[1536,512]{1,0:T(8,128)(2,1)S(1)}, bf16[256,512]{1,0:T(8,128)(2,1)S(1)}, s32[12,128]{1,0:T(8,128)S(1)}, s32[12,128]{1,0:T(8,128)S(1)}, bf16[1024,512]{1,0:T(8,128)(2,1)S(1)}) custom-call(bf16[256,512]{1,0:T(8,128)(2,1)} %node_hbm.3, bf16[1536,512]{1,0:T(8,128)(2,1)} %w1_hbm.1, s32[12,128]{1,0:T(8,128)} %bitcast.11, s32[12,128]{1,0:T(8,128)} %bitcast.12), custom_call_target="tpu_custom_call" | custom-call | tf_op jit(solution)/shard_map/weights/pallas_call | solution.py:508
  11.3 5.3 %collective-permute-start.3 = (bf16[16,512]{1,0:T(8,128)(2,1)S(1)}, bf16[16,512]{1,0:T(8,128)(2,1)S(1)}, u32[]{:S(2)}, u32[]{:S(2)}) collective-permute-start(bf16[16,512]{1,0:T(8,128)(2,1)S(1)} %get-tuple-element.98), channel_id=1, source_target_pairs={{0,4},{1,5},{2,6},{3,7},{4,0},{5,1},{6,2},{7,3},{8,12},{9,13},{10,... | collective-permute-start | bytes 49160 | tf_op jit(solution)/shard_map/ppermute | solution.py:521
  16.6 2.2 %prepare.2 = (bf16[768,512]{1,0:T(8,128)(2,1)S(1)}, f32[768,512]{1,0:T(8,128)S(1)}) custom-call(f32[1,512]{1,0:T(1,128)} %bitcast.13, bf16[1536,512]{1,0:T(8,128)(2,1)} %edge_hbm.3, s32[12,128]{1,0:T(8,128)S(1)} %get-tuple-element.105.moved_ref.sender_ref, s32[12,128]{1,0:T(8,128)S(1)} %get-tuple-element.91.receiver_ref, ...), custom_call_target="tpu_custom_call" | custom-call | tf_op jit(solution)/shard_map/prepare/pallas_call | solution.py:508
  19.7 2.2 %prepare.3 = (bf16[768,512]{1,0:T(8,128)(2,1)S(1)}, f32[768,512]{1,0:T(8,128)S(1)}) custom-call(f32[1,512]{1,0:T(1,128)} %bitcast.14, bf16[1536,512]{1,0:T(8,128)(2,1)} %edge_hbm.3, s32[12,128]{1,0:T(8,128)S(1)} %get-tuple-element.105.moved_ref.sender_ref, s32[12,128]{1,0:T(8,128)S(1)} %get-tuple-element.91.receiver_ref, ...), custom_call_target="tpu_custom_call" | custom-call | tf_op jit(solution)/shard_map/prepare/pallas_call | solution.py:508
  23.2 1.2 %collective-permute-done.5.got_ref = bf16[16,512]{1,0:T(8,128)(2,1)S(1)} collective-permute-done((bf16[16,512]{1,0:T(8,128)(2,1)S(1)}, bf16[16,512]{1,0:T(8,128)(2,1)S(1)}, u32[]{:S(2)}, u32[]{:S(2)}) %collective-permute-start.5) | collective-permute-done | bytes 16416 | tf_op jit(solution)/shard_map/ppermute | solution.py:521
  24.3 8.1 %forward.1 = (bf16[512,512]{1,0:T(8,128)(2,1)S(1)}, f32[1,512]{1,0:T(1,128)S(1)}, bf16[1536,512]{1,0:T(8,128)(2,1)S(1)}, bf16[1536,512]{1,0:T(8,128)(2,1)S(1)}, ...) custom-call(bf16[512,512]{1,0:T(8,128)(2,1)} %w2_hbm.1, ...), custom_call_target="tpu_custom_call" | custom-call | tf_op jit(solution)/shard_map/forward/pallas_call | solution.py:508
  32.7 4.7 %slope.1 = (bf16[1536,512]{1,0:T(8,128)(2,1)S(1)}, bf16[1536,512]{1,0:T(8,128)(2,1)S(1)}, bf16[256,512]{1,0:T(8,128)(2,1)S(1)}, f32[8,32,512]{2,1,0:T(8,128)S(1)}) custom-call(bf16[1536,512]{1,0:T(8,128)(2,1)} %cot_hbm.1, s32[12,128]{1,0:T(8,128)S(1)} %get-tuple-element.91.receiver_ref, bf16[256,512]{1,0:T(8,128)(2,1)S(1)} %get-tuple-element.112.dsum_ref, ...), custom_call_target="tpu_custom_call" | custom-call | tf_op jit(solution)/shard_map/slope/pallas_call | solution.py:508
  38.4 1.8 %edge.1 = bf16[1536,512]{1,0:T(8,128)(2,1)} custom-call(bf16[1536,512]{1,0:T(8,128)(2,1)S(1)} %get-tuple-element.126.dpre_ref, bf16[1536,512]{1,0:T(8,128)(2,1)S(1)} %get-tuple-element.125.cot_ref, bf16[1536,512]{1,0:T(8,128)(2,1)S(1)} %get-tuple-element.110.w1_ref), custom_call_target="tpu_custom_call" | custom-call | tf_op jit(solution)/shard_map/edge/pallas_call | solution.py:508
  40.1 3.9 %first.1 = (bf16[64,512]{1,0:T(8,128)(2,1)S(1)}, bf16[64,512]{1,0:T(8,128)(2,1)S(1)}, bf16[32,512]{1,0:T(8,128)(2,1)S(1)}, f32[256,512]{1,0:T(8,128)S(1)}, bf16[...) custom-call(bf16[1536,512]{1,0:T(8,128)(2,1)S(1)} %get-tuple-element, ...), custom_call_target="tpu_custom_call" | custom-call | tf_op jit(solution)/shard_map/first/pallas_call | solution.py:508
  44.7 4.4 %collective-permute-done.7.refs_1_ = bf16[384,512]{1,0:T(8,128)(2,1)S(1)} collective-permute-done((bf16[384,512]{1,0:T(8,128)(2,1)S(1)}, bf16[384,512]{1,0:T(8,128)(2,1)S(1)}, u32[]{:S(2)}, u32[]{:S(2)}) %collective-permute-start.7) | collective-permute-done | bytes 393248 | tf_op jit(solution)/shard_map/ppermute | solution.py:521
  50.1 1.6 %collective-permute-start.13 = (bf16[192,512]{1,0:T(8,128)(2,1)S(1)}, bf16[192,512]{1,0:T(8,128)(2,1)S(1)}, u32[]{:S(2)}, u32[]{:S(2)}) collective-permute-start(bf16[192,512]{1,0:T(8,128)(2,1)S(1)} %get-tuple-element.138), channel_id=1, source_target_pairs={{0,4},{1,5},{2,6},{3,7},{4,0},{5,1},{6,2},{7,3},{8,12},{9,13},{10,... | collective-permute-start | bytes 589832 | tf_op jit(solution)/shard_map/ppermute | solution.py:521
  51.8 1.3 %collective-permute-start.11 = (bf16[64,512]{1,0:T(8,128)(2,1)S(1)}, bf16[64,512]{1,0:T(8,128)(2,1)S(1)}, u32[]{:S(2)}, u32[]{:S(2)}) collective-permute-start(bf16[64,512]{1,0:T(8,128)(2,1)S(1)} %get-tuple-element.148), channel_id=1, source_target_pairs={{0,1},{1,2},{2,3},{3,4},{4,5},{5,6},{6,7},{7,8},{8,9},{9,10},{10,1... | collective-permute-start | bytes 196616 | tf_op jit(solution)/shard_map/ppermute | solution.py:735
  53.1 1.3 %collective-permute-start.12 = (bf16[64,512]{1,0:T(8,128)(2,1)S(1)}, bf16[64,512]{1,0:T(8,128)(2,1)S(1)}, u32[]{:S(2)}, u32[]{:S(2)}) collective-permute-start(bf16[64,512]{1,0:T(8,128)(2,1)S(1)} %get-tuple-element.149), channel_id=1, source_target_pairs={{1,0},{2,1},{3,2},{4,3},{5,4},{6,5},{7,6},{8,7},{9,8},{10,9},{11,1... | collective-permute-start | bytes 196616 | tf_op jit(solution)/shard_map/ppermute | solution.py:734
  54.4 4.5 %collective-permute-start.18 = (bf16[256,512]{1,0:T(8,128)(2,1)S(1)}, bf16[256,512]{1,0:T(8,128)(2,1)S(1)}, u32[]{:S(2)}, u32[]{:S(2)}) collective-permute-start(bf16[256,512]{1,0:T(8,128)(2,1)S(1)} %get-tuple-element.147), channel_id=1, source_target_pairs={{0,2},{1,3},{2,0},{3,1},{4,6},{5,7},{6,4},{7,5},{8,10},{9,11},{10,... | collective-permute-start | bytes 786440 | tf_op jit(solution)/shard_map/ppermute | solution.py:521
  59.2 1.7 %collective-permute-start.15 = (bf16[144,512]{1,0:T(8,128)(2,1)S(1)}, bf16[144,512]{1,0:T(8,128)(2,1)S(1)}, u32[]{:S(2)}, u32[]{:S(2)}) collective-permute-start(bf16[144,512]{1,0:T(8,128)(2,1)S(1)} %get-tuple-element.156), channel_id=1, source_target_pairs={{0,4},{1,5},{2,6},{3,7},{4,0},{5,1},{6,2},{7,3},{8,12},{9,13},{10,... | collective-permute-start | bytes 442376 | tf_op jit(solution)/shard_map/ppermute | solution.py:521
  61.3 3.6 %collective-permute-done.15.refs_1_ = bf16[144,512]{1,0:T(8,128)(2,1)S(1)} collective-permute-done((bf16[144,512]{1,0:T(8,128)(2,1)S(1)}, bf16[144,512]{1,0:T(8,128)(2,1)S(1)}, u32[]{:S(2)}, u32[]{:S(2)}) %collective-permute-start.15) | collective-permute-done | bytes 147488 | tf_op jit(solution)/shard_map/ppermute | solution.py:521
  65.2 4.4 %collective-permute-done.17.refs_3_ = bf16[96,512]{1,0:T(8,128)(2,1)S(1)} collective-permute-done((bf16[96,512]{1,0:T(8,128)(2,1)S(1)}, bf16[96,512]{1,0:T(8,128)(2,1)S(1)}, u32[]{:S(2)}, u32[]{:S(2)}) %collective-permute-start.17) | collective-permute-done | bytes 98336 | tf_op jit(solution)/shard_map/ppermute | solution.py:521
  70.6 6.4 %collective-permute-done.19.refs_1_ = bf16[128,512]{1,0:T(8,128)(2,1)S(1)} collective-permute-done((bf16[128,512]{1,0:T(8,128)(2,1)S(1)}, bf16[128,512]{1,0:T(8,128)(2,1)S(1)}, u32[]{:S(2)}, u32[]{:S(2)}) %collective-permute-start.19) | collective-permute-done | bytes 131104 | tf_op jit(solution)/shard_map/ppermute | solution.py:521
  77.1 1.4 %node.1 = bf16[256,512]{1,0:T(8,128)(2,1)} custom-call(s32[1,2,16]{2,1,0:T(2,128)S(1)} %bitcast.10, f32[256,512]{1,0:T(8,128)S(1)} %get-tuple-element.131.partial_ref, bf16[64,512]{1,0:T(8,128)(2,1)S(1)} %collective-permute-done.11.below_ref, bf16[64,512]{1,0:T(8,128)(2,1)S(1)} %collective-permute-done.12.above_ref, ...), custom_call_target="tpu_custom_call" | custom-call | tf_op jit(solution)/shard_map/node/pallas_call | solution.py:508
  78.5 3.7 %collective-permute-done.20.refs_5_ = bf16[64,512]{1,0:T(8,128)(2,1)S(1)} collective-permute-done((bf16[64,512]{1,0:T(8,128)(2,1)S(1)}, bf16[64,512]{1,0:T(8,128)(2,1)S(1)}, u32[]{:S(2)}, u32[]{:S(2)}) %collective-permute-start.20) | collective-permute-done | bytes 65568 | tf_op jit(solution)/shard_map/ppermute | solution.py:521
  (42 shorter events, 8.3 us)
Async XLA Ops:
  2.1 8.9 %collective-permute-start.2 = (bf16[16,512]{1,0:T(8,128)(2,1)S(1)}, bf16[16,512]{1,0:T(8,128)(2,1)S(1)}, u32[]{:S(2)}, u32[]{:S(2)}) collective-permute-start(bf16[16,512]{1,0:T(8,128)(2,1)S(1)} %get-tuple-element.89), channel_id=1, source_target_pairs={{0,8},{1,9},{2,10},{3,11},{4,12},{5,13},{6,14},{7,15},{8,0},{9,1},... | collective-permute-start | bytes 49160 | tf_op jit(solution)/shard_map/ppermute | solution.py:521
  6.2 16.9 %collective-permute-start = (bf16[64,512]{1,0:T(8,128)(2,1)S(1)}, bf16[64,512]{1,0:T(8,128)(2,1)S(1)}, u32[]{:S(2)}, u32[]{:S(2)}) collective-permute-start(bf16[64,512]{1,0:T(8,128)(2,1)S(1)} %get-tuple-element.92), channel_id=1, source_target_pairs={{0,1},{1,2},{2,3},{3,4},{4,5},{5,6},{6,7},{7,8},{8,9},{9,10},{10,1... | collective-permute-start | bytes 196616 | tf_op jit(solution)/shard_map/ppermute | solution.py:598
  7.7 15.5 %collective-permute-start.1 = (bf16[64,512]{1,0:T(8,128)(2,1)S(1)}, bf16[64,512]{1,0:T(8,128)(2,1)S(1)}, u32[]{:S(2)}, u32[]{:S(2)}) collective-permute-start(bf16[64,512]{1,0:T(8,128)(2,1)S(1)} %get-tuple-element.93), channel_id=1, source_target_pairs={{1,0},{2,1},{3,2},{4,3},{5,4},{6,5},{7,6},{8,7},{9,8},{10,9},{11,1... | collective-permute-start | bytes 196616 | tf_op jit(solution)/shard_map/ppermute | solution.py:599
  11.3 7.5 %collective-permute-start.3 = (bf16[16,512]{1,0:T(8,128)(2,1)S(1)}, bf16[16,512]{1,0:T(8,128)(2,1)S(1)}, u32[]{:S(2)}, u32[]{:S(2)}) collective-permute-start(bf16[16,512]{1,0:T(8,128)(2,1)S(1)} %get-tuple-element.98), channel_id=1, source_target_pairs={{0,4},{1,5},{2,6},{3,7},{4,0},{5,1},{6,2},{7,3},{8,12},{9,13},{10,... | collective-permute-start | bytes 49160 | tf_op jit(solution)/shard_map/ppermute | solution.py:521
  19.1 3.8 %collective-permute-start.4 = (bf16[16,512]{1,0:T(8,128)(2,1)S(1)}, bf16[16,512]{1,0:T(8,128)(2,1)S(1)}, u32[]{:S(2)}, u32[]{:S(2)}) collective-permute-start(bf16[16,512]{1,0:T(8,128)(2,1)S(1)} %get-tuple-element.104), channel_id=1, source_target_pairs={{0,2},{1,3},{2,0},{3,1},{4,6},{5,7},{6,4},{7,5},{8,10},{9,11},{10,... | collective-permute-start | bytes 49160 | tf_op jit(solution)/shard_map/ppermute | solution.py:521
  23.1 1.2 %collective-permute-start.5 = (bf16[16,512]{1,0:T(8,128)(2,1)S(1)}, bf16[16,512]{1,0:T(8,128)(2,1)S(1)}, u32[]{:S(2)}, u32[]{:S(2)}) collective-permute-start(bf16[16,512]{1,0:T(8,128)(2,1)S(1)} %get-tuple-element.109), channel_id=1, source_target_pairs={{0,1},{1,0},{2,3},{3,2},{4,5},{5,4},{6,7},{7,6},{8,9},{9,8},{10,11... | collective-permute-start | bytes 49160 | tf_op jit(solution)/shard_map/ppermute | solution.py:521
  32.5 5.0 %collective-permute-start.6 = (bf16[768,512]{1,0:T(8,128)(2,1)S(1)}, bf16[768,512]{1,0:T(8,128)(2,1)S(1)}, u32[]{:S(2)}, u32[]{:S(2)}) collective-permute-start(bf16[768,512]{1,0:T(8,128)(2,1)S(1)} %get-tuple-element.122), channel_id=1, source_target_pairs={{0,1},{1,0},{2,3},{3,2},{4,5},{5,4},{6,7},{7,6},{8,9},{9,8},{10,11... | collective-permute-start | bytes 2359304 | tf_op jit(solution)/shard_map/ppermute | solution.py:521
  37.7 11.4 %collective-permute-start.7 = (bf16[384,512]{1,0:T(8,128)(2,1)S(1)}, bf16[384,512]{1,0:T(8,128)(2,1)S(1)}, u32[]{:S(2)}, u32[]{:S(2)}) collective-permute-start(bf16[384,512]{1,0:T(8,128)(2,1)S(1)} %get-tuple-element.123), channel_id=1, source_target_pairs={{0,2},{1,3},{2,0},{3,1},{4,6},{5,7},{6,4},{7,5},{8,10},{9,11},{10,... | collective-permute-start | bytes 1179656 | tf_op jit(solution)/shard_map/ppermute | solution.py:521
  38.3 13.3 %collective-permute-start.10 = (bf16[256,512]{1,0:T(8,128)(2,1)S(1)}, bf16[256,512]{1,0:T(8,128)(2,1)S(1)}, u32[]{:S(2)}, u32[]{:S(2)}) collective-permute-start(bf16[256,512]{1,0:T(8,128)(2,1)S(1)} %get-tuple-element.146), channel_id=1, source_target_pairs={{0,1},{1,0},{2,3},{3,2},{4,5},{5,4},{6,7},{7,6},{8,9},{9,8},{10,11... | collective-permute-start | bytes 786440 | tf_op jit(solution)/shard_map/ppermute | solution.py:521
  44.1 7.6 %collective-permute-start.9 = (bf16[256,512]{1,0:T(8,128)(2,1)S(1)}, bf16[256,512]{1,0:T(8,128)(2,1)S(1)}, u32[]{:S(2)}, u32[]{:S(2)}) collective-permute-start(bf16[256,512]{1,0:T(8,128)(2,1)S(1)} %get-tuple-element.145), channel_id=1, source_target_pairs={{0,1},{1,0},{2,3},{3,2},{4,5},{5,4},{6,7},{7,6},{8,9},{9,8},{10,11... | collective-permute-start | bytes 786440 | tf_op jit(solution)/shard_map/ppermute | solution.py:521
  44.6 4.5 %collective-permute-start.8 = (bf16[528,512]{1,0:T(8,128)(2,1)S(1)}, bf16[528,512]{1,0:T(8,128)(2,1)S(1)}, u32[]{:S(2)}, u32[]{:S(2)}) collective-permute-start(bf16[528,512]{1,0:T(8,128)(2,1)S(1)} %get-tuple-element.140), channel_id=1, source_target_pairs={{0,1},{1,0},{2,3},{3,2},{4,5},{5,4},{6,7},{7,6},{8,9},{9,8},{10,11... | collective-permute-start | bytes 1622024 | tf_op jit(solution)/shard_map/ppermute | solution.py:521
  49.5 9.4 %collective-permute-start.14 = (bf16[272,512]{1,0:T(8,128)(2,1)S(1)}, bf16[272,512]{1,0:T(8,128)(2,1)S(1)}, u32[]{:S(2)}, u32[]{:S(2)}) collective-permute-start(bf16[272,512]{1,0:T(8,128)(2,1)S(1)} %get-tuple-element.142), channel_id=1, source_target_pairs={{0,2},{1,3},{2,0},{3,1},{4,6},{5,7},{6,4},{7,5},{8,10},{9,11},{10,... | collective-permute-start | bytes 835592 | tf_op jit(solution)/shard_map/ppermute | solution.py:521
  50.1 8.7 %collective-permute-start.13 = (bf16[192,512]{1,0:T(8,128)(2,1)S(1)}, bf16[192,512]{1,0:T(8,128)(2,1)S(1)}, u32[]{:S(2)}, u32[]{:S(2)}) collective-permute-start(bf16[192,512]{1,0:T(8,128)(2,1)S(1)} %get-tuple-element.138), channel_id=1, source_target_pairs={{0,4},{1,5},{2,6},{3,7},{4,0},{5,1},{6,2},{7,3},{8,12},{9,13},{10,... | collective-permute-start | bytes 589832 | tf_op jit(solution)/shard_map/ppermute | solution.py:521
  51.8 7.1 %collective-permute-start.11 = (bf16[64,512]{1,0:T(8,128)(2,1)S(1)}, bf16[64,512]{1,0:T(8,128)(2,1)S(1)}, u32[]{:S(2)}, u32[]{:S(2)}) collective-permute-start(bf16[64,512]{1,0:T(8,128)(2,1)S(1)} %get-tuple-element.148), channel_id=1, source_target_pairs={{0,1},{1,2},{2,3},{3,4},{4,5},{5,6},{6,7},{7,8},{8,9},{9,10},{10,1... | collective-permute-start | bytes 196616 | tf_op jit(solution)/shard_map/ppermute | solution.py:735
  53.1 5.8 %collective-permute-start.12 = (bf16[64,512]{1,0:T(8,128)(2,1)S(1)}, bf16[64,512]{1,0:T(8,128)(2,1)S(1)}, u32[]{:S(2)}, u32[]{:S(2)}) collective-permute-start(bf16[64,512]{1,0:T(8,128)(2,1)S(1)} %get-tuple-element.149), channel_id=1, source_target_pairs={{1,0},{2,1},{3,2},{4,3},{5,4},{6,5},{7,6},{8,7},{9,8},{10,9},{11,1... | collective-permute-start | bytes 196616 | tf_op jit(solution)/shard_map/ppermute | solution.py:734
  54.4 15.2 %collective-permute-start.18 = (bf16[256,512]{1,0:T(8,128)(2,1)S(1)}, bf16[256,512]{1,0:T(8,128)(2,1)S(1)}, u32[]{:S(2)}, u32[]{:S(2)}) collective-permute-start(bf16[256,512]{1,0:T(8,128)(2,1)S(1)} %get-tuple-element.147), channel_id=1, source_target_pairs={{0,2},{1,3},{2,0},{3,1},{4,6},{5,7},{6,4},{7,5},{8,10},{9,11},{10,... | collective-permute-start | bytes 786440 | tf_op jit(solution)/shard_map/ppermute | solution.py:521
  59.2 17.9 %copy-start = (s32[1,16,2]{1,2,0:T(2,128)S(1)}, s32[1,16,2]{1,2,0:T(2,128)}, u32[]{:S(2)}) copy-start(s32[1,16,2]{1,2,0:T(2,128)} %param.32) | copy-start | bytes 388
  59.2 5.7 %collective-permute-start.15 = (bf16[144,512]{1,0:T(8,128)(2,1)S(1)}, bf16[144,512]{1,0:T(8,128)(2,1)S(1)}, u32[]{:S(2)}, u32[]{:S(2)}) collective-permute-start(bf16[144,512]{1,0:T(8,128)(2,1)S(1)} %get-tuple-element.156), channel_id=1, source_target_pairs={{0,4},{1,5},{2,6},{3,7},{4,0},{5,1},{6,2},{7,3},{8,12},{9,13},{10,... | collective-permute-start | bytes 442376 | tf_op jit(solution)/shard_map/ppermute | solution.py:521
  60.9 8.6 %collective-permute-start.17 = (bf16[96,512]{1,0:T(8,128)(2,1)S(1)}, bf16[96,512]{1,0:T(8,128)(2,1)S(1)}, u32[]{:S(2)}, u32[]{:S(2)}) collective-permute-start(bf16[96,512]{1,0:T(8,128)(2,1)S(1)} %get-tuple-element.152), channel_id=1, source_target_pairs={{0,8},{1,9},{2,10},{3,11},{4,12},{5,13},{6,14},{7,15},{8,0},{9,1},... | collective-permute-start | bytes 294920 | tf_op jit(solution)/shard_map/ppermute | solution.py:521
  69.6 7.3 %collective-permute-start.19 = (bf16[128,512]{1,0:T(8,128)(2,1)S(1)}, bf16[128,512]{1,0:T(8,128)(2,1)S(1)}, u32[]{:S(2)}, u32[]{:S(2)}) collective-permute-start(bf16[128,512]{1,0:T(8,128)(2,1)S(1)} %get-tuple-element.165), channel_id=1, source_target_pairs={{0,4},{1,5},{2,6},{3,7},{4,0},{5,1},{6,2},{7,3},{8,12},{9,13},{10,... | collective-permute-start | bytes 393224 | tf_op jit(solution)/shard_map/ppermute | solution.py:521
  69.7 7.4 %collective-permute-start.16 = (bf16[80,512]{1,0:T(8,128)(2,1)S(1)}, bf16[80,512]{1,0:T(8,128)(2,1)S(1)}, u32[]{:S(2)}, u32[]{:S(2)}) collective-permute-start(bf16[80,512]{1,0:T(8,128)(2,1)S(1)} %get-tuple-element.159), channel_id=1, source_target_pairs={{0,8},{1,9},{2,10},{3,11},{4,12},{5,13},{6,14},{7,15},{8,0},{9,1},... | collective-permute-start | bytes 245768 | tf_op jit(solution)/shard_map/ppermute | solution.py:521
  77.0 5.2 %collective-permute-start.20 = (bf16[64,512]{1,0:T(8,128)(2,1)S(1)}, bf16[64,512]{1,0:T(8,128)(2,1)S(1)}, u32[]{:S(2)}, u32[]{:S(2)}) collective-permute-start(bf16[64,512]{1,0:T(8,128)(2,1)S(1)} %get-tuple-element.167), channel_id=1, source_target_pairs={{0,8},{1,9},{2,10},{3,11},{4,12},{5,13},{6,14},{7,15},{8,0},{9,1},... | collective-permute-start | bytes 196616 | tf_op jit(solution)/shard_map/ppermute | solution.py:521

commit v7 on v6

--- a/solution.py
+++ b/solution.py
@@ -123,32 +123,18 @@
 
 
 def outgoing_kernel(
-    fast, index_hbm, node_hbm, slots_ref, send_ref, head_ref, tail_ref, index_ref, node_ref, sems
+    index_hbm, node_hbm, slots_ref, head_ref, tail_ref, index_ref, node_ref, sems
 ):
     for copy in fetch([(index_hbm, index_ref), (node_hbm, node_ref)], sems):
         copy.wait()
     places, tiles = index_ref.shape[1], index_ref.shape[2]
     nodes, latent = node_ref.shape
-    origin = lax.axis_index("tiles") if fast else 0
     place = lax.broadcasted_iota(jnp.int32, (nodes, tiles), 0)
-    owner, at = slot_owner(origin, (places * tiles, tiles), 0, places)
-    column = lax.broadcasted_iota(jnp.int32, (places * tiles, tiles), 1)
-    slots = jnp.zeros((places * tiles, latent), F32)
     for j in range(places):
         picks = ones_where(place == index_ref[0, j : j + 1, :])
-        listed = dot(picks, node_ref[...], TN).astype(BF16)
-        slots += dot(ones_where((owner == column) & (at == j)), listed)
-    slots = slots.astype(BF16)
-    slots_ref[...] = slots
-    send_ref[...] = slots_out(3, slots, places) if fast else jnp.zeros_like(send_ref)
+        slots_ref[:, j, :] = dot(picks, node_ref[...], TN).astype(BF16)
     head_ref[...] = node_ref[:NEAR, :]
     tail_ref[...] = node_ref[nodes - NEAR :, :]
-
-
-def shuffle_kernel(bit, places, slots_ref, got_ref, moved_ref, send_ref):
-    slots = slots_in(bit, slots_ref[...], got_ref[...], places)
-    moved_ref[...] = slots
-    send_ref[...] = slots_out(bit - 1, slots, places)
 
 
 def table_index(raw, origin, places, nodes):
@@ -160,21 +146,22 @@
     return jnp.where(raw >= nodes + 2 * NEAR, far, own)
 
 
-def weights_kernel(
+def prepare_kernel(
     places, fast,
-    node_hbm, w1_hbm, sender_hbm, receiver_hbm,
-    w1_ref, node_ref, receiver_ref, moved_ref, weights,
-    sender_ref, sems,
+    node_hbm, w1_hbm, sender_hbm, receiver_hbm, b1_hbm, edge_hbm,
+    edge_ref, w1_ref, node_ref, receiver_ref, moved_ref, partial_ref,
+    weights, sender_ref, b1_ref, sems, edge_sems,
 ):
-    latent = node_ref.shape[1]
+    edges, latent = edge_ref.shape
     nodes = node_ref.shape[0]
     copies = fetch(
         [
             (node_hbm, node_ref), (w1_hbm, w1_ref), (sender_hbm, sender_ref),
-            (receiver_hbm, receiver_ref),
+            (receiver_hbm, receiver_ref), (b1_hbm, b1_ref),
         ],
         sems,
     )
+    edge_copies = fetch(tile_pairs(edge_hbm, edge_ref, edges // 2), edge_sems)
     for copy in copies:
         copy.wait()
     origin = lax.axis_index("tiles") if fast else 0
@@ -184,21 +171,12 @@
         node_ref[...], w1_ref[latent : 2 * latent, :]
     ).astype(BF16)
     weights[latent + nodes :, :] = dot(node_ref[...], w1_ref[2 * latent :, :]).astype(BF16)
-
-
-def prepare_kernel(
-    first, b1_hbm, edge_hbm, moved_ref, receiver_ref, weights, edge_ref, partial_ref,
-    b1_ref, sems,
-):
-    edges, latent = edge_ref.shape
-    nodes = weights.shape[0] - latent >> 1
-    start = pl.ds(first * TILE, edges)
-    for copy in fetch([(b1_hbm, b1_ref), (edge_hbm.at[start], edge_ref)], sems):
+    for copy in edge_copies:
         copy.wait()
     for step in range(edges // TILE):
         tile = slice(step * TILE, (step + 1) * TILE)
-        senders = pick_columns(index_columns(moved_ref, first + step, TILE), 0, nodes)
-        receivers = pick_columns(index_columns(receiver_ref, first + step, TILE), 0, nodes)
+        senders = pick_columns(index_columns(moved_ref, step, TILE), 0, nodes)
+        receivers = pick_columns(index_columns(receiver_ref, step, TILE), 0, nodes)
         inputs = jnp.concatenate([edge_ref[tile, :]] + senders + receivers, axis=1)
         partial_ref[tile, :] = dot(inputs, weights[...]) + b1_ref[...]
 
@@ -207,8 +185,7 @@
     tiles, places, fast,
     w2_hbm, nw1_hbm, nw2_hbm, ncot_hbm,
     b2_hbm, gain_hbm, nb1_hbm, nb2_hbm, ngain_hbm, count_hbm,
-    lower_ref, upper_ref, slots_ref, got_ref, early_ref, later_ref,
-    w1_ref, node_ref, receiver_ref, moved_ref,
+    lower_ref, upper_ref, slots_ref, known_ref, w1_ref, node_ref, receiver_ref, moved_ref,
     w2_ref, gain_ref,
     hidden_ref, slope_ref, normed_ref, inverse_ref, table_ref, dsum_ref, base_ref,
     gsend_ref, gkeep_ref,
@@ -235,10 +212,12 @@
     table_ref[:nodes, :] = node_ref[...]
     table_ref[nodes : nodes + NEAR, :] = lower_ref[...]
     table_ref[nodes + NEAR : nodes + 2 * NEAR, :] = upper_ref[...]
-    slots = slots_ref[...]
-    if fast:
-        slots = slots_in(0, slots, got_ref[...], places)
-    table_ref[nodes + 2 * NEAR : nodes + 2 * NEAR + places * tiles, :] = slots
+    owner, at = slot_owner(here if fast else 0, (places * tiles, tiles), 0, places)
+    source = lax.broadcasted_iota(jnp.int32, (places * tiles, tiles), 1)
+    slots = jnp.zeros((places * tiles, latent), F32)
+    for j in range(places):
+        slots += dot(ones_where((owner == source) & (at == j)), slots_ref[:, j, :])
+    table_ref[nodes + 2 * NEAR : nodes + 2 * NEAR + places * tiles, :] = slots.astype(BF16)
     used = nodes + 2 * NEAR + places * tiles
     if used < rows:
         table_ref[used:, :] = jnp.zeros((rows - used, latent), BF16)
@@ -250,12 +229,7 @@
     def activate(step):
         tile = slice(step * TILE, (step + 1) * TILE)
         senders = pick_columns(index_columns(moved_ref, step, TILE), nodes, rows)
-        part = early_ref.shape[0]
-        if step * TILE < part:
-            known = early_ref[tile, :]
-        else:
-            known = later_ref[step * TILE - part : (step + 1) * TILE - part, :]
-        preact = known + dot(jnp.concatenate(senders, axis=1), weights[...])
+        preact = known_ref[tile, :] + dot(jnp.concatenate(senders, axis=1), weights[...])
         sig = sigmoid(preact)
         slope_ref[tile, :] = (sig * (1.0 + preact * (1.0 - sig))).astype(BF16)
         hidden_ref[tile, :] = (preact * sig).astype(BF16)
@@ -357,7 +331,7 @@
 
 def first_kernel(
     tiles, places, fast,
-    dpre_ref, early_ref, later_ref, sender_ref, receiver_ref, table_ref, node_ref, w1_ref, base_ref,
+    dpre_ref, edge_ref, sender_ref, receiver_ref, table_ref, node_ref, w1_ref, base_ref,
     *refs,
 ):
     out_refs, (grads, sums) = refs[:-2], refs[-2:]
@@ -366,16 +340,11 @@
     edges, latent = dpre_ref.shape
     nodes = node_ref.shape[0]
     rows = table_ref.shape[0]
-    early = early_ref.shape[0]
 
     for step in range(edges // TILE):
         tile = slice(step * TILE, (step + 1) * TILE)
         dpre = dpre_ref[tile, :]
-        if step * TILE < early:
-            edge = early_ref[tile, :]
-        else:
-            edge = later_ref[step * TILE - early : (step + 1) * TILE - early, :]
-        part = dot(edge, dpre, TN)
+        part = dot(edge_ref[tile, :], dpre, TN)
         picks = jnp.concatenate(
             [
                 pick_rows(sender_ref, step, TILE, rows),
@@ -402,7 +371,7 @@
         bit = lax.rem(here, 2)
         block = 3 * latent // tiles
         at = 0
-        for send_ref, keep_ref in (out_refs[4:6], out_refs[6:8]):
+        for send_ref, keep_ref in (out_refs[4:6], out_refs[6:8], out_refs[8:10]):
             part = keep_ref.shape[1]
             split_halves(bit, grads, 0, block, at, part, send_ref, keep_ref, 0)
             at += part
@@ -580,12 +549,11 @@
     else:
         grad_shapes = lambda count: [shaped((latent, latent), F32), shaped((count, latent), F32)]
 
-    outgoing, send, head, tail = call(
-        functools.partial(outgoing_kernel, fast),
+    outgoing, head, tail = call(
+        outgoing_kernel,
         "outgoing",
         [
-            vmem((tiles * places, latent), BF16) if fast else shaped((tiles * places, latent), BF16),
-            vmem((tiles * places // 2, latent), BF16),
+            shaped((tiles, places, latent), BF16),
             vmem((NEAR, latent), BF16),
             vmem((NEAR, latent), BF16),
         ],
@@ -593,55 +561,25 @@
         hbm=2,
         scratch=[vmem(listed.shape, jnp.int32), vmem((nodes, latent), BF16), pltpu.SemaphoreType.DMA((2,))],
     )
-    if fast:
-        far_got = swap(tiles, 8, send)
     lower = lax.ppermute(tail, "tiles", upward)
     upper = lax.ppermute(head, "tiles", downward)
-    w1_kept, node_kept, receiver_kept, moved, weights = call(
-        functools.partial(weights_kernel, places, fast),
-        "weights",
+    slots = lax.all_to_all(outgoing, "tiles", split_axis=0, concat_axis=0, tiled=True)
+    edge_kept, w1_kept, node_kept, receiver_kept, moved, preact = call(
+        functools.partial(prepare_kernel, places, fast),
+        "prepare",
         [
-            vmem(edge_w1.shape, BF16), vmem((nodes, latent), BF16),
+            vmem((edges, latent), BF16), vmem(edge_w1.shape, BF16), vmem((nodes, latent), BF16),
             vmem(receiver.shape, jnp.int32), vmem(sender.shape, jnp.int32),
-            vmem((latent + 2 * nodes, latent), BF16),
+            vmem((edges, latent), F32),
         ],
-        [node_latent, edge_w1, after(sender, send), receiver],
-        hbm=4,
-        scratch=[vmem(sender.shape, jnp.int32), pltpu.SemaphoreType.DMA((4,))],
-    )
-
-    def prepare(first, moved):
-        return call(
-            functools.partial(prepare_kernel, first),
-            "prepare",
-            [vmem((edges // 2, latent), BF16), vmem((edges // 2, latent), F32)],
-            [row(edge_b1), edge_latent, moved, receiver_kept, weights],
-            hbm=2,
-            scratch=[vmem((1, latent), F32), pltpu.SemaphoreType.DMA((2,))],
-        )
-
-    def shuffle(bit, slots, got):
-        return call(
-            functools.partial(shuffle_kernel, bit, places),
-            "shuffle",
-            [vmem(slots.shape, BF16), vmem(got.shape, BF16)],
-            [slots, got],
-        )
-
-    if fast:
-        slots, send = shuffle(3, after(outgoing, moved), far_got)
-        got = swap(tiles, 4, send)
-        edge_early, early = prepare(0, after(moved, send))
-        slots, send = shuffle(2, after(slots, early), got)
-        got = swap(tiles, 2, send)
-        edge_later, later = prepare(steps // 2, after(moved, send))
-        slots, send = shuffle(1, after(slots, later), got)
-        got = swap(tiles, 1, send)
-    else:
-        edge_early, early = prepare(0, moved)
-        edge_later, later = prepare(steps // 2, moved)
-        slots = lax.all_to_all(outgoing, "tiles", split_axis=0, concat_axis=0, tiled=True)
-        got = slots
+        [node_latent, edge_w1, after(sender, outgoing), receiver, row(edge_b1), edge_latent],
+        hbm=6,
+        scratch=[
+            vmem((latent + 2 * nodes, latent), BF16), vmem(sender.shape, jnp.int32),
+            vmem((1, latent), F32), pltpu.SemaphoreType.DMA((5,)), pltpu.SemaphoreType.DMA((2,)),
+        ],
+        flops=AHEAD,
+    )
 
     (
         w2_kept, gain_kept,
@@ -658,7 +596,7 @@
         [
             edge_w2, node_w1, node_w2, node_cot,
             row(edge_b2), row(edge_gain), row(node_b1), row(node_b2), row(node_gain), edge_count,
-            lower, upper, slots, got, early, later, w1_kept, node_kept, receiver_kept, moved,
+            lower, upper, slots, preact, w1_kept, node_kept, receiver_kept, moved,
         ],
         hbm=10,
         scratch=[
@@ -670,6 +608,10 @@
         ],
     )
 
+    if fast:
+        send, chain = halve(1, [node_keep], [swap(tiles, 1, node_send)])
+        dsum = after(dsum, send)
+        got = swap(tiles, 2, send)
     cot_kept, dpre, second_send, second_keep = call(
         functools.partial(slope_kernel, tiles, fast),
         "slope",
@@ -681,20 +623,7 @@
         ],
     )
     if fast:
-        send, chain = halve(1, [after(node_keep, dpre)], [swap(tiles, 1, node_send)])
-        dpre = after(dpre, send)
-        got = swap(tiles, 2, send)
         got_second = swap(tiles, 1, second_send)
-
-    (grad_edge,) = call(
-        edge_kernel,
-        "edge",
-        [shaped((edges, latent), BF16)],
-        [dpre, cot_kept, w1_kept],
-        out_specs=[pl.BlockSpec(memory_space=pltpu.HBM)],
-        scratch=[vmem((edges, latent), BF16), pltpu.SemaphoreType.DMA((steps,))],
-    )
-    dpre = after(dpre, grad_edge)
 
     per = latent // tiles
     to_lower, to_upper, to_far, partial, *first = call(
@@ -707,43 +636,57 @@
             vmem((nodes, latent), F32),
         ] + (
             [
-                vmem((2 * half * per + tiles * places // 2, latent), BF16),
-                vmem((half, 2 * per, latent), F32),
+                vmem((half * per + tiles * places // 2, latent), BF16),
+                vmem((half, per, latent), F32),
+                vmem((half * per, latent), BF16), vmem((half, per, latent), F32),
                 vmem((half * per, latent), BF16), vmem((half, per, latent), F32),
             ]
             if fast else [shaped((3 * latent, latent), F32)]
         ),
-        [dpre, edge_early, edge_later, moved, receiver_kept, table, node_kept, w1_kept, base],
+        [dpre, edge_kept, moved, receiver_kept, table, node_kept, w1_kept, base],
         scratch=[vmem((3 * latent, latent), F32), vmem((rows + nodes, latent), F32)],
     )
 
+    (grad_edge,) = call(
+        edge_kernel,
+        "edge",
+        [shaped((edges, latent), BF16)],
+        [after(dpre, partial), cot_kept, w1_kept],
+        out_specs=[pl.BlockSpec(memory_space=pltpu.HBM)],
+        scratch=[vmem((edges, latent), BF16), pltpu.SemaphoreType.DMA((steps,))],
+    )
+
     if fast:
-        send_a, keep_a, send_b, keep_b = first
-        send, chain = halve(2, [after(chain, partial)], [got], flops=AHEAD)
+        send_a, keep_a, send_more, keep_more, send_b, keep_b = first
+        send, chain = halve(2, [after(chain, grad_edge)], [got])
         got = swap(tiles, 4, send)
         send_a, chain_a, slots = halve(
-            1, [after(keep_a, send)], [swap(tiles, 1, send_a)], to_far, places
-        )
+            1,
+            [after(keep_a, send), keep_more],
+            [swap(tiles, 1, send_a), swap(tiles, 1, send_more)],
+            to_far,
+            places,
+     )
         got_a = swap(tiles, 2, send_a)
         send_b, chain_b = halve(
             1, [after(keep_b, send_a), second_keep], [swap(tiles, 1, send_b), got_second]
-        )
+     )
         got_b = swap(tiles, 2, send_b)
+
         to_lower, to_upper = lax.optimization_barrier((to_lower, to_upper, send_b))[:2]
-
-    above = lax.ppermute(to_lower, "tiles", downward)
-    below = lax.ppermute(to_upper, "tiles", upward)
-    if fast:
-        send, chain = halve(3, [chain], [got])
+        above = lax.ppermute(to_lower, "tiles", downward)
+        below = lax.ppermute(to_upper, "tiles", upward)
+        send, chain = halve(3, [after(chain, above, below)], [got])
         got = swap(tiles, 8, send)
-        chain_a = lax.optimization_barrier((chain_a, send, above, below))[0]
-        send_a, chain_a, slots = halve(2, [chain_a], [got_a], slots, places, AHEAD)
+        send_a, chain_a, slots = halve(2, [after(chain_a, send)], [got_a], slots, places)
         got_a = swap(tiles, 4, send_a)
-        send_a, chain_a, slots = halve(3, [chain_a], [got_a], slots, places)
+        send_b, chain_b = halve(2, [after(chain_b, send_a)], [got_b], flops=AHEAD)
+        got_b = swap(tiles, 4, send_b)
+        chain_a = lax.optimization_barrier((chain_a, send_b, got))[0]
+        send_a, chain_a, slots = halve(3, [chain_a], [got_a], slots, places, AHEAD)
         got_a = swap(tiles, 8, send_a)
-        send_b, chain_b = halve(2, [after(chain_b, send_a, got)], [got_b])
-        got_b = swap(tiles, 4, send_b)
-        send_b, chain_b = halve(3, [chain_b], [got_b])
+        chain_b = after(chain_b, send_a)
+        send_b, chain_b = halve(3, [chain_b], [got_b], flops=AHEAD)
         got_b = swap(tiles, 8, send_b)
         returned = [slots, got_a]
         grad_edge_w1, grad_edge_w2, grad_node_w1, grad_node_w2 = finish(
@@ -753,6 +696,8 @@
             [3 * per, per, 2 * per, per],
         )
     else:
+        above = lax.ppermute(to_lower, "tiles", downward)
+        below = lax.ppermute(to_upper, "tiles", upward)
         returned = [lax.all_to_all(to_far, "tiles", split_axis=0, concat_axis=0, tiled=True)]
         scatter = functools.partial(
             lax.psum_scatter, axis_name="tiles", scatter_dimension=0, tiled=True

time: 83.3 us -> 82 us (0.984); the launches traced: 83 us -> 80.5 us
  waiting for transfers between devices: 24.6 us -> 17.7 us
  local copies, waits for them, and re-layouts: 0.01 us -> 3.52 us
  starting transfers between devices: 26.7 us -> 29.8 us
  Pallas kernels: 30.8 us -> 28.6 us
    ppermute x17 -> x14, waiting for transfers between devices: 24.6 us -> 14.2 us  [swap(): return lax.ppermute(send, 'tiles', [(i, i ^ bit) for i in range(tiles)])]
    all_to_all x0 -> x1, starting transfers between devices: none -> 7.37 us  [shards(): lax.all_to_all(outgoing, 'tiles', split_axis=0, concat_axis=0, tiled=True)]
    ppermute x17 -> x14, starting transfers between devices: 21.3 us -> 16.3 us  [swap(): return lax.ppermute(send, 'tiles', [(i, i ^ bit) for i in range(tiles)])]
    ppermute x1, waiting for transfers between devices: 0.01 us -> 3.53 us  [shards(): above = lax.ppermute(to_lower, 'tiles', downward)]
    unnamed x2 -> x6, local copies, waits for them, and re-layouts: 0.01 us -> 3.52 us
    pallas_call x22 -> x17, Pallas kernels: 30.8 us -> 28.6 us  [call(): pl.pallas_call(kernel, in_specs=[pl.BlockSpec(memory_space=pltpu.HBM)] *...]
    ppermute x1, starting transfers between devices: 1.44 us -> 2.3 us  [shards(): lower = lax.ppermute(tail, 'tiles', upward)]
  transfers between devices with their start and end apart: 21 -> 19, of which waited for: 7 -> 7; matrix products, arithmetic and copies ran while one was open for 0% -> 0% of each run, Pallas kernels for 24% -> 21%
where the time goes in v7:
time: 82 us; the launch traced here: 80.5 us
  starting transfers between devices  29.8 us (36%)
  Pallas kernels  28.6 us (35%)
  waiting for transfers between devices  17.7 us (22%)
  local copies, waits for them, and re-layouts  3.52 us (4%)
    pallas_call x17, Pallas kernels, call(): pl.pallas_call(kernel, in_specs=[pl.BlockSpec(memory_space=pltpu.HBM)] *...  28.6 us
    ppermute x14, starting transfers between devices, swap(): return lax.ppermute(send, 'tiles', [(i, i ^ bit) for i in range(tiles)])  16.3 us
    ppermute x14, waiting for transfers between devices, swap(): return lax.ppermute(send, 'tiles', [(i, i ^ bit) for i in range(tiles)])  14.2 us
    all_to_all x1, starting transfers between devices, shards(): lax.all_to_all(outgoing, 'tiles', split_axis=0, concat_axis=0, tiled=True)  7.37 us
    ppermute x1, waiting for transfers between devices, shards(): above = lax.ppermute(to_lower, 'tiles', downward)  3.53 us
    unnamed x6, local copies, waits for them, and re-layouts  3.52 us
    ppermute x1, starting transfers between devices, shards(): lower = lax.ppermute(tail, 'tiles', upward)  2.3 us
  transfers between devices with their start and end apart: 19, of which 7 were waited for; matrix products, arithmetic and copies ran while one was open for 0% of the time, Pallas kernels for 21%

profile of v7, /device:TPU:0, one launch (start us, length us, event | category | flops | bytes accessed | tf_op | source)
XLA Modules:
  0.0 80.5 jit_solution(4234969135805513979)
XLA Ops:
  0.6 1.8 %outgoing.1 = (bf16[16,2,512]{2,1,0:T(2,128)(2,1)}, bf16[64,512]{1,0:T(8,128)(2,1)}, bf16[64,512]{1,0:T(8,128)(2,1)}) custom-call(s32[1,2,16]{2,1,0:T(2,128)} %bitcast.9, bf16[256,512]{1,0:T(8,128)(2,1)} %node_hbm.3), custom_call_target="tpu_custom_call" | custom-call | tf_op jit(solution)/shard_map/outgoing/pallas_call | solution.py:477
  2.5 7.4 %all-to-all-start = ((bf16[16,2,512]{2,1,0:T(2,128)(2,1)}), bf16[16,2,512]{2,1,0:T(2,128)(2,1)S(1)}, u32[]{:S(2)}, u32[]{:S(2)}) async-start(bf16[16,2,512]{2,1,0:T(2,128)(2,1)} %get-tuple-element.78), calls=%async_computation | async-start | bytes 65536 | tf_op jit(solution)/shard_map/all_to_all | solution.py:566
  9.8 2.3 %collective-permute-start = (bf16[64,512]{1,0:T(8,128)(2,1)}, bf16[64,512]{1,0:T(8,128)(2,1)S(1)}, u32[]{:S(2)}, u32[]{:S(2)}) collective-permute-start(bf16[64,512]{1,0:T(8,128)(2,1)} %get-tuple-element.81), channel_id=1, source_target_pairs={{0,1},{1,2},{2,3},{3,4},{4,5},{5,6},{6,7},{7,8},{8,9},{9,10},{10,1... | collective-permute-start | bytes 196616 | tf_op jit(solution)/shard_map/ppermute | solution.py:564
  12.1 1.3 %collective-permute-start.1 = (bf16[64,512]{1,0:T(8,128)(2,1)}, bf16[64,512]{1,0:T(8,128)(2,1)}, u32[]{:S(2)}, u32[]{:S(2)}) collective-permute-start(bf16[64,512]{1,0:T(8,128)(2,1)} %get-tuple-element.82), channel_id=1, source_target_pairs={{1,0},{2,1},{3,2},{4,3},{5,4},{6,5},{7,6},{8,7},{9,8},{10,9},{11,1... | collective-permute-start | bytes 196616 | tf_op jit(solution)/shard_map/ppermute | solution.py:565
  13.4 3.9 %prepare.1 = (bf16[1536,512]{1,0:T(8,128)(2,1)S(1)}, bf16[1536,512]{1,0:T(8,128)(2,1)S(1)}, bf16[256,512]{1,0:T(8,128)(2,1)S(1)}, s32[12,128]{1,0:T(8,128)S(1)},...) custom-call(bf16[256,512]{1,0:T(8,128)(2,1)} %node_hbm.3, bf16[1536,512]{1,0:T(8,128)(2,1)} %w1_hbm.1, ...), custom_call_target="tpu_custom_call" | custom-call | flops 10000000000 | bytes 100000000 | tf_op jit(solution)/shard_map/prepare/pallas_call | solution.py:477
  17.3 1.6 %copy-done = f32[1536,512]{1,0:T(8,128)} copy-done((f32[1536,512]{1,0:T(8,128)}, f32[1536,512]{1,0:T(8,128)S(1)}, u32[]{:S(2)}) %copy-start) | copy-done | bytes 3145752
  19.0 1.9 %copy-done.1 = f32[1536,512]{1,0:T(8,128)S(1)} copy-done((f32[1536,512]{1,0:T(8,128)S(1)}, f32[1536,512]{1,0:T(8,128)}, u32[]{:S(2)}) %copy-start.1) | copy-done | bytes 3145752
  20.9 8.9 %forward.1 = (bf16[512,512]{1,0:T(8,128)(2,1)S(1)}, f32[1,512]{1,0:T(1,128)S(1)}, bf16[1536,512]{1,0:T(8,128)(2,1)S(1)}, bf16[1536,512]{1,0:T(8,128)(2,1)S(1)}, ...) custom-call(bf16[512,512]{1,0:T(8,128)(2,1)} %w2_hbm.1, ...), custom_call_target="tpu_custom_call" | custom-call | tf_op jit(solution)/shard_map/forward/pallas_call | solution.py:477
  29.8 2.4 %collective-permute-start.2 = (bf16[768,512]{1,0:T(8,128)(2,1)S(1)}, bf16[768,512]{1,0:T(8,128)(2,1)S(1)}, u32[]{:S(2)}, u32[]{:S(2)}) collective-permute-start(bf16[768,512]{1,0:T(8,128)(2,1)S(1)} %get-tuple-element.89), channel_id=1, source_target_pairs={{0,1},{1,0},{2,3},{3,2},{4,5},{5,4},{6,7},{7,6},{8,9},{9,8},{10,11... | collective-permute-start | bytes 2359304 | tf_op jit(solution)/shard_map/ppermute | solution.py:490
  32.1 1.9 %collective-permute-done.2.refs_1_ = bf16[768,512]{1,0:T(8,128)(2,1)S(1)} collective-permute-done((bf16[768,512]{1,0:T(8,128)(2,1)S(1)}, bf16[768,512]{1,0:T(8,128)(2,1)S(1)}, u32[]{:S(2)}, u32[]{:S(2)}) %collective-permute-start.2) | collective-permute-done | bytes 786464 | tf_op jit(solution)/shard_map/ppermute | solution.py:490
  34.2 2.0 %collective-permute-start.3 = (bf16[384,512]{1,0:T(8,128)(2,1)S(1)}, bf16[384,512]{1,0:T(8,128)(2,1)S(1)}, u32[]{:S(2)}, u32[]{:S(2)}) collective-permute-start(bf16[384,512]{1,0:T(8,128)(2,1)S(1)} %get-tuple-element.90), channel_id=1, source_target_pairs={{0,2},{1,3},{2,0},{3,1},{4,6},{5,7},{6,4},{7,5},{8,10},{9,11},{10,... | collective-permute-start | bytes 1179656 | tf_op jit(solution)/shard_map/ppermute | solution.py:490
  36.2 4.7 %slope.1 = (bf16[1536,512]{1,0:T(8,128)(2,1)S(1)}, bf16[1536,512]{1,0:T(8,128)(2,1)S(1)}, bf16[256,512]{1,0:T(8,128)(2,1)S(1)}, f32[8,32,512]{2,1,0:T(8,128)S(1)}) custom-call(bf16[1536,512]{1,0:T(8,128)(2,1)} %cot_hbm.1, s32[12,128]{1,0:T(8,128)S(1)} %get-tuple-element.80.receiver_ref, bf16[256,512]{1,0:T(8,128)(2,1)S(1)} %get-tuple-element.91.dsum_ref, ...), custom_call_target="tpu_custom_call" | custom-call | tf_op jit(solution)/shard_map/slope/pallas_call | solution.py:477
  41.0 3.9 %first.1 = (bf16[64,512]{1,0:T(8,128)(2,1)S(1)}, bf16[64,512]{1,0:T(8,128)(2,1)S(1)}, bf16[32,512]{1,0:T(8,128)(2,1)S(1)}, f32[256,512]{1,0:T(8,128)S(1)}, bf16[...) custom-call(bf16[1536,512]{1,0:T(8,128)(2,1)S(1)} %get-tuple-element, ...), custom_call_target="tpu_custom_call" | custom-call | tf_op jit(solution)/shard_map/first/pallas_call | solution.py:477
  46.0 1.8 %edge.1 = bf16[1536,512]{1,0:T(8,128)(2,1)} custom-call(bf16[1536,512]{1,0:T(8,128)(2,1)S(1)} %get-tuple-element.108.dpre_ref, bf16[1536,512]{1,0:T(8,128)(2,1)S(1)} %get-tuple-element.109.cot_ref, bf16[1536,512]{1,0:T(8,128)(2,1)S(1)} %get-tuple-element.84.w1_ref), custom_call_target="tpu_custom_call" | custom-call | tf_op jit(solution)/shard_map/edge/pallas_call | solution.py:477
  48.4 2.0 %collective-permute-start.12 = (bf16[256,512]{1,0:T(8,128)(2,1)S(1)}, bf16[256,512]{1,0:T(8,128)(2,1)S(1)}, u32[]{:S(2)}, u32[]{:S(2)}) collective-permute-start(bf16[256,512]{1,0:T(8,128)(2,1)S(1)} %get-tuple-element.122), channel_id=1, source_target_pairs={{0,2},{1,3},{2,0},{3,1},{4,6},{5,7},{6,4},{7,5},{8,10},{9,11},{10,... | collective-permute-start | bytes 786440 | tf_op jit(solution)/shard_map/ppermute | solution.py:490
  50.5 1.5 %collective-permute-start.10 = (bf16[192,512]{1,0:T(8,128)(2,1)S(1)}, bf16[192,512]{1,0:T(8,128)(2,1)S(1)}, u32[]{:S(2)}, u32[]{:S(2)}) collective-permute-start(bf16[192,512]{1,0:T(8,128)(2,1)S(1)} %get-tuple-element.111), channel_id=1, source_target_pairs={{0,4},{1,5},{2,6},{3,7},{4,0},{5,1},{6,2},{7,3},{8,12},{9,13},{10,... | collective-permute-start | bytes 589832 | tf_op jit(solution)/shard_map/ppermute | solution.py:490
  54.5 3.5 %collective-permute-done.9.above_ref = bf16[64,512]{1,0:T(8,128)(2,1)S(1)} collective-permute-done((bf16[64,512]{1,0:T(8,128)(2,1)S(1)}, bf16[64,512]{1,0:T(8,128)(2,1)S(1)}, u32[]{:S(2)}, u32[]{:S(2)}) %collective-permute-start.9) | collective-permute-done | bytes 65568 | tf_op jit(solution)/shard_map/ppermute | solution.py:677
  58.1 4.6 %collective-permute-start.13 = (bf16[96,512]{1,0:T(8,128)(2,1)S(1)}, bf16[96,512]{1,0:T(8,128)(2,1)S(1)}, u32[]{:S(2)}, u32[]{:S(2)}) collective-permute-start(bf16[96,512]{1,0:T(8,128)(2,1)S(1)} %get-tuple-element.128), channel_id=1, source_target_pairs={{0,8},{1,9},{2,10},{3,11},{4,12},{5,13},{6,14},{7,15},{8,0},{9,1},... | collective-permute-start | bytes 294920 | tf_op jit(solution)/shard_map/ppermute | solution.py:490
  63.7 1.5 %collective-permute-start.16 = (bf16[128,512]{1,0:T(8,128)(2,1)S(1)}, bf16[128,512]{1,0:T(8,128)(2,1)S(1)}, u32[]{:S(2)}, u32[]{:S(2)}) collective-permute-start(bf16[128,512]{1,0:T(8,128)(2,1)S(1)} %get-tuple-element.135), channel_id=1, source_target_pairs={{0,4},{1,5},{2,6},{3,7},{4,0},{5,1},{6,2},{7,3},{8,12},{9,13},{10,... | collective-permute-start | bytes 393224 | tf_op jit(solution)/shard_map/ppermute | solution.py:490
  66.4 3.2 %collective-permute-done.14.refs_1_ = bf16[144,512]{1,0:T(8,128)(2,1)S(1)} collective-permute-done((bf16[144,512]{1,0:T(8,128)(2,1)S(1)}, bf16[144,512]{1,0:T(8,128)(2,1)S(1)}, u32[]{:S(2)}, u32[]{:S(2)}) %collective-permute-start.14) | collective-permute-done | bytes 147488 | tf_op jit(solution)/shard_map/ppermute | solution.py:490
  69.9 2.5 %collective-permute-done.16.refs_1_ = bf16[128,512]{1,0:T(8,128)(2,1)S(1)} collective-permute-done((bf16[128,512]{1,0:T(8,128)(2,1)S(1)}, bf16[128,512]{1,0:T(8,128)(2,1)S(1)}, u32[]{:S(2)}, u32[]{:S(2)}) %collective-permute-start.16) | collective-permute-done | bytes 131104 | tf_op jit(solution)/shard_map/ppermute | solution.py:490
  72.9 2.5 %collective-permute-done.15.refs_0_.refs_4_ = bf16[80,512]{1,0:T(8,128)(2,1)S(1)} collective-permute-done((bf16[80,512]{1,0:T(8,128)(2,1)S(1)}, bf16[80,512]{1,0:T(8,128)(2,1)S(1)}, u32[]{:S(2)}, u32[]{:S(2)}) %collective-permute-start.15) | collective-permute-done | bytes 81952 | tf_op jit(solution)/shard_map/ppermute | solution.py:490
  75.5 1.4 %node.1 = bf16[256,512]{1,0:T(8,128)(2,1)} custom-call(s32[1,2,16]{2,1,0:T(2,128)S(1)} %bitcast.10, f32[256,512]{1,0:T(8,128)S(1)} %get-tuple-element.102.partial_ref, bf16[64,512]{1,0:T(8,128)(2,1)S(1)} %collective-permute-done.8.below_ref, bf16[64,512]{1,0:T(8,128)(2,1)S(1)} %collective-permute-done.9.above_ref, ...), custom_call_target="tpu_custom_call" | custom-call | tf_op jit(solution)/shard_map/node/pallas_call | solution.py:477
  76.9 2.8 %collective-permute-done.17.refs_5_ = bf16[64,512]{1,0:T(8,128)(2,1)S(1)} collective-permute-done((bf16[64,512]{1,0:T(8,128)(2,1)S(1)}, bf16[64,512]{1,0:T(8,128)(2,1)S(1)}, u32[]{:S(2)}, u32[]{:S(2)}) %collective-permute-start.17) | collective-permute-done | bytes 65568 | tf_op jit(solution)/shard_map/ppermute | solution.py:490
  (37 shorter events, 8.2 us)
Async XLA Ops:
  2.5 16.5 %all-to-all-start = ((bf16[16,2,512]{2,1,0:T(2,128)(2,1)}), bf16[16,2,512]{2,1,0:T(2,128)(2,1)S(1)}, u32[]{:S(2)}, u32[]{:S(2)}) async-start(bf16[16,2,512]{2,1,0:T(2,128)(2,1)} %get-tuple-element.78), calls=%async_computation | async-start | bytes 65536 | tf_op jit(solution)/shard_map/all_to_all | solution.py:566
  9.8 9.1 %collective-permute-start = (bf16[64,512]{1,0:T(8,128)(2,1)}, bf16[64,512]{1,0:T(8,128)(2,1)S(1)}, u32[]{:S(2)}, u32[]{:S(2)}) collective-permute-start(bf16[64,512]{1,0:T(8,128)(2,1)} %get-tuple-element.81), channel_id=1, source_target_pairs={{0,1},{1,2},{2,3},{3,4},{4,5},{5,6},{6,7},{7,8},{8,9},{9,10},{10,1... | collective-permute-start | bytes 196616 | tf_op jit(solution)/shard_map/ppermute | solution.py:564
  12.1 6.8 %collective-permute-start.1 = (bf16[64,512]{1,0:T(8,128)(2,1)}, bf16[64,512]{1,0:T(8,128)(2,1)}, u32[]{:S(2)}, u32[]{:S(2)}) collective-permute-start(bf16[64,512]{1,0:T(8,128)(2,1)} %get-tuple-element.82), channel_id=1, source_target_pairs={{1,0},{2,1},{3,2},{4,3},{5,4},{6,5},{7,6},{8,7},{9,8},{10,9},{11,1... | collective-permute-start | bytes 196616 | tf_op jit(solution)/shard_map/ppermute | solution.py:565
  17.3 1.6 %copy-start = (f32[1536,512]{1,0:T(8,128)}, f32[1536,512]{1,0:T(8,128)S(1)}, u32[]{:S(2)}) copy-start(f32[1536,512]{1,0:T(8,128)S(1)} %get-tuple-element.83.known_ref) | copy-start | bytes 9437188
  19.0 1.9 %copy-start.1 = (f32[1536,512]{1,0:T(8,128)S(1)}, f32[1536,512]{1,0:T(8,128)}, u32[]{:S(2)}) copy-start(f32[1536,512]{1,0:T(8,128)} %copy-done) | copy-start | bytes 9437188
  29.8 4.3 %collective-permute-start.2 = (bf16[768,512]{1,0:T(8,128)(2,1)S(1)}, bf16[768,512]{1,0:T(8,128)(2,1)S(1)}, u32[]{:S(2)}, u32[]{:S(2)}) collective-permute-start(bf16[768,512]{1,0:T(8,128)(2,1)S(1)} %get-tuple-element.89), channel_id=1, source_target_pairs={{0,1},{1,0},{2,3},{3,2},{4,5},{5,4},{6,7},{7,6},{8,9},{9,8},{10,11... | collective-permute-start | bytes 2359304 | tf_op jit(solution)/shard_map/ppermute | solution.py:490
  34.2 13.6 %collective-permute-start.3 = (bf16[384,512]{1,0:T(8,128)(2,1)S(1)}, bf16[384,512]{1,0:T(8,128)(2,1)S(1)}, u32[]{:S(2)}, u32[]{:S(2)}) collective-permute-start(bf16[384,512]{1,0:T(8,128)(2,1)S(1)} %get-tuple-element.90), channel_id=1, source_target_pairs={{0,2},{1,3},{2,0},{3,1},{4,6},{5,7},{6,4},{7,5},{8,10},{9,11},{10,... | collective-permute-start | bytes 1179656 | tf_op jit(solution)/shard_map/ppermute | solution.py:490
  44.9 3.1 %collective-permute-start.4 = (bf16[272,512]{1,0:T(8,128)(2,1)S(1)}, bf16[272,512]{1,0:T(8,128)(2,1)S(1)}, u32[]{:S(2)}, u32[]{:S(2)}) collective-permute-start(bf16[272,512]{1,0:T(8,128)(2,1)S(1)} %get-tuple-element.114), channel_id=1, source_target_pairs={{0,1},{1,0},{2,3},{3,2},{4,5},{5,4},{6,7},{7,6},{8,9},{9,8},{10,11... | collective-permute-start | bytes 835592 | tf_op jit(solution)/shard_map/ppermute | solution.py:490
  45.0 3.0 %collective-permute-start.5 = (bf16[256,512]{1,0:T(8,128)(2,1)S(1)}, bf16[256,512]{1,0:T(8,128)(2,1)S(1)}, u32[]{:S(2)}, u32[]{:S(2)}) collective-permute-start(bf16[256,512]{1,0:T(8,128)(2,1)S(1)} %get-tuple-element.115), channel_id=1, source_target_pairs={{0,1},{1,0},{2,3},{3,2},{4,5},{5,4},{6,7},{7,6},{8,9},{9,8},{10,11... | collective-permute-start | bytes 786440 | tf_op jit(solution)/shard_map/ppermute | solution.py:490
  45.5 2.9 %collective-permute-start.6 = (bf16[256,512]{1,0:T(8,128)(2,1)S(1)}, bf16[256,512]{1,0:T(8,128)(2,1)S(1)}, u32[]{:S(2)}, u32[]{:S(2)}) collective-permute-start(bf16[256,512]{1,0:T(8,128)(2,1)S(1)} %get-tuple-element.120), channel_id=1, source_target_pairs={{0,1},{1,0},{2,3},{3,2},{4,5},{5,4},{6,7},{7,6},{8,9},{9,8},{10,11... | collective-permute-start | bytes 786440 | tf_op jit(solution)/shard_map/ppermute | solution.py:490
  45.6 2.8 %collective-permute-start.7 = (bf16[256,512]{1,0:T(8,128)(2,1)S(1)}, bf16[256,512]{1,0:T(8,128)(2,1)S(1)}, u32[]{:S(2)}, u32[]{:S(2)}) collective-permute-start(bf16[256,512]{1,0:T(8,128)(2,1)S(1)} %get-tuple-element.121), channel_id=1, source_target_pairs={{0,1},{1,0},{2,3},{3,2},{4,5},{5,4},{6,7},{7,6},{8,9},{9,8},{10,11... | collective-permute-start | bytes 786440 | tf_op jit(solution)/shard_map/ppermute | solution.py:490
  48.3 14.5 %collective-permute-start.11 = (bf16[272,512]{1,0:T(8,128)(2,1)S(1)}, bf16[272,512]{1,0:T(8,128)(2,1)S(1)}, u32[]{:S(2)}, u32[]{:S(2)}) collective-permute-start(bf16[272,512]{1,0:T(8,128)(2,1)S(1)} %get-tuple-element.117), channel_id=1, source_target_pairs={{0,2},{1,3},{2,0},{3,1},{4,6},{5,7},{6,4},{7,5},{8,10},{9,11},{10,... | collective-permute-start | bytes 835592 | tf_op jit(solution)/shard_map/ppermute | solution.py:490
  48.4 15.2 %collective-permute-start.12 = (bf16[256,512]{1,0:T(8,128)(2,1)S(1)}, bf16[256,512]{1,0:T(8,128)(2,1)S(1)}, u32[]{:S(2)}, u32[]{:S(2)}) collective-permute-start(bf16[256,512]{1,0:T(8,128)(2,1)S(1)} %get-tuple-element.122), channel_id=1, source_target_pairs={{0,2},{1,3},{2,0},{3,1},{4,6},{5,7},{6,4},{7,5},{8,10},{9,11},{10,... | collective-permute-start | bytes 786440 | tf_op jit(solution)/shard_map/ppermute | solution.py:490
  50.5 7.6 %collective-permute-start.10 = (bf16[192,512]{1,0:T(8,128)(2,1)S(1)}, bf16[192,512]{1,0:T(8,128)(2,1)S(1)}, u32[]{:S(2)}, u32[]{:S(2)}) collective-permute-start(bf16[192,512]{1,0:T(8,128)(2,1)S(1)} %get-tuple-element.111), channel_id=1, source_target_pairs={{0,4},{1,5},{2,6},{3,7},{4,0},{5,1},{6,2},{7,3},{8,12},{9,13},{10,... | collective-permute-start | bytes 589832 | tf_op jit(solution)/shard_map/ppermute | solution.py:490
  51.9 2.6 %collective-permute-start.8 = (bf16[64,512]{1,0:T(8,128)(2,1)S(1)}, bf16[64,512]{1,0:T(8,128)(2,1)S(1)}, u32[]{:S(2)}, u32[]{:S(2)}) collective-permute-start(bf16[64,512]{1,0:T(8,128)(2,1)S(1)} %get-tuple-element.123), channel_id=1, source_target_pairs={{0,1},{1,2},{2,3},{3,4},{4,5},{5,6},{6,7},{7,8},{8,9},{9,10},{10,1... | collective-permute-start | bytes 196616 | tf_op jit(solution)/shard_map/ppermute | solution.py:678
  53.2 4.8 %collective-permute-start.9 = (bf16[64,512]{1,0:T(8,128)(2,1)S(1)}, bf16[64,512]{1,0:T(8,128)(2,1)S(1)}, u32[]{:S(2)}, u32[]{:S(2)}) collective-permute-start(bf16[64,512]{1,0:T(8,128)(2,1)S(1)} %get-tuple-element.124), channel_id=1, source_target_pairs={{1,0},{2,1},{3,2},{4,3},{5,4},{6,5},{7,6},{8,7},{9,8},{10,9},{11,1... | collective-permute-start | bytes 196616 | tf_op jit(solution)/shard_map/ppermute | solution.py:677
  58.1 8.3 %collective-permute-start.13 = (bf16[96,512]{1,0:T(8,128)(2,1)S(1)}, bf16[96,512]{1,0:T(8,128)(2,1)S(1)}, u32[]{:S(2)}, u32[]{:S(2)}) collective-permute-start(bf16[96,512]{1,0:T(8,128)(2,1)S(1)} %get-tuple-element.128), channel_id=1, source_target_pairs={{0,8},{1,9},{2,10},{3,11},{4,12},{5,13},{6,14},{7,15},{8,0},{9,1},... | collective-permute-start | bytes 294920 | tf_op jit(solution)/shard_map/ppermute | solution.py:490
  63.0 6.5 %collective-permute-start.14 = (bf16[144,512]{1,0:T(8,128)(2,1)S(1)}, bf16[144,512]{1,0:T(8,128)(2,1)S(1)}, u32[]{:S(2)}, u32[]{:S(2)}) collective-permute-start(bf16[144,512]{1,0:T(8,128)(2,1)S(1)} %get-tuple-element.133), channel_id=1, source_target_pairs={{0,4},{1,5},{2,6},{3,7},{4,0},{5,1},{6,2},{7,3},{8,12},{9,13},{10,... | collective-permute-start | bytes 442376 | tf_op jit(solution)/shard_map/ppermute | solution.py:490
  63.7 8.7 %collective-permute-start.16 = (bf16[128,512]{1,0:T(8,128)(2,1)S(1)}, bf16[128,512]{1,0:T(8,128)(2,1)S(1)}, u32[]{:S(2)}, u32[]{:S(2)}) collective-permute-start(bf16[128,512]{1,0:T(8,128)(2,1)S(1)} %get-tuple-element.135), channel_id=1, source_target_pairs={{0,4},{1,5},{2,6},{3,7},{4,0},{5,1},{6,2},{7,3},{8,12},{9,13},{10,... | collective-permute-start | bytes 393224 | tf_op jit(solution)/shard_map/ppermute | solution.py:490
  69.9 5.6 %collective-permute-start.15 = (bf16[80,512]{1,0:T(8,128)(2,1)S(1)}, bf16[80,512]{1,0:T(8,128)(2,1)S(1)}, u32[]{:S(2)}, u32[]{:S(2)}) collective-permute-start(bf16[80,512]{1,0:T(8,128)(2,1)S(1)} %get-tuple-element.139), channel_id=1, source_target_pairs={{0,8},{1,9},{2,10},{3,11},{4,12},{5,13},{6,14},{7,15},{8,0},{9,1},... | collective-permute-start | bytes 245768 | tf_op jit(solution)/shard_map/ppermute | solution.py:490
  69.9 5.6 %copy-start.2 = (s32[1,16,2]{1,2,0:T(2,128)S(1)}, s32[1,16,2]{1,2,0:T(2,128)}, u32[]{:S(2)}) copy-start(s32[1,16,2]{1,2,0:T(2,128)} %param.32) | copy-start | bytes 388
  72.4 7.3 %collective-permute-start.17 = (bf16[64,512]{1,0:T(8,128)(2,1)S(1)}, bf16[64,512]{1,0:T(8,128)(2,1)S(1)}, u32[]{:S(2)}, u32[]{:S(2)}) collective-permute-start(bf16[64,512]{1,0:T(8,128)(2,1)S(1)} %get-tuple-element.145), channel_id=1, source_target_pairs={{0,8},{1,9},{2,10},{3,11},{4,12},{5,13},{6,14},{7,15},{8,0},{9,1},... | collective-permute-start | bytes 196616 | tf_op jit(solution)/shard_map/ppermute | solution.py:490

commit v8 on v7

--- a/solution.py
+++ b/solution.py
@@ -123,7 +123,7 @@
 
 
 def outgoing_kernel(
-    index_hbm, node_hbm, slots_ref, head_ref, tail_ref, index_ref, node_ref, sems
+    index_hbm, node_hbm, slots_ref, inner_ref, outer_ref, index_ref, node_ref, sems
 ):
     for copy in fetch([(index_hbm, index_ref), (node_hbm, node_ref)], sems):
         copy.wait()
@@ -133,24 +133,24 @@
     for j in range(places):
         picks = ones_where(place == index_ref[0, j : j + 1, :])
         slots_ref[:, j, :] = dot(picks, node_ref[...], TN).astype(BF16)
-    head_ref[...] = node_ref[:NEAR, :]
-    tail_ref[...] = node_ref[nodes - NEAR :, :]
-
-
-def table_index(raw, origin, places, nodes):
+    odd = lax.rem(lax.axis_index("tiles"), 2)
+    inner_ref[...] = node_ref[pl.ds(pl.multiple_of((1 - odd) * (nodes - NEAR), NEAR), NEAR), :]
+    outer_ref[...] = node_ref[pl.ds(pl.multiple_of(odd * (nodes - NEAR), NEAR), NEAR), :]
+
+
+def table_index(raw, tiles, places, nodes):
     far = raw - (nodes + 2 * NEAR)
-    owner = lax.div(far, places) ^ origin
-    far = nodes + 2 * NEAR + owner * places + lax.rem(far, places)
+    far = nodes + 2 * NEAR + lax.rem(far, places) * tiles + lax.div(far, places)
     rim = jnp.where(raw < NEAR, raw + nodes, raw)
     own = jnp.where((raw >= NEAR) & (raw < NEAR + nodes), raw - NEAR, rim)
     return jnp.where(raw >= nodes + 2 * NEAR, far, own)
 
 
 def prepare_kernel(
-    places, fast,
+    tiles, places,
     node_hbm, w1_hbm, sender_hbm, receiver_hbm, b1_hbm, edge_hbm,
-    edge_ref, w1_ref, node_ref, receiver_ref, moved_ref, partial_ref,
-    weights, sender_ref, b1_ref, sems, edge_sems,
+    node_ref, receiver_ref, moved_ref, partial_ref,
+    edge_ref, w1_ref, weights, sender_ref, b1_ref, sems, edge_sems,
 ):
     edges, latent = edge_ref.shape
     nodes = node_ref.shape[0]
@@ -164,8 +164,7 @@
     edge_copies = fetch(tile_pairs(edge_hbm, edge_ref, edges // 2), edge_sems)
     for copy in copies:
         copy.wait()
-    origin = lax.axis_index("tiles") if fast else 0
-    moved_ref[...] = table_index(sender_ref[...], origin, places, nodes)
+    moved_ref[...] = table_index(sender_ref[...], tiles, places, nodes)
     weights[:latent, :] = w1_ref[:latent, :]
     weights[latent : latent + nodes, :] = dot(
         node_ref[...], w1_ref[latent : 2 * latent, :]
@@ -183,10 +182,10 @@
 
 def forward_kernel(
     tiles, places, fast,
-    w2_hbm, nw1_hbm, nw2_hbm, ncot_hbm,
+    w1_hbm, edge_hbm, w2_hbm, nw1_hbm, nw2_hbm, ncot_hbm,
     b2_hbm, gain_hbm, nb1_hbm, nb2_hbm, ngain_hbm, count_hbm,
-    lower_ref, upper_ref, slots_ref, known_ref, w1_ref, node_ref, receiver_ref, moved_ref,
-    w2_ref, gain_ref,
+    inner_ref, outer_ref, far_ref, known_ref, node_ref, receiver_ref, moved_ref,
+    w1_ref, edge_ref, w2_ref, gain_ref,
     hidden_ref, slope_ref, normed_ref, inverse_ref, table_ref, dsum_ref, base_ref,
     gsend_ref, gkeep_ref,
     weights, summed, grads, nw1_ref, nw2_ref, ncot_ref,
@@ -199,31 +198,33 @@
     steps = edges // TILE
 
     early = fetch(
-        [(count_hbm, count_ref), (b2_hbm, b2_ref), (gain_hbm, gain_ref), (w2_hbm, w2_ref)], sems
+        [
+            (w1_hbm, w1_ref), (count_hbm, count_ref), (b2_hbm, b2_ref), (gain_hbm, gain_ref),
+            (w2_hbm, w2_ref),
+        ],
+        sems,
     )
     late = fetch(
         [
             (nw1_hbm, nw1_ref), (nw2_hbm, nw2_ref), (ncot_hbm, ncot_ref),
-            (nb1_hbm, nb1_ref), (nb2_hbm, nb2_ref), (ngain_hbm, ngain_ref),
-        ],
-        sems.at[pl.ds(len(early), 6)],
+            (nb1_hbm, nb1_ref), (nb2_hbm, nb2_ref), (ngain_hbm, ngain_ref), (edge_hbm, edge_ref),
+        ],
+        sems.at[pl.ds(len(early), 7)],
     )
 
     table_ref[:nodes, :] = node_ref[...]
-    table_ref[nodes : nodes + NEAR, :] = lower_ref[...]
-    table_ref[nodes + NEAR : nodes + 2 * NEAR, :] = upper_ref[...]
-    owner, at = slot_owner(here if fast else 0, (places * tiles, tiles), 0, places)
-    source = lax.broadcasted_iota(jnp.int32, (places * tiles, tiles), 1)
-    slots = jnp.zeros((places * tiles, latent), F32)
+    odd = lax.rem(here, 2)
+    table_ref[pl.ds(pl.multiple_of(nodes + (1 - odd) * NEAR, NEAR), NEAR), :] = inner_ref[...]
+    table_ref[pl.ds(pl.multiple_of(nodes + odd * NEAR, NEAR), NEAR), :] = outer_ref[...]
     for j in range(places):
-        slots += dot(ones_where((owner == source) & (at == j)), slots_ref[:, j, :])
-    table_ref[nodes + 2 * NEAR : nodes + 2 * NEAR + places * tiles, :] = slots.astype(BF16)
+        at = nodes + 2 * NEAR + j * tiles
+        table_ref[at : at + tiles, :] = far_ref[:, j, :]
     used = nodes + 2 * NEAR + places * tiles
     if used < rows:
         table_ref[used:, :] = jnp.zeros((rows - used, latent), BF16)
-    weights[...] = dot(table_ref[nodes:, :], w1_ref[latent : 2 * latent, :]).astype(BF16)
     for copy in early:
         copy.wait()
+    weights[...] = dot(table_ref[nodes:, :], w1_ref[latent : 2 * latent, :]).astype(BF16)
     live = count_ref[here]
 
     def activate(step):
@@ -282,38 +283,37 @@
 
 
 def slope_kernel(
-    tiles, fast,
+    tiles, fast, start, last,
     cot_hbm, receiver_ref, dsum_ref, hidden_ref, slope_ref, normed_ref, inverse_ref, w2_ref, gain_ref,
-    cot_ref, dpre_ref, gsend_ref, gkeep_ref,
-    grads, dout, sems,
+    *refs,
 ):
+    cot_ref, dpre_ref, *out_refs, grads, dout, sem = refs[0 if start == 0 else 1 :]
     here = lax.axis_index("tiles")
     edges, latent = cot_ref.shape
     nodes = dsum_ref.shape[0]
-    copies = fetch(tile_pairs(cot_hbm, cot_ref, edges // 2), sems)
+    copy = pltpu.make_async_copy(cot_hbm.at[pl.ds(start, edges)], cot_ref, sem)
+    copy.start()
     steps = edges // TILE
-    for copy in copies:
-        copy.wait()
+    grads[...] = jnp.zeros_like(grads) if start == 0 else refs[0][...]
+    copy.wait()
 
     def outer(step):
         tile = slice(step * TILE, (step + 1) * TILE)
+        whole = slice(start + step * TILE, start + (step + 1) * TILE)
         receivers = jnp.concatenate(
-            pick_columns(index_columns(receiver_ref, step, TILE), 0, nodes), axis=1
+            pick_columns(index_columns(receiver_ref, start // TILE + step, TILE), 0, nodes), axis=1
         )
         grad_update = cot_ref[tile, :].astype(F32) + dot(receivers, dsum_ref[...])
-        inverse = inverse_ref[tile, :1]
-        dout[tile, :] = norm_backward(grad_update * gain_ref[...], normed_ref[tile, :], inverse)
+        inverse = inverse_ref[whole, :1]
+        dout[tile, :] = norm_backward(grad_update * gain_ref[...], normed_ref[whole, :], inverse)
 
     def inner(step):
         tile = slice(step * TILE, (step + 1) * TILE)
+        whole = slice(start + step * TILE, start + (step + 1) * TILE)
         dpre_ref[tile, :] = (
-            dot(dout[tile, :], w2_ref[...], NT) * slope_ref[tile, :].astype(F32)
+            dot(dout[tile, :], w2_ref[...], NT) * slope_ref[whole, :].astype(F32)
         ).astype(BF16)
-        part = dot(hidden_ref[tile, :], dout[tile, :], TN)
-        if step == 0:
-            grads[...] = part
-        else:
-            grads[...] += part
+        grads[...] += dot(hidden_ref[whole, :], dout[tile, :], TN)
 
     for step in range(steps + 1):
         if step < steps:
@@ -321,29 +321,35 @@
         if step > 0:
             inner(step - 1)
 
-    if fast:
+    if not last:
+        out_refs[0][...] = grads[...]
+    elif fast:
         rows = latent // tiles
-        split_halves(lax.rem(here, 2), grads, 0, rows, 0, rows, gsend_ref, gkeep_ref, 0)
+        split_halves(lax.rem(here, 2), grads, 0, rows, 0, rows, *out_refs, 0)
     else:
-        gkeep_ref[...] = grads[...]
-        gsend_ref[...] = jnp.zeros_like(gsend_ref)
+        out_refs[0][...] = jnp.zeros_like(out_refs[0])
+        out_refs[1][...] = grads[...]
 
 
 def first_kernel(
     tiles, places, fast,
-    dpre_ref, edge_ref, sender_ref, receiver_ref, table_ref, node_ref, w1_ref, base_ref,
+    dpre_a_ref, dpre_b_ref, edge_ref, sender_ref, receiver_ref, table_ref, node_ref, w1_ref, base_ref,
     *refs,
 ):
-    out_refs, (grads, sums) = refs[:-2], refs[-2:]
-    lower_ref, upper_ref, far_ref, partial_ref = out_refs[:4]
+    out_refs, (grads, sums, rims) = refs[:-3], refs[-3:]
+    inner_ref, outer_ref, far_ref, partial_ref = out_refs[:4]
     here = lax.axis_index("tiles")
-    edges, latent = dpre_ref.shape
+    edges, latent = edge_ref.shape
+    early = dpre_a_ref.shape[0]
     nodes = node_ref.shape[0]
     rows = table_ref.shape[0]
 
     for step in range(edges // TILE):
         tile = slice(step * TILE, (step + 1) * TILE)
-        dpre = dpre_ref[tile, :]
+        if step * TILE < early:
+            dpre = dpre_a_ref[tile, :]
+        else:
+            dpre = dpre_b_ref[step * TILE - early : (step + 1) * TILE - early, :]
         part = dot(edge_ref[tile, :], dpre, TN)
         picks = jnp.concatenate(
             [
@@ -366,6 +372,9 @@
     grads[2 * latent :, :] = dot(node_ref[...], by_receiver, TN)
     back = dot(by_sender, w1_ref[latent : 2 * latent, :], NT)
     far = back[nodes + 2 * NEAR : nodes + 2 * NEAR + places * tiles, :].astype(BF16)
+    owner, at = slot_owner(here if fast else 0, (places * tiles, places * tiles), 0, places)
+    column = lax.broadcasted_iota(jnp.int32, (places * tiles, places * tiles), 1)
+    far = dot(ones_where(at * tiles + owner == column), far).astype(BF16)
     far_ref[...] = far
     if fast:
         bit = lax.rem(here, 2)
@@ -378,30 +387,36 @@
         out_refs[4][tiles // 2 * out_refs[5].shape[1] :, :] = slots_out(0, far, places)
     else:
         out_refs[4][...] = grads[...]
-    lower_ref[...] = back[nodes : nodes + NEAR, :].astype(BF16)
-    upper_ref[...] = back[nodes + NEAR : nodes + 2 * NEAR, :].astype(BF16)
+    rims[...] = back[nodes : nodes + 2 * NEAR, :]
+    odd = lax.rem(here, 2)
+    inner_ref[...] = rims[pl.ds(pl.multiple_of((1 - odd) * NEAR, NEAR), NEAR), :].astype(BF16)
+    outer_ref[...] = rims[pl.ds(pl.multiple_of(odd * NEAR, NEAR), NEAR), :].astype(BF16)
     partial_ref[...] = (
         base_ref[...] + back[:nodes, :] + dot(by_receiver, w1_ref[2 * latent :, :], NT)
     )
 
 
-def edge_kernel(dpre_ref, cot_ref, w1_ref, out_hbm, out_ref, sems):
-    edges, latent = cot_ref.shape
+def edge_kernel(dpre_a_ref, dpre_b_ref, cot_a_ref, cot_b_ref, w1_ref, out_hbm, out_ref, sems):
+    early, latent = cot_a_ref.shape
     copies = []
-    for step in range(edges // TILE):
-        tile = pl.ds(step * TILE, TILE)
-        out_ref[tile, :] = (
-            cot_ref[tile, :].astype(F32) + dot(dpre_ref[tile, :], w1_ref[:latent, :], NT)
-        ).astype(BF16)
-        copy = pltpu.make_async_copy(out_ref.at[tile], out_hbm.at[tile], sems.at[step])
-        copy.start()
-        copies.append(copy)
+    for dpre_ref, cot_ref, base in ((dpre_a_ref, cot_a_ref, 0), (dpre_b_ref, cot_b_ref, early)):
+        for at in range(0, early, TILE):
+            part = slice(at, at + TILE)
+            tile = pl.ds(base + at, TILE)
+            out_ref[tile, :] = (
+                cot_ref[part, :].astype(F32) + dot(dpre_ref[part, :], w1_ref[:latent, :], NT)
+            ).astype(BF16)
+            copy = pltpu.make_async_copy(
+                out_ref.at[tile], out_hbm.at[tile], sems.at[(base + at) // TILE]
+            )
+            copy.start()
+            copies.append(copy)
     for copy in copies:
         copy.wait()
 
 
-def node_kernel(fast, index_ref, partial_ref, below_ref, above_ref, slots_ref, *refs):
-    out_ref = refs[-1]
+def node_kernel(fast, index_ref, partial_ref, inner_ref, outer_ref, slots_ref, *refs):
+    out_ref, sums = refs[-2:]
     places, tiles = index_ref.shape[1], index_ref.shape[2]
     nodes = partial_ref.shape[0]
     origin = lax.axis_index("tiles") if fast else 0
@@ -417,11 +432,13 @@
         picks = ones_where(place == index_ref[0, j : j + 1, :])
         far = dot(ones_where((owner == row) & (at == j)), slots).astype(BF16)
         total = total + dot(picks, far)
-    out_ref[:NEAR, :] = (total[:NEAR, :] + below_ref[...].astype(F32)).astype(BF16)
-    out_ref[NEAR : nodes - NEAR, :] = total[NEAR : nodes - NEAR, :].astype(BF16)
-    out_ref[nodes - NEAR :, :] = (
-        total[nodes - NEAR :, :] + above_ref[...].astype(F32)
-    ).astype(BF16)
+    sums[...] = total
+    odd = lax.rem(lax.axis_index("tiles"), 2)
+    inner_at = pl.ds(pl.multiple_of((1 - odd) * (nodes - NEAR), NEAR), NEAR)
+    outer_at = pl.ds(pl.multiple_of(odd * (nodes - NEAR), NEAR), NEAR)
+    sums[inner_at, :] += inner_ref[...].astype(F32)
+    sums[outer_at, :] += outer_ref[...].astype(F32)
+    out_ref[...] = sums[...].astype(BF16)
 
 
 def halve_kernel(shift, count, places, *refs):
@@ -533,8 +550,8 @@
     rows = -(-used // LANES) * LANES
     fast = tiles == 16
     half = tiles // 2
-    upward = [(i, i + 1) for i in range(tiles - 1)]
-    downward = [(i + 1, i) for i in range(tiles - 1)]
+    inside = [(i, i ^ 1) for i in range(tiles)]
+    across = [(i, i + 1 if i % 2 else i - 1) for i in range(1, tiles - 1)]
     sender = edge_sender.reshape(edges // LANES, LANES)
     receiver = edge_receiver.reshape(edges // LANES, LANES)
     listed = jnp.swapaxes(send_index, 1, 2)
@@ -549,7 +566,7 @@
     else:
         grad_shapes = lambda count: [shaped((latent, latent), F32), shaped((count, latent), F32)]
 
-    outgoing, head, tail = call(
+    outgoing, inner, outer = call(
         outgoing_kernel,
         "outgoing",
         [
@@ -561,20 +578,21 @@
         hbm=2,
         scratch=[vmem(listed.shape, jnp.int32), vmem((nodes, latent), BF16), pltpu.SemaphoreType.DMA((2,))],
     )
-    lower = lax.ppermute(tail, "tiles", upward)
-    upper = lax.ppermute(head, "tiles", downward)
+    inner = lax.ppermute(inner, "tiles", inside)
+    outer = lax.ppermute(outer, "tiles", across)
     slots = lax.all_to_all(outgoing, "tiles", split_axis=0, concat_axis=0, tiled=True)
-    edge_kept, w1_kept, node_kept, receiver_kept, moved, preact = call(
-        functools.partial(prepare_kernel, places, fast),
+    node_kept, receiver_kept, moved, preact = call(
+        functools.partial(prepare_kernel, tiles, places),
         "prepare",
         [
-            vmem((edges, latent), BF16), vmem(edge_w1.shape, BF16), vmem((nodes, latent), BF16),
+            vmem((nodes, latent), BF16),
             vmem(receiver.shape, jnp.int32), vmem(sender.shape, jnp.int32),
             vmem((edges, latent), F32),
         ],
         [node_latent, edge_w1, after(sender, outgoing), receiver, row(edge_b1), edge_latent],
         hbm=6,
         scratch=[
+            vmem((edges, latent), BF16), vmem(edge_w1.shape, BF16),
             vmem((latent + 2 * nodes, latent), BF16), vmem(sender.shape, jnp.int32),
             vmem((1, latent), F32), pltpu.SemaphoreType.DMA((5,)), pltpu.SemaphoreType.DMA((2,)),
         ],
@@ -582,51 +600,60 @@
     )
 
     (
-        w2_kept, gain_kept,
+        w1_kept, edge_kept, w2_kept, gain_kept,
         hidden, slope, normed, inverse, table, dsum, base, node_send, node_keep,
     ) = call(
         functools.partial(forward_kernel, tiles, places, fast),
         "forward",
         [
+            vmem(edge_w1.shape, BF16), vmem((edges, latent), BF16),
             vmem(edge_w2.shape, BF16), vmem((1, latent), F32),
             vmem((edges, latent), BF16), vmem((edges, latent), BF16), vmem((edges, latent), F32),
             vmem((edges, LANES), F32), vmem((rows, latent), BF16),
             vmem((nodes, latent), BF16), vmem((nodes, latent), F32),
         ] + grad_shapes(3 * latent if fast else 2 * latent),
         [
-            edge_w2, node_w1, node_w2, node_cot,
+            edge_w1, edge_latent, edge_w2, node_w1, node_w2, node_cot,
             row(edge_b2), row(edge_gain), row(node_b1), row(node_b2), row(node_gain), edge_count,
-            lower, upper, slots, preact, w1_kept, node_kept, receiver_kept, moved,
-        ],
-        hbm=10,
+            inner, outer, slots, preact, node_kept, receiver_kept, moved,
+        ],
+        hbm=12,
         scratch=[
             vmem((rows - nodes, latent), BF16), vmem((nodes, latent), F32),
             vmem((3 * latent, latent), F32), vmem(node_w1.shape, BF16), vmem(node_w2.shape, BF16),
             vmem((nodes, latent), BF16),
         ] + [vmem((1, latent), F32)] * 4 + [
-            pltpu.SMEM(edge_count.shape, jnp.int32), pltpu.SemaphoreType.DMA((10,)),
-        ],
-    )
-
+            pltpu.SMEM(edge_count.shape, jnp.int32), pltpu.SemaphoreType.DMA((12,)),
+        ],
+    )
+
+    early = edges // 2
+
+    def slope_call(start, last, dsum, outs, more):
+        return call(
+            functools.partial(slope_kernel, tiles, fast, start, last),
+            "slope",
+            [vmem((early, latent), BF16), vmem((early, latent), BF16)] + outs,
+            [edge_cot, receiver_kept, dsum, hidden, slope, normed, inverse, w2_kept, gain_kept] + more,
+            hbm=1,
+            scratch=[
+                vmem((latent, latent), F32), vmem((early, latent), BF16), pltpu.SemaphoreType.DMA,
+            ],
+        )
+
+    cot_a, dpre_a, grads = slope_call(0, False, dsum, [vmem((latent, latent), F32)], [])
     if fast:
-        send, chain = halve(1, [node_keep], [swap(tiles, 1, node_send)])
+        send, chain = halve(1, [after(node_keep, grads)], [swap(tiles, 1, node_send)])
         dsum = after(dsum, send)
         got = swap(tiles, 2, send)
-    cot_kept, dpre, second_send, second_keep = call(
-        functools.partial(slope_kernel, tiles, fast),
-        "slope",
-        [vmem((edges, latent), BF16), vmem((edges, latent), BF16)] + grad_shapes(latent),
-        [edge_cot, receiver_kept, dsum, hidden, slope, normed, inverse, w2_kept, gain_kept],
-        hbm=1,
-        scratch=[
-            vmem((latent, latent), F32), vmem((edges, latent), BF16), pltpu.SemaphoreType.DMA((2,)),
-        ],
+    cot_b, dpre_b, second_send, second_keep = slope_call(
+        early, True, dsum, grad_shapes(latent), [grads]
     )
     if fast:
         got_second = swap(tiles, 1, second_send)
 
     per = latent // tiles
-    to_lower, to_upper, to_far, partial, *first = call(
+    to_inner, to_outer, to_far, partial, *first = call(
         functools.partial(first_kernel, tiles, places, fast),
         "first",
         [
@@ -643,26 +670,27 @@
             ]
             if fast else [shaped((3 * latent, latent), F32)]
         ),
-        [dpre, edge_kept, moved, receiver_kept, table, node_kept, w1_kept, base],
-        scratch=[vmem((3 * latent, latent), F32), vmem((rows + nodes, latent), F32)],
+        [dpre_a, dpre_b, edge_kept, moved, receiver_kept, table, node_kept, w1_kept, base],
+        scratch=[
+            vmem((3 * latent, latent), F32), vmem((rows + nodes, latent), F32),
+            vmem((2 * NEAR, latent), F32),
+        ],
     )
 
     (grad_edge,) = call(
         edge_kernel,
         "edge",
         [shaped((edges, latent), BF16)],
-        [after(dpre, partial), cot_kept, w1_kept],
+        [after(dpre_a, partial), dpre_b, cot_a, cot_b, w1_kept],
         out_specs=[pl.BlockSpec(memory_space=pltpu.HBM)],
         scratch=[vmem((edges, latent), BF16), pltpu.SemaphoreType.DMA((steps,))],
     )
 
     if fast:
         send_a, keep_a, send_more, keep_more, send_b, keep_b = first
-        send, chain = halve(2, [after(chain, grad_edge)], [got])
-        got = swap(tiles, 4, send)
         send_a, chain_a, slots = halve(
             1,
-            [after(keep_a, send), keep_more],
+            [after(keep_a, grad_edge), keep_more],
             [swap(tiles, 1, send_a), swap(tiles, 1, send_more)],
             to_far,
             places,
@@ -672,11 +700,12 @@
             1, [after(keep_b, send_a), second_keep], [swap(tiles, 1, send_b), got_second]
      )
         got_b = swap(tiles, 2, send_b)
-
-        to_lower, to_upper = lax.optimization_barrier((to_lower, to_upper, send_b))[:2]
-        above = lax.ppermute(to_lower, "tiles", downward)
-        below = lax.ppermute(to_upper, "tiles", upward)
-        send, chain = halve(3, [after(chain, above, below)], [got])
+        send, chain = halve(2, [after(chain, send_b)], [got])
+        got = swap(tiles, 4, send)
+        to_inner, to_outer = lax.optimization_barrier((to_inner, to_outer, send))[:2]
+        inner = lax.ppermute(to_inner, "tiles", inside)
+        outer = lax.ppermute(to_outer, "tiles", across)
+        send, chain = halve(3, [after(chain, inner, outer)], [got])
         got = swap(tiles, 8, send)
         send_a, chain_a, slots = halve(2, [after(chain_a, send)], [got_a], slots, places)
         got_a = swap(tiles, 4, send_a)
@@ -696,8 +725,8 @@
             [3 * per, per, 2 * per, per],
         )
     else:
-        above = lax.ppermute(to_lower, "tiles", downward)
-        below = lax.ppermute(to_upper, "tiles", upward)
+        inner = lax.ppermute(to_inner, "tiles", inside)
+        outer = lax.ppermute(to_outer, "tiles", across)
         returned = [lax.all_to_all(to_far, "tiles", split_axis=0, concat_axis=0, tiled=True)]
         scatter = functools.partial(
             lax.psum_scatter, axis_name="tiles", scatter_dimension=0, tiled=True
@@ -708,7 +737,8 @@
         functools.partial(node_kernel, fast),
         "node",
         [shaped((nodes, latent), BF16)],
-        [listed, partial, below, above, *returned],
+        [listed, partial, inner, outer, *returned],
+        scratch=[vmem((nodes, latent), F32)],
     )
     return (grad_node, grad_edge, grad_edge_w1, grad_edge_w2, grad_node_w1, grad_node_w2)
 

time: 82 us -> 73.5 us (0.90)
  the two profiles are of different devices: /device:TPU:0 before, /device:TPU:1 now
where the time goes in v8:
time: 73.5 us; the launch traced here: 73.2 us
  Pallas kernels  30.6 us (42%)
  starting transfers between devices  27.6 us (38%)
  waiting for transfers between devices  14.2 us (19%)
  between operations  0.81 us (1%)
    pallas_call x18, Pallas kernels, call(): pl.pallas_call(kernel, in_specs=[pl.BlockSpec(memory_space=pltpu.HBM)] *...  30.6 us
    ppermute x14, starting transfers between devices, swap(): return lax.ppermute(send, 'tiles', [(i, i ^ bit) for i in range(tiles)])  13.3 us
    ppermute x1, waiting for transfers between devices, shards(): outer = lax.ppermute(to_outer, 'tiles', across)  8.39 us
    all_to_all x1, starting transfers between devices, shards(): lax.all_to_all(outgoing, 'tiles', split_axis=0, concat_axis=0, tiled=True)  7.33 us
    ppermute x14, waiting for transfers between devices, swap(): return lax.ppermute(send, 'tiles', [(i, i ^ bit) for i in range(tiles)])  5.78 us
    ppermute x1, starting transfers between devices, shards(): outer = lax.ppermute(outer, 'tiles', across)  3.51 us
    ppermute x1, starting transfers between devices, shards(): outer = lax.ppermute(to_outer, 'tiles', across)  2.07 us
  transfers between devices with their start and end apart: 19, of which 5 were waited for; matrix products, arithmetic and copies ran while one was open for 0% of the time, Pallas kernels for 25%

profile of v8, /device:TPU:1, one launch (start us, length us, event | category | flops | bytes accessed | tf_op | source)
XLA Modules:
  0.0 73.2 jit_solution(6688053114242915480)
XLA Ops:
  0.6 1.8 %outgoing.1 = (bf16[16,2,512]{2,1,0:T(2,128)(2,1)}, bf16[64,512]{1,0:T(8,128)(2,1)}, bf16[64,512]{1,0:T(8,128)(2,1)}) custom-call(s32[1,2,16]{2,1,0:T(2,128)} %bitcast.9, bf16[256,512]{1,0:T(8,128)(2,1)} %node_hbm.3), custom_call_target="tpu_custom_call" | custom-call | tf_op jit(solution)/shard_map/outgoing/pallas_call | solution.py:494
  2.5 7.3 %all-to-all-start = ((bf16[16,2,512]{2,1,0:T(2,128)(2,1)}), bf16[16,2,512]{2,1,0:T(2,128)(2,1)S(1)}, u32[]{:S(2)}, u32[]{:S(2)}) async-start(bf16[16,2,512]{2,1,0:T(2,128)(2,1)} %get-tuple-element.82), calls=%async_computation | async-start | bytes 65536 | tf_op jit(solution)/shard_map/all_to_all | solution.py:583
  10.0 3.5 %collective-permute-start.1 = (bf16[64,512]{1,0:T(8,128)(2,1)}, bf16[64,512]{1,0:T(8,128)(2,1)}, u32[]{:S(2)}, u32[]{:S(2)}) collective-permute-start(bf16[64,512]{1,0:T(8,128)(2,1)} %get-tuple-element.86), channel_id=1, source_target_pairs={{1,2},{2,1},{3,4},{4,3},{5,6},{6,5},{7,8},{8,7},{9,10},{10,9},{11,... | collective-permute-start | bytes 196616 | tf_op jit(solution)/shard_map/ppermute | solution.py:582
  13.5 3.8 %prepare.1 = (bf16[256,512]{1,0:T(8,128)(2,1)S(1)}, s32[12,128]{1,0:T(8,128)S(1)}, s32[12,128]{1,0:T(8,128)S(1)}, f32[1536,512]{1,0:T(8,128)S(1)}) custom-call(bf16[256,512]{1,0:T(8,128)(2,1)} %node_hbm.3, bf16[1536,512]{1,0:T(8,128)(2,1)} %w1_hbm.3, s32[12,128]{1,0:T(8,128)} %bitcast.16, s32[12,128]{1,0:T(8,128)} %bitcast.17, f32[1,512]{1,0:T(1,128)} %bitcast.18, ...), custom_call_target="tpu_custom_call" | custom-call | flops 10000000000 | bytes 100000000 | tf_op jit(solution)/shard_map/prepare/pallas_call | solution.py:494
  17.4 9.5 %forward.1 = (bf16[1536,512]{1,0:T(8,128)(2,1)S(1)}, bf16[1536,512]{1,0:T(8,128)(2,1)S(1)}, bf16[512,512]{1,0:T(8,128)(2,1)S(1)}, f32[1,512]{1,0:T(1,128)S(1)}, ...) custom-call(bf16[1536,512]{1,0:T(8,128)(2,1)} %w1_hbm.3, ...), custom_call_target="tpu_custom_call" | custom-call | tf_op jit(solution)/shard_map/forward/pallas_call | solution.py:494
  27.0 2.9 %slope.2 = (bf16[768,512]{1,0:T(8,128)(2,1)S(1)}, bf16[768,512]{1,0:T(8,128)(2,1)S(1)}, f32[512,512]{1,0:T(8,128)S(1)}) custom-call(bf16[1536,512]{1,0:T(8,128)(2,1)} %cot_hbm.3, s32[12,128]{1,0:T(8,128)S(1)} %get-tuple-element.84.receiver_ref, bf16[256,512]{1,0:T(8,128)(2,1)S(1)} %get-tuple-element.103.dsum_ref, ...), custom_call_target="tpu_custom_call" | custom-call | tf_op jit(solution)/shard_map/slope/pallas_call | solution.py:494
  30.0 1.2 %collective-permute-start.7 = (bf16[384,512]{1,0:T(8,128)(2,1)S(1)}, bf16[384,512]{1,0:T(8,128)(2,1)S(1)}, u32[]{:S(2)}, u32[]{:S(2)}) collective-permute-start(bf16[384,512]{1,0:T(8,128)(2,1)S(1)} %get-tuple-element.102), channel_id=1, source_target_pairs={{0,2},{1,3},{2,0},{3,1},{4,6},{5,7},{6,4},{7,5},{8,10},{9,11},{10,... | collective-permute-start | bytes 1179656 | tf_op jit(solution)/shard_map/ppermute | solution.py:507
  31.3 3.1 %slope.3 = (bf16[768,512]{1,0:T(8,128)(2,1)S(1)}, bf16[768,512]{1,0:T(8,128)(2,1)S(1)}, bf16[256,512]{1,0:T(8,128)(2,1)S(1)}, f32[8,32,512]{2,1,0:T(8,128)S(1)}) custom-call(bf16[1536,512]{1,0:T(8,128)(2,1)} %cot_hbm.3, s32[12,128]{1,0:T(8,128)S(1)} %get-tuple-element.84.receiver_ref, bf16[256,512]{1,0:T(8,128)(2,1)S(1)} %get-tuple-element.103.dsum_ref, ...), custom_call_target="tpu_custom_call" | custom-call | tf_op jit(solution)/shard_map/slope/pallas_call | solution.py:494
  34.3 4.1 %first.1 = (bf16[64,512]{1,0:T(8,128)(2,1)S(1)}, bf16[64,512]{1,0:T(8,128)(2,1)S(1)}, bf16[32,512]{1,0:T(8,128)(2,1)S(1)}, f32[256,512]{1,0:T(8,128)S(1)}, bf16[...) custom-call(bf16[768,512]{1,0:T(8,128)(2,1)S(1)} %get-tuple-element., ...), custom_call_target="tpu_custom_call" | custom-call | tf_op jit(solution)/shard_map/first/pallas_call | solution.py:494
  38.4 0.8 %collective-permute-start.3 = (bf16[272,512]{1,0:T(8,128)(2,1)S(1)}, bf16[272,512]{1,0:T(8,128)(2,1)S(1)}, u32[]{:S(2)}, u32[]{:S(2)}) collective-permute-start(bf16[272,512]{1,0:T(8,128)(2,1)S(1)} %get-tuple-element.120), channel_id=1, source_target_pairs={{0,1},{1,0},{2,3},{3,2},{4,5},{5,4},{6,7},{7,6},{8,9},{9,8},{10,11... | collective-permute-start | bytes 835592 | tf_op jit(solution)/shard_map/ppermute | solution.py:507
  39.8 1.8 %edge.1 = bf16[1536,512]{1,0:T(8,128)(2,1)} custom-call(bf16[768,512]{1,0:T(8,128)(2,1)S(1)} %get-tuple-element.115.dpre_a_ref, bf16[768,512]{1,0:T(8,128)(2,1)S(1)} %get-tuple-element.104.dpre_b_ref, bf16[768,512]{1,0:T(8,128)(2,1)S(1)} %get-tuple-element.116.cot_a_ref, bf16[768,512]{1,0:T(8,128)(2,1)S(1)} %get-tuple-element.117.cot_b_ref, ...), custom_call_target="tpu_custom_call" | custom-call | tf_op jit(solution)/shard_map/edge/pallas_call | solution.py:494
  42.3 1.2 %collective-permute-start.12 = (bf16[256,512]{1,0:T(8,128)(2,1)S(1)}, bf16[256,512]{1,0:T(8,128)(2,1)S(1)}, u32[]{:S(2)}, u32[]{:S(2)}) collective-permute-start(bf16[256,512]{1,0:T(8,128)(2,1)S(1)} %get-tuple-element.128), channel_id=1, source_target_pairs={{0,2},{1,3},{2,0},{3,1},{4,6},{5,7},{6,4},{7,5},{8,10},{9,11},{10,... | collective-permute-start | bytes 786440 | tf_op jit(solution)/shard_map/ppermute | solution.py:507
  43.7 1.3 %collective-permute-start.10 = (bf16[192,512]{1,0:T(8,128)(2,1)S(1)}, bf16[192,512]{1,0:T(8,128)(2,1)S(1)}, u32[]{:S(2)}, u32[]{:S(2)}) collective-permute-start(bf16[192,512]{1,0:T(8,128)(2,1)S(1)} %get-tuple-element.130), channel_id=1, source_target_pairs={{0,4},{1,5},{2,6},{3,7},{4,0},{5,1},{6,2},{7,3},{8,12},{9,13},{10,... | collective-permute-start | bytes 589832 | tf_op jit(solution)/shard_map/ppermute | solution.py:507
  44.9 1.3 %collective-permute-start.8 = (bf16[64,512]{1,0:T(8,128)(2,1)S(1)}, bf16[64,512]{1,0:T(8,128)(2,1)S(1)}, u32[]{:S(2)}, u32[]{:S(2)}) collective-permute-start(bf16[64,512]{1,0:T(8,128)(2,1)S(1)} %get-tuple-element.131), channel_id=1, source_target_pairs={{0,1},{1,0},{2,3},{3,2},{4,5},{5,4},{6,7},{7,6},{8,9},{9,8},{10,11... | collective-permute-start | bytes 196616 | tf_op jit(solution)/shard_map/ppermute | solution.py:706
  46.2 2.1 %collective-permute-start.9 = (bf16[64,512]{1,0:T(8,128)(2,1)S(1)}, bf16[64,512]{1,0:T(8,128)(2,1)S(1)}, u32[]{:S(2)}, u32[]{:S(2)}) collective-permute-start(bf16[64,512]{1,0:T(8,128)(2,1)S(1)} %get-tuple-element.132), channel_id=1, source_target_pairs={{1,2},{2,1},{3,4},{4,3},{5,6},{6,5},{7,8},{8,7},{9,10},{10,9},{11,... | collective-permute-start | bytes 196616 | tf_op jit(solution)/shard_map/ppermute | solution.py:707
  48.3 8.4 %collective-permute-done.9.outer_ref = bf16[64,512]{1,0:T(8,128)(2,1)S(1)} collective-permute-done((bf16[64,512]{1,0:T(8,128)(2,1)S(1)}, bf16[64,512]{1,0:T(8,128)(2,1)S(1)}, u32[]{:S(2)}, u32[]{:S(2)}) %collective-permute-start.9) | collective-permute-done | bytes 65568 | tf_op jit(solution)/shard_map/ppermute | solution.py:707
  56.7 3.2 %collective-permute-start.13 = (bf16[96,512]{1,0:T(8,128)(2,1)S(1)}, bf16[96,512]{1,0:T(8,128)(2,1)S(1)}, u32[]{:S(2)}, u32[]{:S(2)}) collective-permute-start(bf16[96,512]{1,0:T(8,128)(2,1)S(1)} %get-tuple-element.136), channel_id=1, source_target_pairs={{0,8},{1,9},{2,10},{3,11},{4,12},{5,13},{6,14},{7,15},{8,0},{9,1},... | collective-permute-start | bytes 294920 | tf_op jit(solution)/shard_map/ppermute | solution.py:507
  60.5 1.2 %collective-permute-start.16 = (bf16[128,512]{1,0:T(8,128)(2,1)S(1)}, bf16[128,512]{1,0:T(8,128)(2,1)S(1)}, u32[]{:S(2)}, u32[]{:S(2)}) collective-permute-start(bf16[128,512]{1,0:T(8,128)(2,1)S(1)} %get-tuple-element.143), channel_id=1, source_target_pairs={{0,4},{1,5},{2,6},{3,7},{4,0},{5,1},{6,2},{7,3},{8,12},{9,13},{10,... | collective-permute-start | bytes 393224 | tf_op jit(solution)/shard_map/ppermute | solution.py:507
  62.4 2.6 %collective-permute-done.14.refs_1_ = bf16[144,512]{1,0:T(8,128)(2,1)S(1)} collective-permute-done((bf16[144,512]{1,0:T(8,128)(2,1)S(1)}, bf16[144,512]{1,0:T(8,128)(2,1)S(1)}, u32[]{:S(2)}, u32[]{:S(2)}) %collective-permute-start.14) | collective-permute-done | bytes 147488 | tf_op jit(solution)/shard_map/ppermute | solution.py:507
  65.4 1.8 %collective-permute-start.15 = (bf16[80,512]{1,0:T(8,128)(2,1)S(1)}, bf16[80,512]{1,0:T(8,128)(2,1)S(1)}, u32[]{:S(2)}, u32[]{:S(2)}) collective-permute-start(bf16[80,512]{1,0:T(8,128)(2,1)S(1)} %get-tuple-element.147), channel_id=1, source_target_pairs={{0,8},{1,9},{2,10},{3,11},{4,12},{5,13},{6,14},{7,15},{8,0},{9,1},... | collective-permute-start | bytes 245768 | tf_op jit(solution)/shard_map/ppermute | solution.py:507
  67.2 1.2 %collective-permute-start.17 = (bf16[64,512]{1,0:T(8,128)(2,1)S(1)}, bf16[64,512]{1,0:T(8,128)(2,1)S(1)}, u32[]{:S(2)}, u32[]{:S(2)}) collective-permute-start(bf16[64,512]{1,0:T(8,128)(2,1)S(1)} %get-tuple-element.153), channel_id=1, source_target_pairs={{0,8},{1,9},{2,10},{3,11},{4,12},{5,13},{6,14},{7,15},{8,0},{9,1},... | collective-permute-start | bytes 196616 | tf_op jit(solution)/shard_map/ppermute | solution.py:507
  68.4 1.2 %collective-permute-done.15.refs_0_.refs_4_ = bf16[80,512]{1,0:T(8,128)(2,1)S(1)} collective-permute-done((bf16[80,512]{1,0:T(8,128)(2,1)S(1)}, bf16[80,512]{1,0:T(8,128)(2,1)S(1)}, u32[]{:S(2)}, u32[]{:S(2)}) %collective-permute-start.15) | collective-permute-done | bytes 81952 | tf_op jit(solution)/shard_map/ppermute | solution.py:507
  69.6 1.5 %node.1 = bf16[256,512]{1,0:T(8,128)(2,1)} custom-call(s32[1,2,16]{2,1,0:T(2,128)S(1)} %bitcast.10, f32[256,512]{1,0:T(8,128)S(1)} %get-tuple-element.109.partial_ref, bf16[64,512]{1,0:T(8,128)(2,1)S(1)} %collective-permute-done.8.inner_ref, bf16[64,512]{1,0:T(8,128)(2,1)S(1)} %collective-permute-done.9.outer_ref, ...), custom_call_target="tpu_custom_call" | custom-call | tf_op jit(solution)/shard_map/node/pallas_call | solution.py:494
  71.1 1.3 %collective-permute-done.17.refs_5_ = bf16[64,512]{1,0:T(8,128)(2,1)S(1)} collective-permute-done((bf16[64,512]{1,0:T(8,128)(2,1)S(1)}, bf16[64,512]{1,0:T(8,128)(2,1)S(1)}, u32[]{:S(2)}, u32[]{:S(2)}) %collective-permute-start.17) | collective-permute-done | bytes 65568 | tf_op jit(solution)/shard_map/ppermute | solution.py:507
  (34 shorter events, 4.3 us)
Async XLA Ops:
  2.5 14.9 %all-to-all-start = ((bf16[16,2,512]{2,1,0:T(2,128)(2,1)}), bf16[16,2,512]{2,1,0:T(2,128)(2,1)S(1)}, u32[]{:S(2)}, u32[]{:S(2)}) async-start(bf16[16,2,512]{2,1,0:T(2,128)(2,1)} %get-tuple-element.82), calls=%async_computation | async-start | bytes 65536 | tf_op jit(solution)/shard_map/all_to_all | solution.py:583
  9.8 7.6 %collective-permute-start = (bf16[64,512]{1,0:T(8,128)(2,1)}, bf16[64,512]{1,0:T(8,128)(2,1)S(1)}, u32[]{:S(2)}, u32[]{:S(2)}) collective-permute-start(bf16[64,512]{1,0:T(8,128)(2,1)} %get-tuple-element.85), channel_id=1, source_target_pairs={{0,1},{1,0},{2,3},{3,2},{4,5},{5,4},{6,7},{7,6},{8,9},{9,8},{10,11... | collective-permute-start | bytes 196616 | tf_op jit(solution)/shard_map/ppermute | solution.py:581
  10.0 7.4 %collective-permute-start.1 = (bf16[64,512]{1,0:T(8,128)(2,1)}, bf16[64,512]{1,0:T(8,128)(2,1)}, u32[]{:S(2)}, u32[]{:S(2)}) collective-permute-start(bf16[64,512]{1,0:T(8,128)(2,1)} %get-tuple-element.86), channel_id=1, source_target_pairs={{1,2},{2,1},{3,4},{4,3},{5,6},{6,5},{7,8},{8,7},{9,10},{10,9},{11,... | collective-permute-start | bytes 196616 | tf_op jit(solution)/shard_map/ppermute | solution.py:582
  26.9 3.0 %collective-permute-start.2 = (bf16[768,512]{1,0:T(8,128)(2,1)S(1)}, bf16[768,512]{1,0:T(8,128)(2,1)S(1)}, u32[]{:S(2)}, u32[]{:S(2)}) collective-permute-start(bf16[768,512]{1,0:T(8,128)(2,1)S(1)} %get-tuple-element.101), channel_id=1, source_target_pairs={{0,1},{1,0},{2,3},{3,2},{4,5},{5,4},{6,7},{7,6},{8,9},{9,8},{10,11... | collective-permute-start | bytes 2359304 | tf_op jit(solution)/shard_map/ppermute | solution.py:507
  30.0 13.6 %collective-permute-start.7 = (bf16[384,512]{1,0:T(8,128)(2,1)S(1)}, bf16[384,512]{1,0:T(8,128)(2,1)S(1)}, u32[]{:S(2)}, u32[]{:S(2)}) collective-permute-start(bf16[384,512]{1,0:T(8,128)(2,1)S(1)} %get-tuple-element.102), channel_id=1, source_target_pairs={{0,2},{1,3},{2,0},{3,1},{4,6},{5,7},{6,4},{7,5},{8,10},{9,11},{10,... | collective-permute-start | bytes 1179656 | tf_op jit(solution)/shard_map/ppermute | solution.py:507
  38.4 3.2 %collective-permute-start.3 = (bf16[272,512]{1,0:T(8,128)(2,1)S(1)}, bf16[272,512]{1,0:T(8,128)(2,1)S(1)}, u32[]{:S(2)}, u32[]{:S(2)}) collective-permute-start(bf16[272,512]{1,0:T(8,128)(2,1)S(1)} %get-tuple-element.120), channel_id=1, source_target_pairs={{0,1},{1,0},{2,3},{3,2},{4,5},{5,4},{6,7},{7,6},{8,9},{9,8},{10,11... | collective-permute-start | bytes 835592 | tf_op jit(solution)/shard_map/ppermute | solution.py:507
  39.2 2.4 %collective-permute-start.4 = (bf16[256,512]{1,0:T(8,128)(2,1)S(1)}, bf16[256,512]{1,0:T(8,128)(2,1)S(1)}, u32[]{:S(2)}, u32[]{:S(2)}) collective-permute-start(bf16[256,512]{1,0:T(8,128)(2,1)S(1)} %get-tuple-element.121), channel_id=1, source_target_pairs={{0,1},{1,0},{2,3},{3,2},{4,5},{5,4},{6,7},{7,6},{8,9},{9,8},{10,11... | collective-permute-start | bytes 786440 | tf_op jit(solution)/shard_map/ppermute | solution.py:507
  39.3 2.9 %collective-permute-start.5 = (bf16[256,512]{1,0:T(8,128)(2,1)S(1)}, bf16[256,512]{1,0:T(8,128)(2,1)S(1)}, u32[]{:S(2)}, u32[]{:S(2)}) collective-permute-start(bf16[256,512]{1,0:T(8,128)(2,1)S(1)} %get-tuple-element.126), channel_id=1, source_target_pairs={{0,1},{1,0},{2,3},{3,2},{4,5},{5,4},{6,7},{7,6},{8,9},{9,8},{10,11... | collective-permute-start | bytes 786440 | tf_op jit(solution)/shard_map/ppermute | solution.py:507
  39.8 2.5 %collective-permute-start.6 = (bf16[256,512]{1,0:T(8,128)(2,1)S(1)}, bf16[256,512]{1,0:T(8,128)(2,1)S(1)}, u32[]{:S(2)}, u32[]{:S(2)}) collective-permute-start(bf16[256,512]{1,0:T(8,128)(2,1)S(1)} %get-tuple-element.127), channel_id=1, source_target_pairs={{0,1},{1,0},{2,3},{3,2},{4,5},{5,4},{6,7},{7,6},{8,9},{9,8},{10,11... | collective-permute-start | bytes 786440 | tf_op jit(solution)/shard_map/ppermute | solution.py:507
  42.0 17.9 %collective-permute-start.11 = (bf16[272,512]{1,0:T(8,128)(2,1)S(1)}, bf16[272,512]{1,0:T(8,128)(2,1)S(1)}, u32[]{:S(2)}, u32[]{:S(2)}) collective-permute-start(bf16[272,512]{1,0:T(8,128)(2,1)S(1)} %get-tuple-element.123), channel_id=1, source_target_pairs={{0,2},{1,3},{2,0},{3,1},{4,6},{5,7},{6,4},{7,5},{8,10},{9,11},{10,... | collective-permute-start | bytes 835592 | tf_op jit(solution)/shard_map/ppermute | solution.py:507
  42.3 18.2 %collective-permute-start.12 = (bf16[256,512]{1,0:T(8,128)(2,1)S(1)}, bf16[256,512]{1,0:T(8,128)(2,1)S(1)}, u32[]{:S(2)}, u32[]{:S(2)}) collective-permute-start(bf16[256,512]{1,0:T(8,128)(2,1)S(1)} %get-tuple-element.128), channel_id=1, source_target_pairs={{0,2},{1,3},{2,0},{3,1},{4,6},{5,7},{6,4},{7,5},{8,10},{9,11},{10,... | collective-permute-start | bytes 786440 | tf_op jit(solution)/shard_map/ppermute | solution.py:507
  43.7 13.0 %collective-permute-start.10 = (bf16[192,512]{1,0:T(8,128)(2,1)S(1)}, bf16[192,512]{1,0:T(8,128)(2,1)S(1)}, u32[]{:S(2)}, u32[]{:S(2)}) collective-permute-start(bf16[192,512]{1,0:T(8,128)(2,1)S(1)} %get-tuple-element.130), channel_id=1, source_target_pairs={{0,4},{1,5},{2,6},{3,7},{4,0},{5,1},{6,2},{7,3},{8,12},{9,13},{10,... | collective-permute-start | bytes 589832 | tf_op jit(solution)/shard_map/ppermute | solution.py:507
  44.9 3.4 %collective-permute-start.8 = (bf16[64,512]{1,0:T(8,128)(2,1)S(1)}, bf16[64,512]{1,0:T(8,128)(2,1)S(1)}, u32[]{:S(2)}, u32[]{:S(2)}) collective-permute-start(bf16[64,512]{1,0:T(8,128)(2,1)S(1)} %get-tuple-element.131), channel_id=1, source_target_pairs={{0,1},{1,0},{2,3},{3,2},{4,5},{5,4},{6,7},{7,6},{8,9},{9,8},{10,11... | collective-permute-start | bytes 196616 | tf_op jit(solution)/shard_map/ppermute | solution.py:706
  46.2 10.5 %collective-permute-start.9 = (bf16[64,512]{1,0:T(8,128)(2,1)S(1)}, bf16[64,512]{1,0:T(8,128)(2,1)S(1)}, u32[]{:S(2)}, u32[]{:S(2)}) collective-permute-start(bf16[64,512]{1,0:T(8,128)(2,1)S(1)} %get-tuple-element.132), channel_id=1, source_target_pairs={{1,2},{2,1},{3,4},{4,3},{5,6},{6,5},{7,8},{8,7},{9,10},{10,9},{11,... | collective-permute-start | bytes 196616 | tf_op jit(solution)/shard_map/ppermute | solution.py:707
  56.7 5.7 %collective-permute-start.13 = (bf16[96,512]{1,0:T(8,128)(2,1)S(1)}, bf16[96,512]{1,0:T(8,128)(2,1)S(1)}, u32[]{:S(2)}, u32[]{:S(2)}) collective-permute-start(bf16[96,512]{1,0:T(8,128)(2,1)S(1)} %get-tuple-element.136), channel_id=1, source_target_pairs={{0,8},{1,9},{2,10},{3,11},{4,12},{5,13},{6,14},{7,15},{8,0},{9,1},... | collective-permute-start | bytes 294920 | tf_op jit(solution)/shard_map/ppermute | solution.py:507
  60.2 4.9 %collective-permute-start.14 = (bf16[144,512]{1,0:T(8,128)(2,1)S(1)}, bf16[144,512]{1,0:T(8,128)(2,1)S(1)}, u32[]{:S(2)}, u32[]{:S(2)}) collective-permute-start(bf16[144,512]{1,0:T(8,128)(2,1)S(1)} %get-tuple-element.141), channel_id=1, source_target_pairs={{0,4},{1,5},{2,6},{3,7},{4,0},{5,1},{6,2},{7,3},{8,12},{9,13},{10,... | collective-permute-start | bytes 442376 | tf_op jit(solution)/shard_map/ppermute | solution.py:507
  60.5 6.7 %collective-permute-start.16 = (bf16[128,512]{1,0:T(8,128)(2,1)S(1)}, bf16[128,512]{1,0:T(8,128)(2,1)S(1)}, u32[]{:S(2)}, u32[]{:S(2)}) collective-permute-start(bf16[128,512]{1,0:T(8,128)(2,1)S(1)} %get-tuple-element.143), channel_id=1, source_target_pairs={{0,4},{1,5},{2,6},{3,7},{4,0},{5,1},{6,2},{7,3},{8,12},{9,13},{10,... | collective-permute-start | bytes 393224 | tf_op jit(solution)/shard_map/ppermute | solution.py:507
  65.4 4.2 %collective-permute-start.15 = (bf16[80,512]{1,0:T(8,128)(2,1)S(1)}, bf16[80,512]{1,0:T(8,128)(2,1)S(1)}, u32[]{:S(2)}, u32[]{:S(2)}) collective-permute-start(bf16[80,512]{1,0:T(8,128)(2,1)S(1)} %get-tuple-element.147), channel_id=1, source_target_pairs={{0,8},{1,9},{2,10},{3,11},{4,12},{5,13},{6,14},{7,15},{8,0},{9,1},... | collective-permute-start | bytes 245768 | tf_op jit(solution)/shard_map/ppermute | solution.py:507
  67.2 2.4 %copy-start = (s32[1,16,2]{1,2,0:T(2,128)S(1)}, s32[1,16,2]{1,2,0:T(2,128)}, u32[]{:S(2)}) copy-start(s32[1,16,2]{1,2,0:T(2,128)} %param.32) | copy-start | bytes 388
  67.2 5.2 %collective-permute-start.17 = (bf16[64,512]{1,0:T(8,128)(2,1)S(1)}, bf16[64,512]{1,0:T(8,128)(2,1)S(1)}, u32[]{:S(2)}, u32[]{:S(2)}) collective-permute-start(bf16[64,512]{1,0:T(8,128)(2,1)S(1)} %get-tuple-element.153), channel_id=1, source_target_pairs={{0,8},{1,9},{2,10},{3,11},{4,12},{5,13},{6,14},{7,15},{8,0},{9,1},... | collective-permute-start | bytes 196616 | tf_op jit(solution)/shard_map/ppermute | solution.py:507

commit v9 on v8

--- a/solution.py
+++ b/solution.py
@@ -123,10 +123,18 @@
 
 
 def outgoing_kernel(
-    index_hbm, node_hbm, slots_ref, inner_ref, outer_ref, index_ref, node_ref, sems
+    index_hbm, node_hbm, w1_hbm, edge_hbm,
+    slots_ref, inner_ref, outer_ref, node_ref, w1_ref, edge_ref,
+    index_ref, sems,
 ):
-    for copy in fetch([(index_hbm, index_ref), (node_hbm, node_ref)], sems):
-        copy.wait()
+    copies = fetch(
+        [
+            (index_hbm, index_ref), (node_hbm, node_ref), (w1_hbm, w1_ref), (edge_hbm, edge_ref),
+        ],
+        sems,
+    )
+    copies[0].wait()
+    copies[1].wait()
     places, tiles = index_ref.shape[1], index_ref.shape[2]
     nodes, latent = node_ref.shape
     place = lax.broadcasted_iota(jnp.int32, (nodes, tiles), 0)
@@ -136,6 +144,8 @@
     odd = lax.rem(lax.axis_index("tiles"), 2)
     inner_ref[...] = node_ref[pl.ds(pl.multiple_of((1 - odd) * (nodes - NEAR), NEAR), NEAR), :]
     outer_ref[...] = node_ref[pl.ds(pl.multiple_of(odd * (nodes - NEAR), NEAR), NEAR), :]
+    copies[2].wait()
+    copies[3].wait()
 
 
 def table_index(raw, tiles, places, nodes):
@@ -148,30 +158,23 @@
 
 def prepare_kernel(
     tiles, places,
-    node_hbm, w1_hbm, sender_hbm, receiver_hbm, b1_hbm, edge_hbm,
-    node_ref, receiver_ref, moved_ref, partial_ref,
-    edge_ref, w1_ref, weights, sender_ref, b1_ref, sems, edge_sems,
+    sender_hbm, receiver_hbm, b1_hbm, node_ref, w1_ref, edge_ref,
+    receiver_ref, moved_ref, partial_ref,
+    weights, sender_ref, b1_ref, sems,
 ):
     edges, latent = edge_ref.shape
     nodes = node_ref.shape[0]
     copies = fetch(
-        [
-            (node_hbm, node_ref), (w1_hbm, w1_ref), (sender_hbm, sender_ref),
-            (receiver_hbm, receiver_ref), (b1_hbm, b1_ref),
-        ],
-        sems,
-    )
-    edge_copies = fetch(tile_pairs(edge_hbm, edge_ref, edges // 2), edge_sems)
-    for copy in copies:
-        copy.wait()
-    moved_ref[...] = table_index(sender_ref[...], tiles, places, nodes)
+        [(sender_hbm, sender_ref), (receiver_hbm, receiver_ref), (b1_hbm, b1_ref)], sems
+    )
     weights[:latent, :] = w1_ref[:latent, :]
     weights[latent : latent + nodes, :] = dot(
         node_ref[...], w1_ref[latent : 2 * latent, :]
     ).astype(BF16)
     weights[latent + nodes :, :] = dot(node_ref[...], w1_ref[2 * latent :, :]).astype(BF16)
-    for copy in edge_copies:
+    for copy in copies:
         copy.wait()
+    moved_ref[...] = table_index(sender_ref[...], tiles, places, nodes)
     for step in range(edges // TILE):
         tile = slice(step * TILE, (step + 1) * TILE)
         senders = pick_columns(index_columns(moved_ref, step, TILE), 0, nodes)
@@ -182,10 +185,10 @@
 
 def forward_kernel(
     tiles, places, fast,
-    w1_hbm, edge_hbm, w2_hbm, nw1_hbm, nw2_hbm, ncot_hbm,
+    w1_hbm, edge_hbm, cot_hbm, w2_hbm, nw1_hbm, nw2_hbm, ncot_hbm,
     b2_hbm, gain_hbm, nb1_hbm, nb2_hbm, ngain_hbm, count_hbm,
     inner_ref, outer_ref, far_ref, known_ref, node_ref, receiver_ref, moved_ref,
-    w1_ref, edge_ref, w2_ref, gain_ref,
+    w1_ref, edge_ref, cot_ref, w2_ref, gain_ref,
     hidden_ref, slope_ref, normed_ref, inverse_ref, table_ref, dsum_ref, base_ref,
     gsend_ref, gkeep_ref,
     weights, summed, grads, nw1_ref, nw2_ref, ncot_ref,
@@ -197,19 +200,24 @@
     rows = table_ref.shape[0]
     steps = edges // TILE
 
+    senders_part = pl.ds(latent, latent)
     early = fetch(
         [
-            (w1_hbm, w1_ref), (count_hbm, count_ref), (b2_hbm, b2_ref), (gain_hbm, gain_ref),
-            (w2_hbm, w2_ref),
+            (w1_hbm.at[senders_part], w1_ref.at[senders_part]), (count_hbm, count_ref),
+            (b2_hbm, b2_ref), (gain_hbm, gain_ref), (w2_hbm, w2_ref),
         ],
         sems,
     )
+    edges_part, receivers_part = pl.ds(0, latent), pl.ds(2 * latent, latent)
     late = fetch(
         [
             (nw1_hbm, nw1_ref), (nw2_hbm, nw2_ref), (ncot_hbm, ncot_ref),
-            (nb1_hbm, nb1_ref), (nb2_hbm, nb2_ref), (ngain_hbm, ngain_ref), (edge_hbm, edge_ref),
-        ],
-        sems.at[pl.ds(len(early), 7)],
+            (nb1_hbm, nb1_ref), (nb2_hbm, nb2_ref), (ngain_hbm, ngain_ref),
+            (cot_hbm, cot_ref), (edge_hbm, edge_ref),
+            (w1_hbm.at[edges_part], w1_ref.at[edges_part]),
+            (w1_hbm.at[receivers_part], w1_ref.at[receivers_part]),
+        ],
+        sems.at[pl.ds(len(early), 10)],
     )
 
     table_ref[:nodes, :] = node_ref[...]
@@ -222,9 +230,10 @@
     used = nodes + 2 * NEAR + places * tiles
     if used < rows:
         table_ref[used:, :] = jnp.zeros((rows - used, latent), BF16)
-    for copy in early:
+    early[0].wait()
+    weights[...] = dot(table_ref[nodes:, :], w1_ref[latent : 2 * latent, :]).astype(BF16)
+    for copy in early[1:]:
         copy.wait()
-    weights[...] = dot(table_ref[nodes:, :], w1_ref[latent : 2 * latent, :]).astype(BF16)
     live = count_ref[here]
 
     def activate(step):
@@ -284,18 +293,15 @@
 
 def slope_kernel(
     tiles, fast, start, last,
-    cot_hbm, receiver_ref, dsum_ref, hidden_ref, slope_ref, normed_ref, inverse_ref, w2_ref, gain_ref,
+    cot_ref, receiver_ref, dsum_ref, hidden_ref, slope_ref, normed_ref, inverse_ref, w2_ref, gain_ref,
     *refs,
 ):
-    cot_ref, dpre_ref, *out_refs, grads, dout, sem = refs[0 if start == 0 else 1 :]
+    dpre_ref, *out_refs, grads, dout = refs[0 if start == 0 else 1 :]
     here = lax.axis_index("tiles")
-    edges, latent = cot_ref.shape
+    edges, latent = dpre_ref.shape
     nodes = dsum_ref.shape[0]
-    copy = pltpu.make_async_copy(cot_hbm.at[pl.ds(start, edges)], cot_ref, sem)
-    copy.start()
     steps = edges // TILE
     grads[...] = jnp.zeros_like(grads) if start == 0 else refs[0][...]
-    copy.wait()
 
     def outer(step):
         tile = slice(step * TILE, (step + 1) * TILE)
@@ -303,7 +309,7 @@
         receivers = jnp.concatenate(
             pick_columns(index_columns(receiver_ref, start // TILE + step, TILE), 0, nodes), axis=1
         )
-        grad_update = cot_ref[tile, :].astype(F32) + dot(receivers, dsum_ref[...])
+        grad_update = cot_ref[whole, :].astype(F32) + dot(receivers, dsum_ref[...])
         inverse = inverse_ref[whole, :1]
         dout[tile, :] = norm_backward(grad_update * gain_ref[...], normed_ref[whole, :], inverse)
 
@@ -396,15 +402,15 @@
     )
 
 
-def edge_kernel(dpre_a_ref, dpre_b_ref, cot_a_ref, cot_b_ref, w1_ref, out_hbm, out_ref, sems):
-    early, latent = cot_a_ref.shape
+def edge_kernel(dpre_a_ref, dpre_b_ref, cot_ref, w1_ref, out_hbm, out_ref, sems):
+    early, latent = dpre_a_ref.shape
     copies = []
-    for dpre_ref, cot_ref, base in ((dpre_a_ref, cot_a_ref, 0), (dpre_b_ref, cot_b_ref, early)):
+    for dpre_ref, base in ((dpre_a_ref, 0), (dpre_b_ref, early)):
         for at in range(0, early, TILE):
             part = slice(at, at + TILE)
             tile = pl.ds(base + at, TILE)
             out_ref[tile, :] = (
-                cot_ref[part, :].astype(F32) + dot(dpre_ref[part, :], w1_ref[:latent, :], NT)
+                cot_ref[tile, :].astype(F32) + dot(dpre_ref[part, :], w1_ref[:latent, :], NT)
             ).astype(BF16)
             copy = pltpu.make_async_copy(
                 out_ref.at[tile], out_hbm.at[tile], sems.at[(base + at) // TILE]
@@ -566,64 +572,65 @@
     else:
         grad_shapes = lambda count: [shaped((latent, latent), F32), shaped((count, latent), F32)]
 
-    outgoing, inner, outer = call(
+    outgoing, inner, outer, node_kept, w1_early, edge_early = call(
         outgoing_kernel,
         "outgoing",
         [
             shaped((tiles, places, latent), BF16),
             vmem((NEAR, latent), BF16),
             vmem((NEAR, latent), BF16),
-        ],
-        [listed, node_latent],
-        hbm=2,
-        scratch=[vmem(listed.shape, jnp.int32), vmem((nodes, latent), BF16), pltpu.SemaphoreType.DMA((2,))],
+            vmem((nodes, latent), BF16),
+            vmem(edge_w1.shape, BF16),
+            vmem((edges, latent), BF16),
+        ],
+        [listed, node_latent, edge_w1, edge_latent],
+        hbm=4,
+        scratch=[vmem(listed.shape, jnp.int32), pltpu.SemaphoreType.DMA((4,))],
     )
     inner = lax.ppermute(inner, "tiles", inside)
     outer = lax.ppermute(outer, "tiles", across)
     slots = lax.all_to_all(outgoing, "tiles", split_axis=0, concat_axis=0, tiled=True)
-    node_kept, receiver_kept, moved, preact = call(
+    receiver_kept, moved, preact = call(
         functools.partial(prepare_kernel, tiles, places),
         "prepare",
         [
-            vmem((nodes, latent), BF16),
             vmem(receiver.shape, jnp.int32), vmem(sender.shape, jnp.int32),
             vmem((edges, latent), F32),
         ],
-        [node_latent, edge_w1, after(sender, outgoing), receiver, row(edge_b1), edge_latent],
-        hbm=6,
+        [sender, receiver, row(edge_b1), node_kept, w1_early, edge_early],
+        hbm=3,
         scratch=[
-            vmem((edges, latent), BF16), vmem(edge_w1.shape, BF16),
             vmem((latent + 2 * nodes, latent), BF16), vmem(sender.shape, jnp.int32),
-            vmem((1, latent), F32), pltpu.SemaphoreType.DMA((5,)), pltpu.SemaphoreType.DMA((2,)),
+            vmem((1, latent), F32), pltpu.SemaphoreType.DMA((3,)),
         ],
         flops=AHEAD,
     )
 
     (
-        w1_kept, edge_kept, w2_kept, gain_kept,
+        w1_kept, edge_kept, cot_kept, w2_kept, gain_kept,
         hidden, slope, normed, inverse, table, dsum, base, node_send, node_keep,
     ) = call(
         functools.partial(forward_kernel, tiles, places, fast),
         "forward",
         [
-            vmem(edge_w1.shape, BF16), vmem((edges, latent), BF16),
+            vmem(edge_w1.shape, BF16), vmem((edges, latent), BF16), vmem((edges, latent), BF16),
             vmem(edge_w2.shape, BF16), vmem((1, latent), F32),
             vmem((edges, latent), BF16), vmem((edges, latent), BF16), vmem((edges, latent), F32),
             vmem((edges, LANES), F32), vmem((rows, latent), BF16),
             vmem((nodes, latent), BF16), vmem((nodes, latent), F32),
         ] + grad_shapes(3 * latent if fast else 2 * latent),
         [
-            edge_w1, edge_latent, edge_w2, node_w1, node_w2, node_cot,
+            edge_w1, edge_latent, edge_cot, edge_w2, node_w1, node_w2, node_cot,
             row(edge_b2), row(edge_gain), row(node_b1), row(node_b2), row(node_gain), edge_count,
             inner, outer, slots, preact, node_kept, receiver_kept, moved,
         ],
-        hbm=12,
+        hbm=13,
         scratch=[
             vmem((rows - nodes, latent), BF16), vmem((nodes, latent), F32),
             vmem((3 * latent, latent), F32), vmem(node_w1.shape, BF16), vmem(node_w2.shape, BF16),
             vmem((nodes, latent), BF16),
         ] + [vmem((1, latent), F32)] * 4 + [
-            pltpu.SMEM(edge_count.shape, jnp.int32), pltpu.SemaphoreType.DMA((12,)),
+            pltpu.SMEM(edge_count.shape, jnp.int32), pltpu.SemaphoreType.DMA((15,)),
         ],
     )
 
@@ -633,20 +640,17 @@
         return call(
             functools.partial(slope_kernel, tiles, fast, start, last),
             "slope",
-            [vmem((early, latent), BF16), vmem((early, latent), BF16)] + outs,
-            [edge_cot, receiver_kept, dsum, hidden, slope, normed, inverse, w2_kept, gain_kept] + more,
-            hbm=1,
-            scratch=[
-                vmem((latent, latent), F32), vmem((early, latent), BF16), pltpu.SemaphoreType.DMA,
-            ],
+            [vmem((early, latent), BF16)] + outs,
+            [cot_kept, receiver_kept, dsum, hidden, slope, normed, inverse, w2_kept, gain_kept] + more,
+            scratch=[vmem((latent, latent), F32), vmem((early, latent), BF16)],
         )
 
-    cot_a, dpre_a, grads = slope_call(0, False, dsum, [vmem((latent, latent), F32)], [])
+    dpre_a, grads = slope_call(0, False, dsum, [vmem((latent, latent), F32)], [])
     if fast:
         send, chain = halve(1, [after(node_keep, grads)], [swap(tiles, 1, node_send)])
         dsum = after(dsum, send)
         got = swap(tiles, 2, send)
-    cot_b, dpre_b, second_send, second_keep = slope_call(
+    dpre_b, second_send, second_keep = slope_call(
         early, True, dsum, grad_shapes(latent), [grads]
     )
     if fast:
@@ -681,7 +685,7 @@
         edge_kernel,
         "edge",
         [shaped((edges, latent), BF16)],
-        [after(dpre_a, partial), dpre_b, cot_a, cot_b, w1_kept],
+        [after(dpre_a, partial), dpre_b, cot_kept, w1_kept],
         out_specs=[pl.BlockSpec(memory_space=pltpu.HBM)],
         scratch=[vmem((edges, latent), BF16), pltpu.SemaphoreType.DMA((steps,))],
     )
@@ -702,15 +706,15 @@
         got_b = swap(tiles, 2, send_b)
         send, chain = halve(2, [after(chain, send_b)], [got])
         got = swap(tiles, 4, send)
-        to_inner, to_outer = lax.optimization_barrier((to_inner, to_outer, send))[:2]
-        inner = lax.ppermute(to_inner, "tiles", inside)
-        outer = lax.ppermute(to_outer, "tiles", across)
-        send, chain = halve(3, [after(chain, inner, outer)], [got])
+        send, chain = halve(3, [chain], [got])
         got = swap(tiles, 8, send)
         send_a, chain_a, slots = halve(2, [after(chain_a, send)], [got_a], slots, places)
         got_a = swap(tiles, 4, send_a)
         send_b, chain_b = halve(2, [after(chain_b, send_a)], [got_b], flops=AHEAD)
         got_b = swap(tiles, 4, send_b)
+        to_inner, to_outer = lax.optimization_barrier((to_inner, to_outer, send_b))[:2]
+        inner = lax.ppermute(to_inner, "tiles", inside)
+        outer = lax.ppermute(to_outer, "tiles", across)
         chain_a = lax.optimization_barrier((chain_a, send_b, got))[0]
         send_a, chain_a, slots = halve(3, [chain_a], [got_a], slots, places, AHEAD)
         got_a = swap(tiles, 8, send_a)

time: 73.5 us -> 74.2 us (level)
  the two profiles are of different devices: /device:TPU:1 before, /device:TPU:0 now
where the time goes in v9:
time: 74.2 us; the launch traced here: 73.8 us
  Pallas kernels  27.7 us (37%)
  starting transfers between devices  27.5 us (37%)
  waiting for transfers between devices  12.6 us (17%)
  local copies, waits for them, and re-layouts  5.14 us (7%)
  between operations  0.8 us (1%)
    pallas_call x18, Pallas kernels, call(): pl.pallas_call(kernel, in_specs=[pl.BlockSpec(memory_space=pltpu.HBM)] *...  27.7 us
    ppermute x14, starting transfers between devices, swap(): return lax.ppermute(send, 'tiles', [(i, i ^ bit) for i in range(tiles)])  17.8 us
    ppermute x14, waiting for transfers between devices, swap(): return lax.ppermute(send, 'tiles', [(i, i ^ bit) for i in range(tiles)])  12.6 us
    all_to_all x1, starting transfers between devices, shards(): lax.all_to_all(outgoing, 'tiles', split_axis=0, concat_axis=0, tiled=True)  7.36 us
    unnamed x10, local copies, waits for them, and re-layouts  5.14 us
  transfers between devices with their start and end apart: 19, of which 6 were waited for; matrix products, arithmetic and copies ran while one was open for 0% of the time, Pallas kernels for 20%

profile of v9, /device:TPU:0, one launch (start us, length us, event | category | flops | bytes accessed | tf_op | source)
XLA Modules:
  0.0 73.8 jit_solution(15874281039567590874)
XLA Ops:
  0.6 2.7 %outgoing.1 = (bf16[16,2,512]{2,1,0:T(2,128)(2,1)}, bf16[64,512]{1,0:T(8,128)(2,1)}, bf16[64,512]{1,0:T(8,128)(2,1)}, bf16[256,512]{1,0:T(8,128)(2,1)S(1)}, bf16...) custom-call(s32[1,2,16]{2,1,0:T(2,128)} %bitcast.9, bf16[256,512]{1,0:T(8,128)(2,1)} %node_hbm.1, ...), custom_call_target="tpu_custom_call" | custom-call | tf_op jit(solution)/shard_map/outgoing/pallas_call | solution.py:500
  4.5 1.2 %copy-done.3 = bf16[1536,512]{1,0:T(8,128)(2,1)} copy-done((bf16[1536,512]{1,0:T(8,128)(2,1)}, bf16[1536,512]{1,0:T(8,128)(2,1)S(1)}, u32[]{:S(2)}) %copy-start.3) | copy-done | bytes 1572888
  5.7 7.4 %all-to-all-start = ((bf16[16,2,512]{2,1,0:T(2,128)(2,1)}), bf16[16,2,512]{2,1,0:T(2,128)(2,1)S(1)}, u32[]{:S(2)}, u32[]{:S(2)}) async-start(bf16[16,2,512]{2,1,0:T(2,128)(2,1)} %get-tuple-element.83), calls=%async_computation | async-start | bytes 65536 | tf_op jit(solution)/shard_map/all_to_all | solution.py:592
  13.4 1.3 %collective-permute-start.1 = (bf16[64,512]{1,0:T(8,128)(2,1)}, bf16[64,512]{1,0:T(8,128)(2,1)}, u32[]{:S(2)}, u32[]{:S(2)}) collective-permute-start(bf16[64,512]{1,0:T(8,128)(2,1)} %get-tuple-element.82), channel_id=1, source_target_pairs={{1,2},{2,1},{3,4},{4,3},{5,6},{6,5},{7,8},{8,7},{9,10},{10,9},{11,... | collective-permute-start | bytes 196616 | tf_op jit(solution)/shard_map/ppermute | solution.py:591
  14.7 1.4 %copy-done.2 = bf16[1536,512]{1,0:T(8,128)(2,1)S(1)} copy-done((bf16[1536,512]{1,0:T(8,128)(2,1)S(1)}, bf16[1536,512]{1,0:T(8,128)(2,1)}, u32[]{:S(2)}) %copy-start.2) | copy-done | bytes 1572888
  16.1 1.4 %copy-done.4 = bf16[1536,512]{1,0:T(8,128)(2,1)S(1)} copy-done((bf16[1536,512]{1,0:T(8,128)(2,1)S(1)}, bf16[1536,512]{1,0:T(8,128)(2,1)}, u32[]{:S(2)}) %copy-start.4) | copy-done | bytes 1572888
  17.5 2.9 %prepare.1 = (s32[12,128]{1,0:T(8,128)S(1)}, s32[12,128]{1,0:T(8,128)S(1)}, f32[1536,512]{1,0:T(8,128)S(1)}) custom-call(s32[12,128]{1,0:T(8,128)} %bitcast.16, s32[12,128]{1,0:T(8,128)} %bitcast.17, f32[1,512]{1,0:T(1,128)} %bitcast.18, bf16[256,512]{1,0:T(8,128)(2,1)S(1)} %get-tuple-element.84.node_ref, bf16[1536,512]{1,0:T(8,128)(2,1)S(1)} %copy-done.2, ...), custom_call_target="tpu_custom_call" | custom-call | flops 10000000000 | bytes 100000000 | tf_op jit(solution)/shard_map/prepare/pallas_call | solution.py:500
  20.4 9.1 %forward.1 = (bf16[1536,512]{1,0:T(8,128)(2,1)S(1)}, bf16[1536,512]{1,0:T(8,128)(2,1)S(1)}, bf16[1536,512]{1,0:T(8,128)(2,1)S(1)}, bf16[512,512]{1,0:T(8,128)(2,...) custom-call(bf16[1536,512]{1,0:T(8,128)(2,1)} %w1_hbm.3, ...), custom_call_target="tpu_custom_call" | custom-call | tf_op jit(solution)/shard_map/forward/pallas_call | solution.py:500
  29.5 2.5 %collective-permute-start.2 = (bf16[768,512]{1,0:T(8,128)(2,1)S(1)}, bf16[768,512]{1,0:T(8,128)(2,1)S(1)}, u32[]{:S(2)}, u32[]{:S(2)}) collective-permute-start(bf16[768,512]{1,0:T(8,128)(2,1)S(1)} %get-tuple-element.102), channel_id=1, source_target_pairs={{0,1},{1,0},{2,3},{3,2},{4,5},{5,4},{6,7},{7,6},{8,9},{9,8},{10,11... | collective-permute-start | bytes 2359304 | tf_op jit(solution)/shard_map/ppermute | solution.py:513
  32.0 1.7 %slope.2 = (bf16[768,512]{1,0:T(8,128)(2,1)S(1)}, f32[512,512]{1,0:T(8,128)S(1)}) custom-call(bf16[1536,512]{1,0:T(8,128)(2,1)S(1)} %get-tuple-element.90.cot_ref, s32[12,128]{1,0:T(8,128)S(1)} %get-tuple-element.88.receiver_ref, bf16[256,512]{1,0:T(8,128)(2,1)S(1)} %get-tuple-element.104.dsum_ref, bf16[1536,512]{1,0:T(8,128)(2,1)S(1)} %get-tuple-element.92.hidden_ref, ...), custom_call_target="tpu_custom_call" | custom-call | tf_op jit(solution)/shard_map/slope/pallas_call | solution.py:500
  34.1 1.5 %collective-permute-start.7 = (bf16[384,512]{1,0:T(8,128)(2,1)S(1)}, bf16[384,512]{1,0:T(8,128)(2,1)S(1)}, u32[]{:S(2)}, u32[]{:S(2)}) collective-permute-start(bf16[384,512]{1,0:T(8,128)(2,1)S(1)} %get-tuple-element.103), channel_id=1, source_target_pairs={{0,2},{1,3},{2,0},{3,1},{4,6},{5,7},{6,4},{7,5},{8,10},{9,11},{10,... | collective-permute-start | bytes 1179656 | tf_op jit(solution)/shard_map/ppermute | solution.py:513
  35.6 1.9 %slope.3 = (bf16[768,512]{1,0:T(8,128)(2,1)S(1)}, bf16[256,512]{1,0:T(8,128)(2,1)S(1)}, f32[8,32,512]{2,1,0:T(8,128)S(1)}) custom-call(bf16[1536,512]{1,0:T(8,128)(2,1)S(1)} %get-tuple-element.90.cot_ref, s32[12,128]{1,0:T(8,128)S(1)} %get-tuple-element.88.receiver_ref, bf16[256,512]{1,0:T(8,128)(2,1)S(1)} %get-tuple-element.104.dsum_ref, ...), custom_call_target="tpu_custom_call" | custom-call | tf_op jit(solution)/shard_map/slope/pallas_call | solution.py:500
  37.5 4.1 %first.1 = (bf16[64,512]{1,0:T(8,128)(2,1)S(1)}, bf16[64,512]{1,0:T(8,128)(2,1)S(1)}, bf16[32,512]{1,0:T(8,128)(2,1)S(1)}, f32[256,512]{1,0:T(8,128)S(1)}, bf16[...) custom-call(bf16[768,512]{1,0:T(8,128)(2,1)S(1)} %get-tuple-element., ...), custom_call_target="tpu_custom_call" | custom-call | tf_op jit(solution)/shard_map/first/pallas_call | solution.py:500
  42.7 1.8 %edge.1 = bf16[1536,512]{1,0:T(8,128)(2,1)} custom-call(bf16[768,512]{1,0:T(8,128)(2,1)S(1)} %get-tuple-element.115.dpre_a_ref, bf16[768,512]{1,0:T(8,128)(2,1)S(1)} %get-tuple-element.105.dpre_b_ref, bf16[1536,512]{1,0:T(8,128)(2,1)S(1)} %get-tuple-element.90.cot_ref, bf16[1536,512]{1,0:T(8,128)(2,1)S(1)} %get-tuple-element.108.w1_ref), custom_call_target="tpu_custom_call" | custom-call | tf_op jit(solution)/shard_map/edge/pallas_call | solution.py:500
  45.5 1.5 %collective-permute-start.10 = (bf16[256,512]{1,0:T(8,128)(2,1)S(1)}, bf16[256,512]{1,0:T(8,128)(2,1)S(1)}, u32[]{:S(2)}, u32[]{:S(2)}) collective-permute-start(bf16[256,512]{1,0:T(8,128)(2,1)S(1)} %get-tuple-element.129), channel_id=1, source_target_pairs={{0,2},{1,3},{2,0},{3,1},{4,6},{5,7},{6,4},{7,5},{8,10},{9,11},{10,... | collective-permute-start | bytes 786440 | tf_op jit(solution)/shard_map/ppermute | solution.py:513
  47.1 1.5 %collective-permute-start.8 = (bf16[192,512]{1,0:T(8,128)(2,1)S(1)}, bf16[192,512]{1,0:T(8,128)(2,1)S(1)}, u32[]{:S(2)}, u32[]{:S(2)}) collective-permute-start(bf16[192,512]{1,0:T(8,128)(2,1)S(1)} %get-tuple-element.132), channel_id=1, source_target_pairs={{0,4},{1,5},{2,6},{3,7},{4,0},{5,1},{6,2},{7,3},{8,12},{9,13},{10,... | collective-permute-start | bytes 589832 | tf_op jit(solution)/shard_map/ppermute | solution.py:513
  48.6 4.9 %collective-permute-done.8.refs_1_ = bf16[192,512]{1,0:T(8,128)(2,1)S(1)} collective-permute-done((bf16[192,512]{1,0:T(8,128)(2,1)S(1)}, bf16[192,512]{1,0:T(8,128)(2,1)S(1)}, u32[]{:S(2)}, u32[]{:S(2)}) %collective-permute-start.8) | collective-permute-done | bytes 196640 | tf_op jit(solution)/shard_map/ppermute | solution.py:513
  53.6 2.4 %collective-permute-start.13 = (bf16[96,512]{1,0:T(8,128)(2,1)S(1)}, bf16[96,512]{1,0:T(8,128)(2,1)S(1)}, u32[]{:S(2)}, u32[]{:S(2)}) collective-permute-start(bf16[96,512]{1,0:T(8,128)(2,1)S(1)} %get-tuple-element.133), channel_id=1, source_target_pairs={{0,8},{1,9},{2,10},{3,11},{4,12},{5,13},{6,14},{7,15},{8,0},{9,1},... | collective-permute-start | bytes 294920 | tf_op jit(solution)/shard_map/ppermute | solution.py:513
  57.1 2.0 %collective-permute-done.10.refs_1_ = bf16[256,512]{1,0:T(8,128)(2,1)S(1)} collective-permute-done((bf16[256,512]{1,0:T(8,128)(2,1)S(1)}, bf16[256,512]{1,0:T(8,128)(2,1)S(1)}, u32[]{:S(2)}, u32[]{:S(2)}) %collective-permute-start.10) | collective-permute-done | bytes 262176 | tf_op jit(solution)/shard_map/ppermute | solution.py:513
  59.1 1.5 %collective-permute-start.16 = (bf16[128,512]{1,0:T(8,128)(2,1)S(1)}, bf16[128,512]{1,0:T(8,128)(2,1)S(1)}, u32[]{:S(2)}, u32[]{:S(2)}) collective-permute-start(bf16[128,512]{1,0:T(8,128)(2,1)S(1)} %get-tuple-element.138), channel_id=1, source_target_pairs={{0,4},{1,5},{2,6},{3,7},{4,0},{5,1},{6,2},{7,3},{8,12},{9,13},{10,... | collective-permute-start | bytes 393224 | tf_op jit(solution)/shard_map/ppermute | solution.py:513
  62.3 2.8 %collective-permute-start.15 = (bf16[80,512]{1,0:T(8,128)(2,1)S(1)}, bf16[80,512]{1,0:T(8,128)(2,1)S(1)}, u32[]{:S(2)}, u32[]{:S(2)}) collective-permute-start(bf16[80,512]{1,0:T(8,128)(2,1)S(1)} %get-tuple-element.145), channel_id=1, source_target_pairs={{0,8},{1,9},{2,10},{3,11},{4,12},{5,13},{6,14},{7,15},{8,0},{9,1},... | collective-permute-start | bytes 245768 | tf_op jit(solution)/shard_map/ppermute | solution.py:513
  65.1 1.5 %collective-permute-start.17 = (bf16[64,512]{1,0:T(8,128)(2,1)S(1)}, bf16[64,512]{1,0:T(8,128)(2,1)S(1)}, u32[]{:S(2)}, u32[]{:S(2)}) collective-permute-start(bf16[64,512]{1,0:T(8,128)(2,1)S(1)} %get-tuple-element.151), channel_id=1, source_target_pairs={{0,8},{1,9},{2,10},{3,11},{4,12},{5,13},{6,14},{7,15},{8,0},{9,1},... | collective-permute-start | bytes 196616 | tf_op jit(solution)/shard_map/ppermute | solution.py:513
  66.7 4.2 %collective-permute-done.15.refs_0_.refs_4_ = bf16[80,512]{1,0:T(8,128)(2,1)S(1)} collective-permute-done((bf16[80,512]{1,0:T(8,128)(2,1)S(1)}, bf16[80,512]{1,0:T(8,128)(2,1)S(1)}, u32[]{:S(2)}, u32[]{:S(2)}) %collective-permute-start.15) | collective-permute-done | bytes 81952 | tf_op jit(solution)/shard_map/ppermute | solution.py:513
  70.9 1.5 %node.1 = bf16[256,512]{1,0:T(8,128)(2,1)} custom-call(s32[1,2,16]{2,1,0:T(2,128)S(1)} %bitcast.10, f32[256,512]{1,0:T(8,128)S(1)} %get-tuple-element.110.partial_ref, bf16[64,512]{1,0:T(8,128)(2,1)S(1)} %collective-permute-done.11.inner_ref, bf16[64,512]{1,0:T(8,128)(2,1)S(1)} %collective-permute-done.12.outer_ref, ...), custom_call_target="tpu_custom_call" | custom-call | tf_op jit(solution)/shard_map/node/pallas_call | solution.py:500
  (42 shorter events, 8.2 us)
Async XLA Ops:
  3.3 1.1 %copy-start.1 = (bf16[1536,512]{1,0:T(8,128)(2,1)}, bf16[1536,512]{1,0:T(8,128)(2,1)S(1)}, u32[]{:S(2)}) copy-start(bf16[1536,512]{1,0:T(8,128)(2,1)S(1)} %get-tuple-element.85.w1_ref) | copy-start | bytes 4718596
  4.5 1.2 %copy-start.3 = (bf16[1536,512]{1,0:T(8,128)(2,1)}, bf16[1536,512]{1,0:T(8,128)(2,1)S(1)}, u32[]{:S(2)}) copy-start(bf16[1536,512]{1,0:T(8,128)(2,1)S(1)} %get-tuple-element.86.edge_ref) | copy-start | bytes 4718596
  5.7 14.7 %all-to-all-start = ((bf16[16,2,512]{2,1,0:T(2,128)(2,1)}), bf16[16,2,512]{2,1,0:T(2,128)(2,1)S(1)}, u32[]{:S(2)}, u32[]{:S(2)}) async-start(bf16[16,2,512]{2,1,0:T(2,128)(2,1)} %get-tuple-element.83), calls=%async_computation | async-start | bytes 65536 | tf_op jit(solution)/shard_map/all_to_all | solution.py:592
  13.0 7.4 %collective-permute-start = (bf16[64,512]{1,0:T(8,128)(2,1)}, bf16[64,512]{1,0:T(8,128)(2,1)S(1)}, u32[]{:S(2)}, u32[]{:S(2)}) collective-permute-start(bf16[64,512]{1,0:T(8,128)(2,1)} %get-tuple-element.81), channel_id=1, source_target_pairs={{0,1},{1,0},{2,3},{3,2},{4,5},{5,4},{6,7},{7,6},{8,9},{9,8},{10,11... | collective-permute-start | bytes 196616 | tf_op jit(solution)/shard_map/ppermute | solution.py:590
  13.4 7.0 %collective-permute-start.1 = (bf16[64,512]{1,0:T(8,128)(2,1)}, bf16[64,512]{1,0:T(8,128)(2,1)}, u32[]{:S(2)}, u32[]{:S(2)}) collective-permute-start(bf16[64,512]{1,0:T(8,128)(2,1)} %get-tuple-element.82), channel_id=1, source_target_pairs={{1,2},{2,1},{3,4},{4,3},{5,6},{6,5},{7,8},{8,7},{9,10},{10,9},{11,... | collective-permute-start | bytes 196616 | tf_op jit(solution)/shard_map/ppermute | solution.py:591
  14.7 1.4 %copy-start.2 = (bf16[1536,512]{1,0:T(8,128)(2,1)S(1)}, bf16[1536,512]{1,0:T(8,128)(2,1)}, u32[]{:S(2)}) copy-start(bf16[1536,512]{1,0:T(8,128)(2,1)} %copy-done.1) | copy-start | bytes 4718596
  16.1 1.4 %copy-start.4 = (bf16[1536,512]{1,0:T(8,128)(2,1)S(1)}, bf16[1536,512]{1,0:T(8,128)(2,1)}, u32[]{:S(2)}) copy-start(bf16[1536,512]{1,0:T(8,128)(2,1)} %copy-done.3) | copy-start | bytes 4718596
  29.5 4.4 %collective-permute-start.2 = (bf16[768,512]{1,0:T(8,128)(2,1)S(1)}, bf16[768,512]{1,0:T(8,128)(2,1)S(1)}, u32[]{:S(2)}, u32[]{:S(2)}) collective-permute-start(bf16[768,512]{1,0:T(8,128)(2,1)S(1)} %get-tuple-element.102), channel_id=1, source_target_pairs={{0,1},{1,0},{2,3},{3,2},{4,5},{5,4},{6,7},{7,6},{8,9},{9,8},{10,11... | collective-permute-start | bytes 2359304 | tf_op jit(solution)/shard_map/ppermute | solution.py:513
  34.1 12.9 %collective-permute-start.7 = (bf16[384,512]{1,0:T(8,128)(2,1)S(1)}, bf16[384,512]{1,0:T(8,128)(2,1)S(1)}, u32[]{:S(2)}, u32[]{:S(2)}) collective-permute-start(bf16[384,512]{1,0:T(8,128)(2,1)S(1)} %get-tuple-element.103), channel_id=1, source_target_pairs={{0,2},{1,3},{2,0},{3,1},{4,6},{5,7},{6,4},{7,5},{8,10},{9,11},{10,... | collective-permute-start | bytes 1179656 | tf_op jit(solution)/shard_map/ppermute | solution.py:513
  41.6 2.9 %collective-permute-start.3 = (bf16[272,512]{1,0:T(8,128)(2,1)S(1)}, bf16[272,512]{1,0:T(8,128)(2,1)S(1)}, u32[]{:S(2)}, u32[]{:S(2)}) collective-permute-start(bf16[272,512]{1,0:T(8,128)(2,1)S(1)} %get-tuple-element.118), channel_id=1, source_target_pairs={{0,1},{1,0},{2,3},{3,2},{4,5},{5,4},{6,7},{7,6},{8,9},{9,8},{10,11... | collective-permute-start | bytes 835592 | tf_op jit(solution)/shard_map/ppermute | solution.py:513
  41.8 2.7 %collective-permute-start.4 = (bf16[256,512]{1,0:T(8,128)(2,1)S(1)}, bf16[256,512]{1,0:T(8,128)(2,1)S(1)}, u32[]{:S(2)}, u32[]{:S(2)}) collective-permute-start(bf16[256,512]{1,0:T(8,128)(2,1)S(1)} %get-tuple-element.119), channel_id=1, source_target_pairs={{0,1},{1,0},{2,3},{3,2},{4,5},{5,4},{6,7},{7,6},{8,9},{9,8},{10,11... | collective-permute-start | bytes 786440 | tf_op jit(solution)/shard_map/ppermute | solution.py:513
  42.2 3.2 %collective-permute-start.5 = (bf16[256,512]{1,0:T(8,128)(2,1)S(1)}, bf16[256,512]{1,0:T(8,128)(2,1)S(1)}, u32[]{:S(2)}, u32[]{:S(2)}) collective-permute-start(bf16[256,512]{1,0:T(8,128)(2,1)S(1)} %get-tuple-element.124), channel_id=1, source_target_pairs={{0,1},{1,0},{2,3},{3,2},{4,5},{5,4},{6,7},{7,6},{8,9},{9,8},{10,11... | collective-permute-start | bytes 786440 | tf_op jit(solution)/shard_map/ppermute | solution.py:513
  42.3 3.1 %collective-permute-start.6 = (bf16[256,512]{1,0:T(8,128)(2,1)S(1)}, bf16[256,512]{1,0:T(8,128)(2,1)S(1)}, u32[]{:S(2)}, u32[]{:S(2)}) collective-permute-start(bf16[256,512]{1,0:T(8,128)(2,1)S(1)} %get-tuple-element.125), channel_id=1, source_target_pairs={{0,1},{1,0},{2,3},{3,2},{4,5},{5,4},{6,7},{7,6},{8,9},{9,8},{10,11... | collective-permute-start | bytes 786440 | tf_op jit(solution)/shard_map/ppermute | solution.py:513
  44.8 11.2 %collective-permute-start.9 = (bf16[272,512]{1,0:T(8,128)(2,1)S(1)}, bf16[272,512]{1,0:T(8,128)(2,1)S(1)}, u32[]{:S(2)}, u32[]{:S(2)}) collective-permute-start(bf16[272,512]{1,0:T(8,128)(2,1)S(1)} %get-tuple-element.121), channel_id=1, source_target_pairs={{0,2},{1,3},{2,0},{3,1},{4,6},{5,7},{6,4},{7,5},{8,10},{9,11},{10,... | collective-permute-start | bytes 835592 | tf_op jit(solution)/shard_map/ppermute | solution.py:513
  45.5 13.6 %collective-permute-start.10 = (bf16[256,512]{1,0:T(8,128)(2,1)S(1)}, bf16[256,512]{1,0:T(8,128)(2,1)S(1)}, u32[]{:S(2)}, u32[]{:S(2)}) collective-permute-start(bf16[256,512]{1,0:T(8,128)(2,1)S(1)} %get-tuple-element.129), channel_id=1, source_target_pairs={{0,2},{1,3},{2,0},{3,1},{4,6},{5,7},{6,4},{7,5},{8,10},{9,11},{10,... | collective-permute-start | bytes 786440 | tf_op jit(solution)/shard_map/ppermute | solution.py:513
  47.1 6.4 %collective-permute-start.8 = (bf16[192,512]{1,0:T(8,128)(2,1)S(1)}, bf16[192,512]{1,0:T(8,128)(2,1)S(1)}, u32[]{:S(2)}, u32[]{:S(2)}) collective-permute-start(bf16[192,512]{1,0:T(8,128)(2,1)S(1)} %get-tuple-element.132), channel_id=1, source_target_pairs={{0,4},{1,5},{2,6},{3,7},{4,0},{5,1},{6,2},{7,3},{8,12},{9,13},{10,... | collective-permute-start | bytes 589832 | tf_op jit(solution)/shard_map/ppermute | solution.py:513
  53.6 7.8 %collective-permute-start.13 = (bf16[96,512]{1,0:T(8,128)(2,1)S(1)}, bf16[96,512]{1,0:T(8,128)(2,1)S(1)}, u32[]{:S(2)}, u32[]{:S(2)}) collective-permute-start(bf16[96,512]{1,0:T(8,128)(2,1)S(1)} %get-tuple-element.133), channel_id=1, source_target_pairs={{0,8},{1,9},{2,10},{3,11},{4,12},{5,13},{6,14},{7,15},{8,0},{9,1},... | collective-permute-start | bytes 294920 | tf_op jit(solution)/shard_map/ppermute | solution.py:513
  56.3 5.7 %collective-permute-start.14 = (bf16[144,512]{1,0:T(8,128)(2,1)S(1)}, bf16[144,512]{1,0:T(8,128)(2,1)S(1)}, u32[]{:S(2)}, u32[]{:S(2)}) collective-permute-start(bf16[144,512]{1,0:T(8,128)(2,1)S(1)} %get-tuple-element.136), channel_id=1, source_target_pairs={{0,4},{1,5},{2,6},{3,7},{4,0},{5,1},{6,2},{7,3},{8,12},{9,13},{10,... | collective-permute-start | bytes 442376 | tf_op jit(solution)/shard_map/ppermute | solution.py:513
  59.1 5.9 %collective-permute-start.16 = (bf16[128,512]{1,0:T(8,128)(2,1)S(1)}, bf16[128,512]{1,0:T(8,128)(2,1)S(1)}, u32[]{:S(2)}, u32[]{:S(2)}) collective-permute-start(bf16[128,512]{1,0:T(8,128)(2,1)S(1)} %get-tuple-element.138), channel_id=1, source_target_pairs={{0,4},{1,5},{2,6},{3,7},{4,0},{5,1},{6,2},{7,3},{8,12},{9,13},{10,... | collective-permute-start | bytes 393224 | tf_op jit(solution)/shard_map/ppermute | solution.py:513
  60.7 6.0 %collective-permute-start.11 = (bf16[64,512]{1,0:T(8,128)(2,1)S(1)}, bf16[64,512]{1,0:T(8,128)(2,1)S(1)}, u32[]{:S(2)}, u32[]{:S(2)}) collective-permute-start(bf16[64,512]{1,0:T(8,128)(2,1)S(1)} %get-tuple-element.139), channel_id=1, source_target_pairs={{0,1},{1,0},{2,3},{3,2},{4,5},{5,4},{6,7},{7,6},{8,9},{9,8},{10,11... | collective-permute-start | bytes 196616 | tf_op jit(solution)/shard_map/ppermute | solution.py:716
  60.7 6.0 %collective-permute-start.12 = (bf16[64,512]{1,0:T(8,128)(2,1)S(1)}, bf16[64,512]{1,0:T(8,128)(2,1)S(1)}, u32[]{:S(2)}, u32[]{:S(2)}) collective-permute-start(bf16[64,512]{1,0:T(8,128)(2,1)S(1)} %get-tuple-element.140), channel_id=1, source_target_pairs={{1,2},{2,1},{3,4},{4,3},{5,6},{6,5},{7,8},{8,7},{9,10},{10,9},{11,... | collective-permute-start | bytes 196616 | tf_op jit(solution)/shard_map/ppermute | solution.py:717
  62.3 8.6 %collective-permute-start.15 = (bf16[80,512]{1,0:T(8,128)(2,1)S(1)}, bf16[80,512]{1,0:T(8,128)(2,1)S(1)}, u32[]{:S(2)}, u32[]{:S(2)}) collective-permute-start(bf16[80,512]{1,0:T(8,128)(2,1)S(1)} %get-tuple-element.145), channel_id=1, source_target_pairs={{0,8},{1,9},{2,10},{3,11},{4,12},{5,13},{6,14},{7,15},{8,0},{9,1},... | collective-permute-start | bytes 245768 | tf_op jit(solution)/shard_map/ppermute | solution.py:513
  65.1 5.8 %copy-start = (s32[1,16,2]{1,2,0:T(2,128)S(1)}, s32[1,16,2]{1,2,0:T(2,128)}, u32[]{:S(2)}) copy-start(s32[1,16,2]{1,2,0:T(2,128)} %param.32) | copy-start | bytes 388
  65.1 7.9 %collective-permute-start.17 = (bf16[64,512]{1,0:T(8,128)(2,1)S(1)}, bf16[64,512]{1,0:T(8,128)(2,1)S(1)}, u32[]{:S(2)}, u32[]{:S(2)}) collective-permute-start(bf16[64,512]{1,0:T(8,128)(2,1)S(1)} %get-tuple-element.151), channel_id=1, source_target_pairs={{0,8},{1,9},{2,10},{3,11},{4,12},{5,13},{6,14},{7,15},{8,0},{9,1},... | collective-permute-start | bytes 196616 | tf_op jit(solution)/shard_map/ppermute | solution.py:513

commit v10 on v9

--- a/solution.py
+++ b/solution.py
@@ -69,14 +69,15 @@
     ).astype(BF16)
 
 
-def split_halves(bit, total_ref, at, block, first, rows, send_ref, keep_ref, offset):
+def split_halves(bit, total_ref, at, block, first, rows, send_ref, keep_ref, offset, x_last=False):
     half, size = keep_ref.shape[:2]
-    for q in range(half):
+    for to in range(half):
+        q = 2 * to % half + 2 * to // half if x_last else to
+        to = to * size + offset
         there = pl.multiple_of(at + first + (2 * q + 1 - bit) * block, 32)
         here = pl.multiple_of(at + first + (2 * q + bit) * block, 32)
-        to = q * size + offset
         send_ref[to : to + rows, :] = total_ref[pl.ds(there, rows), :].astype(BF16)
-        keep_ref[q, offset : offset + rows, :] = total_ref[pl.ds(here, rows), :]
+        keep_ref[to // size, offset : offset + rows, :] = total_ref[pl.ds(here, rows), :]
 
 
 def fetch(pairs, sems):
@@ -123,18 +124,10 @@
 
 
 def outgoing_kernel(
-    index_hbm, node_hbm, w1_hbm, edge_hbm,
-    slots_ref, inner_ref, outer_ref, node_ref, w1_ref, edge_ref,
-    index_ref, sems,
+    index_hbm, node_hbm, slots_ref, inner_ref, outer_ref, index_ref, node_ref, sems
 ):
-    copies = fetch(
-        [
-            (index_hbm, index_ref), (node_hbm, node_ref), (w1_hbm, w1_ref), (edge_hbm, edge_ref),
-        ],
-        sems,
-    )
-    copies[0].wait()
-    copies[1].wait()
+    for copy in fetch([(index_hbm, index_ref), (node_hbm, node_ref)], sems):
+        copy.wait()
     places, tiles = index_ref.shape[1], index_ref.shape[2]
     nodes, latent = node_ref.shape
     place = lax.broadcasted_iota(jnp.int32, (nodes, tiles), 0)
@@ -144,8 +137,6 @@
     odd = lax.rem(lax.axis_index("tiles"), 2)
     inner_ref[...] = node_ref[pl.ds(pl.multiple_of((1 - odd) * (nodes - NEAR), NEAR), NEAR), :]
     outer_ref[...] = node_ref[pl.ds(pl.multiple_of(odd * (nodes - NEAR), NEAR), NEAR), :]
-    copies[2].wait()
-    copies[3].wait()
 
 
 def table_index(raw, tiles, places, nodes):
@@ -158,23 +149,30 @@
 
 def prepare_kernel(
     tiles, places,
-    sender_hbm, receiver_hbm, b1_hbm, node_ref, w1_ref, edge_ref,
-    receiver_ref, moved_ref, partial_ref,
-    weights, sender_ref, b1_ref, sems,
+    node_hbm, w1_hbm, sender_hbm, receiver_hbm, b1_hbm, edge_hbm,
+    node_ref, receiver_ref, moved_ref, partial_ref,
+    edge_ref, w1_ref, weights, sender_ref, b1_ref, sems, edge_sems,
 ):
     edges, latent = edge_ref.shape
     nodes = node_ref.shape[0]
     copies = fetch(
-        [(sender_hbm, sender_ref), (receiver_hbm, receiver_ref), (b1_hbm, b1_ref)], sems
-    )
+        [
+            (node_hbm, node_ref), (w1_hbm, w1_ref), (sender_hbm, sender_ref),
+            (receiver_hbm, receiver_ref), (b1_hbm, b1_ref),
+        ],
+        sems,
+    )
+    edge_copies = fetch(tile_pairs(edge_hbm, edge_ref, edges // 2), edge_sems)
+    for copy in copies:
+        copy.wait()
+    moved_ref[...] = table_index(sender_ref[...], tiles, places, nodes)
     weights[:latent, :] = w1_ref[:latent, :]
     weights[latent : latent + nodes, :] = dot(
         node_ref[...], w1_ref[latent : 2 * latent, :]
     ).astype(BF16)
     weights[latent + nodes :, :] = dot(node_ref[...], w1_ref[2 * latent :, :]).astype(BF16)
-    for copy in copies:
+    for copy in edge_copies:
         copy.wait()
-    moved_ref[...] = table_index(sender_ref[...], tiles, places, nodes)
     for step in range(edges // TILE):
         tile = slice(step * TILE, (step + 1) * TILE)
         senders = pick_columns(index_columns(moved_ref, step, TILE), 0, nodes)
@@ -283,9 +281,9 @@
     if fast:
         bit = lax.rem(here, 2)
         first = 2 * latent // tiles
-        split_halves(bit, grads, 0, first, 0, first, gsend_ref, gkeep_ref, 0)
+        split_halves(bit, grads, 0, first, 0, first, gsend_ref, gkeep_ref, 0, True)
         second = latent // tiles
-        split_halves(bit, grads, 2 * latent, second, 0, second, gsend_ref, gkeep_ref, first)
+        split_halves(bit, grads, 2 * latent, second, 0, second, gsend_ref, gkeep_ref, first, True)
     else:
         gkeep_ref[...] = grads[: 2 * latent, :]
         gsend_ref[...] = grads[2 * latent :, :]
@@ -572,36 +570,35 @@
     else:
         grad_shapes = lambda count: [shaped((latent, latent), F32), shaped((count, latent), F32)]
 
-    outgoing, inner, outer, node_kept, w1_early, edge_early = call(
+    outgoing, inner, outer = call(
         outgoing_kernel,
         "outgoing",
         [
             shaped((tiles, places, latent), BF16),
             vmem((NEAR, latent), BF16),
             vmem((NEAR, latent), BF16),
-            vmem((nodes, latent), BF16),
-            vmem(edge_w1.shape, BF16),
-            vmem((edges, latent), BF16),
-        ],
-        [listed, node_latent, edge_w1, edge_latent],
-        hbm=4,
-        scratch=[vmem(listed.shape, jnp.int32), pltpu.SemaphoreType.DMA((4,))],
+        ],
+        [listed, node_latent],
+        hbm=2,
+        scratch=[vmem(listed.shape, jnp.int32), vmem((nodes, latent), BF16), pltpu.SemaphoreType.DMA((2,))],
     )
     inner = lax.ppermute(inner, "tiles", inside)
     outer = lax.ppermute(outer, "tiles", across)
     slots = lax.all_to_all(outgoing, "tiles", split_axis=0, concat_axis=0, tiled=True)
-    receiver_kept, moved, preact = call(
+    node_kept, receiver_kept, moved, preact = call(
         functools.partial(prepare_kernel, tiles, places),
         "prepare",
         [
+            vmem((nodes, latent), BF16),
             vmem(receiver.shape, jnp.int32), vmem(sender.shape, jnp.int32),
             vmem((edges, latent), F32),
         ],
-        [sender, receiver, row(edge_b1), node_kept, w1_early, edge_early],
-        hbm=3,
+        [node_latent, edge_w1, after(sender, outgoing), receiver, row(edge_b1), edge_latent],
+        hbm=6,
         scratch=[
+            vmem((edges, latent), BF16), vmem(edge_w1.shape, BF16),
             vmem((latent + 2 * nodes, latent), BF16), vmem(sender.shape, jnp.int32),
-            vmem((1, latent), F32), pltpu.SemaphoreType.DMA((3,)),
+            vmem((1, latent), F32), pltpu.SemaphoreType.DMA((5,)), pltpu.SemaphoreType.DMA((2,)),
         ],
         flops=AHEAD,
     )
@@ -647,9 +644,9 @@
 
     dpre_a, grads = slope_call(0, False, dsum, [vmem((latent, latent), F32)], [])
     if fast:
-        send, chain = halve(1, [after(node_keep, grads)], [swap(tiles, 1, node_send)])
+        send, chain = halve(2, [after(node_keep, grads)], [swap(tiles, 1, node_send)])
         dsum = after(dsum, send)
-        got = swap(tiles, 2, send)
+        got = swap(tiles, 4, send)
     dpre_b, second_send, second_keep = slope_call(
         early, True, dsum, grad_shapes(latent), [grads]
     )
@@ -704,18 +701,18 @@
             1, [after(keep_b, send_a), second_keep], [swap(tiles, 1, send_b), got_second]
      )
         got_b = swap(tiles, 2, send_b)
-        send, chain = halve(2, [after(chain, send_b)], [got])
-        got = swap(tiles, 4, send)
-        send, chain = halve(3, [chain], [got])
+        send, chain = halve(3, [after(chain, send_b)], [got], flops=AHEAD)
         got = swap(tiles, 8, send)
+        to_inner, to_outer = lax.optimization_barrier((to_inner, to_outer, send))[:2]
+        inner = lax.ppermute(to_inner, "tiles", inside)
+        outer = lax.ppermute(to_outer, "tiles", across)
         send_a, chain_a, slots = halve(2, [after(chain_a, send)], [got_a], slots, places)
         got_a = swap(tiles, 4, send_a)
-        send_b, chain_b = halve(2, [after(chain_b, send_a)], [got_b], flops=AHEAD)
+        send_b, chain_b = halve(2, [after(chain_b, send_a, inner, outer)], [got_b])
         got_b = swap(tiles, 4, send_b)
-        to_inner, to_outer = lax.optimization_barrier((to_inner, to_outer, send_b))[:2]
-        inner = lax.ppermute(to_inner, "tiles", inside)
-        outer = lax.ppermute(to_outer, "tiles", across)
-        chain_a = lax.optimization_barrier((chain_a, send_b, got))[0]
+        send, chain = halve(1, [after(chain, send_b)], [got])
+        got = swap(tiles, 2, send)
+        chain_a = after(chain_a, send)
         send_a, chain_a, slots = halve(3, [chain_a], [got_a], slots, places, AHEAD)
         got_a = swap(tiles, 8, send_a)
         chain_b = after(chain_b, send_a)

time: 74.2 us -> 70.9 us (0.956)
  local copies, waits for them, and re-layouts: 5.14 us -> 0.01 us
  starting transfers between devices: 27.5 us -> 29.6 us
    unnamed x10 -> x2, local copies, waits for them, and re-layouts: 5.14 us -> 0.01 us
    ppermute x14, starting transfers between devices: 17.8 us -> 19.9 us  [swap(): return lax.ppermute(send, 'tiles', [(i, i ^ bit) for i in range(tiles)])]
    ppermute x14, waiting for transfers between devices: 12.6 us -> 10.9 us  [swap(): return lax.ppermute(send, 'tiles', [(i, i ^ bit) for i in range(tiles)])]
    all_to_all x1, waiting for transfers between devices: 0.01 us -> 1.09 us  [shards(): lax.all_to_all(outgoing, 'tiles', split_axis=0, concat_axis=0, tiled=True)]
  transfers between devices with their start and end apart: 19 -> 19, of which waited for: 6 -> 8; matrix products, arithmetic and copies ran while one was open for 0% -> 0% of each run, Pallas kernels for 20% -> 23%
where the time goes in v10:
time: 70.9 us; the launch traced here: 70.7 us
  starting transfers between devices  29.6 us (42%)
  Pallas kernels  27.7 us (39%)
  waiting for transfers between devices  12.5 us (18%)
  between operations  0.76 us (1%)
    pallas_call x18, Pallas kernels, call(): pl.pallas_call(kernel, in_specs=[pl.BlockSpec(memory_space=pltpu.HBM)] *...  27.7 us
    ppermute x14, starting transfers between devices, swap(): return lax.ppermute(send, 'tiles', [(i, i ^ bit) for i in range(tiles)])  19.9 us
    ppermute x14, waiting for transfers between devices, swap(): return lax.ppermute(send, 'tiles', [(i, i ^ bit) for i in range(tiles)])  10.9 us
    all_to_all x1, starting transfers between devices, shards(): lax.all_to_all(outgoing, 'tiles', split_axis=0, concat_axis=0, tiled=True)  7.37 us
  transfers between devices with their start and end apart: 19, of which 8 were waited for; matrix products, arithmetic and copies ran while one was open for 0% of the time, Pallas kernels for 23%

profile of v10, /device:TPU:0, one launch (start us, length us, event | category | flops | bytes accessed | tf_op | source)
XLA Modules:
  0.0 70.7 jit_solution(9227574606279178168)
XLA Ops:
  0.6 1.8 %outgoing.1 = (bf16[16,2,512]{2,1,0:T(2,128)(2,1)}, bf16[64,512]{1,0:T(8,128)(2,1)}, bf16[64,512]{1,0:T(8,128)(2,1)}) custom-call(s32[1,2,16]{2,1,0:T(2,128)} %bitcast.9, bf16[256,512]{1,0:T(8,128)(2,1)} %node_hbm.3), custom_call_target="tpu_custom_call" | custom-call | tf_op jit(solution)/shard_map/outgoing/pallas_call | solution.py:498
  2.5 7.4 %all-to-all-start = ((bf16[16,2,512]{2,1,0:T(2,128)(2,1)}), bf16[16,2,512]{2,1,0:T(2,128)(2,1)S(1)}, u32[]{:S(2)}, u32[]{:S(2)}) async-start(bf16[16,2,512]{2,1,0:T(2,128)(2,1)} %get-tuple-element.83), calls=%async_computation | async-start | bytes 65536 | tf_op jit(solution)/shard_map/all_to_all | solution.py:587
  10.2 1.3 %collective-permute-start.1 = (bf16[64,512]{1,0:T(8,128)(2,1)}, bf16[64,512]{1,0:T(8,128)(2,1)}, u32[]{:S(2)}, u32[]{:S(2)}) collective-permute-start(bf16[64,512]{1,0:T(8,128)(2,1)} %get-tuple-element.82), channel_id=1, source_target_pairs={{1,2},{2,1},{3,4},{4,3},{5,6},{6,5},{7,8},{8,7},{9,10},{10,9},{11,... | collective-permute-start | bytes 196616 | tf_op jit(solution)/shard_map/ppermute | solution.py:586
  11.5 3.8 %prepare.1 = (bf16[256,512]{1,0:T(8,128)(2,1)S(1)}, s32[12,128]{1,0:T(8,128)S(1)}, s32[12,128]{1,0:T(8,128)S(1)}, f32[1536,512]{1,0:T(8,128)S(1)}) custom-call(bf16[256,512]{1,0:T(8,128)(2,1)} %node_hbm.3, bf16[1536,512]{1,0:T(8,128)(2,1)} %w1_hbm.3, s32[12,128]{1,0:T(8,128)} %bitcast.16, s32[12,128]{1,0:T(8,128)} %bitcast.17, f32[1,512]{1,0:T(1,128)} %bitcast.18, ...), custom_call_target="tpu_custom_call" | custom-call | flops 10000000000 | bytes 100000000 | tf_op jit(solution)/shard_map/prepare/pallas_call | solution.py:498
  15.4 1.1 %all-to-all-done.far_ref = bf16[16,2,512]{2,1,0:T(2,128)(2,1)S(1)} async-done(((bf16[16,2,512]{2,1,0:T(2,128)(2,1)}), bf16[16,2,512]{2,1,0:T(2,128)(2,1)S(1)}, u32[]{:S(2)}, u32[]{:S(2)}) %all-to-all-start) | async-done | bytes 32800 | tf_op jit(solution)/shard_map/all_to_all | solution.py:587
  16.5 9.0 %forward.1 = (bf16[1536,512]{1,0:T(8,128)(2,1)S(1)}, bf16[1536,512]{1,0:T(8,128)(2,1)S(1)}, bf16[1536,512]{1,0:T(8,128)(2,1)S(1)}, bf16[512,512]{1,0:T(8,128)(2,...) custom-call(bf16[1536,512]{1,0:T(8,128)(2,1)} %w1_hbm.3, ...), custom_call_target="tpu_custom_call" | custom-call | tf_op jit(solution)/shard_map/forward/pallas_call | solution.py:498
  25.5 1.5 %collective-permute-start.2 = (bf16[768,512]{1,0:T(8,128)(2,1)S(1)}, bf16[768,512]{1,0:T(8,128)(2,1)S(1)}, u32[]{:S(2)}, u32[]{:S(2)}) collective-permute-start(bf16[768,512]{1,0:T(8,128)(2,1)S(1)} %get-tuple-element.101), channel_id=1, source_target_pairs={{0,1},{1,0},{2,3},{3,2},{4,5},{5,4},{6,7},{7,6},{8,9},{9,8},{10,11... | collective-permute-start | bytes 2359304 | tf_op jit(solution)/shard_map/ppermute | solution.py:511
  27.0 1.7 %slope.2 = (bf16[768,512]{1,0:T(8,128)(2,1)S(1)}, f32[512,512]{1,0:T(8,128)S(1)}) custom-call(bf16[1536,512]{1,0:T(8,128)(2,1)S(1)} %get-tuple-element.89.cot_ref, s32[12,128]{1,0:T(8,128)S(1)} %get-tuple-element.87.receiver_ref, bf16[256,512]{1,0:T(8,128)(2,1)S(1)} %get-tuple-element.103.dsum_ref, bf16[1536,512]{1,0:T(8,128)(2,1)S(1)} %get-tuple-element.91.hidden_ref, ...), custom_call_target="tpu_custom_call" | custom-call | tf_op jit(solution)/shard_map/slope/pallas_call | solution.py:498
  29.1 1.7 %collective-permute-start.7 = (bf16[384,512]{1,0:T(8,128)(2,1)S(1)}, bf16[384,512]{1,0:T(8,128)(2,1)S(1)}, u32[]{:S(2)}, u32[]{:S(2)}) collective-permute-start(bf16[384,512]{1,0:T(8,128)(2,1)S(1)} %get-tuple-element.102), channel_id=1, source_target_pairs={{0,4},{1,5},{2,6},{3,7},{4,0},{5,1},{6,2},{7,3},{8,12},{9,13},{10,... | collective-permute-start | bytes 1179656 | tf_op jit(solution)/shard_map/ppermute | solution.py:511
  30.8 1.9 %slope.3 = (bf16[768,512]{1,0:T(8,128)(2,1)S(1)}, bf16[256,512]{1,0:T(8,128)(2,1)S(1)}, f32[8,32,512]{2,1,0:T(8,128)S(1)}) custom-call(bf16[1536,512]{1,0:T(8,128)(2,1)S(1)} %get-tuple-element.89.cot_ref, s32[12,128]{1,0:T(8,128)S(1)} %get-tuple-element.87.receiver_ref, bf16[256,512]{1,0:T(8,128)(2,1)S(1)} %get-tuple-element.103.dsum_ref, ...), custom_call_target="tpu_custom_call" | custom-call | tf_op jit(solution)/shard_map/slope/pallas_call | solution.py:498
  32.7 4.0 %first.1 = (bf16[64,512]{1,0:T(8,128)(2,1)S(1)}, bf16[64,512]{1,0:T(8,128)(2,1)S(1)}, bf16[32,512]{1,0:T(8,128)(2,1)S(1)}, f32[256,512]{1,0:T(8,128)S(1)}, bf16[...) custom-call(bf16[768,512]{1,0:T(8,128)(2,1)S(1)} %get-tuple-element., ...), custom_call_target="tpu_custom_call" | custom-call | tf_op jit(solution)/shard_map/first/pallas_call | solution.py:498
  37.8 1.8 %edge.1 = bf16[1536,512]{1,0:T(8,128)(2,1)} custom-call(bf16[768,512]{1,0:T(8,128)(2,1)S(1)} %get-tuple-element.115.dpre_a_ref, bf16[768,512]{1,0:T(8,128)(2,1)S(1)} %get-tuple-element.104.dpre_b_ref, bf16[1536,512]{1,0:T(8,128)(2,1)S(1)} %get-tuple-element.89.cot_ref, bf16[1536,512]{1,0:T(8,128)(2,1)S(1)} %get-tuple-element.107.w1_ref), custom_call_target="tpu_custom_call" | custom-call | tf_op jit(solution)/shard_map/edge/pallas_call | solution.py:498
  39.9 1.3 %collective-permute-start.10 = (bf16[272,512]{1,0:T(8,128)(2,1)S(1)}, bf16[272,512]{1,0:T(8,128)(2,1)S(1)}, u32[]{:S(2)}, u32[]{:S(2)}) collective-permute-start(bf16[272,512]{1,0:T(8,128)(2,1)S(1)} %get-tuple-element.121), channel_id=1, source_target_pairs={{0,2},{1,3},{2,0},{3,1},{4,6},{5,7},{6,4},{7,5},{8,10},{9,11},{10,... | collective-permute-start | bytes 835592 | tf_op jit(solution)/shard_map/ppermute | solution.py:511
  41.3 0.8 %collective-permute-start.11 = (bf16[256,512]{1,0:T(8,128)(2,1)S(1)}, bf16[256,512]{1,0:T(8,128)(2,1)S(1)}, u32[]{:S(2)}, u32[]{:S(2)}) collective-permute-start(bf16[256,512]{1,0:T(8,128)(2,1)S(1)} %get-tuple-element.126), channel_id=1, source_target_pairs={{0,2},{1,3},{2,0},{3,1},{4,6},{5,7},{6,4},{7,5},{8,10},{9,11},{10,... | collective-permute-start | bytes 786440 | tf_op jit(solution)/shard_map/ppermute | solution.py:511
  42.3 2.4 %collective-permute-start.12 = (bf16[192,512]{1,0:T(8,128)(2,1)S(1)}, bf16[192,512]{1,0:T(8,128)(2,1)S(1)}, u32[]{:S(2)}, u32[]{:S(2)}) collective-permute-start(bf16[192,512]{1,0:T(8,128)(2,1)S(1)} %get-tuple-element.128), channel_id=1, source_target_pairs={{0,8},{1,9},{2,10},{3,11},{4,12},{5,13},{6,14},{7,15},{8,0},{9,1},... | collective-permute-start | bytes 589832 | tf_op jit(solution)/shard_map/ppermute | solution.py:511
  44.7 4.8 %collective-permute-done.10.refs_1_ = bf16[272,512]{1,0:T(8,128)(2,1)S(1)} collective-permute-done((bf16[272,512]{1,0:T(8,128)(2,1)S(1)}, bf16[272,512]{1,0:T(8,128)(2,1)S(1)}, u32[]{:S(2)}, u32[]{:S(2)}) %collective-permute-start.10) | collective-permute-done | bytes 278560 | tf_op jit(solution)/shard_map/ppermute | solution.py:511
  50.2 0.7 collective-permute-start.9
  51.4 2.8 %collective-permute-done.11.refs_1_ = bf16[256,512]{1,0:T(8,128)(2,1)S(1)} collective-permute-done((bf16[256,512]{1,0:T(8,128)(2,1)S(1)}, bf16[256,512]{1,0:T(8,128)(2,1)S(1)}, u32[]{:S(2)}, u32[]{:S(2)}) %collective-permute-start.11) | collective-permute-done | bytes 262176 | tf_op jit(solution)/shard_map/ppermute | solution.py:511
  54.3 4.3 %collective-permute-start.15 = (bf16[128,512]{1,0:T(8,128)(2,1)S(1)}, bf16[128,512]{1,0:T(8,128)(2,1)S(1)}, u32[]{:S(2)}, u32[]{:S(2)}) collective-permute-start(bf16[128,512]{1,0:T(8,128)(2,1)S(1)} %get-tuple-element.139), channel_id=1, source_target_pairs={{0,4},{1,5},{2,6},{3,7},{4,0},{5,1},{6,2},{7,3},{8,12},{9,13},{10,... | collective-permute-start | bytes 393224 | tf_op jit(solution)/shard_map/ppermute | solution.py:511
  59.2 2.7 %collective-permute-start.14 = (bf16[80,512]{1,0:T(8,128)(2,1)S(1)}, bf16[80,512]{1,0:T(8,128)(2,1)S(1)}, u32[]{:S(2)}, u32[]{:S(2)}) collective-permute-start(bf16[80,512]{1,0:T(8,128)(2,1)S(1)} %get-tuple-element.145), channel_id=1, source_target_pairs={{0,8},{1,9},{2,10},{3,11},{4,12},{5,13},{6,14},{7,15},{8,0},{9,1},... | collective-permute-start | bytes 245768 | tf_op jit(solution)/shard_map/ppermute | solution.py:511
  62.4 3.4 %collective-permute-start.17 = (bf16[64,512]{1,0:T(8,128)(2,1)S(1)}, bf16[64,512]{1,0:T(8,128)(2,1)S(1)}, u32[]{:S(2)}, u32[]{:S(2)}) collective-permute-start(bf16[64,512]{1,0:T(8,128)(2,1)S(1)} %get-tuple-element.151), channel_id=1, source_target_pairs={{0,8},{1,9},{2,10},{3,11},{4,12},{5,13},{6,14},{7,15},{8,0},{9,1},... | collective-permute-start | bytes 196616 | tf_op jit(solution)/shard_map/ppermute | solution.py:511
  65.9 2.0 %collective-permute-done.14.refs_0_.refs_4_ = bf16[80,512]{1,0:T(8,128)(2,1)S(1)} collective-permute-done((bf16[80,512]{1,0:T(8,128)(2,1)S(1)}, bf16[80,512]{1,0:T(8,128)(2,1)S(1)}, u32[]{:S(2)}, u32[]{:S(2)}) %collective-permute-start.14) | collective-permute-done | bytes 81952 | tf_op jit(solution)/shard_map/ppermute | solution.py:511
  67.9 1.5 %node.1 = bf16[256,512]{1,0:T(8,128)(2,1)} custom-call(s32[1,2,16]{2,1,0:T(2,128)S(1)} %bitcast.10, f32[256,512]{1,0:T(8,128)S(1)} %get-tuple-element.109.partial_ref, bf16[64,512]{1,0:T(8,128)(2,1)S(1)} %collective-permute-done.8.inner_ref, bf16[64,512]{1,0:T(8,128)(2,1)S(1)} %collective-permute-done.9.outer_ref, ...), custom_call_target="tpu_custom_call" | custom-call | tf_op jit(solution)/shard_map/node/pallas_call | solution.py:498
  69.8 0.8 %finish.1 = (f32[96,512]{1,0:T(8,128)}, f32[32,512]{1,0:T(8,128)}, f32[64,512]{1,0:T(8,128)}, f32[32,512]{1,0:T(8,128)}) custom-call(f32[1,96,512]{2,1,0:T(8,128)S(1)} %get-tuple-element.146.refs_0_, f32[1,64,512]{2,1,0:T(8,128)S(1)} %get-tuple-element.147.refs_1_, f32[1,64,512]{2,1,0:T(8,128)S(1)} %get-tuple-element.150.refs_2_, ...), custom_call_target="tpu_custom_call" | custom-call | tf_op jit(solution)/shard_map/finish/pallas_call | solution.py:498
  (34 shorter events, 5.4 us)
Async XLA Ops:
  2.5 14.0 %all-to-all-start = ((bf16[16,2,512]{2,1,0:T(2,128)(2,1)}), bf16[16,2,512]{2,1,0:T(2,128)(2,1)S(1)}, u32[]{:S(2)}, u32[]{:S(2)}) async-start(bf16[16,2,512]{2,1,0:T(2,128)(2,1)} %get-tuple-element.83), calls=%async_computation | async-start | bytes 65536 | tf_op jit(solution)/shard_map/all_to_all | solution.py:587
  9.8 6.6 %collective-permute-start = (bf16[64,512]{1,0:T(8,128)(2,1)}, bf16[64,512]{1,0:T(8,128)(2,1)S(1)}, u32[]{:S(2)}, u32[]{:S(2)}) collective-permute-start(bf16[64,512]{1,0:T(8,128)(2,1)} %get-tuple-element.81), channel_id=1, source_target_pairs={{0,1},{1,0},{2,3},{3,2},{4,5},{5,4},{6,7},{7,6},{8,9},{9,8},{10,11... | collective-permute-start | bytes 196616 | tf_op jit(solution)/shard_map/ppermute | solution.py:585
  10.2 6.2 %collective-permute-start.1 = (bf16[64,512]{1,0:T(8,128)(2,1)}, bf16[64,512]{1,0:T(8,128)(2,1)}, u32[]{:S(2)}, u32[]{:S(2)}) collective-permute-start(bf16[64,512]{1,0:T(8,128)(2,1)} %get-tuple-element.82), channel_id=1, source_target_pairs={{1,2},{2,1},{3,4},{4,3},{5,6},{6,5},{7,8},{8,7},{9,10},{10,9},{11,... | collective-permute-start | bytes 196616 | tf_op jit(solution)/shard_map/ppermute | solution.py:586
  25.5 3.4 %collective-permute-start.2 = (bf16[768,512]{1,0:T(8,128)(2,1)S(1)}, bf16[768,512]{1,0:T(8,128)(2,1)S(1)}, u32[]{:S(2)}, u32[]{:S(2)}) collective-permute-start(bf16[768,512]{1,0:T(8,128)(2,1)S(1)} %get-tuple-element.101), channel_id=1, source_target_pairs={{0,1},{1,0},{2,3},{3,2},{4,5},{5,4},{6,7},{7,6},{8,9},{9,8},{10,11... | collective-permute-start | bytes 2359304 | tf_op jit(solution)/shard_map/ppermute | solution.py:511
  29.1 13.1 %collective-permute-start.7 = (bf16[384,512]{1,0:T(8,128)(2,1)S(1)}, bf16[384,512]{1,0:T(8,128)(2,1)S(1)}, u32[]{:S(2)}, u32[]{:S(2)}) collective-permute-start(bf16[384,512]{1,0:T(8,128)(2,1)S(1)} %get-tuple-element.102), channel_id=1, source_target_pairs={{0,4},{1,5},{2,6},{3,7},{4,0},{5,1},{6,2},{7,3},{8,12},{9,13},{10,... | collective-permute-start | bytes 1179656 | tf_op jit(solution)/shard_map/ppermute | solution.py:511
  36.7 2.9 %collective-permute-start.3 = (bf16[272,512]{1,0:T(8,128)(2,1)S(1)}, bf16[272,512]{1,0:T(8,128)(2,1)S(1)}, u32[]{:S(2)}, u32[]{:S(2)}) collective-permute-start(bf16[272,512]{1,0:T(8,128)(2,1)S(1)} %get-tuple-element.118), channel_id=1, source_target_pairs={{0,1},{1,0},{2,3},{3,2},{4,5},{5,4},{6,7},{7,6},{8,9},{9,8},{10,11... | collective-permute-start | bytes 835592 | tf_op jit(solution)/shard_map/ppermute | solution.py:511
  36.8 2.8 %collective-permute-start.4 = (bf16[256,512]{1,0:T(8,128)(2,1)S(1)}, bf16[256,512]{1,0:T(8,128)(2,1)S(1)}, u32[]{:S(2)}, u32[]{:S(2)}) collective-permute-start(bf16[256,512]{1,0:T(8,128)(2,1)S(1)} %get-tuple-element.119), channel_id=1, source_target_pairs={{0,1},{1,0},{2,3},{3,2},{4,5},{5,4},{6,7},{7,6},{8,9},{9,8},{10,11... | collective-permute-start | bytes 786440 | tf_op jit(solution)/shard_map/ppermute | solution.py:511
  37.3 3.9 %collective-permute-start.5 = (bf16[256,512]{1,0:T(8,128)(2,1)S(1)}, bf16[256,512]{1,0:T(8,128)(2,1)S(1)}, u32[]{:S(2)}, u32[]{:S(2)}) collective-permute-start(bf16[256,512]{1,0:T(8,128)(2,1)S(1)} %get-tuple-element.124), channel_id=1, source_target_pairs={{0,1},{1,0},{2,3},{3,2},{4,5},{5,4},{6,7},{7,6},{8,9},{9,8},{10,11... | collective-permute-start | bytes 786440 | tf_op jit(solution)/shard_map/ppermute | solution.py:511
  37.4 3.8 %collective-permute-start.6 = (bf16[256,512]{1,0:T(8,128)(2,1)S(1)}, bf16[256,512]{1,0:T(8,128)(2,1)S(1)}, u32[]{:S(2)}, u32[]{:S(2)}) collective-permute-start(bf16[256,512]{1,0:T(8,128)(2,1)S(1)} %get-tuple-element.125), channel_id=1, source_target_pairs={{0,1},{1,0},{2,3},{3,2},{4,5},{5,4},{6,7},{7,6},{8,9},{9,8},{10,11... | collective-permute-start | bytes 786440 | tf_op jit(solution)/shard_map/ppermute | solution.py:511
  39.9 9.5 %collective-permute-start.10 = (bf16[272,512]{1,0:T(8,128)(2,1)S(1)}, bf16[272,512]{1,0:T(8,128)(2,1)S(1)}, u32[]{:S(2)}, u32[]{:S(2)}) collective-permute-start(bf16[272,512]{1,0:T(8,128)(2,1)S(1)} %get-tuple-element.121), channel_id=1, source_target_pairs={{0,2},{1,3},{2,0},{3,1},{4,6},{5,7},{6,4},{7,5},{8,10},{9,11},{10,... | collective-permute-start | bytes 835592 | tf_op jit(solution)/shard_map/ppermute | solution.py:511
  41.3 12.9 %collective-permute-start.11 = (bf16[256,512]{1,0:T(8,128)(2,1)S(1)}, bf16[256,512]{1,0:T(8,128)(2,1)S(1)}, u32[]{:S(2)}, u32[]{:S(2)}) collective-permute-start(bf16[256,512]{1,0:T(8,128)(2,1)S(1)} %get-tuple-element.126), channel_id=1, source_target_pairs={{0,2},{1,3},{2,0},{3,1},{4,6},{5,7},{6,4},{7,5},{8,10},{9,11},{10,... | collective-permute-start | bytes 786440 | tf_op jit(solution)/shard_map/ppermute | solution.py:511
  42.3 16.3 %collective-permute-start.12 = (bf16[192,512]{1,0:T(8,128)(2,1)S(1)}, bf16[192,512]{1,0:T(8,128)(2,1)S(1)}, u32[]{:S(2)}, u32[]{:S(2)}) collective-permute-start(bf16[192,512]{1,0:T(8,128)(2,1)S(1)} %get-tuple-element.128), channel_id=1, source_target_pairs={{0,8},{1,9},{2,10},{3,11},{4,12},{5,13},{6,14},{7,15},{8,0},{9,1},... | collective-permute-start | bytes 589832 | tf_op jit(solution)/shard_map/ppermute | solution.py:511
  49.8 9.1 %collective-permute-start.13 = (bf16[144,512]{1,0:T(8,128)(2,1)S(1)}, bf16[144,512]{1,0:T(8,128)(2,1)S(1)}, u32[]{:S(2)}, u32[]{:S(2)}) collective-permute-start(bf16[144,512]{1,0:T(8,128)(2,1)S(1)} %get-tuple-element.137), channel_id=1, source_target_pairs={{0,4},{1,5},{2,6},{3,7},{4,0},{5,1},{6,2},{7,3},{8,12},{9,13},{10,... | collective-permute-start | bytes 442376 | tf_op jit(solution)/shard_map/ppermute | solution.py:511
  50.2 1.3 %collective-permute-start.8 = (bf16[64,512]{1,0:T(8,128)(2,1)S(1)}, bf16[64,512]{1,0:T(8,128)(2,1)S(1)}, u32[]{:S(2)}, u32[]{:S(2)}) collective-permute-start(bf16[64,512]{1,0:T(8,128)(2,1)S(1)} %get-tuple-element.129), channel_id=1, source_target_pairs={{0,1},{1,0},{2,3},{3,2},{4,5},{5,4},{6,7},{7,6},{8,9},{9,8},{10,11... | collective-permute-start | bytes 196616 | tf_op jit(solution)/shard_map/ppermute | solution.py:707
  50.2 1.3 %collective-permute-start.9 = (bf16[64,512]{1,0:T(8,128)(2,1)S(1)}, bf16[64,512]{1,0:T(8,128)(2,1)S(1)}, u32[]{:S(2)}, u32[]{:S(2)}) collective-permute-start(bf16[64,512]{1,0:T(8,128)(2,1)S(1)} %get-tuple-element.130), channel_id=1, source_target_pairs={{1,2},{2,1},{3,4},{4,3},{5,6},{6,5},{7,8},{8,7},{9,10},{10,9},{11,... | collective-permute-start | bytes 196616 | tf_op jit(solution)/shard_map/ppermute | solution.py:708
  54.3 8.1 %collective-permute-start.15 = (bf16[128,512]{1,0:T(8,128)(2,1)S(1)}, bf16[128,512]{1,0:T(8,128)(2,1)S(1)}, u32[]{:S(2)}, u32[]{:S(2)}) collective-permute-start(bf16[128,512]{1,0:T(8,128)(2,1)S(1)} %get-tuple-element.139), channel_id=1, source_target_pairs={{0,4},{1,5},{2,6},{3,7},{4,0},{5,1},{6,2},{7,3},{8,12},{9,13},{10,... | collective-permute-start | bytes 393224 | tf_op jit(solution)/shard_map/ppermute | solution.py:511
  58.6 10.8 %collective-permute-start.16 = (bf16[96,512]{1,0:T(8,128)(2,1)S(1)}, bf16[96,512]{1,0:T(8,128)(2,1)S(1)}, u32[]{:S(2)}, u32[]{:S(2)}) collective-permute-start(bf16[96,512]{1,0:T(8,128)(2,1)S(1)} %get-tuple-element.141), channel_id=1, source_target_pairs={{0,2},{1,3},{2,0},{3,1},{4,6},{5,7},{6,4},{7,5},{8,10},{9,11},{10,... | collective-permute-start | bytes 294920 | tf_op jit(solution)/shard_map/ppermute | solution.py:511
  59.2 8.7 %collective-permute-start.14 = (bf16[80,512]{1,0:T(8,128)(2,1)S(1)}, bf16[80,512]{1,0:T(8,128)(2,1)S(1)}, u32[]{:S(2)}, u32[]{:S(2)}) collective-permute-start(bf16[80,512]{1,0:T(8,128)(2,1)S(1)} %get-tuple-element.145), channel_id=1, source_target_pairs={{0,8},{1,9},{2,10},{3,11},{4,12},{5,13},{6,14},{7,15},{8,0},{9,1},... | collective-permute-start | bytes 245768 | tf_op jit(solution)/shard_map/ppermute | solution.py:511
  61.8 6.0 %copy-start = (s32[1,16,2]{1,2,0:T(2,128)S(1)}, s32[1,16,2]{1,2,0:T(2,128)}, u32[]{:S(2)}) copy-start(s32[1,16,2]{1,2,0:T(2,128)} %param.32) | copy-start | bytes 388
  62.4 7.4 %collective-permute-start.17 = (bf16[64,512]{1,0:T(8,128)(2,1)S(1)}, bf16[64,512]{1,0:T(8,128)(2,1)S(1)}, u32[]{:S(2)}, u32[]{:S(2)}) collective-permute-start(bf16[64,512]{1,0:T(8,128)(2,1)S(1)} %get-tuple-element.151), channel_id=1, source_target_pairs={{0,8},{1,9},{2,10},{3,11},{4,12},{5,13},{6,14},{7,15},{8,0},{9,1},... | collective-permute-start | bytes 196616 | tf_op jit(solution)/shard_map/ppermute | solution.py:511

commit v11 on v10

--- a/solution.py
+++ b/solution.py
@@ -375,6 +375,11 @@
     grads[latent : 2 * latent, :] = dot(table_ref[...], by_sender, TN)
     grads[2 * latent :, :] = dot(node_ref[...], by_receiver, TN)
     back = dot(by_sender, w1_ref[latent : 2 * latent, :], NT)
+    rims[...] = back[nodes : nodes + 2 * NEAR, :]
+    odd = lax.rem(here, 2)
+    inner = rims[pl.ds(pl.multiple_of((1 - odd) * NEAR, NEAR), NEAR), :].astype(BF16)
+    inner_ref[...] = inner
+    outer_ref[...] = rims[pl.ds(pl.multiple_of(odd * NEAR, NEAR), NEAR), :].astype(BF16)
     far = back[nodes + 2 * NEAR : nodes + 2 * NEAR + places * tiles, :].astype(BF16)
     owner, at = slot_owner(here if fast else 0, (places * tiles, places * tiles), 0, places)
     column = lax.broadcasted_iota(jnp.int32, (places * tiles, places * tiles), 1)
@@ -389,12 +394,9 @@
             split_halves(bit, grads, 0, block, at, part, send_ref, keep_ref, 0)
             at += part
         out_refs[4][tiles // 2 * out_refs[5].shape[1] :, :] = slots_out(0, far, places)
+        out_refs[8][tiles // 2 * out_refs[9].shape[1] :, :] = inner
     else:
         out_refs[4][...] = grads[...]
-    rims[...] = back[nodes : nodes + 2 * NEAR, :]
-    odd = lax.rem(here, 2)
-    inner_ref[...] = rims[pl.ds(pl.multiple_of((1 - odd) * NEAR, NEAR), NEAR), :].astype(BF16)
-    outer_ref[...] = rims[pl.ds(pl.multiple_of(odd * NEAR, NEAR), NEAR), :].astype(BF16)
     partial_ref[...] = (
         base_ref[...] + back[:nodes, :] + dot(by_receiver, w1_ref[2 * latent :, :], NT)
     )
@@ -440,7 +442,7 @@
     odd = lax.rem(lax.axis_index("tiles"), 2)
     inner_at = pl.ds(pl.multiple_of((1 - odd) * (nodes - NEAR), NEAR), NEAR)
     outer_at = pl.ds(pl.multiple_of(odd * (nodes - NEAR), NEAR), NEAR)
-    sums[inner_at, :] += inner_ref[...].astype(F32)
+    sums[inner_at, :] += inner_ref[inner_ref.shape[0] - NEAR :, :].astype(F32)
     sums[outer_at, :] += outer_ref[...].astype(F32)
     out_ref[...] = sums[...].astype(BF16)
 
@@ -667,7 +669,7 @@
                 vmem((half * per + tiles * places // 2, latent), BF16),
                 vmem((half, per, latent), F32),
                 vmem((half * per, latent), BF16), vmem((half, per, latent), F32),
-                vmem((half * per, latent), BF16), vmem((half, per, latent), F32),
+                vmem((half * per + NEAR, latent), BF16), vmem((half, per, latent), F32),
             ]
             if fast else [shaped((3 * latent, latent), F32)]
         ),
@@ -678,37 +680,41 @@
         ],
     )
 
-    (grad_edge,) = call(
-        edge_kernel,
-        "edge",
-        [shaped((edges, latent), BF16)],
-        [after(dpre_a, partial), dpre_b, cot_kept, w1_kept],
-        out_specs=[pl.BlockSpec(memory_space=pltpu.HBM)],
-        scratch=[vmem((edges, latent), BF16), pltpu.SemaphoreType.DMA((steps,))],
-    )
+    def edge_call(dpre_a):
+        return call(
+            edge_kernel,
+            "edge",
+            [shaped((edges, latent), BF16)],
+            [dpre_a, dpre_b, cot_kept, w1_kept],
+            out_specs=[pl.BlockSpec(memory_space=pltpu.HBM)],
+            scratch=[vmem((edges, latent), BF16), pltpu.SemaphoreType.DMA((steps,))],
+        )[0]
 
     if fast:
         send_a, keep_a, send_more, keep_more, send_b, keep_b = first
+        send_a, send_more, send_b, to_outer = lax.optimization_barrier(
+            (send_a, send_more, send_b, to_outer, got_second)
+        )[:4]
+        inner = swap(tiles, 1, send_b)
+        outer = lax.ppermute(to_outer, "tiles", across)
         send_a, chain_a, slots = halve(
             1,
-            [after(keep_a, grad_edge), keep_more],
+            [keep_a, keep_more],
             [swap(tiles, 1, send_a), swap(tiles, 1, send_more)],
             to_far,
             places,
      )
         got_a = swap(tiles, 2, send_a)
         send_b, chain_b = halve(
-            1, [after(keep_b, send_a), second_keep], [swap(tiles, 1, send_b), got_second]
+            1, [after(keep_b, send_a), second_keep], [inner, got_second]
      )
         got_b = swap(tiles, 2, send_b)
-        send, chain = halve(3, [after(chain, send_b)], [got], flops=AHEAD)
+        grad_edge = edge_call(after(dpre_a, send_b))
+        send, chain = halve(3, [after(chain, grad_edge, outer)], [got], flops=AHEAD)
         got = swap(tiles, 8, send)
-        to_inner, to_outer = lax.optimization_barrier((to_inner, to_outer, send))[:2]
-        inner = lax.ppermute(to_inner, "tiles", inside)
-        outer = lax.ppermute(to_outer, "tiles", across)
         send_a, chain_a, slots = halve(2, [after(chain_a, send)], [got_a], slots, places)
         got_a = swap(tiles, 4, send_a)
-        send_b, chain_b = halve(2, [after(chain_b, send_a, inner, outer)], [got_b])
+        send_b, chain_b = halve(2, [after(chain_b, send_a)], [got_b])
         got_b = swap(tiles, 4, send_b)
         send, chain = halve(1, [after(chain, send_b)], [got])
         got = swap(tiles, 2, send)
@@ -726,6 +732,7 @@
             [3 * per, per, 2 * per, per],
         )
     else:
+        grad_edge = edge_call(dpre_a)
         inner = lax.ppermute(to_inner, "tiles", inside)
         outer = lax.ppermute(to_outer, "tiles", across)
         returned = [lax.all_to_all(to_far, "tiles", split_axis=0, concat_axis=0, tiled=True)]

time: 70.9 us -> 70.8 us (level)
  starting transfers between devices: 29.6 us -> 27.3 us
  waiting for transfers between devices: 12.5 us -> 14.6 us
    ppermute x14, waiting for transfers between devices: 10.9 us -> 13.5 us  [swap(): return lax.ppermute(send, 'tiles', [(i, i ^ bit) for i in range(tiles)])]
    ppermute x14, starting transfers between devices: 19.9 us -> 17.6 us  [swap(): return lax.ppermute(send, 'tiles', [(i, i ^ bit) for i in range(tiles)])]
  transfers between devices with their start and end apart: 19 -> 18, of which waited for: 8 -> 8; matrix products, arithmetic and copies ran while one was open for 0% -> 0% of each run, Pallas kernels for 23% -> 20%
where the time goes in v11:
time: 70.8 us; the launch traced here: 70.5 us
  Pallas kernels  27.9 us (39%)
  starting transfers between devices  27.3 us (39%)
  waiting for transfers between devices  14.6 us (21%)
  between operations  0.75 us (1%)
    pallas_call x18, Pallas kernels, call(): pl.pallas_call(kernel, in_specs=[pl.BlockSpec(memory_space=pltpu.HBM)] *...  27.9 us
    ppermute x14, starting transfers between devices, swap(): return lax.ppermute(send, 'tiles', [(i, i ^ bit) for i in range(tiles)])  17.6 us
    ppermute x14, waiting for transfers between devices, swap(): return lax.ppermute(send, 'tiles', [(i, i ^ bit) for i in range(tiles)])  13.5 us
    all_to_all x1, starting transfers between devices, shards(): lax.all_to_all(outgoing, 'tiles', split_axis=0, concat_axis=0, tiled=True)  7.37 us
  transfers between devices with their start and end apart: 18, of which 8 were waited for; matrix products, arithmetic and copies ran while one was open for 0% of the time, Pallas kernels for 20%

profile of v11, /device:TPU:0, one launch (start us, length us, event | category | flops | bytes accessed | tf_op | source)
XLA Modules:
  0.0 70.5 jit_solution(7142273300196595410)
XLA Ops:
  0.6 1.8 %outgoing.1 = (bf16[16,2,512]{2,1,0:T(2,128)(2,1)}, bf16[64,512]{1,0:T(8,128)(2,1)}, bf16[64,512]{1,0:T(8,128)(2,1)}) custom-call(s32[1,2,16]{2,1,0:T(2,128)} %bitcast.9, bf16[256,512]{1,0:T(8,128)(2,1)} %node_hbm.3), custom_call_target="tpu_custom_call" | custom-call | tf_op jit(solution)/shard_map/outgoing/pallas_call | solution.py:500
  2.5 7.4 %all-to-all-start = ((bf16[16,2,512]{2,1,0:T(2,128)(2,1)}), bf16[16,2,512]{2,1,0:T(2,128)(2,1)S(1)}, u32[]{:S(2)}, u32[]{:S(2)}) async-start(bf16[16,2,512]{2,1,0:T(2,128)(2,1)} %get-tuple-element.83), calls=%async_computation | async-start | bytes 65536 | tf_op jit(solution)/shard_map/all_to_all | solution.py:589
  10.2 1.3 %collective-permute-start.1 = (bf16[64,512]{1,0:T(8,128)(2,1)}, bf16[64,512]{1,0:T(8,128)(2,1)}, u32[]{:S(2)}, u32[]{:S(2)}) collective-permute-start(bf16[64,512]{1,0:T(8,128)(2,1)} %get-tuple-element.82), channel_id=1, source_target_pairs={{1,2},{2,1},{3,4},{4,3},{5,6},{6,5},{7,8},{8,7},{9,10},{10,9},{11,... | collective-permute-start | bytes 196616 | tf_op jit(solution)/shard_map/ppermute | solution.py:588
  11.5 3.8 %prepare.1 = (bf16[256,512]{1,0:T(8,128)(2,1)S(1)}, s32[12,128]{1,0:T(8,128)S(1)}, s32[12,128]{1,0:T(8,128)S(1)}, f32[1536,512]{1,0:T(8,128)S(1)}) custom-call(bf16[256,512]{1,0:T(8,128)(2,1)} %node_hbm.3, bf16[1536,512]{1,0:T(8,128)(2,1)} %w1_hbm.3, s32[12,128]{1,0:T(8,128)} %bitcast.16, s32[12,128]{1,0:T(8,128)} %bitcast.17, f32[1,512]{1,0:T(1,128)} %bitcast.18, ...), custom_call_target="tpu_custom_call" | custom-call | flops 10000000000 | bytes 100000000 | tf_op jit(solution)/shard_map/prepare/pallas_call | solution.py:500
  16.5 9.0 %forward.1 = (bf16[1536,512]{1,0:T(8,128)(2,1)S(1)}, bf16[1536,512]{1,0:T(8,128)(2,1)S(1)}, bf16[1536,512]{1,0:T(8,128)(2,1)S(1)}, bf16[512,512]{1,0:T(8,128)(2,...) custom-call(bf16[1536,512]{1,0:T(8,128)(2,1)} %w1_hbm.3, ...), custom_call_target="tpu_custom_call" | custom-call | tf_op jit(solution)/shard_map/forward/pallas_call | solution.py:500
  25.5 1.5 %collective-permute-start.2 = (bf16[768,512]{1,0:T(8,128)(2,1)S(1)}, bf16[768,512]{1,0:T(8,128)(2,1)S(1)}, u32[]{:S(2)}, u32[]{:S(2)}) collective-permute-start(bf16[768,512]{1,0:T(8,128)(2,1)S(1)} %get-tuple-element.101), channel_id=1, source_target_pairs={{0,1},{1,0},{2,3},{3,2},{4,5},{5,4},{6,7},{7,6},{8,9},{9,8},{10,11... | collective-permute-start | bytes 2359304 | tf_op jit(solution)/shard_map/ppermute | solution.py:513
  27.0 1.7 %slope.2 = (bf16[768,512]{1,0:T(8,128)(2,1)S(1)}, f32[512,512]{1,0:T(8,128)S(1)}) custom-call(bf16[1536,512]{1,0:T(8,128)(2,1)S(1)} %get-tuple-element.89.cot_ref, s32[12,128]{1,0:T(8,128)S(1)} %get-tuple-element.87.receiver_ref, bf16[256,512]{1,0:T(8,128)(2,1)S(1)} %get-tuple-element.103.dsum_ref, bf16[1536,512]{1,0:T(8,128)(2,1)S(1)} %get-tuple-element.91.hidden_ref, ...), custom_call_target="tpu_custom_call" | custom-call | tf_op jit(solution)/shard_map/slope/pallas_call | solution.py:500
  29.1 1.9 %slope.3 = (bf16[768,512]{1,0:T(8,128)(2,1)S(1)}, bf16[256,512]{1,0:T(8,128)(2,1)S(1)}, f32[8,32,512]{2,1,0:T(8,128)S(1)}) custom-call(bf16[1536,512]{1,0:T(8,128)(2,1)S(1)} %get-tuple-element.89.cot_ref, s32[12,128]{1,0:T(8,128)S(1)} %get-tuple-element.87.receiver_ref, bf16[256,512]{1,0:T(8,128)(2,1)S(1)} %get-tuple-element.103.dsum_ref, ...), custom_call_target="tpu_custom_call" | custom-call | tf_op jit(solution)/shard_map/slope/pallas_call | solution.py:500
  31.4 1.5 %collective-permute-start.8 = (bf16[384,512]{1,0:T(8,128)(2,1)S(1)}, bf16[384,512]{1,0:T(8,128)(2,1)S(1)}, u32[]{:S(2)}, u32[]{:S(2)}) collective-permute-start(bf16[384,512]{1,0:T(8,128)(2,1)S(1)} %get-tuple-element.102), channel_id=1, source_target_pairs={{0,4},{1,5},{2,6},{3,7},{4,0},{5,1},{6,2},{7,3},{8,12},{9,13},{10,... | collective-permute-start | bytes 1179656 | tf_op jit(solution)/shard_map/ppermute | solution.py:513
  32.8 4.2 %first.1 = (bf16[64,512]{1,0:T(8,128)(2,1)}, bf16[64,512]{1,0:T(8,128)(2,1)S(1)}, bf16[32,512]{1,0:T(8,128)(2,1)S(1)}, f32[256,512]{1,0:T(8,128)S(1)}, bf16[272,...) custom-call(bf16[768,512]{1,0:T(8,128)(2,1)S(1)} %get-tuple-element., ...), custom_call_target="tpu_custom_call" | custom-call | tf_op jit(solution)/shard_map/first/pallas_call | solution.py:500
  38.3 1.1 %collective-permute-done.7.refs_3_ = bf16[256,512]{1,0:T(8,128)(2,1)S(1)} collective-permute-done((bf16[256,512]{1,0:T(8,128)(2,1)S(1)}, bf16[256,512]{1,0:T(8,128)(2,1)S(1)}, u32[]{:S(2)}, u32[]{:S(2)}) %collective-permute-start.7) | collective-permute-done | bytes 262176 | tf_op jit(solution)/shard_map/ppermute | solution.py:513
  39.8 2.2 %collective-permute-start.9 = (bf16[272,512]{1,0:T(8,128)(2,1)S(1)}, bf16[272,512]{1,0:T(8,128)(2,1)S(1)}, u32[]{:S(2)}, u32[]{:S(2)}) collective-permute-start(bf16[272,512]{1,0:T(8,128)(2,1)S(1)} %get-tuple-element.125), channel_id=1, source_target_pairs={{0,2},{1,3},{2,0},{3,1},{4,6},{5,7},{6,4},{7,5},{8,10},{9,11},{10,... | collective-permute-start | bytes 835592 | tf_op jit(solution)/shard_map/ppermute | solution.py:513
  42.1 1.8 %edge.1 = bf16[1536,512]{1,0:T(8,128)(2,1)} custom-call(bf16[768,512]{1,0:T(8,128)(2,1)S(1)} %get-tuple-element.129.dpre_a_ref, bf16[768,512]{1,0:T(8,128)(2,1)S(1)} %get-tuple-element.104.dpre_b_ref, bf16[1536,512]{1,0:T(8,128)(2,1)S(1)} %get-tuple-element.89.cot_ref, bf16[1536,512]{1,0:T(8,128)(2,1)S(1)} %get-tuple-element.107.w1_ref), custom_call_target="tpu_custom_call" | custom-call | tf_op jit(solution)/shard_map/edge/pallas_call | solution.py:500
  44.0 3.0 %collective-permute-start.11 = (bf16[192,512]{1,0:T(8,128)(2,1)S(1)}, bf16[192,512]{1,0:T(8,128)(2,1)S(1)}, u32[]{:S(2)}, u32[]{:S(2)}) collective-permute-start(bf16[192,512]{1,0:T(8,128)(2,1)S(1)} %get-tuple-element.131), channel_id=1, source_target_pairs={{0,8},{1,9},{2,10},{3,11},{4,12},{5,13},{6,14},{7,15},{8,0},{9,1},... | collective-permute-start | bytes 589832 | tf_op jit(solution)/shard_map/ppermute | solution.py:513
  47.0 2.7 %collective-permute-done.9.refs_1_ = bf16[272,512]{1,0:T(8,128)(2,1)S(1)} collective-permute-done((bf16[272,512]{1,0:T(8,128)(2,1)S(1)}, bf16[272,512]{1,0:T(8,128)(2,1)S(1)}, u32[]{:S(2)}, u32[]{:S(2)}) %collective-permute-start.9) | collective-permute-done | bytes 278560 | tf_op jit(solution)/shard_map/ppermute | solution.py:513
  50.0 2.7 %collective-permute-start.12 = (bf16[144,512]{1,0:T(8,128)(2,1)S(1)}, bf16[144,512]{1,0:T(8,128)(2,1)S(1)}, u32[]{:S(2)}, u32[]{:S(2)}) collective-permute-start(bf16[144,512]{1,0:T(8,128)(2,1)S(1)} %get-tuple-element.137), channel_id=1, source_target_pairs={{0,4},{1,5},{2,6},{3,7},{4,0},{5,1},{6,2},{7,3},{8,12},{9,13},{10,... | collective-permute-start | bytes 442376 | tf_op jit(solution)/shard_map/ppermute | solution.py:513
  52.7 2.5 %collective-permute-done.10.refs_1_ = bf16[256,512]{1,0:T(8,128)(2,1)S(1)} collective-permute-done((bf16[256,512]{1,0:T(8,128)(2,1)S(1)}, bf16[256,512]{1,0:T(8,128)(2,1)S(1)}, u32[]{:S(2)}, u32[]{:S(2)}) %collective-permute-start.10) | collective-permute-done | bytes 262176 | tf_op jit(solution)/shard_map/ppermute | solution.py:513
  55.3 1.8 %collective-permute-start.14 = (bf16[128,512]{1,0:T(8,128)(2,1)S(1)}, bf16[128,512]{1,0:T(8,128)(2,1)S(1)}, u32[]{:S(2)}, u32[]{:S(2)}) collective-permute-start(bf16[128,512]{1,0:T(8,128)(2,1)S(1)} %get-tuple-element.139), channel_id=1, source_target_pairs={{0,4},{1,5},{2,6},{3,7},{4,0},{5,1},{6,2},{7,3},{8,12},{9,13},{10,... | collective-permute-start | bytes 393224 | tf_op jit(solution)/shard_map/ppermute | solution.py:513
  57.1 1.3 %collective-permute-start.15 = (bf16[96,512]{1,0:T(8,128)(2,1)S(1)}, bf16[96,512]{1,0:T(8,128)(2,1)S(1)}, u32[]{:S(2)}, u32[]{:S(2)}) collective-permute-start(bf16[96,512]{1,0:T(8,128)(2,1)S(1)} %get-tuple-element.141), channel_id=1, source_target_pairs={{0,2},{1,3},{2,0},{3,1},{4,6},{5,7},{6,4},{7,5},{8,10},{9,11},{10,... | collective-permute-start | bytes 294920 | tf_op jit(solution)/shard_map/ppermute | solution.py:513
  58.4 1.8 %collective-permute-done.12.refs_1_ = bf16[144,512]{1,0:T(8,128)(2,1)S(1)} collective-permute-done((bf16[144,512]{1,0:T(8,128)(2,1)S(1)}, bf16[144,512]{1,0:T(8,128)(2,1)S(1)}, u32[]{:S(2)}, u32[]{:S(2)}) %collective-permute-start.12) | collective-permute-done | bytes 147488 | tf_op jit(solution)/shard_map/ppermute | solution.py:513
  60.9 1.4 %collective-permute-done.14.refs_1_ = bf16[128,512]{1,0:T(8,128)(2,1)S(1)} collective-permute-done((bf16[128,512]{1,0:T(8,128)(2,1)S(1)}, bf16[128,512]{1,0:T(8,128)(2,1)S(1)}, u32[]{:S(2)}, u32[]{:S(2)}) %collective-permute-start.14) | collective-permute-done | bytes 131104 | tf_op jit(solution)/shard_map/ppermute | solution.py:513
  62.3 2.2 %collective-permute-start.16 = (bf16[64,512]{1,0:T(8,128)(2,1)S(1)}, bf16[64,512]{1,0:T(8,128)(2,1)S(1)}, u32[]{:S(2)}, u32[]{:S(2)}) collective-permute-start(bf16[64,512]{1,0:T(8,128)(2,1)S(1)} %get-tuple-element.151), channel_id=1, source_target_pairs={{0,8},{1,9},{2,10},{3,11},{4,12},{5,13},{6,14},{7,15},{8,0},{9,1},... | collective-permute-start | bytes 196616 | tf_op jit(solution)/shard_map/ppermute | solution.py:513
  64.5 3.7 %collective-permute-done.13.refs_0_.refs_4_ = bf16[80,512]{1,0:T(8,128)(2,1)S(1)} collective-permute-done((bf16[80,512]{1,0:T(8,128)(2,1)S(1)}, bf16[80,512]{1,0:T(8,128)(2,1)S(1)}, u32[]{:S(2)}, u32[]{:S(2)}) %collective-permute-start.13) | collective-permute-done | bytes 81952 | tf_op jit(solution)/shard_map/ppermute | solution.py:513
  68.2 1.5 %node.1 = bf16[256,512]{1,0:T(8,128)(2,1)} custom-call(s32[1,2,16]{2,1,0:T(2,128)S(1)} %bitcast.10, f32[256,512]{1,0:T(8,128)S(1)} %get-tuple-element.109.partial_ref, bf16[320,512]{1,0:T(8,128)(2,1)S(1)} %collective-permute-done.4.refs_2_.inner_ref, bf16[64,512]{1,0:T(8,128)(2,1)S(1)} %collective-permute-done.5.outer_ref, ...), custom_call_target="tpu_custom_call" | custom-call | tf_op jit(solution)/shard_map/node/pallas_call | solution.py:500
  (32 shorter events, 6.1 us)
Async XLA Ops:
  2.5 14.0 %all-to-all-start = ((bf16[16,2,512]{2,1,0:T(2,128)(2,1)}), bf16[16,2,512]{2,1,0:T(2,128)(2,1)S(1)}, u32[]{:S(2)}, u32[]{:S(2)}) async-start(bf16[16,2,512]{2,1,0:T(2,128)(2,1)} %get-tuple-element.83), calls=%async_computation | async-start | bytes 65536 | tf_op jit(solution)/shard_map/all_to_all | solution.py:589
  9.8 6.6 %collective-permute-start = (bf16[64,512]{1,0:T(8,128)(2,1)}, bf16[64,512]{1,0:T(8,128)(2,1)S(1)}, u32[]{:S(2)}, u32[]{:S(2)}) collective-permute-start(bf16[64,512]{1,0:T(8,128)(2,1)} %get-tuple-element.81), channel_id=1, source_target_pairs={{0,1},{1,0},{2,3},{3,2},{4,5},{5,4},{6,7},{7,6},{8,9},{9,8},{10,11... | collective-permute-start | bytes 196616 | tf_op jit(solution)/shard_map/ppermute | solution.py:587
  10.2 6.2 %collective-permute-start.1 = (bf16[64,512]{1,0:T(8,128)(2,1)}, bf16[64,512]{1,0:T(8,128)(2,1)}, u32[]{:S(2)}, u32[]{:S(2)}) collective-permute-start(bf16[64,512]{1,0:T(8,128)(2,1)} %get-tuple-element.82), channel_id=1, source_target_pairs={{1,2},{2,1},{3,4},{4,3},{5,6},{6,5},{7,8},{8,7},{9,10},{10,9},{11,... | collective-permute-start | bytes 196616 | tf_op jit(solution)/shard_map/ppermute | solution.py:588
  25.5 3.4 %collective-permute-start.2 = (bf16[768,512]{1,0:T(8,128)(2,1)S(1)}, bf16[768,512]{1,0:T(8,128)(2,1)S(1)}, u32[]{:S(2)}, u32[]{:S(2)}) collective-permute-start(bf16[768,512]{1,0:T(8,128)(2,1)S(1)} %get-tuple-element.101), channel_id=1, source_target_pairs={{0,1},{1,0},{2,3},{3,2},{4,5},{5,4},{6,7},{7,6},{8,9},{9,8},{10,11... | collective-permute-start | bytes 2359304 | tf_op jit(solution)/shard_map/ppermute | solution.py:513
  30.9 6.1 %collective-permute-start.3 = (bf16[256,512]{1,0:T(8,128)(2,1)S(1)}, bf16[256,512]{1,0:T(8,128)(2,1)S(1)}, u32[]{:S(2)}, u32[]{:S(2)}) collective-permute-start(bf16[256,512]{1,0:T(8,128)(2,1)S(1)} %get-tuple-element.114), channel_id=1, source_target_pairs={{0,1},{1,0},{2,3},{3,2},{4,5},{5,4},{6,7},{7,6},{8,9},{9,8},{10,11... | collective-permute-start | bytes 786440 | tf_op jit(solution)/shard_map/ppermute | solution.py:513
  31.4 12.5 %collective-permute-start.8 = (bf16[384,512]{1,0:T(8,128)(2,1)S(1)}, bf16[384,512]{1,0:T(8,128)(2,1)S(1)}, u32[]{:S(2)}, u32[]{:S(2)}) collective-permute-start(bf16[384,512]{1,0:T(8,128)(2,1)S(1)} %get-tuple-element.102), channel_id=1, source_target_pairs={{0,4},{1,5},{2,6},{3,7},{4,0},{5,1},{6,2},{7,3},{8,12},{9,13},{10,... | collective-permute-start | bytes 1179656 | tf_op jit(solution)/shard_map/ppermute | solution.py:513
  37.0 4.9 %collective-permute-start.4 = (bf16[320,512]{1,0:T(8,128)(2,1)S(1)}, bf16[320,512]{1,0:T(8,128)(2,1)S(1)}, u32[]{:S(2)}, u32[]{:S(2)}) collective-permute-start(bf16[320,512]{1,0:T(8,128)(2,1)S(1)} %get-tuple-element.115), channel_id=1, source_target_pairs={{0,1},{1,0},{2,3},{3,2},{4,5},{5,4},{6,7},{7,6},{8,9},{9,8},{10,11... | collective-permute-start | bytes 983048 | tf_op jit(solution)/shard_map/ppermute | solution.py:513
  37.1 2.3 %collective-permute-start.6 = (bf16[272,512]{1,0:T(8,128)(2,1)S(1)}, bf16[272,512]{1,0:T(8,128)(2,1)S(1)}, u32[]{:S(2)}, u32[]{:S(2)}) collective-permute-start(bf16[272,512]{1,0:T(8,128)(2,1)S(1)} %get-tuple-element.119), channel_id=1, source_target_pairs={{0,1},{1,0},{2,3},{3,2},{4,5},{5,4},{6,7},{7,6},{8,9},{9,8},{10,11... | collective-permute-start | bytes 835592 | tf_op jit(solution)/shard_map/ppermute | solution.py:513
  37.5 1.9 %collective-permute-start.7 = (bf16[256,512]{1,0:T(8,128)(2,1)S(1)}, bf16[256,512]{1,0:T(8,128)(2,1)S(1)}, u32[]{:S(2)}, u32[]{:S(2)}) collective-permute-start(bf16[256,512]{1,0:T(8,128)(2,1)S(1)} %get-tuple-element.120), channel_id=1, source_target_pairs={{0,1},{1,0},{2,3},{3,2},{4,5},{5,4},{6,7},{7,6},{8,9},{9,8},{10,11... | collective-permute-start | bytes 786440 | tf_op jit(solution)/shard_map/ppermute | solution.py:513
  37.6 6.3 %collective-permute-start.5 = (bf16[64,512]{1,0:T(8,128)(2,1)S(1)}, bf16[64,512]{1,0:T(8,128)(2,1)S(1)}, u32[]{:S(2)}, u32[]{:S(2)}) collective-permute-start(bf16[64,512]{1,0:T(8,128)(2,1)S(1)} %get-tuple-element.116), channel_id=1, source_target_pairs={{1,2},{2,1},{3,4},{4,3},{5,6},{6,5},{7,8},{8,7},{9,10},{10,9},{11,... | collective-permute-start | bytes 196616 | tf_op jit(solution)/shard_map/ppermute | solution.py:699
  39.8 10.0 %collective-permute-start.9 = (bf16[272,512]{1,0:T(8,128)(2,1)S(1)}, bf16[272,512]{1,0:T(8,128)(2,1)S(1)}, u32[]{:S(2)}, u32[]{:S(2)}) collective-permute-start(bf16[272,512]{1,0:T(8,128)(2,1)S(1)} %get-tuple-element.125), channel_id=1, source_target_pairs={{0,2},{1,3},{2,0},{3,1},{4,6},{5,7},{6,4},{7,5},{8,10},{9,11},{10,... | collective-permute-start | bytes 835592 | tf_op jit(solution)/shard_map/ppermute | solution.py:513
  42.0 13.2 %collective-permute-start.10 = (bf16[256,512]{1,0:T(8,128)(2,1)S(1)}, bf16[256,512]{1,0:T(8,128)(2,1)S(1)}, u32[]{:S(2)}, u32[]{:S(2)}) collective-permute-start(bf16[256,512]{1,0:T(8,128)(2,1)S(1)} %get-tuple-element.128), channel_id=1, source_target_pairs={{0,2},{1,3},{2,0},{3,1},{4,6},{5,7},{6,4},{7,5},{8,10},{9,11},{10,... | collective-permute-start | bytes 786440 | tf_op jit(solution)/shard_map/ppermute | solution.py:513
  44.0 13.1 %collective-permute-start.11 = (bf16[192,512]{1,0:T(8,128)(2,1)S(1)}, bf16[192,512]{1,0:T(8,128)(2,1)S(1)}, u32[]{:S(2)}, u32[]{:S(2)}) collective-permute-start(bf16[192,512]{1,0:T(8,128)(2,1)S(1)} %get-tuple-element.131), channel_id=1, source_target_pairs={{0,8},{1,9},{2,10},{3,11},{4,12},{5,13},{6,14},{7,15},{8,0},{9,1},... | collective-permute-start | bytes 589832 | tf_op jit(solution)/shard_map/ppermute | solution.py:513
  50.0 10.2 %collective-permute-start.12 = (bf16[144,512]{1,0:T(8,128)(2,1)S(1)}, bf16[144,512]{1,0:T(8,128)(2,1)S(1)}, u32[]{:S(2)}, u32[]{:S(2)}) collective-permute-start(bf16[144,512]{1,0:T(8,128)(2,1)S(1)} %get-tuple-element.137), channel_id=1, source_target_pairs={{0,4},{1,5},{2,6},{3,7},{4,0},{5,1},{6,2},{7,3},{8,12},{9,13},{10,... | collective-permute-start | bytes 442376 | tf_op jit(solution)/shard_map/ppermute | solution.py:513
  55.3 7.0 %collective-permute-start.14 = (bf16[128,512]{1,0:T(8,128)(2,1)S(1)}, bf16[128,512]{1,0:T(8,128)(2,1)S(1)}, u32[]{:S(2)}, u32[]{:S(2)}) collective-permute-start(bf16[128,512]{1,0:T(8,128)(2,1)S(1)} %get-tuple-element.139), channel_id=1, source_target_pairs={{0,4},{1,5},{2,6},{3,7},{4,0},{5,1},{6,2},{7,3},{8,12},{9,13},{10,... | collective-permute-start | bytes 393224 | tf_op jit(solution)/shard_map/ppermute | solution.py:513
  57.1 12.6 %collective-permute-start.15 = (bf16[96,512]{1,0:T(8,128)(2,1)S(1)}, bf16[96,512]{1,0:T(8,128)(2,1)S(1)}, u32[]{:S(2)}, u32[]{:S(2)}) collective-permute-start(bf16[96,512]{1,0:T(8,128)(2,1)S(1)} %get-tuple-element.141), channel_id=1, source_target_pairs={{0,2},{1,3},{2,0},{3,1},{4,6},{5,7},{6,4},{7,5},{8,10},{9,11},{10,... | collective-permute-start | bytes 294920 | tf_op jit(solution)/shard_map/ppermute | solution.py:513
  60.5 7.7 %collective-permute-start.13 = (bf16[80,512]{1,0:T(8,128)(2,1)S(1)}, bf16[80,512]{1,0:T(8,128)(2,1)S(1)}, u32[]{:S(2)}, u32[]{:S(2)}) collective-permute-start(bf16[80,512]{1,0:T(8,128)(2,1)S(1)} %get-tuple-element.145), channel_id=1, source_target_pairs={{0,8},{1,9},{2,10},{3,11},{4,12},{5,13},{6,14},{7,15},{8,0},{9,1},... | collective-permute-start | bytes 245768 | tf_op jit(solution)/shard_map/ppermute | solution.py:513
  60.9 7.3 %copy-start = (s32[1,16,2]{1,2,0:T(2,128)S(1)}, s32[1,16,2]{1,2,0:T(2,128)}, u32[]{:S(2)}) copy-start(s32[1,16,2]{1,2,0:T(2,128)} %param.32) | copy-start | bytes 388
  62.3 7.4 %collective-permute-start.16 = (bf16[64,512]{1,0:T(8,128)(2,1)S(1)}, bf16[64,512]{1,0:T(8,128)(2,1)S(1)}, u32[]{:S(2)}, u32[]{:S(2)}) collective-permute-start(bf16[64,512]{1,0:T(8,128)(2,1)S(1)} %get-tuple-element.151), channel_id=1, source_target_pairs={{0,8},{1,9},{2,10},{3,11},{4,12},{5,13},{6,14},{7,15},{8,0},{9,1},... | collective-permute-start | bytes 196616 | tf_op jit(solution)/shard_map/ppermute | solution.py:513

commit v12 on v11

--- a/solution.py
+++ b/solution.py
@@ -337,11 +337,11 @@
 
 def first_kernel(
     tiles, places, fast,
-    dpre_a_ref, dpre_b_ref, edge_ref, sender_ref, receiver_ref, table_ref, node_ref, w1_ref, base_ref,
+    dpre_a_ref, dpre_b_ref, edge_ref, sender_ref, receiver_ref, table_ref, node_ref, w1_ref,
     *refs,
 ):
     out_refs, (grads, sums, rims) = refs[:-3], refs[-3:]
-    inner_ref, outer_ref, far_ref, partial_ref = out_refs[:4]
+    inner_ref, outer_ref, far_ref, sums_ref = out_refs[:4]
     here = lax.axis_index("tiles")
     edges, latent = edge_ref.shape
     early = dpre_a_ref.shape[0]
@@ -374,13 +374,13 @@
     by_receiver = sums[rows:, :].astype(BF16)
     grads[latent : 2 * latent, :] = dot(table_ref[...], by_sender, TN)
     grads[2 * latent :, :] = dot(node_ref[...], by_receiver, TN)
-    back = dot(by_sender, w1_ref[latent : 2 * latent, :], NT)
-    rims[...] = back[nodes : nodes + 2 * NEAR, :]
+    back = dot(by_sender[nodes:, :], w1_ref[latent : 2 * latent, :], NT)
+    rims[...] = back[: 2 * NEAR, :]
     odd = lax.rem(here, 2)
     inner = rims[pl.ds(pl.multiple_of((1 - odd) * NEAR, NEAR), NEAR), :].astype(BF16)
     inner_ref[...] = inner
     outer_ref[...] = rims[pl.ds(pl.multiple_of(odd * NEAR, NEAR), NEAR), :].astype(BF16)
-    far = back[nodes + 2 * NEAR : nodes + 2 * NEAR + places * tiles, :].astype(BF16)
+    far = back[2 * NEAR : 2 * NEAR + places * tiles, :].astype(BF16)
     owner, at = slot_owner(here if fast else 0, (places * tiles, places * tiles), 0, places)
     column = lax.broadcasted_iota(jnp.int32, (places * tiles, places * tiles), 1)
     far = dot(ones_where(at * tiles + owner == column), far).astype(BF16)
@@ -397,12 +397,13 @@
         out_refs[8][tiles // 2 * out_refs[9].shape[1] :, :] = inner
     else:
         out_refs[4][...] = grads[...]
-    partial_ref[...] = (
-        base_ref[...] + back[:nodes, :] + dot(by_receiver, w1_ref[2 * latent :, :], NT)
-    )
-
-
-def edge_kernel(dpre_a_ref, dpre_b_ref, cot_ref, w1_ref, out_hbm, out_ref, sems):
+    sums_ref[:nodes, :] = by_sender[:nodes, :]
+    sums_ref[nodes:, :] = by_receiver
+
+
+def edge_kernel(
+    dpre_a_ref, dpre_b_ref, cot_ref, w1_ref, base_ref, sums_ref, out_hbm, partial_ref, out_ref, sems
+):
     early, latent = dpre_a_ref.shape
     copies = []
     for dpre_ref, base in ((dpre_a_ref, 0), (dpre_b_ref, early)):
@@ -417,34 +418,61 @@
             )
             copy.start()
             copies.append(copy)
+    nodes = base_ref.shape[0]
+    partial_ref[...] = (
+        base_ref[...]
+        + dot(sums_ref[:nodes, :], w1_ref[latent : 2 * latent, :], NT)
+        + dot(sums_ref[nodes:, :], w1_ref[2 * latent :, :], NT)
+    )
     for copy in copies:
         copy.wait()
 
 
-def node_kernel(fast, index_ref, partial_ref, inner_ref, outer_ref, slots_ref, *refs):
-    out_ref, sums = refs[-2:]
+def add_rims(total, inner_ref, outer_ref, sums_ref):
+    nodes = total.shape[0]
+    odd = lax.rem(lax.axis_index("tiles"), 2)
+    inner_at = pl.ds(pl.multiple_of((1 - odd) * (nodes - NEAR), NEAR), NEAR)
+    outer_at = pl.ds(pl.multiple_of(odd * (nodes - NEAR), NEAR), NEAR)
+    sums_ref[...] = total
+    sums_ref[inner_at, :] += inner_ref[inner_ref.shape[0] - NEAR :, :].astype(F32)
+    sums_ref[outer_at, :] += outer_ref[...].astype(F32)
+
+
+def slot_picks(origin, index_ref, nodes):
     places, tiles = index_ref.shape[1], index_ref.shape[2]
-    nodes = partial_ref.shape[0]
-    origin = lax.axis_index("tiles") if fast else 0
-    slots = slots_ref[...]
-    if fast:
-        got_ref = refs[0]
-        slots = slots_in(3, slots, got_ref[got_ref.shape[0] - slots.shape[0] // 2 :, :], places)
     place = lax.broadcasted_iota(jnp.int32, (nodes, tiles), 0)
     owner, at = slot_owner(origin, (tiles, places * tiles), 1, places)
     row = lax.broadcasted_iota(jnp.int32, (tiles, places * tiles), 0)
-    total = partial_ref[...]
+    picks = jnp.zeros((nodes, places * tiles), F32)
     for j in range(places):
-        picks = ones_where(place == index_ref[0, j : j + 1, :])
-        far = dot(ones_where((owner == row) & (at == j)), slots).astype(BF16)
-        total = total + dot(picks, far)
-    sums[...] = total
-    odd = lax.rem(lax.axis_index("tiles"), 2)
-    inner_at = pl.ds(pl.multiple_of((1 - odd) * (nodes - NEAR), NEAR), NEAR)
-    outer_at = pl.ds(pl.multiple_of(odd * (nodes - NEAR), NEAR), NEAR)
-    sums[inner_at, :] += inner_ref[inner_ref.shape[0] - NEAR :, :].astype(F32)
-    sums[outer_at, :] += outer_ref[...].astype(F32)
-    out_ref[...] = sums[...].astype(BF16)
+        listed = ones_where(place == index_ref[0, j : j + 1, :])
+        picks += dot(listed, ones_where((owner == row) & (at == j)))
+    return picks.astype(BF16)
+
+
+def settle_kernel(
+    index_ref, partial_ref, inner_ref, outer_ref, slots_ref, sums_ref, picks_ref
+):
+    places = index_ref.shape[1]
+    rows = slots_ref.shape[0]
+    picks = slot_picks(lax.axis_index("tiles"), index_ref, partial_ref.shape[0])
+    column = lax.broadcasted_iota(jnp.int32, picks.shape, 1)
+    here = ones_where((picks > 0) & ((lax.div(column, places) >> 3) & 1 == 0))
+    moved = ones_where(bit_slots(3, (rows // 2, rows), places))
+    picks_ref[...] = dot(picks, moved, NT).astype(BF16)
+    add_rims(partial_ref[...] + dot(here, slots_ref[...]), inner_ref, outer_ref, sums_ref)
+
+
+def last_kernel(sums_ref, picks_ref, got_ref, out_ref):
+    rows = picks_ref.shape[1]
+    got = got_ref[got_ref.shape[0] - rows :, :]
+    out_ref[...] = (sums_ref[...] + dot(picks_ref[...], got)).astype(BF16)
+
+
+def node_kernel(index_ref, partial_ref, inner_ref, outer_ref, slots_ref, out_ref, sums_ref):
+    picks = slot_picks(0, index_ref, partial_ref.shape[0])
+    add_rims(partial_ref[...] + dot(picks, slots_ref[...]), inner_ref, outer_ref, sums_ref)
+    out_ref[...] = sums_ref[...].astype(BF16)
 
 
 def halve_kernel(shift, count, places, *refs):
@@ -656,14 +684,14 @@
         got_second = swap(tiles, 1, second_send)
 
     per = latent // tiles
-    to_inner, to_outer, to_far, partial, *first = call(
+    to_inner, to_outer, to_far, sums, *first = call(
         functools.partial(first_kernel, tiles, places, fast),
         "first",
         [
             vmem((NEAR, latent), BF16),
             vmem((NEAR, latent), BF16),
             vmem((tiles * places, latent), BF16) if fast else shaped((tiles * places, latent), BF16),
-            vmem((nodes, latent), F32),
+            vmem((2 * nodes, latent), BF16),
         ] + (
             [
                 vmem((half * per + tiles * places // 2, latent), BF16),
@@ -673,7 +701,7 @@
             ]
             if fast else [shaped((3 * latent, latent), F32)]
         ),
-        [dpre_a, dpre_b, edge_kept, moved, receiver_kept, table, node_kept, w1_kept, base],
+        [dpre_a, dpre_b, edge_kept, moved, receiver_kept, table, node_kept, w1_kept],
         scratch=[
             vmem((3 * latent, latent), F32), vmem((rows + nodes, latent), F32),
             vmem((2 * NEAR, latent), F32),
@@ -684,11 +712,13 @@
         return call(
             edge_kernel,
             "edge",
-            [shaped((edges, latent), BF16)],
-            [dpre_a, dpre_b, cot_kept, w1_kept],
-            out_specs=[pl.BlockSpec(memory_space=pltpu.HBM)],
+            [shaped((edges, latent), BF16), vmem((nodes, latent), F32)],
+            [dpre_a, dpre_b, cot_kept, w1_kept, base, sums],
+            out_specs=[
+                pl.BlockSpec(memory_space=pltpu.HBM), pl.BlockSpec(memory_space=pltpu.VMEM),
+            ],
             scratch=[vmem((edges, latent), BF16), pltpu.SemaphoreType.DMA((steps,))],
-        )[0]
+        )
 
     if fast:
         send_a, keep_a, send_more, keep_more, send_b, keep_b = first
@@ -709,7 +739,7 @@
             1, [after(keep_b, send_a), second_keep], [inner, got_second]
      )
         got_b = swap(tiles, 2, send_b)
-        grad_edge = edge_call(after(dpre_a, send_b))
+        grad_edge, partial = edge_call(after(dpre_a, send_b))
         send, chain = halve(3, [after(chain, grad_edge, outer)], [got], flops=AHEAD)
         got = swap(tiles, 8, send)
         send_a, chain_a, slots = halve(2, [after(chain_a, send)], [got_a], slots, places)
@@ -724,7 +754,15 @@
         chain_b = after(chain_b, send_a)
         send_b, chain_b = halve(3, [chain_b], [got_b], flops=AHEAD)
         got_b = swap(tiles, 8, send_b)
-        returned = [slots, got_a]
+        node_sums, picks = call(
+            settle_kernel,
+            "settle",
+            [vmem((nodes, latent), F32), vmem((nodes, places * half), BF16)],
+            [listed, partial, inner, outer, slots],
+        )
+        (grad_node,) = call(
+            last_kernel, "last", [shaped((nodes, latent), BF16)], [node_sums, picks, got_a]
+        )
         grad_edge_w1, grad_edge_w2, grad_node_w1, grad_node_w2 = finish(
             [chain, chain_a, chain_b],
             [got, got_a, got_b],
@@ -732,22 +770,22 @@
             [3 * per, per, 2 * per, per],
         )
     else:
-        grad_edge = edge_call(dpre_a)
+        grad_edge, partial = edge_call(dpre_a)
         inner = lax.ppermute(to_inner, "tiles", inside)
         outer = lax.ppermute(to_outer, "tiles", across)
-        returned = [lax.all_to_all(to_far, "tiles", split_axis=0, concat_axis=0, tiled=True)]
+        returned = lax.all_to_all(to_far, "tiles", split_axis=0, concat_axis=0, tiled=True)
+        (grad_node,) = call(
+            node_kernel,
+            "node",
+            [shaped((nodes, latent), BF16)],
+            [listed, partial, inner, outer, returned],
+            scratch=[vmem((nodes, latent), F32)],
+        )
         scatter = functools.partial(
             lax.psum_scatter, axis_name="tiles", scatter_dimension=0, tiled=True
         )
         grad_node_w1, grad_node_w2 = scatter(node_keep), scatter(node_send)
         grad_edge_w1, grad_edge_w2 = scatter(first[0]), scatter(second_keep)
-    (grad_node,) = call(
-        functools.partial(node_kernel, fast),
-        "node",
-        [shaped((nodes, latent), BF16)],
-        [listed, partial, inner, outer, *returned],
-        scratch=[vmem((nodes, latent), F32)],
-    )
     return (grad_node, grad_edge, grad_edge_w1, grad_edge_w2, grad_node_w1, grad_node_w2)
 
 

time: 70.8 us -> 70 us (0.989)
    pallas_call x18 -> x19, Pallas kernels: 27.9 us -> 27.6 us  [call(): pl.pallas_call(kernel, in_specs=[pl.BlockSpec(memory_space=pltpu.HBM)] *...]
where the time goes in v12:
time: 70 us; the launch traced here: 69.7 us
  Pallas kernels  27.6 us (39%)
  starting transfers between devices  27.3 us (39%)
  waiting for transfers between devices  14.1 us (20%)
  between operations  0.75 us (1%)
    pallas_call x19, Pallas kernels, call(): pl.pallas_call(kernel, in_specs=[pl.BlockSpec(memory_space=pltpu.HBM)] *...  27.6 us
    ppermute x14, starting transfers between devices, swap(): return lax.ppermute(send, 'tiles', [(i, i ^ bit) for i in range(tiles)])  17.6 us
    ppermute x14, waiting for transfers between devices, swap(): return lax.ppermute(send, 'tiles', [(i, i ^ bit) for i in range(tiles)])  13 us
    all_to_all x1, starting transfers between devices, shards(): lax.all_to_all(outgoing, 'tiles', split_axis=0, concat_axis=0, tiled=True)  7.37 us
  transfers between devices with their start and end apart: 18, of which 8 were waited for; matrix products, arithmetic and copies ran while one was open for 0% of the time, Pallas kernels for 20%

profile of v12, /device:TPU:0, one launch (start us, length us, event | category | flops | bytes accessed | tf_op | source)
XLA Modules:
  0.0 69.7 jit_solution(700593447477322959)
XLA Ops:
  0.6 1.8 %outgoing.1 = (bf16[16,2,512]{2,1,0:T(2,128)(2,1)}, bf16[64,512]{1,0:T(8,128)(2,1)}, bf16[64,512]{1,0:T(8,128)(2,1)}) custom-call(s32[1,2,16]{2,1,0:T(2,128)} %bitcast.9, bf16[256,512]{1,0:T(8,128)(2,1)} %node_hbm.3), custom_call_target="tpu_custom_call" | custom-call | tf_op jit(solution)/shard_map/outgoing/pallas_call | solution.py:528
  2.5 7.4 %all-to-all-start = ((bf16[16,2,512]{2,1,0:T(2,128)(2,1)}), bf16[16,2,512]{2,1,0:T(2,128)(2,1)S(1)}, u32[]{:S(2)}, u32[]{:S(2)}) async-start(bf16[16,2,512]{2,1,0:T(2,128)(2,1)} %get-tuple-element.87), calls=%async_computation | async-start | bytes 65536 | tf_op jit(solution)/shard_map/all_to_all | solution.py:617
  10.2 1.3 %collective-permute-start.1 = (bf16[64,512]{1,0:T(8,128)(2,1)}, bf16[64,512]{1,0:T(8,128)(2,1)}, u32[]{:S(2)}, u32[]{:S(2)}) collective-permute-start(bf16[64,512]{1,0:T(8,128)(2,1)} %get-tuple-element.86), channel_id=1, source_target_pairs={{1,2},{2,1},{3,4},{4,3},{5,6},{6,5},{7,8},{8,7},{9,10},{10,9},{11,... | collective-permute-start | bytes 196616 | tf_op jit(solution)/shard_map/ppermute | solution.py:616
  11.5 3.8 %prepare.1 = (bf16[256,512]{1,0:T(8,128)(2,1)S(1)}, s32[12,128]{1,0:T(8,128)S(1)}, s32[12,128]{1,0:T(8,128)S(1)}, f32[1536,512]{1,0:T(8,128)S(1)}) custom-call(bf16[256,512]{1,0:T(8,128)(2,1)} %node_hbm.3, bf16[1536,512]{1,0:T(8,128)(2,1)} %w1_hbm.3, s32[12,128]{1,0:T(8,128)} %bitcast.16, s32[12,128]{1,0:T(8,128)} %bitcast.17, f32[1,512]{1,0:T(1,128)} %bitcast.18, ...), custom_call_target="tpu_custom_call" | custom-call | flops 10000000000 | bytes 100000000 | tf_op jit(solution)/shard_map/prepare/pallas_call | solution.py:528
  15.4 1.1 %all-to-all-done.far_ref = bf16[16,2,512]{2,1,0:T(2,128)(2,1)S(1)} async-done(((bf16[16,2,512]{2,1,0:T(2,128)(2,1)}), bf16[16,2,512]{2,1,0:T(2,128)(2,1)S(1)}, u32[]{:S(2)}, u32[]{:S(2)}) %all-to-all-start) | async-done | bytes 32800 | tf_op jit(solution)/shard_map/all_to_all | solution.py:617
  16.5 9.0 %forward.1 = (bf16[1536,512]{1,0:T(8,128)(2,1)S(1)}, bf16[1536,512]{1,0:T(8,128)(2,1)S(1)}, bf16[1536,512]{1,0:T(8,128)(2,1)S(1)}, bf16[512,512]{1,0:T(8,128)(2,...) custom-call(bf16[1536,512]{1,0:T(8,128)(2,1)} %w1_hbm.3, ...), custom_call_target="tpu_custom_call" | custom-call | tf_op jit(solution)/shard_map/forward/pallas_call | solution.py:528
  25.5 1.5 %collective-permute-start.2 = (bf16[768,512]{1,0:T(8,128)(2,1)S(1)}, bf16[768,512]{1,0:T(8,128)(2,1)S(1)}, u32[]{:S(2)}, u32[]{:S(2)}) collective-permute-start(bf16[768,512]{1,0:T(8,128)(2,1)S(1)} %get-tuple-element.105), channel_id=1, source_target_pairs={{0,1},{1,0},{2,3},{3,2},{4,5},{5,4},{6,7},{7,6},{8,9},{9,8},{10,11... | collective-permute-start | bytes 2359304 | tf_op jit(solution)/shard_map/ppermute | solution.py:541
  27.0 1.7 %slope.2 = (bf16[768,512]{1,0:T(8,128)(2,1)S(1)}, f32[512,512]{1,0:T(8,128)S(1)}) custom-call(bf16[1536,512]{1,0:T(8,128)(2,1)S(1)} %get-tuple-element.93.cot_ref, s32[12,128]{1,0:T(8,128)S(1)} %get-tuple-element.91.receiver_ref, bf16[256,512]{1,0:T(8,128)(2,1)S(1)} %get-tuple-element.107.dsum_ref, bf16[1536,512]{1,0:T(8,128)(2,1)S(1)} %get-tuple-element.95.hidden_ref, ...), custom_call_target="tpu_custom_call" | custom-call | tf_op jit(solution)/shard_map/slope/pallas_call | solution.py:528
  29.1 1.9 %slope.3 = (bf16[768,512]{1,0:T(8,128)(2,1)S(1)}, bf16[256,512]{1,0:T(8,128)(2,1)S(1)}, f32[8,32,512]{2,1,0:T(8,128)S(1)}) custom-call(bf16[1536,512]{1,0:T(8,128)(2,1)S(1)} %get-tuple-element.93.cot_ref, s32[12,128]{1,0:T(8,128)S(1)} %get-tuple-element.91.receiver_ref, bf16[256,512]{1,0:T(8,128)(2,1)S(1)} %get-tuple-element.107.dsum_ref, ...), custom_call_target="tpu_custom_call" | custom-call | tf_op jit(solution)/shard_map/slope/pallas_call | solution.py:528
  31.4 1.4 %collective-permute-start.8 = (bf16[384,512]{1,0:T(8,128)(2,1)S(1)}, bf16[384,512]{1,0:T(8,128)(2,1)S(1)}, u32[]{:S(2)}, u32[]{:S(2)}) collective-permute-start(bf16[384,512]{1,0:T(8,128)(2,1)S(1)} %get-tuple-element.106), channel_id=1, source_target_pairs={{0,4},{1,5},{2,6},{3,7},{4,0},{5,1},{6,2},{7,3},{8,12},{9,13},{10,... | collective-permute-start | bytes 1179656 | tf_op jit(solution)/shard_map/ppermute | solution.py:541
  32.8 4.0 %first.1 = (bf16[64,512]{1,0:T(8,128)(2,1)}, bf16[64,512]{1,0:T(8,128)(2,1)S(1)}, bf16[32,512]{1,0:T(8,128)(2,1)S(1)}, bf16[512,512]{1,0:T(8,128)(2,1)S(1)}, bf1...) custom-call(bf16[768,512]{1,0:T(8,128)(2,1)S(1)} %get-tuple-element., ...), custom_call_target="tpu_custom_call" | custom-call | tf_op jit(solution)/shard_map/first/pallas_call | solution.py:528
  38.2 1.1 %collective-permute-done.5.refs_3_ = bf16[256,512]{1,0:T(8,128)(2,1)S(1)} collective-permute-done((bf16[256,512]{1,0:T(8,128)(2,1)S(1)}, bf16[256,512]{1,0:T(8,128)(2,1)S(1)}, u32[]{:S(2)}, u32[]{:S(2)}) %collective-permute-start.5) | collective-permute-done | bytes 262176 | tf_op jit(solution)/shard_map/ppermute | solution.py:541
  39.6 2.2 %collective-permute-start.9 = (bf16[272,512]{1,0:T(8,128)(2,1)S(1)}, bf16[272,512]{1,0:T(8,128)(2,1)S(1)}, u32[]{:S(2)}, u32[]{:S(2)}) collective-permute-start(bf16[272,512]{1,0:T(8,128)(2,1)S(1)} %get-tuple-element.123), channel_id=1, source_target_pairs={{0,2},{1,3},{2,0},{3,1},{4,6},{5,7},{6,4},{7,5},{8,10},{9,11},{10,... | collective-permute-start | bytes 835592 | tf_op jit(solution)/shard_map/ppermute | solution.py:541
  42.0 1.8 %edge.1 = (bf16[1536,512]{1,0:T(8,128)(2,1)}, f32[256,512]{1,0:T(8,128)S(1)}) custom-call(bf16[768,512]{1,0:T(8,128)(2,1)S(1)} %get-tuple-element.128.dpre_a_ref, bf16[768,512]{1,0:T(8,128)(2,1)S(1)} %get-tuple-element.108.dpre_b_ref, bf16[1536,512]{1,0:T(8,128)(2,1)S(1)} %get-tuple-element.93.cot_ref, bf16[1536,512]{1,0:T(8,128)(2,1)S(1)} %get-tuple-element.111.w1_ref, ...), custom_call_target="tpu_custom_call" | custom-call | tf_op jit(solution)/shard_map/edge/pallas_call | solution.py:528
  43.9 3.0 %collective-permute-start.11 = (bf16[192,512]{1,0:T(8,128)(2,1)S(1)}, bf16[192,512]{1,0:T(8,128)(2,1)S(1)}, u32[]{:S(2)}, u32[]{:S(2)}) collective-permute-start(bf16[192,512]{1,0:T(8,128)(2,1)S(1)} %get-tuple-element.137), channel_id=1, source_target_pairs={{0,8},{1,9},{2,10},{3,11},{4,12},{5,13},{6,14},{7,15},{8,0},{9,1},... | collective-permute-start | bytes 589832 | tf_op jit(solution)/shard_map/ppermute | solution.py:541
  46.9 2.7 %collective-permute-done.9.refs_1_ = bf16[272,512]{1,0:T(8,128)(2,1)S(1)} collective-permute-done((bf16[272,512]{1,0:T(8,128)(2,1)S(1)}, bf16[272,512]{1,0:T(8,128)(2,1)S(1)}, u32[]{:S(2)}, u32[]{:S(2)}) %collective-permute-start.9) | collective-permute-done | bytes 278560 | tf_op jit(solution)/shard_map/ppermute | solution.py:541
  49.9 2.7 %collective-permute-start.12 = (bf16[144,512]{1,0:T(8,128)(2,1)S(1)}, bf16[144,512]{1,0:T(8,128)(2,1)S(1)}, u32[]{:S(2)}, u32[]{:S(2)}) collective-permute-start(bf16[144,512]{1,0:T(8,128)(2,1)S(1)} %get-tuple-element.143), channel_id=1, source_target_pairs={{0,4},{1,5},{2,6},{3,7},{4,0},{5,1},{6,2},{7,3},{8,12},{9,13},{10,... | collective-permute-start | bytes 442376 | tf_op jit(solution)/shard_map/ppermute | solution.py:541
  52.5 2.5 %collective-permute-done.10.refs_1_ = bf16[256,512]{1,0:T(8,128)(2,1)S(1)} collective-permute-done((bf16[256,512]{1,0:T(8,128)(2,1)S(1)}, bf16[256,512]{1,0:T(8,128)(2,1)S(1)}, u32[]{:S(2)}, u32[]{:S(2)}) %collective-permute-start.10) | collective-permute-done | bytes 262176 | tf_op jit(solution)/shard_map/ppermute | solution.py:541
  55.2 1.9 %collective-permute-start.14 = (bf16[128,512]{1,0:T(8,128)(2,1)S(1)}, bf16[128,512]{1,0:T(8,128)(2,1)S(1)}, u32[]{:S(2)}, u32[]{:S(2)}) collective-permute-start(bf16[128,512]{1,0:T(8,128)(2,1)S(1)} %get-tuple-element.145), channel_id=1, source_target_pairs={{0,4},{1,5},{2,6},{3,7},{4,0},{5,1},{6,2},{7,3},{8,12},{9,13},{10,... | collective-permute-start | bytes 393224 | tf_op jit(solution)/shard_map/ppermute | solution.py:541
  57.1 1.1 %collective-permute-start.15 = (bf16[96,512]{1,0:T(8,128)(2,1)S(1)}, bf16[96,512]{1,0:T(8,128)(2,1)S(1)}, u32[]{:S(2)}, u32[]{:S(2)}) collective-permute-start(bf16[96,512]{1,0:T(8,128)(2,1)S(1)} %get-tuple-element.147), channel_id=1, source_target_pairs={{0,2},{1,3},{2,0},{3,1},{4,6},{5,7},{6,4},{7,5},{8,10},{9,11},{10,... | collective-permute-start | bytes 294920 | tf_op jit(solution)/shard_map/ppermute | solution.py:541
  58.2 1.8 %collective-permute-done.12.refs_1_ = bf16[144,512]{1,0:T(8,128)(2,1)S(1)} collective-permute-done((bf16[144,512]{1,0:T(8,128)(2,1)S(1)}, bf16[144,512]{1,0:T(8,128)(2,1)S(1)}, u32[]{:S(2)}, u32[]{:S(2)}) %collective-permute-start.12) | collective-permute-done | bytes 147488 | tf_op jit(solution)/shard_map/ppermute | solution.py:541
  60.7 1.4 %collective-permute-done.14.refs_1_ = bf16[128,512]{1,0:T(8,128)(2,1)S(1)} collective-permute-done((bf16[128,512]{1,0:T(8,128)(2,1)S(1)}, bf16[128,512]{1,0:T(8,128)(2,1)S(1)}, u32[]{:S(2)}, u32[]{:S(2)}) %collective-permute-start.14) | collective-permute-done | bytes 131104 | tf_op jit(solution)/shard_map/ppermute | solution.py:541
  62.1 2.3 %collective-permute-start.16 = (bf16[64,512]{1,0:T(8,128)(2,1)S(1)}, bf16[64,512]{1,0:T(8,128)(2,1)S(1)}, u32[]{:S(2)}, u32[]{:S(2)}) collective-permute-start(bf16[64,512]{1,0:T(8,128)(2,1)S(1)} %get-tuple-element.159), channel_id=1, source_target_pairs={{0,8},{1,9},{2,10},{3,11},{4,12},{5,13},{6,14},{7,15},{8,0},{9,1},... | collective-permute-start | bytes 196616 | tf_op jit(solution)/shard_map/ppermute | solution.py:541
  64.9 3.2 %collective-permute-done.13.got_ref.refs_4_ = bf16[80,512]{1,0:T(8,128)(2,1)S(1)} collective-permute-done((bf16[80,512]{1,0:T(8,128)(2,1)S(1)}, bf16[80,512]{1,0:T(8,128)(2,1)S(1)}, u32[]{:S(2)}, u32[]{:S(2)}) %collective-permute-start.13) | collective-permute-done | bytes 81952 | tf_op jit(solution)/shard_map/ppermute | solution.py:541
  (33 shorter events, 6.3 us)
Async XLA Ops:
  2.5 14.0 %all-to-all-start = ((bf16[16,2,512]{2,1,0:T(2,128)(2,1)}), bf16[16,2,512]{2,1,0:T(2,128)(2,1)S(1)}, u32[]{:S(2)}, u32[]{:S(2)}) async-start(bf16[16,2,512]{2,1,0:T(2,128)(2,1)} %get-tuple-element.87), calls=%async_computation | async-start | bytes 65536 | tf_op jit(solution)/shard_map/all_to_all | solution.py:617
  9.8 6.6 %collective-permute-start = (bf16[64,512]{1,0:T(8,128)(2,1)}, bf16[64,512]{1,0:T(8,128)(2,1)S(1)}, u32[]{:S(2)}, u32[]{:S(2)}) collective-permute-start(bf16[64,512]{1,0:T(8,128)(2,1)} %get-tuple-element.85), channel_id=1, source_target_pairs={{0,1},{1,0},{2,3},{3,2},{4,5},{5,4},{6,7},{7,6},{8,9},{9,8},{10,11... | collective-permute-start | bytes 196616 | tf_op jit(solution)/shard_map/ppermute | solution.py:615
  10.2 6.2 %collective-permute-start.1 = (bf16[64,512]{1,0:T(8,128)(2,1)}, bf16[64,512]{1,0:T(8,128)(2,1)}, u32[]{:S(2)}, u32[]{:S(2)}) collective-permute-start(bf16[64,512]{1,0:T(8,128)(2,1)} %get-tuple-element.86), channel_id=1, source_target_pairs={{1,2},{2,1},{3,4},{4,3},{5,6},{6,5},{7,8},{8,7},{9,10},{10,9},{11,... | collective-permute-start | bytes 196616 | tf_op jit(solution)/shard_map/ppermute | solution.py:616
  25.5 3.4 %collective-permute-start.2 = (bf16[768,512]{1,0:T(8,128)(2,1)S(1)}, bf16[768,512]{1,0:T(8,128)(2,1)S(1)}, u32[]{:S(2)}, u32[]{:S(2)}) collective-permute-start(bf16[768,512]{1,0:T(8,128)(2,1)S(1)} %get-tuple-element.105), channel_id=1, source_target_pairs={{0,1},{1,0},{2,3},{3,2},{4,5},{5,4},{6,7},{7,6},{8,9},{9,8},{10,11... | collective-permute-start | bytes 2359304 | tf_op jit(solution)/shard_map/ppermute | solution.py:541
  31.0 5.9 %collective-permute-start.3 = (bf16[256,512]{1,0:T(8,128)(2,1)S(1)}, bf16[256,512]{1,0:T(8,128)(2,1)S(1)}, u32[]{:S(2)}, u32[]{:S(2)}) collective-permute-start(bf16[256,512]{1,0:T(8,128)(2,1)S(1)} %get-tuple-element.119), channel_id=1, source_target_pairs={{0,1},{1,0},{2,3},{3,2},{4,5},{5,4},{6,7},{7,6},{8,9},{9,8},{10,11... | collective-permute-start | bytes 786440 | tf_op jit(solution)/shard_map/ppermute | solution.py:541
  31.4 12.4 %collective-permute-start.8 = (bf16[384,512]{1,0:T(8,128)(2,1)S(1)}, bf16[384,512]{1,0:T(8,128)(2,1)S(1)}, u32[]{:S(2)}, u32[]{:S(2)}) collective-permute-start(bf16[384,512]{1,0:T(8,128)(2,1)S(1)} %get-tuple-element.106), channel_id=1, source_target_pairs={{0,4},{1,5},{2,6},{3,7},{4,0},{5,1},{6,2},{7,3},{8,12},{9,13},{10,... | collective-permute-start | bytes 1179656 | tf_op jit(solution)/shard_map/ppermute | solution.py:541
  36.9 4.9 %collective-permute-start.6 = (bf16[320,512]{1,0:T(8,128)(2,1)S(1)}, bf16[320,512]{1,0:T(8,128)(2,1)S(1)}, u32[]{:S(2)}, u32[]{:S(2)}) collective-permute-start(bf16[320,512]{1,0:T(8,128)(2,1)S(1)} %get-tuple-element.126), channel_id=1, source_target_pairs={{0,1},{1,0},{2,3},{3,2},{4,5},{5,4},{6,7},{7,6},{8,9},{9,8},{10,11... | collective-permute-start | bytes 983048 | tf_op jit(solution)/shard_map/ppermute | solution.py:541
  37.0 2.3 %collective-permute-start.4 = (bf16[272,512]{1,0:T(8,128)(2,1)S(1)}, bf16[272,512]{1,0:T(8,128)(2,1)S(1)}, u32[]{:S(2)}, u32[]{:S(2)}) collective-permute-start(bf16[272,512]{1,0:T(8,128)(2,1)S(1)} %get-tuple-element.120), channel_id=1, source_target_pairs={{0,1},{1,0},{2,3},{3,2},{4,5},{5,4},{6,7},{7,6},{8,9},{9,8},{10,11... | collective-permute-start | bytes 835592 | tf_op jit(solution)/shard_map/ppermute | solution.py:541
  37.4 1.9 %collective-permute-start.5 = (bf16[256,512]{1,0:T(8,128)(2,1)S(1)}, bf16[256,512]{1,0:T(8,128)(2,1)S(1)}, u32[]{:S(2)}, u32[]{:S(2)}) collective-permute-start(bf16[256,512]{1,0:T(8,128)(2,1)S(1)} %get-tuple-element.121), channel_id=1, source_target_pairs={{0,1},{1,0},{2,3},{3,2},{4,5},{5,4},{6,7},{7,6},{8,9},{9,8},{10,11... | collective-permute-start | bytes 786440 | tf_op jit(solution)/shard_map/ppermute | solution.py:541
  37.5 6.2 %collective-permute-start.7 = (bf16[64,512]{1,0:T(8,128)(2,1)S(1)}, bf16[64,512]{1,0:T(8,128)(2,1)S(1)}, u32[]{:S(2)}, u32[]{:S(2)}) collective-permute-start(bf16[64,512]{1,0:T(8,128)(2,1)S(1)} %get-tuple-element.132), channel_id=1, source_target_pairs={{1,2},{2,1},{3,4},{4,3},{5,6},{6,5},{7,8},{8,7},{9,10},{10,9},{11,... | collective-permute-start | bytes 196616 | tf_op jit(solution)/shard_map/ppermute | solution.py:729
  39.6 10.0 %collective-permute-start.9 = (bf16[272,512]{1,0:T(8,128)(2,1)S(1)}, bf16[272,512]{1,0:T(8,128)(2,1)S(1)}, u32[]{:S(2)}, u32[]{:S(2)}) collective-permute-start(bf16[272,512]{1,0:T(8,128)(2,1)S(1)} %get-tuple-element.123), channel_id=1, source_target_pairs={{0,2},{1,3},{2,0},{3,1},{4,6},{5,7},{6,4},{7,5},{8,10},{9,11},{10,... | collective-permute-start | bytes 835592 | tf_op jit(solution)/shard_map/ppermute | solution.py:541
  41.9 13.2 %collective-permute-start.10 = (bf16[256,512]{1,0:T(8,128)(2,1)S(1)}, bf16[256,512]{1,0:T(8,128)(2,1)S(1)}, u32[]{:S(2)}, u32[]{:S(2)}) collective-permute-start(bf16[256,512]{1,0:T(8,128)(2,1)S(1)} %get-tuple-element.127), channel_id=1, source_target_pairs={{0,2},{1,3},{2,0},{3,1},{4,6},{5,7},{6,4},{7,5},{8,10},{9,11},{10,... | collective-permute-start | bytes 786440 | tf_op jit(solution)/shard_map/ppermute | solution.py:541
  43.9 13.2 %collective-permute-start.11 = (bf16[192,512]{1,0:T(8,128)(2,1)S(1)}, bf16[192,512]{1,0:T(8,128)(2,1)S(1)}, u32[]{:S(2)}, u32[]{:S(2)}) collective-permute-start(bf16[192,512]{1,0:T(8,128)(2,1)S(1)} %get-tuple-element.137), channel_id=1, source_target_pairs={{0,8},{1,9},{2,10},{3,11},{4,12},{5,13},{6,14},{7,15},{8,0},{9,1},... | collective-permute-start | bytes 589832 | tf_op jit(solution)/shard_map/ppermute | solution.py:541
  49.9 10.2 %collective-permute-start.12 = (bf16[144,512]{1,0:T(8,128)(2,1)S(1)}, bf16[144,512]{1,0:T(8,128)(2,1)S(1)}, u32[]{:S(2)}, u32[]{:S(2)}) collective-permute-start(bf16[144,512]{1,0:T(8,128)(2,1)S(1)} %get-tuple-element.143), channel_id=1, source_target_pairs={{0,4},{1,5},{2,6},{3,7},{4,0},{5,1},{6,2},{7,3},{8,12},{9,13},{10,... | collective-permute-start | bytes 442376 | tf_op jit(solution)/shard_map/ppermute | solution.py:541
  55.2 6.9 %collective-permute-start.14 = (bf16[128,512]{1,0:T(8,128)(2,1)S(1)}, bf16[128,512]{1,0:T(8,128)(2,1)S(1)}, u32[]{:S(2)}, u32[]{:S(2)}) collective-permute-start(bf16[128,512]{1,0:T(8,128)(2,1)S(1)} %get-tuple-element.145), channel_id=1, source_target_pairs={{0,4},{1,5},{2,6},{3,7},{4,0},{5,1},{6,2},{7,3},{8,12},{9,13},{10,... | collective-permute-start | bytes 393224 | tf_op jit(solution)/shard_map/ppermute | solution.py:541
  57.1 11.9 %collective-permute-start.15 = (bf16[96,512]{1,0:T(8,128)(2,1)S(1)}, bf16[96,512]{1,0:T(8,128)(2,1)S(1)}, u32[]{:S(2)}, u32[]{:S(2)}) collective-permute-start(bf16[96,512]{1,0:T(8,128)(2,1)S(1)} %get-tuple-element.147), channel_id=1, source_target_pairs={{0,2},{1,3},{2,0},{3,1},{4,6},{5,7},{6,4},{7,5},{8,10},{9,11},{10,... | collective-permute-start | bytes 294920 | tf_op jit(solution)/shard_map/ppermute | solution.py:541
  60.4 7.7 %collective-permute-start.13 = (bf16[80,512]{1,0:T(8,128)(2,1)S(1)}, bf16[80,512]{1,0:T(8,128)(2,1)S(1)}, u32[]{:S(2)}, u32[]{:S(2)}) collective-permute-start(bf16[80,512]{1,0:T(8,128)(2,1)S(1)} %get-tuple-element.153), channel_id=1, source_target_pairs={{0,8},{1,9},{2,10},{3,11},{4,12},{5,13},{6,14},{7,15},{8,0},{9,1},... | collective-permute-start | bytes 245768 | tf_op jit(solution)/shard_map/ppermute | solution.py:541
  60.7 3.7 %copy-start = (s32[1,16,2]{1,2,0:T(2,128)S(1)}, s32[1,16,2]{1,2,0:T(2,128)}, u32[]{:S(2)}) copy-start(s32[1,16,2]{1,2,0:T(2,128)} %param.32) | copy-start | bytes 388
  62.1 6.8 %collective-permute-start.16 = (bf16[64,512]{1,0:T(8,128)(2,1)S(1)}, bf16[64,512]{1,0:T(8,128)(2,1)S(1)}, u32[]{:S(2)}, u32[]{:S(2)}) collective-permute-start(bf16[64,512]{1,0:T(8,128)(2,1)S(1)} %get-tuple-element.159), channel_id=1, source_target_pairs={{0,8},{1,9},{2,10},{3,11},{4,12},{5,13},{6,14},{7,15},{8,0},{9,1},... | collective-permute-start | bytes 196616 | tf_op jit(solution)/shard_map/ppermute | solution.py:541

commit v13 on v12

--- a/solution.py
+++ b/solution.py
@@ -9,7 +9,7 @@
 
 NEAR = 64
 EPSILON = 1e-05
-TILE = 256
+TILE = 384
 LANES = 128
 F32 = jnp.float32
 BF16 = jnp.bfloat16
@@ -157,20 +157,22 @@
     nodes = node_ref.shape[0]
     copies = fetch(
         [
-            (node_hbm, node_ref), (w1_hbm, w1_ref), (sender_hbm, sender_ref),
-            (receiver_hbm, receiver_ref), (b1_hbm, b1_ref),
+            (node_hbm, node_ref), (w1_hbm.at[pl.ds(latent, 2 * latent)], w1_ref),
+            (sender_hbm, sender_ref), (receiver_hbm, receiver_ref), (b1_hbm, b1_ref),
         ],
         sems,
     )
-    edge_copies = fetch(tile_pairs(edge_hbm, edge_ref, edges // 2), edge_sems)
+    edge_copies = fetch(
+        [(w1_hbm.at[pl.ds(0, latent)], weights.at[pl.ds(0, latent)]), (edge_hbm, edge_ref)],
+        edge_sems,
+    )
     for copy in copies:
         copy.wait()
     moved_ref[...] = table_index(sender_ref[...], tiles, places, nodes)
-    weights[:latent, :] = w1_ref[:latent, :]
     weights[latent : latent + nodes, :] = dot(
-        node_ref[...], w1_ref[latent : 2 * latent, :]
+        node_ref[...], w1_ref[:latent, :]
     ).astype(BF16)
-    weights[latent + nodes :, :] = dot(node_ref[...], w1_ref[2 * latent :, :]).astype(BF16)
+    weights[latent + nodes :, :] = dot(node_ref[...], w1_ref[latent:, :]).astype(BF16)
     for copy in edge_copies:
         copy.wait()
     for step in range(edges // TILE):
@@ -626,7 +628,7 @@
         [node_latent, edge_w1, after(sender, outgoing), receiver, row(edge_b1), edge_latent],
         hbm=6,
         scratch=[
-            vmem((edges, latent), BF16), vmem(edge_w1.shape, BF16),
+            vmem((edges, latent), BF16), vmem((2 * latent, latent), BF16),
             vmem((latent + 2 * nodes, latent), BF16), vmem(sender.shape, jnp.int32),
             vmem((1, latent), F32), pltpu.SemaphoreType.DMA((5,)), pltpu.SemaphoreType.DMA((2,)),
         ],

time: 70 us -> 70.7 us (1.010)
  Pallas kernels: 27.6 us -> 28.5 us
    pallas_call x19, Pallas kernels: 27.6 us -> 28.5 us  [call(): pl.pallas_call(kernel, in_specs=[pl.BlockSpec(memory_space=pltpu.HBM)] *...]
  transfers between devices with their start and end apart: 18 -> 18, of which waited for: 8 -> 8; matrix products, arithmetic and copies ran while one was open for 0% -> 0% of each run, Pallas kernels for 20% -> 21%
where the time goes in v13:
time: 70.7 us; the launch traced here: 70.4 us
  Pallas kernels  28.5 us (40%)
  starting transfers between devices  27.1 us (38%)
  waiting for transfers between devices  14 us (20%)
  between operations  0.75 us (1%)
    pallas_call x19, Pallas kernels, call(): pl.pallas_call(kernel, in_specs=[pl.BlockSpec(memory_space=pltpu.HBM)] *...  28.5 us
    ppermute x14, starting transfers between devices, swap(): return lax.ppermute(send, 'tiles', [(i, i ^ bit) for i in range(tiles)])  17.4 us
    ppermute x14, waiting for transfers between devices, swap(): return lax.ppermute(send, 'tiles', [(i, i ^ bit) for i in range(tiles)])  13 us
    all_to_all x1, starting transfers between devices, shards(): lax.all_to_all(outgoing, 'tiles', split_axis=0, concat_axis=0, tiled=True)  7.37 us
  transfers between devices with their start and end apart: 18, of which 8 were waited for; matrix products, arithmetic and copies ran while one was open for 0% of the time, Pallas kernels for 21%

profile of v13, /device:TPU:0, one launch (start us, length us, event | category | flops | bytes accessed | tf_op | source)
XLA Modules:
  0.0 70.4 jit_solution(3849572676313408655)
XLA Ops:
  0.6 1.8 %outgoing.1 = (bf16[16,2,512]{2,1,0:T(2,128)(2,1)}, bf16[64,512]{1,0:T(8,128)(2,1)}, bf16[64,512]{1,0:T(8,128)(2,1)}) custom-call(s32[1,2,16]{2,1,0:T(2,128)} %bitcast.9, bf16[256,512]{1,0:T(8,128)(2,1)} %node_hbm.3), custom_call_target="tpu_custom_call" | custom-call | tf_op jit(solution)/shard_map/outgoing/pallas_call | solution.py:530
  2.5 7.4 %all-to-all-start = ((bf16[16,2,512]{2,1,0:T(2,128)(2,1)}), bf16[16,2,512]{2,1,0:T(2,128)(2,1)S(1)}, u32[]{:S(2)}, u32[]{:S(2)}) async-start(bf16[16,2,512]{2,1,0:T(2,128)(2,1)} %get-tuple-element.87), calls=%async_computation | async-start | bytes 65536 | tf_op jit(solution)/shard_map/all_to_all | solution.py:619
  10.2 1.3 %collective-permute-start.1 = (bf16[64,512]{1,0:T(8,128)(2,1)}, bf16[64,512]{1,0:T(8,128)(2,1)}, u32[]{:S(2)}, u32[]{:S(2)}) collective-permute-start(bf16[64,512]{1,0:T(8,128)(2,1)} %get-tuple-element.86), channel_id=1, source_target_pairs={{1,2},{2,1},{3,4},{4,3},{5,6},{6,5},{7,8},{8,7},{9,10},{10,9},{11,... | collective-permute-start | bytes 196616 | tf_op jit(solution)/shard_map/ppermute | solution.py:618
  11.5 3.9 %prepare.1 = (bf16[256,512]{1,0:T(8,128)(2,1)S(1)}, s32[12,128]{1,0:T(8,128)S(1)}, s32[12,128]{1,0:T(8,128)S(1)}, f32[1536,512]{1,0:T(8,128)S(1)}) custom-call(bf16[256,512]{1,0:T(8,128)(2,1)} %node_hbm.3, bf16[1536,512]{1,0:T(8,128)(2,1)} %w1_hbm.3, s32[12,128]{1,0:T(8,128)} %bitcast.16, s32[12,128]{1,0:T(8,128)} %bitcast.17, f32[1,512]{1,0:T(1,128)} %bitcast.18, ...), custom_call_target="tpu_custom_call" | custom-call | flops 10000000000 | bytes 100000000 | tf_op jit(solution)/shard_map/prepare/pallas_call | solution.py:530
  15.4 1.1 %all-to-all-done.far_ref = bf16[16,2,512]{2,1,0:T(2,128)(2,1)S(1)} async-done(((bf16[16,2,512]{2,1,0:T(2,128)(2,1)}), bf16[16,2,512]{2,1,0:T(2,128)(2,1)S(1)}, u32[]{:S(2)}, u32[]{:S(2)}) %all-to-all-start) | async-done | bytes 32800 | tf_op jit(solution)/shard_map/all_to_all | solution.py:619
  16.5 9.0 %forward.1 = (bf16[1536,512]{1,0:T(8,128)(2,1)S(1)}, bf16[1536,512]{1,0:T(8,128)(2,1)S(1)}, bf16[1536,512]{1,0:T(8,128)(2,1)S(1)}, bf16[512,512]{1,0:T(8,128)(2,...) custom-call(bf16[1536,512]{1,0:T(8,128)(2,1)} %w1_hbm.3, ...), custom_call_target="tpu_custom_call" | custom-call | tf_op jit(solution)/shard_map/forward/pallas_call | solution.py:530
  25.4 1.6 %collective-permute-start.2 = (bf16[768,512]{1,0:T(8,128)(2,1)S(1)}, bf16[768,512]{1,0:T(8,128)(2,1)S(1)}, u32[]{:S(2)}, u32[]{:S(2)}) collective-permute-start(bf16[768,512]{1,0:T(8,128)(2,1)S(1)} %get-tuple-element.105), channel_id=1, source_target_pairs={{0,1},{1,0},{2,3},{3,2},{4,5},{5,4},{6,7},{7,6},{8,9},{9,8},{10,11... | collective-permute-start | bytes 2359304 | tf_op jit(solution)/shard_map/ppermute | solution.py:543
  27.0 1.9 %slope.2 = (bf16[768,512]{1,0:T(8,128)(2,1)S(1)}, f32[512,512]{1,0:T(8,128)S(1)}) custom-call(bf16[1536,512]{1,0:T(8,128)(2,1)S(1)} %get-tuple-element.93.cot_ref, s32[12,128]{1,0:T(8,128)S(1)} %get-tuple-element.91.receiver_ref, bf16[256,512]{1,0:T(8,128)(2,1)S(1)} %get-tuple-element.107.dsum_ref, bf16[1536,512]{1,0:T(8,128)(2,1)S(1)} %get-tuple-element.95.hidden_ref, ...), custom_call_target="tpu_custom_call" | custom-call | tf_op jit(solution)/shard_map/slope/pallas_call | solution.py:530
  29.0 2.0 %slope.3 = (bf16[768,512]{1,0:T(8,128)(2,1)S(1)}, bf16[256,512]{1,0:T(8,128)(2,1)S(1)}, f32[8,32,512]{2,1,0:T(8,128)S(1)}) custom-call(bf16[1536,512]{1,0:T(8,128)(2,1)S(1)} %get-tuple-element.93.cot_ref, s32[12,128]{1,0:T(8,128)S(1)} %get-tuple-element.91.receiver_ref, bf16[256,512]{1,0:T(8,128)(2,1)S(1)} %get-tuple-element.107.dsum_ref, ...), custom_call_target="tpu_custom_call" | custom-call | tf_op jit(solution)/shard_map/slope/pallas_call | solution.py:530
  31.5 1.5 %collective-permute-start.8 = (bf16[384,512]{1,0:T(8,128)(2,1)S(1)}, bf16[384,512]{1,0:T(8,128)(2,1)S(1)}, u32[]{:S(2)}, u32[]{:S(2)}) collective-permute-start(bf16[384,512]{1,0:T(8,128)(2,1)S(1)} %get-tuple-element.106), channel_id=1, source_target_pairs={{0,4},{1,5},{2,6},{3,7},{4,0},{5,1},{6,2},{7,3},{8,12},{9,13},{10,... | collective-permute-start | bytes 1179656 | tf_op jit(solution)/shard_map/ppermute | solution.py:543
  33.0 4.6 %first.1 = (bf16[64,512]{1,0:T(8,128)(2,1)}, bf16[64,512]{1,0:T(8,128)(2,1)S(1)}, bf16[32,512]{1,0:T(8,128)(2,1)S(1)}, bf16[512,512]{1,0:T(8,128)(2,1)S(1)}, bf1...) custom-call(bf16[768,512]{1,0:T(8,128)(2,1)S(1)} %get-tuple-element., ...), custom_call_target="tpu_custom_call" | custom-call | tf_op jit(solution)/shard_map/first/pallas_call | solution.py:530
  38.9 1.1 %collective-permute-done.5.refs_3_ = bf16[256,512]{1,0:T(8,128)(2,1)S(1)} collective-permute-done((bf16[256,512]{1,0:T(8,128)(2,1)S(1)}, bf16[256,512]{1,0:T(8,128)(2,1)S(1)}, u32[]{:S(2)}, u32[]{:S(2)}) %collective-permute-start.5) | collective-permute-done | bytes 262176 | tf_op jit(solution)/shard_map/ppermute | solution.py:543
  40.3 2.2 %collective-permute-start.9 = (bf16[272,512]{1,0:T(8,128)(2,1)S(1)}, bf16[272,512]{1,0:T(8,128)(2,1)S(1)}, u32[]{:S(2)}, u32[]{:S(2)}) collective-permute-start(bf16[272,512]{1,0:T(8,128)(2,1)S(1)} %get-tuple-element.123), channel_id=1, source_target_pairs={{0,2},{1,3},{2,0},{3,1},{4,6},{5,7},{6,4},{7,5},{8,10},{9,11},{10,... | collective-permute-start | bytes 835592 | tf_op jit(solution)/shard_map/ppermute | solution.py:543
  42.7 1.8 %edge.1 = (bf16[1536,512]{1,0:T(8,128)(2,1)}, f32[256,512]{1,0:T(8,128)S(1)}) custom-call(bf16[768,512]{1,0:T(8,128)(2,1)S(1)} %get-tuple-element.128.dpre_a_ref, bf16[768,512]{1,0:T(8,128)(2,1)S(1)} %get-tuple-element.108.dpre_b_ref, bf16[1536,512]{1,0:T(8,128)(2,1)S(1)} %get-tuple-element.93.cot_ref, bf16[1536,512]{1,0:T(8,128)(2,1)S(1)} %get-tuple-element.111.w1_ref, ...), custom_call_target="tpu_custom_call" | custom-call | tf_op jit(solution)/shard_map/edge/pallas_call | solution.py:530
  44.6 3.0 %collective-permute-start.11 = (bf16[192,512]{1,0:T(8,128)(2,1)S(1)}, bf16[192,512]{1,0:T(8,128)(2,1)S(1)}, u32[]{:S(2)}, u32[]{:S(2)}) collective-permute-start(bf16[192,512]{1,0:T(8,128)(2,1)S(1)} %get-tuple-element.137), channel_id=1, source_target_pairs={{0,8},{1,9},{2,10},{3,11},{4,12},{5,13},{6,14},{7,15},{8,0},{9,1},... | collective-permute-start | bytes 589832 | tf_op jit(solution)/shard_map/ppermute | solution.py:543
  47.6 2.7 %collective-permute-done.9.refs_1_ = bf16[272,512]{1,0:T(8,128)(2,1)S(1)} collective-permute-done((bf16[272,512]{1,0:T(8,128)(2,1)S(1)}, bf16[272,512]{1,0:T(8,128)(2,1)S(1)}, u32[]{:S(2)}, u32[]{:S(2)}) %collective-permute-start.9) | collective-permute-done | bytes 278560 | tf_op jit(solution)/shard_map/ppermute | solution.py:543
  50.6 2.7 %collective-permute-start.12 = (bf16[144,512]{1,0:T(8,128)(2,1)S(1)}, bf16[144,512]{1,0:T(8,128)(2,1)S(1)}, u32[]{:S(2)}, u32[]{:S(2)}) collective-permute-start(bf16[144,512]{1,0:T(8,128)(2,1)S(1)} %get-tuple-element.143), channel_id=1, source_target_pairs={{0,4},{1,5},{2,6},{3,7},{4,0},{5,1},{6,2},{7,3},{8,12},{9,13},{10,... | collective-permute-start | bytes 442376 | tf_op jit(solution)/shard_map/ppermute | solution.py:543
  53.3 2.5 %collective-permute-done.10.refs_1_ = bf16[256,512]{1,0:T(8,128)(2,1)S(1)} collective-permute-done((bf16[256,512]{1,0:T(8,128)(2,1)S(1)}, bf16[256,512]{1,0:T(8,128)(2,1)S(1)}, u32[]{:S(2)}, u32[]{:S(2)}) %collective-permute-start.10) | collective-permute-done | bytes 262176 | tf_op jit(solution)/shard_map/ppermute | solution.py:543
  55.9 1.7 %collective-permute-start.14 = (bf16[128,512]{1,0:T(8,128)(2,1)S(1)}, bf16[128,512]{1,0:T(8,128)(2,1)S(1)}, u32[]{:S(2)}, u32[]{:S(2)}) collective-permute-start(bf16[128,512]{1,0:T(8,128)(2,1)S(1)} %get-tuple-element.145), channel_id=1, source_target_pairs={{0,4},{1,5},{2,6},{3,7},{4,0},{5,1},{6,2},{7,3},{8,12},{9,13},{10,... | collective-permute-start | bytes 393224 | tf_op jit(solution)/shard_map/ppermute | solution.py:543
  57.6 1.3 %collective-permute-start.15 = (bf16[96,512]{1,0:T(8,128)(2,1)S(1)}, bf16[96,512]{1,0:T(8,128)(2,1)S(1)}, u32[]{:S(2)}, u32[]{:S(2)}) collective-permute-start(bf16[96,512]{1,0:T(8,128)(2,1)S(1)} %get-tuple-element.147), channel_id=1, source_target_pairs={{0,2},{1,3},{2,0},{3,1},{4,6},{5,7},{6,4},{7,5},{8,10},{9,11},{10,... | collective-permute-start | bytes 294920 | tf_op jit(solution)/shard_map/ppermute | solution.py:543
  58.9 1.9 %collective-permute-done.12.refs_1_ = bf16[144,512]{1,0:T(8,128)(2,1)S(1)} collective-permute-done((bf16[144,512]{1,0:T(8,128)(2,1)S(1)}, bf16[144,512]{1,0:T(8,128)(2,1)S(1)}, u32[]{:S(2)}, u32[]{:S(2)}) %collective-permute-start.12) | collective-permute-done | bytes 147488 | tf_op jit(solution)/shard_map/ppermute | solution.py:543
  61.4 1.5 %collective-permute-done.14.refs_1_ = bf16[128,512]{1,0:T(8,128)(2,1)S(1)} collective-permute-done((bf16[128,512]{1,0:T(8,128)(2,1)S(1)}, bf16[128,512]{1,0:T(8,128)(2,1)S(1)}, u32[]{:S(2)}, u32[]{:S(2)}) %collective-permute-start.14) | collective-permute-done | bytes 131104 | tf_op jit(solution)/shard_map/ppermute | solution.py:543
  62.9 2.2 %collective-permute-start.16 = (bf16[64,512]{1,0:T(8,128)(2,1)S(1)}, bf16[64,512]{1,0:T(8,128)(2,1)S(1)}, u32[]{:S(2)}, u32[]{:S(2)}) collective-permute-start(bf16[64,512]{1,0:T(8,128)(2,1)S(1)} %get-tuple-element.159), channel_id=1, source_target_pairs={{0,8},{1,9},{2,10},{3,11},{4,12},{5,13},{6,14},{7,15},{8,0},{9,1},... | collective-permute-start | bytes 196616 | tf_op jit(solution)/shard_map/ppermute | solution.py:543
  65.6 3.2 %collective-permute-done.13.got_ref.refs_4_ = bf16[80,512]{1,0:T(8,128)(2,1)S(1)} collective-permute-done((bf16[80,512]{1,0:T(8,128)(2,1)S(1)}, bf16[80,512]{1,0:T(8,128)(2,1)S(1)}, u32[]{:S(2)}, u32[]{:S(2)}) %collective-permute-start.13) | collective-permute-done | bytes 81952 | tf_op jit(solution)/shard_map/ppermute | solution.py:543
  (33 shorter events, 6.1 us)
Async XLA Ops:
  2.5 14.0 %all-to-all-start = ((bf16[16,2,512]{2,1,0:T(2,128)(2,1)}), bf16[16,2,512]{2,1,0:T(2,128)(2,1)S(1)}, u32[]{:S(2)}, u32[]{:S(2)}) async-start(bf16[16,2,512]{2,1,0:T(2,128)(2,1)} %get-tuple-element.87), calls=%async_computation | async-start | bytes 65536 | tf_op jit(solution)/shard_map/all_to_all | solution.py:619
  9.8 6.6 %collective-permute-start = (bf16[64,512]{1,0:T(8,128)(2,1)}, bf16[64,512]{1,0:T(8,128)(2,1)S(1)}, u32[]{:S(2)}, u32[]{:S(2)}) collective-permute-start(bf16[64,512]{1,0:T(8,128)(2,1)} %get-tuple-element.85), channel_id=1, source_target_pairs={{0,1},{1,0},{2,3},{3,2},{4,5},{5,4},{6,7},{7,6},{8,9},{9,8},{10,11... | collective-permute-start | bytes 196616 | tf_op jit(solution)/shard_map/ppermute | solution.py:617
  10.2 6.2 %collective-permute-start.1 = (bf16[64,512]{1,0:T(8,128)(2,1)}, bf16[64,512]{1,0:T(8,128)(2,1)}, u32[]{:S(2)}, u32[]{:S(2)}) collective-permute-start(bf16[64,512]{1,0:T(8,128)(2,1)} %get-tuple-element.86), channel_id=1, source_target_pairs={{1,2},{2,1},{3,4},{4,3},{5,6},{6,5},{7,8},{8,7},{9,10},{10,9},{11,... | collective-permute-start | bytes 196616 | tf_op jit(solution)/shard_map/ppermute | solution.py:618
  25.4 3.5 %collective-permute-start.2 = (bf16[768,512]{1,0:T(8,128)(2,1)S(1)}, bf16[768,512]{1,0:T(8,128)(2,1)S(1)}, u32[]{:S(2)}, u32[]{:S(2)}) collective-permute-start(bf16[768,512]{1,0:T(8,128)(2,1)S(1)} %get-tuple-element.105), channel_id=1, source_target_pairs={{0,1},{1,0},{2,3},{3,2},{4,5},{5,4},{6,7},{7,6},{8,9},{9,8},{10,11... | collective-permute-start | bytes 2359304 | tf_op jit(solution)/shard_map/ppermute | solution.py:543
  31.1 6.5 %collective-permute-start.3 = (bf16[256,512]{1,0:T(8,128)(2,1)S(1)}, bf16[256,512]{1,0:T(8,128)(2,1)S(1)}, u32[]{:S(2)}, u32[]{:S(2)}) collective-permute-start(bf16[256,512]{1,0:T(8,128)(2,1)S(1)} %get-tuple-element.119), channel_id=1, source_target_pairs={{0,1},{1,0},{2,3},{3,2},{4,5},{5,4},{6,7},{7,6},{8,9},{9,8},{10,11... | collective-permute-start | bytes 786440 | tf_op jit(solution)/shard_map/ppermute | solution.py:543
  31.5 13.0 %collective-permute-start.8 = (bf16[384,512]{1,0:T(8,128)(2,1)S(1)}, bf16[384,512]{1,0:T(8,128)(2,1)S(1)}, u32[]{:S(2)}, u32[]{:S(2)}) collective-permute-start(bf16[384,512]{1,0:T(8,128)(2,1)S(1)} %get-tuple-element.106), channel_id=1, source_target_pairs={{0,4},{1,5},{2,6},{3,7},{4,0},{5,1},{6,2},{7,3},{8,12},{9,13},{10,... | collective-permute-start | bytes 1179656 | tf_op jit(solution)/shard_map/ppermute | solution.py:543
  37.6 4.9 %collective-permute-start.6 = (bf16[320,512]{1,0:T(8,128)(2,1)S(1)}, bf16[320,512]{1,0:T(8,128)(2,1)S(1)}, u32[]{:S(2)}, u32[]{:S(2)}) collective-permute-start(bf16[320,512]{1,0:T(8,128)(2,1)S(1)} %get-tuple-element.126), channel_id=1, source_target_pairs={{0,1},{1,0},{2,3},{3,2},{4,5},{5,4},{6,7},{7,6},{8,9},{9,8},{10,11... | collective-permute-start | bytes 983048 | tf_op jit(solution)/shard_map/ppermute | solution.py:543
  37.7 2.3 %collective-permute-start.4 = (bf16[272,512]{1,0:T(8,128)(2,1)S(1)}, bf16[272,512]{1,0:T(8,128)(2,1)S(1)}, u32[]{:S(2)}, u32[]{:S(2)}) collective-permute-start(bf16[272,512]{1,0:T(8,128)(2,1)S(1)} %get-tuple-element.120), channel_id=1, source_target_pairs={{0,1},{1,0},{2,3},{3,2},{4,5},{5,4},{6,7},{7,6},{8,9},{9,8},{10,11... | collective-permute-start | bytes 835592 | tf_op jit(solution)/shard_map/ppermute | solution.py:543
  38.1 1.9 %collective-permute-start.5 = (bf16[256,512]{1,0:T(8,128)(2,1)S(1)}, bf16[256,512]{1,0:T(8,128)(2,1)S(1)}, u32[]{:S(2)}, u32[]{:S(2)}) collective-permute-start(bf16[256,512]{1,0:T(8,128)(2,1)S(1)} %get-tuple-element.121), channel_id=1, source_target_pairs={{0,1},{1,0},{2,3},{3,2},{4,5},{5,4},{6,7},{7,6},{8,9},{9,8},{10,11... | collective-permute-start | bytes 786440 | tf_op jit(solution)/shard_map/ppermute | solution.py:543
  38.2 6.3 %collective-permute-start.7 = (bf16[64,512]{1,0:T(8,128)(2,1)S(1)}, bf16[64,512]{1,0:T(8,128)(2,1)S(1)}, u32[]{:S(2)}, u32[]{:S(2)}) collective-permute-start(bf16[64,512]{1,0:T(8,128)(2,1)S(1)} %get-tuple-element.132), channel_id=1, source_target_pairs={{1,2},{2,1},{3,4},{4,3},{5,6},{6,5},{7,8},{8,7},{9,10},{10,9},{11,... | collective-permute-start | bytes 196616 | tf_op jit(solution)/shard_map/ppermute | solution.py:731
  40.3 10.0 %collective-permute-start.9 = (bf16[272,512]{1,0:T(8,128)(2,1)S(1)}, bf16[272,512]{1,0:T(8,128)(2,1)S(1)}, u32[]{:S(2)}, u32[]{:S(2)}) collective-permute-start(bf16[272,512]{1,0:T(8,128)(2,1)S(1)} %get-tuple-element.123), channel_id=1, source_target_pairs={{0,2},{1,3},{2,0},{3,1},{4,6},{5,7},{6,4},{7,5},{8,10},{9,11},{10,... | collective-permute-start | bytes 835592 | tf_op jit(solution)/shard_map/ppermute | solution.py:543
  42.6 13.2 %collective-permute-start.10 = (bf16[256,512]{1,0:T(8,128)(2,1)S(1)}, bf16[256,512]{1,0:T(8,128)(2,1)S(1)}, u32[]{:S(2)}, u32[]{:S(2)}) collective-permute-start(bf16[256,512]{1,0:T(8,128)(2,1)S(1)} %get-tuple-element.127), channel_id=1, source_target_pairs={{0,2},{1,3},{2,0},{3,1},{4,6},{5,7},{6,4},{7,5},{8,10},{9,11},{10,... | collective-permute-start | bytes 786440 | tf_op jit(solution)/shard_map/ppermute | solution.py:543
  44.6 13.0 %collective-permute-start.11 = (bf16[192,512]{1,0:T(8,128)(2,1)S(1)}, bf16[192,512]{1,0:T(8,128)(2,1)S(1)}, u32[]{:S(2)}, u32[]{:S(2)}) collective-permute-start(bf16[192,512]{1,0:T(8,128)(2,1)S(1)} %get-tuple-element.137), channel_id=1, source_target_pairs={{0,8},{1,9},{2,10},{3,11},{4,12},{5,13},{6,14},{7,15},{8,0},{9,1},... | collective-permute-start | bytes 589832 | tf_op jit(solution)/shard_map/ppermute | solution.py:543
  50.6 10.2 %collective-permute-start.12 = (bf16[144,512]{1,0:T(8,128)(2,1)S(1)}, bf16[144,512]{1,0:T(8,128)(2,1)S(1)}, u32[]{:S(2)}, u32[]{:S(2)}) collective-permute-start(bf16[144,512]{1,0:T(8,128)(2,1)S(1)} %get-tuple-element.143), channel_id=1, source_target_pairs={{0,4},{1,5},{2,6},{3,7},{4,0},{5,1},{6,2},{7,3},{8,12},{9,13},{10,... | collective-permute-start | bytes 442376 | tf_op jit(solution)/shard_map/ppermute | solution.py:543
  55.9 7.0 %collective-permute-start.14 = (bf16[128,512]{1,0:T(8,128)(2,1)S(1)}, bf16[128,512]{1,0:T(8,128)(2,1)S(1)}, u32[]{:S(2)}, u32[]{:S(2)}) collective-permute-start(bf16[128,512]{1,0:T(8,128)(2,1)S(1)} %get-tuple-element.145), channel_id=1, source_target_pairs={{0,4},{1,5},{2,6},{3,7},{4,0},{5,1},{6,2},{7,3},{8,12},{9,13},{10,... | collective-permute-start | bytes 393224 | tf_op jit(solution)/shard_map/ppermute | solution.py:543
  57.6 12.0 %collective-permute-start.15 = (bf16[96,512]{1,0:T(8,128)(2,1)S(1)}, bf16[96,512]{1,0:T(8,128)(2,1)S(1)}, u32[]{:S(2)}, u32[]{:S(2)}) collective-permute-start(bf16[96,512]{1,0:T(8,128)(2,1)S(1)} %get-tuple-element.147), channel_id=1, source_target_pairs={{0,2},{1,3},{2,0},{3,1},{4,6},{5,7},{6,4},{7,5},{8,10},{9,11},{10,... | collective-permute-start | bytes 294920 | tf_op jit(solution)/shard_map/ppermute | solution.py:543
  61.1 7.6 %collective-permute-start.13 = (bf16[80,512]{1,0:T(8,128)(2,1)S(1)}, bf16[80,512]{1,0:T(8,128)(2,1)S(1)}, u32[]{:S(2)}, u32[]{:S(2)}) collective-permute-start(bf16[80,512]{1,0:T(8,128)(2,1)S(1)} %get-tuple-element.153), channel_id=1, source_target_pairs={{0,8},{1,9},{2,10},{3,11},{4,12},{5,13},{6,14},{7,15},{8,0},{9,1},... | collective-permute-start | bytes 245768 | tf_op jit(solution)/shard_map/ppermute | solution.py:543
  61.4 3.7 %copy-start = (s32[1,16,2]{1,2,0:T(2,128)S(1)}, s32[1,16,2]{1,2,0:T(2,128)}, u32[]{:S(2)}) copy-start(s32[1,16,2]{1,2,0:T(2,128)} %param.32) | copy-start | bytes 388
  62.9 6.7 %collective-permute-start.16 = (bf16[64,512]{1,0:T(8,128)(2,1)S(1)}, bf16[64,512]{1,0:T(8,128)(2,1)S(1)}, u32[]{:S(2)}, u32[]{:S(2)}) collective-permute-start(bf16[64,512]{1,0:T(8,128)(2,1)S(1)} %get-tuple-element.159), channel_id=1, source_target_pairs={{0,8},{1,9},{2,10},{3,11},{4,12},{5,13},{6,14},{7,15},{8,0},{9,1},... | collective-permute-start | bytes 196616 | tf_op jit(solution)/shard_map/ppermute | solution.py:543

commit v14 on v12

--- a/solution.py
+++ b/solution.py
@@ -257,11 +257,11 @@
         else:
             summed[...] += part
 
-    for step in range(steps + 1):
+    for step in range(steps + 2):
         if step < steps:
             activate(step)
-        if step > 0:
-            normalize(step - 1)
+        if step > 1:
+            normalize(step - 2)
 
     for copy in late:
         copy.wait()

time: 70 us -> 70.1 us (level)
  no operation moved by 1% of the time
where the time goes in v14:
time: 70.1 us; the launch traced here: 69.9 us
  Pallas kernels  27.8 us (40%)
  starting transfers between devices  27.2 us (39%)
  waiting for transfers between devices  14.2 us (20%)
  between operations  0.75 us (1%)
    pallas_call x19, Pallas kernels, call(): pl.pallas_call(kernel, in_specs=[pl.BlockSpec(memory_space=pltpu.HBM)] *...  27.8 us
    ppermute x14, starting transfers between devices, swap(): return lax.ppermute(send, 'tiles', [(i, i ^ bit) for i in range(tiles)])  17.5 us
    ppermute x14, waiting for transfers between devices, swap(): return lax.ppermute(send, 'tiles', [(i, i ^ bit) for i in range(tiles)])  13 us
    all_to_all x1, starting transfers between devices, shards(): lax.all_to_all(outgoing, 'tiles', split_axis=0, concat_axis=0, tiled=True)  7.37 us
  transfers between devices with their start and end apart: 18, of which 8 were waited for; matrix products, arithmetic and copies ran while one was open for 0% of the time, Pallas kernels for 20%

profile of v14, /device:TPU:0, one launch (start us, length us, event | category | flops | bytes accessed | tf_op | source)
XLA Modules:
  0.0 69.9 jit_solution(16312588447853396985)
XLA Ops:
  0.6 1.8 %outgoing.1 = (bf16[16,2,512]{2,1,0:T(2,128)(2,1)}, bf16[64,512]{1,0:T(8,128)(2,1)}, bf16[64,512]{1,0:T(8,128)(2,1)}) custom-call(s32[1,2,16]{2,1,0:T(2,128)} %bitcast.9, bf16[256,512]{1,0:T(8,128)(2,1)} %node_hbm.3), custom_call_target="tpu_custom_call" | custom-call | tf_op jit(solution)/shard_map/outgoing/pallas_call | solution.py:528
  2.5 7.4 %all-to-all-start = ((bf16[16,2,512]{2,1,0:T(2,128)(2,1)}), bf16[16,2,512]{2,1,0:T(2,128)(2,1)S(1)}, u32[]{:S(2)}, u32[]{:S(2)}) async-start(bf16[16,2,512]{2,1,0:T(2,128)(2,1)} %get-tuple-element.87), calls=%async_computation | async-start | bytes 65536 | tf_op jit(solution)/shard_map/all_to_all | solution.py:617
  10.2 1.3 %collective-permute-start.1 = (bf16[64,512]{1,0:T(8,128)(2,1)}, bf16[64,512]{1,0:T(8,128)(2,1)}, u32[]{:S(2)}, u32[]{:S(2)}) collective-permute-start(bf16[64,512]{1,0:T(8,128)(2,1)} %get-tuple-element.86), channel_id=1, source_target_pairs={{1,2},{2,1},{3,4},{4,3},{5,6},{6,5},{7,8},{8,7},{9,10},{10,9},{11,... | collective-permute-start | bytes 196616 | tf_op jit(solution)/shard_map/ppermute | solution.py:616
  11.5 3.8 %prepare.1 = (bf16[256,512]{1,0:T(8,128)(2,1)S(1)}, s32[12,128]{1,0:T(8,128)S(1)}, s32[12,128]{1,0:T(8,128)S(1)}, f32[1536,512]{1,0:T(8,128)S(1)}) custom-call(bf16[256,512]{1,0:T(8,128)(2,1)} %node_hbm.3, bf16[1536,512]{1,0:T(8,128)(2,1)} %w1_hbm.3, s32[12,128]{1,0:T(8,128)} %bitcast.16, s32[12,128]{1,0:T(8,128)} %bitcast.17, f32[1,512]{1,0:T(1,128)} %bitcast.18, ...), custom_call_target="tpu_custom_call" | custom-call | flops 10000000000 | bytes 100000000 | tf_op jit(solution)/shard_map/prepare/pallas_call | solution.py:528
  15.4 1.1 %all-to-all-done.far_ref = bf16[16,2,512]{2,1,0:T(2,128)(2,1)S(1)} async-done(((bf16[16,2,512]{2,1,0:T(2,128)(2,1)}), bf16[16,2,512]{2,1,0:T(2,128)(2,1)S(1)}, u32[]{:S(2)}, u32[]{:S(2)}) %all-to-all-start) | async-done | bytes 32800 | tf_op jit(solution)/shard_map/all_to_all | solution.py:617
  16.5 9.2 %forward.1 = (bf16[1536,512]{1,0:T(8,128)(2,1)S(1)}, bf16[1536,512]{1,0:T(8,128)(2,1)S(1)}, bf16[1536,512]{1,0:T(8,128)(2,1)S(1)}, bf16[512,512]{1,0:T(8,128)(2,...) custom-call(bf16[1536,512]{1,0:T(8,128)(2,1)} %w1_hbm.3, ...), custom_call_target="tpu_custom_call" | custom-call | tf_op jit(solution)/shard_map/forward/pallas_call | solution.py:528
  25.6 1.5 %collective-permute-start.2 = (bf16[768,512]{1,0:T(8,128)(2,1)S(1)}, bf16[768,512]{1,0:T(8,128)(2,1)S(1)}, u32[]{:S(2)}, u32[]{:S(2)}) collective-permute-start(bf16[768,512]{1,0:T(8,128)(2,1)S(1)} %get-tuple-element.105), channel_id=1, source_target_pairs={{0,1},{1,0},{2,3},{3,2},{4,5},{5,4},{6,7},{7,6},{8,9},{9,8},{10,11... | collective-permute-start | bytes 2359304 | tf_op jit(solution)/shard_map/ppermute | solution.py:541
  27.1 1.7 %slope.2 = (bf16[768,512]{1,0:T(8,128)(2,1)S(1)}, f32[512,512]{1,0:T(8,128)S(1)}) custom-call(bf16[1536,512]{1,0:T(8,128)(2,1)S(1)} %get-tuple-element.93.cot_ref, s32[12,128]{1,0:T(8,128)S(1)} %get-tuple-element.91.receiver_ref, bf16[256,512]{1,0:T(8,128)(2,1)S(1)} %get-tuple-element.107.dsum_ref, bf16[1536,512]{1,0:T(8,128)(2,1)S(1)} %get-tuple-element.95.hidden_ref, ...), custom_call_target="tpu_custom_call" | custom-call | tf_op jit(solution)/shard_map/slope/pallas_call | solution.py:528
  29.2 1.9 %slope.3 = (bf16[768,512]{1,0:T(8,128)(2,1)S(1)}, bf16[256,512]{1,0:T(8,128)(2,1)S(1)}, f32[8,32,512]{2,1,0:T(8,128)S(1)}) custom-call(bf16[1536,512]{1,0:T(8,128)(2,1)S(1)} %get-tuple-element.93.cot_ref, s32[12,128]{1,0:T(8,128)S(1)} %get-tuple-element.91.receiver_ref, bf16[256,512]{1,0:T(8,128)(2,1)S(1)} %get-tuple-element.107.dsum_ref, ...), custom_call_target="tpu_custom_call" | custom-call | tf_op jit(solution)/shard_map/slope/pallas_call | solution.py:528
  31.5 1.5 %collective-permute-start.8 = (bf16[384,512]{1,0:T(8,128)(2,1)S(1)}, bf16[384,512]{1,0:T(8,128)(2,1)S(1)}, u32[]{:S(2)}, u32[]{:S(2)}) collective-permute-start(bf16[384,512]{1,0:T(8,128)(2,1)S(1)} %get-tuple-element.106), channel_id=1, source_target_pairs={{0,4},{1,5},{2,6},{3,7},{4,0},{5,1},{6,2},{7,3},{8,12},{9,13},{10,... | collective-permute-start | bytes 1179656 | tf_op jit(solution)/shard_map/ppermute | solution.py:541
  33.0 4.0 %first.1 = (bf16[64,512]{1,0:T(8,128)(2,1)}, bf16[64,512]{1,0:T(8,128)(2,1)S(1)}, bf16[32,512]{1,0:T(8,128)(2,1)S(1)}, bf16[512,512]{1,0:T(8,128)(2,1)S(1)}, bf1...) custom-call(bf16[768,512]{1,0:T(8,128)(2,1)S(1)} %get-tuple-element., ...), custom_call_target="tpu_custom_call" | custom-call | tf_op jit(solution)/shard_map/first/pallas_call | solution.py:528
  38.3 1.1 %collective-permute-done.5.refs_3_ = bf16[256,512]{1,0:T(8,128)(2,1)S(1)} collective-permute-done((bf16[256,512]{1,0:T(8,128)(2,1)S(1)}, bf16[256,512]{1,0:T(8,128)(2,1)S(1)}, u32[]{:S(2)}, u32[]{:S(2)}) %collective-permute-start.5) | collective-permute-done | bytes 262176 | tf_op jit(solution)/shard_map/ppermute | solution.py:541
  39.7 2.2 %collective-permute-start.9 = (bf16[272,512]{1,0:T(8,128)(2,1)S(1)}, bf16[272,512]{1,0:T(8,128)(2,1)S(1)}, u32[]{:S(2)}, u32[]{:S(2)}) collective-permute-start(bf16[272,512]{1,0:T(8,128)(2,1)S(1)} %get-tuple-element.123), channel_id=1, source_target_pairs={{0,2},{1,3},{2,0},{3,1},{4,6},{5,7},{6,4},{7,5},{8,10},{9,11},{10,... | collective-permute-start | bytes 835592 | tf_op jit(solution)/shard_map/ppermute | solution.py:541
  42.1 1.8 %edge.1 = (bf16[1536,512]{1,0:T(8,128)(2,1)}, f32[256,512]{1,0:T(8,128)S(1)}) custom-call(bf16[768,512]{1,0:T(8,128)(2,1)S(1)} %get-tuple-element.128.dpre_a_ref, bf16[768,512]{1,0:T(8,128)(2,1)S(1)} %get-tuple-element.108.dpre_b_ref, bf16[1536,512]{1,0:T(8,128)(2,1)S(1)} %get-tuple-element.93.cot_ref, bf16[1536,512]{1,0:T(8,128)(2,1)S(1)} %get-tuple-element.111.w1_ref, ...), custom_call_target="tpu_custom_call" | custom-call | tf_op jit(solution)/shard_map/edge/pallas_call | solution.py:528
  44.0 3.0 %collective-permute-start.11 = (bf16[192,512]{1,0:T(8,128)(2,1)S(1)}, bf16[192,512]{1,0:T(8,128)(2,1)S(1)}, u32[]{:S(2)}, u32[]{:S(2)}) collective-permute-start(bf16[192,512]{1,0:T(8,128)(2,1)S(1)} %get-tuple-element.137), channel_id=1, source_target_pairs={{0,8},{1,9},{2,10},{3,11},{4,12},{5,13},{6,14},{7,15},{8,0},{9,1},... | collective-permute-start | bytes 589832 | tf_op jit(solution)/shard_map/ppermute | solution.py:541
  47.0 2.7 %collective-permute-done.9.refs_1_ = bf16[272,512]{1,0:T(8,128)(2,1)S(1)} collective-permute-done((bf16[272,512]{1,0:T(8,128)(2,1)S(1)}, bf16[272,512]{1,0:T(8,128)(2,1)S(1)}, u32[]{:S(2)}, u32[]{:S(2)}) %collective-permute-start.9) | collective-permute-done | bytes 278560 | tf_op jit(solution)/shard_map/ppermute | solution.py:541
  50.0 2.7 %collective-permute-start.12 = (bf16[144,512]{1,0:T(8,128)(2,1)S(1)}, bf16[144,512]{1,0:T(8,128)(2,1)S(1)}, u32[]{:S(2)}, u32[]{:S(2)}) collective-permute-start(bf16[144,512]{1,0:T(8,128)(2,1)S(1)} %get-tuple-element.143), channel_id=1, source_target_pairs={{0,4},{1,5},{2,6},{3,7},{4,0},{5,1},{6,2},{7,3},{8,12},{9,13},{10,... | collective-permute-start | bytes 442376 | tf_op jit(solution)/shard_map/ppermute | solution.py:541
  52.7 2.5 %collective-permute-done.10.refs_1_ = bf16[256,512]{1,0:T(8,128)(2,1)S(1)} collective-permute-done((bf16[256,512]{1,0:T(8,128)(2,1)S(1)}, bf16[256,512]{1,0:T(8,128)(2,1)S(1)}, u32[]{:S(2)}, u32[]{:S(2)}) %collective-permute-start.10) | collective-permute-done | bytes 262176 | tf_op jit(solution)/shard_map/ppermute | solution.py:541
  55.3 1.9 %collective-permute-start.14 = (bf16[128,512]{1,0:T(8,128)(2,1)S(1)}, bf16[128,512]{1,0:T(8,128)(2,1)S(1)}, u32[]{:S(2)}, u32[]{:S(2)}) collective-permute-start(bf16[128,512]{1,0:T(8,128)(2,1)S(1)} %get-tuple-element.145), channel_id=1, source_target_pairs={{0,4},{1,5},{2,6},{3,7},{4,0},{5,1},{6,2},{7,3},{8,12},{9,13},{10,... | collective-permute-start | bytes 393224 | tf_op jit(solution)/shard_map/ppermute | solution.py:541
  57.2 1.2 %collective-permute-start.15 = (bf16[96,512]{1,0:T(8,128)(2,1)S(1)}, bf16[96,512]{1,0:T(8,128)(2,1)S(1)}, u32[]{:S(2)}, u32[]{:S(2)}) collective-permute-start(bf16[96,512]{1,0:T(8,128)(2,1)S(1)} %get-tuple-element.147), channel_id=1, source_target_pairs={{0,2},{1,3},{2,0},{3,1},{4,6},{5,7},{6,4},{7,5},{8,10},{9,11},{10,... | collective-permute-start | bytes 294920 | tf_op jit(solution)/shard_map/ppermute | solution.py:541
  58.4 1.8 %collective-permute-done.12.refs_1_ = bf16[144,512]{1,0:T(8,128)(2,1)S(1)} collective-permute-done((bf16[144,512]{1,0:T(8,128)(2,1)S(1)}, bf16[144,512]{1,0:T(8,128)(2,1)S(1)}, u32[]{:S(2)}, u32[]{:S(2)}) %collective-permute-start.12) | collective-permute-done | bytes 147488 | tf_op jit(solution)/shard_map/ppermute | solution.py:541
  60.8 1.4 %collective-permute-done.14.refs_1_ = bf16[128,512]{1,0:T(8,128)(2,1)S(1)} collective-permute-done((bf16[128,512]{1,0:T(8,128)(2,1)S(1)}, bf16[128,512]{1,0:T(8,128)(2,1)S(1)}, u32[]{:S(2)}, u32[]{:S(2)}) %collective-permute-start.14) | collective-permute-done | bytes 131104 | tf_op jit(solution)/shard_map/ppermute | solution.py:541
  62.3 2.2 %collective-permute-start.16 = (bf16[64,512]{1,0:T(8,128)(2,1)S(1)}, bf16[64,512]{1,0:T(8,128)(2,1)S(1)}, u32[]{:S(2)}, u32[]{:S(2)}) collective-permute-start(bf16[64,512]{1,0:T(8,128)(2,1)S(1)} %get-tuple-element.159), channel_id=1, source_target_pairs={{0,8},{1,9},{2,10},{3,11},{4,12},{5,13},{6,14},{7,15},{8,0},{9,1},... | collective-permute-start | bytes 196616 | tf_op jit(solution)/shard_map/ppermute | solution.py:541
  65.0 3.2 %collective-permute-done.13.got_ref.refs_4_ = bf16[80,512]{1,0:T(8,128)(2,1)S(1)} collective-permute-done((bf16[80,512]{1,0:T(8,128)(2,1)S(1)}, bf16[80,512]{1,0:T(8,128)(2,1)S(1)}, u32[]{:S(2)}, u32[]{:S(2)}) %collective-permute-start.13) | collective-permute-done | bytes 81952 | tf_op jit(solution)/shard_map/ppermute | solution.py:541
  (33 shorter events, 6.3 us)
Async XLA Ops:
  2.5 14.0 %all-to-all-start = ((bf16[16,2,512]{2,1,0:T(2,128)(2,1)}), bf16[16,2,512]{2,1,0:T(2,128)(2,1)S(1)}, u32[]{:S(2)}, u32[]{:S(2)}) async-start(bf16[16,2,512]{2,1,0:T(2,128)(2,1)} %get-tuple-element.87), calls=%async_computation | async-start | bytes 65536 | tf_op jit(solution)/shard_map/all_to_all | solution.py:617
  9.8 6.6 %collective-permute-start = (bf16[64,512]{1,0:T(8,128)(2,1)}, bf16[64,512]{1,0:T(8,128)(2,1)S(1)}, u32[]{:S(2)}, u32[]{:S(2)}) collective-permute-start(bf16[64,512]{1,0:T(8,128)(2,1)} %get-tuple-element.85), channel_id=1, source_target_pairs={{0,1},{1,0},{2,3},{3,2},{4,5},{5,4},{6,7},{7,6},{8,9},{9,8},{10,11... | collective-permute-start | bytes 196616 | tf_op jit(solution)/shard_map/ppermute | solution.py:615
  10.2 6.2 %collective-permute-start.1 = (bf16[64,512]{1,0:T(8,128)(2,1)}, bf16[64,512]{1,0:T(8,128)(2,1)}, u32[]{:S(2)}, u32[]{:S(2)}) collective-permute-start(bf16[64,512]{1,0:T(8,128)(2,1)} %get-tuple-element.86), channel_id=1, source_target_pairs={{1,2},{2,1},{3,4},{4,3},{5,6},{6,5},{7,8},{8,7},{9,10},{10,9},{11,... | collective-permute-start | bytes 196616 | tf_op jit(solution)/shard_map/ppermute | solution.py:616
  25.6 3.4 %collective-permute-start.2 = (bf16[768,512]{1,0:T(8,128)(2,1)S(1)}, bf16[768,512]{1,0:T(8,128)(2,1)S(1)}, u32[]{:S(2)}, u32[]{:S(2)}) collective-permute-start(bf16[768,512]{1,0:T(8,128)(2,1)S(1)} %get-tuple-element.105), channel_id=1, source_target_pairs={{0,1},{1,0},{2,3},{3,2},{4,5},{5,4},{6,7},{7,6},{8,9},{9,8},{10,11... | collective-permute-start | bytes 2359304 | tf_op jit(solution)/shard_map/ppermute | solution.py:541
  31.1 5.9 %collective-permute-start.3 = (bf16[256,512]{1,0:T(8,128)(2,1)S(1)}, bf16[256,512]{1,0:T(8,128)(2,1)S(1)}, u32[]{:S(2)}, u32[]{:S(2)}) collective-permute-start(bf16[256,512]{1,0:T(8,128)(2,1)S(1)} %get-tuple-element.119), channel_id=1, source_target_pairs={{0,1},{1,0},{2,3},{3,2},{4,5},{5,4},{6,7},{7,6},{8,9},{9,8},{10,11... | collective-permute-start | bytes 786440 | tf_op jit(solution)/shard_map/ppermute | solution.py:541
  31.5 12.4 %collective-permute-start.8 = (bf16[384,512]{1,0:T(8,128)(2,1)S(1)}, bf16[384,512]{1,0:T(8,128)(2,1)S(1)}, u32[]{:S(2)}, u32[]{:S(2)}) collective-permute-start(bf16[384,512]{1,0:T(8,128)(2,1)S(1)} %get-tuple-element.106), channel_id=1, source_target_pairs={{0,4},{1,5},{2,6},{3,7},{4,0},{5,1},{6,2},{7,3},{8,12},{9,13},{10,... | collective-permute-start | bytes 1179656 | tf_op jit(solution)/shard_map/ppermute | solution.py:541
  37.0 4.9 %collective-permute-start.6 = (bf16[320,512]{1,0:T(8,128)(2,1)S(1)}, bf16[320,512]{1,0:T(8,128)(2,1)S(1)}, u32[]{:S(2)}, u32[]{:S(2)}) collective-permute-start(bf16[320,512]{1,0:T(8,128)(2,1)S(1)} %get-tuple-element.126), channel_id=1, source_target_pairs={{0,1},{1,0},{2,3},{3,2},{4,5},{5,4},{6,7},{7,6},{8,9},{9,8},{10,11... | collective-permute-start | bytes 983048 | tf_op jit(solution)/shard_map/ppermute | solution.py:541
  37.1 2.3 %collective-permute-start.4 = (bf16[272,512]{1,0:T(8,128)(2,1)S(1)}, bf16[272,512]{1,0:T(8,128)(2,1)S(1)}, u32[]{:S(2)}, u32[]{:S(2)}) collective-permute-start(bf16[272,512]{1,0:T(8,128)(2,1)S(1)} %get-tuple-element.120), channel_id=1, source_target_pairs={{0,1},{1,0},{2,3},{3,2},{4,5},{5,4},{6,7},{7,6},{8,9},{9,8},{10,11... | collective-permute-start | bytes 835592 | tf_op jit(solution)/shard_map/ppermute | solution.py:541
  37.5 1.9 %collective-permute-start.5 = (bf16[256,512]{1,0:T(8,128)(2,1)S(1)}, bf16[256,512]{1,0:T(8,128)(2,1)S(1)}, u32[]{:S(2)}, u32[]{:S(2)}) collective-permute-start(bf16[256,512]{1,0:T(8,128)(2,1)S(1)} %get-tuple-element.121), channel_id=1, source_target_pairs={{0,1},{1,0},{2,3},{3,2},{4,5},{5,4},{6,7},{7,6},{8,9},{9,8},{10,11... | collective-permute-start | bytes 786440 | tf_op jit(solution)/shard_map/ppermute | solution.py:541
  37.6 6.3 %collective-permute-start.7 = (bf16[64,512]{1,0:T(8,128)(2,1)S(1)}, bf16[64,512]{1,0:T(8,128)(2,1)S(1)}, u32[]{:S(2)}, u32[]{:S(2)}) collective-permute-start(bf16[64,512]{1,0:T(8,128)(2,1)S(1)} %get-tuple-element.132), channel_id=1, source_target_pairs={{1,2},{2,1},{3,4},{4,3},{5,6},{6,5},{7,8},{8,7},{9,10},{10,9},{11,... | collective-permute-start | bytes 196616 | tf_op jit(solution)/shard_map/ppermute | solution.py:729
  39.7 10.0 %collective-permute-start.9 = (bf16[272,512]{1,0:T(8,128)(2,1)S(1)}, bf16[272,512]{1,0:T(8,128)(2,1)S(1)}, u32[]{:S(2)}, u32[]{:S(2)}) collective-permute-start(bf16[272,512]{1,0:T(8,128)(2,1)S(1)} %get-tuple-element.123), channel_id=1, source_target_pairs={{0,2},{1,3},{2,0},{3,1},{4,6},{5,7},{6,4},{7,5},{8,10},{9,11},{10,... | collective-permute-start | bytes 835592 | tf_op jit(solution)/shard_map/ppermute | solution.py:541
  42.0 13.2 %collective-permute-start.10 = (bf16[256,512]{1,0:T(8,128)(2,1)S(1)}, bf16[256,512]{1,0:T(8,128)(2,1)S(1)}, u32[]{:S(2)}, u32[]{:S(2)}) collective-permute-start(bf16[256,512]{1,0:T(8,128)(2,1)S(1)} %get-tuple-element.127), channel_id=1, source_target_pairs={{0,2},{1,3},{2,0},{3,1},{4,6},{5,7},{6,4},{7,5},{8,10},{9,11},{10,... | collective-permute-start | bytes 786440 | tf_op jit(solution)/shard_map/ppermute | solution.py:541
  44.0 13.1 %collective-permute-start.11 = (bf16[192,512]{1,0:T(8,128)(2,1)S(1)}, bf16[192,512]{1,0:T(8,128)(2,1)S(1)}, u32[]{:S(2)}, u32[]{:S(2)}) collective-permute-start(bf16[192,512]{1,0:T(8,128)(2,1)S(1)} %get-tuple-element.137), channel_id=1, source_target_pairs={{0,8},{1,9},{2,10},{3,11},{4,12},{5,13},{6,14},{7,15},{8,0},{9,1},... | collective-permute-start | bytes 589832 | tf_op jit(solution)/shard_map/ppermute | solution.py:541
  50.0 10.2 %collective-permute-start.12 = (bf16[144,512]{1,0:T(8,128)(2,1)S(1)}, bf16[144,512]{1,0:T(8,128)(2,1)S(1)}, u32[]{:S(2)}, u32[]{:S(2)}) collective-permute-start(bf16[144,512]{1,0:T(8,128)(2,1)S(1)} %get-tuple-element.143), channel_id=1, source_target_pairs={{0,4},{1,5},{2,6},{3,7},{4,0},{5,1},{6,2},{7,3},{8,12},{9,13},{10,... | collective-permute-start | bytes 442376 | tf_op jit(solution)/shard_map/ppermute | solution.py:541
  55.3 7.0 %collective-permute-start.14 = (bf16[128,512]{1,0:T(8,128)(2,1)S(1)}, bf16[128,512]{1,0:T(8,128)(2,1)S(1)}, u32[]{:S(2)}, u32[]{:S(2)}) collective-permute-start(bf16[128,512]{1,0:T(8,128)(2,1)S(1)} %get-tuple-element.145), channel_id=1, source_target_pairs={{0,4},{1,5},{2,6},{3,7},{4,0},{5,1},{6,2},{7,3},{8,12},{9,13},{10,... | collective-permute-start | bytes 393224 | tf_op jit(solution)/shard_map/ppermute | solution.py:541
  57.2 11.9 %collective-permute-start.15 = (bf16[96,512]{1,0:T(8,128)(2,1)S(1)}, bf16[96,512]{1,0:T(8,128)(2,1)S(1)}, u32[]{:S(2)}, u32[]{:S(2)}) collective-permute-start(bf16[96,512]{1,0:T(8,128)(2,1)S(1)} %get-tuple-element.147), channel_id=1, source_target_pairs={{0,2},{1,3},{2,0},{3,1},{4,6},{5,7},{6,4},{7,5},{8,10},{9,11},{10,... | collective-permute-start | bytes 294920 | tf_op jit(solution)/shard_map/ppermute | solution.py:541
  60.5 7.7 %collective-permute-start.13 = (bf16[80,512]{1,0:T(8,128)(2,1)S(1)}, bf16[80,512]{1,0:T(8,128)(2,1)S(1)}, u32[]{:S(2)}, u32[]{:S(2)}) collective-permute-start(bf16[80,512]{1,0:T(8,128)(2,1)S(1)} %get-tuple-element.153), channel_id=1, source_target_pairs={{0,8},{1,9},{2,10},{3,11},{4,12},{5,13},{6,14},{7,15},{8,0},{9,1},... | collective-permute-start | bytes 245768 | tf_op jit(solution)/shard_map/ppermute | solution.py:541
  60.8 3.7 %copy-start = (s32[1,16,2]{1,2,0:T(2,128)S(1)}, s32[1,16,2]{1,2,0:T(2,128)}, u32[]{:S(2)}) copy-start(s32[1,16,2]{1,2,0:T(2,128)} %param.32) | copy-start | bytes 388
  62.3 6.8 %collective-permute-start.16 = (bf16[64,512]{1,0:T(8,128)(2,1)S(1)}, bf16[64,512]{1,0:T(8,128)(2,1)S(1)}, u32[]{:S(2)}, u32[]{:S(2)}) collective-permute-start(bf16[64,512]{1,0:T(8,128)(2,1)S(1)} %get-tuple-element.159), channel_id=1, source_target_pairs={{0,8},{1,9},{2,10},{3,11},{4,12},{5,13},{6,14},{7,15},{8,0},{9,1},... | collective-permute-start | bytes 196616 | tf_op jit(solution)/shard_map/ppermute | solution.py:541
